TPU v7x, 128 devices: a whole 4x4x4 slice. The times are simulated.
128 devices in a mesh: rep: 16 (over z, y), ep: 8 (over x, core).
Axes of the slice: x: 4, y: 4, z: 4, core: 2. Of those that a mesh axis runs over, the one named last changes fastest.
Arguments:
- tokens: bfloat16 [32768, 1024], P(('rep', 'ep')), may hold values from -6 to 6
- segments: int32 [16, 2048], P('rep'), may hold values from 0 to 2, as said below
- routes: int32 [32768, 8], P(('rep', 'ep')), may hold values from 0 to 31, all different within a row; in each aligned block of 256 rows (0 to 255, 256 to 511, ...) at most 88 rows name the same one
- w_query: bfloat16 [1024, 1024], P(('rep', 'ep')), may hold values from -0.1875 to 0.1875
- w_key: bfloat16 [1024, 512], P(('rep', 'ep')), may hold values from -0.1875 to 0.1875
- w_value: bfloat16 [1024, 512], P(('rep', 'ep')), may hold values from -0.1875 to 0.1875
- w_out: bfloat16 [1024, 1024], P(('rep', 'ep')), may hold values from -1.5 to 1.5
- w_router: bfloat16 [1024, 32], P(('rep', 'ep')), may hold values from -0.09375 to 0.09375
- gain_attn: bfloat16 [1024], P(('rep', 'ep')), may hold values from 0.25 to 1.75
- gain_query: bfloat16 [1024], P(('rep', 'ep')), may hold values from 0.25 to 1.75
- gain_key: bfloat16 [512], P(('rep', 'ep')), may hold values from 0.25 to 1.75
- gain_ffn: bfloat16 [1024], P(('rep', 'ep')), may hold values from 0.25 to 1.75
- w_gate: bfloat16 [32, 1024, 512], P('ep'), may hold values from -0.1875 to 0.1875
- w_up: bfloat16 [32, 1024, 512], P('ep'), may hold values from -0.1875 to 0.1875
- w_down: bfloat16 [32, 512, 1024], P('ep'), may hold values from -1 to 1
- out_grad: bfloat16 [32768, 1024], P(('rep', 'ep')), may hold values from -6 to 6
Outputs:
- output: bfloat16 [32768, 1024], P(('rep', 'ep'))
- input_grad: float32 [32768, 1024], P(('rep', 'ep'))
- grad_query: float32 [1024, 1024], P(('rep', 'ep'))
- grad_key: float32 [1024, 512], P(('rep', 'ep'))
- grad_value: float32 [1024, 512], P(('rep', 'ep'))
- grad_out: float32 [1024, 1024], P(('rep', 'ep'))
- grad_router: float32 [1024, 32], P(('rep', 'ep'))
- grad_gain_attn: float32 [1024], P(('rep', 'ep'))
- grad_gain_query: float32 [1024], P(('rep', 'ep'))
- grad_gain_key: float32 [512], P(('rep', 'ep'))
- grad_gain_ffn: float32 [1024], P(('rep', 'ep'))
- grad_gate: float32 [32, 1024, 512], P('ep', 'rep')
- grad_up: float32 [32, 1024, 512], P('ep', 'rep')
- grad_down: float32 [32, 512, 1024], P('ep', 'rep')
Inputs may be any that keep to these rules, and one draw needn't show every extreme that they name: `routes`: each row names 8 different experts. In the rows of one device no expert is named more than 88 times, and that count is reached in every draw. `segments`: along each sequence the numbers never fall.
All inputs are finite; a program needn't handle non-finite values.
Results may differ from a plain program's by a relative error of at most 0.03.
Values may be sent and summed in bfloat16 or wider, within the bound.
A program may use at most 192 MiB of HBM per device.

v0:
```python
import jax
import jax.numpy as jnp
from jax import lax
from jax.sharding import PartitionSpec as P

HEADS = 16
KV_HEADS = 8
HEAD_DIM = 64
TOP = 8
WINDOW = 1024


EPSILON = 1e-06
ROPE_BASE = 10000.0
MASKED = -1e30


def shifted(block, axis, distance):
    devices = range(lax.axis_size(axis))
    route = [(i - distance, i) for i in devices if i - distance in devices]
    return lax.ppermute(block, axis, route)


def rms_scale(values):
    return lax.rsqrt(jnp.mean(values * values, axis=-1, keepdims=True) + EPSILON)


def norm_back(grad_normed, values, scaling, norm_gain):
    normal = values * scaling
    weighted = grad_normed * norm_gain
    grad_values = scaling * (
        weighted - normal * jnp.mean(weighted * normal, axis=-1, keepdims=True)
    )
    return (grad_values, jnp.sum(grad_normed * normal, axis=0))


def turn_tables(length, offset):
    halfway = HEAD_DIM // 2
    frequency = ROPE_BASE ** (-(jnp.arange(halfway, dtype=jnp.float32) * 2.0 / HEAD_DIM))
    places = (offset + jnp.arange(length, dtype=jnp.int32)).astype(jnp.float32)
    angles = places[:, None] * frequency[None, :]
    return (jnp.cos(angles)[:, None, :], jnp.sin(angles)[:, None, :])


def rotate(values, cosine, sine_part):
    halfway = HEAD_DIM // 2
    former = values[..., :halfway]
    latter = values[..., halfway:]
    return jnp.concatenate(
        [former * cosine - latter * sine_part, latter * cosine + former * sine_part], axis=-1
    )


def past_context(own_rows, reach_count):
    pieces = []
    for behind in range(reach_count, 0, -1):
        pieces.append(shifted(own_rows, "ep", behind))
    return jnp.concatenate(pieces + [own_rows], axis=0)


def past_context_again(own_rows, reach_count):
    pieces = []
    for behind in range(reach_count, 0, -1):
        pieces.append(shifted(own_rows, "ep", behind))
    return jnp.concatenate(pieces + [own_rows], axis=0)


def attention_scores(query_rot, context, allowed, kv_width):
    row_count = query_rot.shape[0]
    key_heads = context[:, :kv_width].reshape(context.shape[0], KV_HEADS, HEAD_DIM)
    grouped = query_rot.reshape(row_count, KV_HEADS, HEADS // KV_HEADS, HEAD_DIM)
    scores = jnp.einsum(
        "tgrd,kgd->grtk", grouped, key_heads, preferred_element_type=jnp.float32
    ) * HEAD_DIM ** (-0.5)
    return jnp.where(allowed, scores, MASKED)


def body(
    tokens,
    segments,
    routes,
    w_query,
    w_key,
    w_value,
    w_out,
    w_router,
    gain_attn,
    gain_query,
    gain_key,
    gain_ffn,
    w_gate,
    w_up,
    w_down,
    out_grad,
):
    group_size = lax.axis_size("ep")
    member = lax.axis_index("ep")
    row_count = tokens.shape[0]
    model_width = tokens.shape[1]
    kv_width = w_key.shape[1]
    local_experts = w_gate.shape[0]
    hidden_width = w_gate.shape[2]
    experts = local_experts * group_size
    capacity = 8 * (row_count * TOP * 4 // (24 * experts) + 1)
    reach_count = min((WINDOW - 2) // row_count + 1, group_size - 1)
    ratio_heads = HEADS // KV_HEADS
    scale_factor = HEAD_DIM ** (-0.5)
    contract_rows = (((0,), (0,)), ((), ()))
    contract_cols = (((1,), (1,)), ((), ()))
    shards = (w_query, w_key, w_value, w_out, w_router, gain_attn, gain_query, gain_key, gain_ffn)
    gathered = (
        lax.all_gather(shards[0], ("rep", "ep"), axis=0, tiled=True),
        lax.all_gather(shards[1], ("rep", "ep"), axis=0, tiled=True),
        lax.all_gather(shards[2], ("rep", "ep"), axis=0, tiled=True),
        lax.all_gather(shards[3], ("rep", "ep"), axis=0, tiled=True),
        lax.all_gather(shards[4], ("rep", "ep"), axis=0, tiled=True),
        lax.all_gather(shards[5], ("rep", "ep"), axis=0, tiled=True),
        lax.all_gather(shards[6], ("rep", "ep"), axis=0, tiled=True),
        lax.all_gather(shards[7], ("rep", "ep"), axis=0, tiled=True),
        lax.all_gather(shards[8], ("rep", "ep"), axis=0, tiled=True),
    )
    whole_query, whole_key, whole_value, whole_out, whole_router = gathered[:5]
    attn_gain = gathered[5].astype(jnp.float32)
    query_gain = gathered[6].astype(jnp.float32)
    key_gain = gathered[7].astype(jnp.float32)
    ffn_gain = gathered[8].astype(jnp.float32)
    inputs = tokens.astype(jnp.float32)
    scale_first = rms_scale(inputs)
    normed = (inputs * scale_first * attn_gain).astype(jnp.bfloat16)
    query_lin = jnp.dot(normed, whole_query, preferred_element_type=jnp.float32)
    key_lin = jnp.dot(normed, whole_key, preferred_element_type=jnp.float32)
    value_rows = jnp.dot(normed, whole_value, preferred_element_type=jnp.float32).astype(
        jnp.bfloat16
    )
    scale_query = rms_scale(query_lin)
    scale_key = rms_scale(key_lin)
    cosine, sine_part = turn_tables(row_count, member * row_count)
    query_rot = rotate(
        (query_lin * scale_query * query_gain).reshape(row_count, HEADS, HEAD_DIM),
        cosine,
        sine_part,
    ).astype(jnp.bfloat16)
    key_rot = rotate(
        (key_lin * scale_key * key_gain).reshape(row_count, KV_HEADS, HEAD_DIM), cosine, sine_part
    ).astype(jnp.bfloat16)
    own_rows = jnp.concatenate([key_rot.reshape(row_count, kv_width), value_rows], axis=1)
    context = past_context(own_rows, reach_count)
    key_count = context.shape[0]
    query_place = member * row_count + jnp.arange(row_count, dtype=jnp.int32)
    key_place = (member - reach_count) * row_count + jnp.arange(key_count, dtype=jnp.int32)
    sequence_seg = segments[0]
    query_seg = lax.dynamic_slice_in_dim(sequence_seg, member * row_count, row_count, 0)
    key_seg = sequence_seg[jnp.clip(key_place, 0, sequence_seg.shape[0] - 1)]
    distance = query_place[:, None] - key_place[None, :]
    allowed = (
        (distance >= 0)
        & (distance < WINDOW)
        & (key_place[None, :] >= 0)
        & (query_seg[:, None] == key_seg[None, :])
    )
    scores = attention_scores(query_rot, context, allowed, kv_width)
    score_peak = jnp.max(scores, axis=-1, keepdims=True)
    raised = jnp.exp(scores - score_peak)
    totals = jnp.sum(raised, axis=-1, keepdims=True)
    attn_probs = raised / totals
    log_total = score_peak + jnp.log(totals)
    value_heads = context[:, kv_width:].reshape(key_count, KV_HEADS, HEAD_DIM)
    attended = jnp.einsum(
        "grtk,kgd->tgrd",
        attn_probs.astype(jnp.bfloat16),
        value_heads,
        preferred_element_type=jnp.float32,
    )
    attended = attended.reshape(row_count, model_width).astype(jnp.bfloat16)
    hidden = inputs + jnp.dot(attended, whole_out, preferred_element_type=jnp.float32)
    scale_second = rms_scale(hidden)
    moe_in = (hidden * scale_second * ffn_gain).astype(jnp.bfloat16)
    logits = jnp.dot(moe_in, whole_router, preferred_element_type=jnp.float32)
    expert_ids = jnp.arange(experts, dtype=jnp.int32)
    route_hits = routes[:, :, None] == expert_ids[None, None, :]
    chosen = jnp.sum(jnp.where(route_hits, logits[:, None, :], 0.0), axis=2)
    lifted = jnp.exp(chosen - jnp.max(chosen, axis=1, keepdims=True))
    gate_weights = lifted / jnp.sum(lifted, axis=1, keepdims=True)
    flat_routes = routes.reshape(-1)
    one_hot = (flat_routes[:, None] == expert_ids[None, :]).astype(jnp.int32)
    slot_rank = jnp.sum((jnp.cumsum(one_hot, axis=0) - 1) * one_hot, axis=1)
    slot_index = flat_routes * capacity + slot_rank
    pair_count = row_count * TOP
    slot_pair = (
        jnp.full((experts * capacity,), -1, jnp.int32)
        .at[slot_index]
        .set(jnp.arange(pair_count, dtype=jnp.int32))
    )
    filled = slot_pair >= 0
    slot_source = jnp.maximum(slot_pair, 0)
    send_rows = jnp.where(filled[:, None], moe_in[slot_source // TOP], jnp.zeros((), jnp.bfloat16))
    send_rows = send_rows.reshape(experts, capacity, model_width)
    arrived_rows = lax.all_to_all(send_rows, "ep", split_axis=0, concat_axis=0, tiled=True)
    slot_count = arrived_rows.shape[1]
    grouped = arrived_rows.reshape(group_size, local_experts, slot_count, model_width)
    gate_lin = jnp.einsum("sxcd,xdf->sxcf", grouped, w_gate, preferred_element_type=jnp.float32)
    up_lin = jnp.einsum("sxcd,xdf->sxcf", grouped, w_up, preferred_element_type=jnp.float32)
    activated = (gate_lin * jax.nn.sigmoid(gate_lin) * up_lin).astype(jnp.bfloat16)
    produced = jnp.einsum("sxcf,xfd->sxcd", activated, w_down, preferred_element_type=jnp.float32)
    produced = produced.astype(jnp.bfloat16).reshape(
        group_size * local_experts, slot_count, model_width
    )
    came_back = lax.all_to_all(produced, "ep", split_axis=0, concat_axis=0, tiled=True)
    flat_shape = (group_size * local_experts, slot_count, hidden_width)
    gate_pre = gate_lin.reshape(flat_shape)
    up_pre = up_lin.reshape(flat_shape)
    picked = came_back.reshape(experts * capacity, model_width)[slot_index]
    picked = picked.reshape(row_count, TOP, model_width).astype(jnp.float32)
    mixture = jnp.einsum("tk,tkd->td", gate_weights, picked)
    output = (hidden + mixture).astype(jnp.bfloat16)
    back_query, back_key, back_value, back_out, back_router = gathered[:5]
    grad_output = out_grad.astype(jnp.float32)
    grad_gates = jnp.einsum("td,tkd->tk", grad_output, picked)
    grad_picked = (
        (gate_weights[:, :, None] * grad_output[:, None, :])
        .astype(jnp.bfloat16)
        .reshape(pair_count, model_width)
    )
    grad_send = jnp.where(filled[:, None], grad_picked[slot_source], jnp.zeros((), jnp.bfloat16))
    grad_send = grad_send.reshape(experts, capacity, model_width)
    grad_arrived = lax.all_to_all(grad_send, "ep", split_axis=0, concat_axis=0, tiled=True)
    shape_four = (group_size, local_experts, capacity, hidden_width)
    gate_four = gate_pre.reshape(shape_four)
    up_four = up_pre.reshape(shape_four)
    sigmoid_gate = jax.nn.sigmoid(gate_four)
    activated = (gate_four * sigmoid_gate * up_four).astype(jnp.bfloat16)
    grad_four = grad_arrived.reshape(group_size, local_experts, capacity, model_width)
    rows_four = arrived_rows.reshape(group_size, local_experts, capacity, model_width)
    grad_wdown = jnp.einsum(
        "sxcf,sxcd->xfd", activated, grad_four, preferred_element_type=jnp.float32
    )
    grad_act = jnp.einsum("sxcd,xfd->sxcf", grad_four, w_down, preferred_element_type=jnp.float32)
    grad_gate_pre = (
        grad_act * up_four * sigmoid_gate * (1.0 + gate_four * (1.0 - sigmoid_gate))
    ).astype(jnp.bfloat16)
    grad_up_pre = (grad_act * gate_four * sigmoid_gate).astype(jnp.bfloat16)
    grad_wgate = jnp.einsum(
        "sxcd,sxcf->xdf", rows_four, grad_gate_pre, preferred_element_type=jnp.float32
    )
    grad_wup = jnp.einsum(
        "sxcd,sxcf->xdf", rows_four, grad_up_pre, preferred_element_type=jnp.float32
    )
    grad_rows = jnp.einsum(
        "sxcf,xdf->sxcd", grad_gate_pre, w_gate, preferred_element_type=jnp.float32
    )
    grad_rows = grad_rows + jnp.einsum(
        "sxcf,xdf->sxcd", grad_up_pre, w_up, preferred_element_type=jnp.float32
    )
    grad_rows = grad_rows.astype(jnp.bfloat16).reshape(
        group_size * local_experts, capacity, model_width
    )
    grad_returned = lax.all_to_all(grad_rows, "ep", split_axis=0, concat_axis=0, tiled=True)
    expert_sums = (
        lax.psum_scatter(
            grad_wgate.astype(jnp.bfloat16), "rep", scatter_dimension=1, tiled=True
        ).astype(jnp.float32),
        lax.psum_scatter(
            grad_wup.astype(jnp.bfloat16), "rep", scatter_dimension=1, tiled=True
        ).astype(jnp.float32),
        lax.psum_scatter(
            grad_wdown.astype(jnp.bfloat16), "rep", scatter_dimension=1, tiled=True
        ).astype(jnp.float32),
    )
    grad_pairs = grad_returned.reshape(experts * capacity, model_width)[slot_index]
    grad_moe_in = jnp.sum(
        grad_pairs.reshape(row_count, TOP, model_width).astype(jnp.float32), axis=1
    )
    grad_chosen = gate_weights * (
        grad_gates - jnp.sum(gate_weights * grad_gates, axis=1, keepdims=True)
    )
    grad_logits = jnp.sum(jnp.where(route_hits, grad_chosen[:, :, None], 0.0), axis=1).astype(
        jnp.bfloat16
    )
    grad_router = lax.dot_general(
        moe_in, grad_logits, contract_rows, preferred_element_type=jnp.float32
    )
    grad_moe_in = grad_moe_in + lax.dot_general(
        grad_logits, back_router, contract_cols, preferred_element_type=jnp.float32
    )
    grad_hidden_norm, grad_ffn_gain = norm_back(grad_moe_in, hidden, scale_second, ffn_gain)
    grad_hidden = grad_output + grad_hidden_norm
    grad_branch = grad_hidden.astype(jnp.bfloat16)
    grad_wout = lax.dot_general(
        attended, grad_branch, contract_rows, preferred_element_type=jnp.float32
    )
    grad_attended = lax.dot_general(
        grad_branch, back_out, contract_cols, preferred_element_type=jnp.float32
    ).astype(jnp.bfloat16)
    context_back = past_context_again(own_rows, reach_count)
    scores = attention_scores(query_rot, context_back, allowed, kv_width)
    attn_probs = jnp.exp(scores - log_total)
    back_values = context_back[:, kv_width:].reshape(key_count, KV_HEADS, HEAD_DIM)
    back_keys = context_back[:, :kv_width].reshape(key_count, KV_HEADS, HEAD_DIM)
    grad_heads = grad_attended.reshape(row_count, KV_HEADS, ratio_heads, HEAD_DIM)
    grad_probs = jnp.einsum(
        "tgrd,kgd->grtk", grad_heads, back_values, preferred_element_type=jnp.float32
    )
    grad_values = jnp.einsum(
        "grtk,tgrd->kgd",
        attn_probs.astype(jnp.bfloat16),
        grad_heads,
        preferred_element_type=jnp.float32,
    )
    settle = jnp.sum(attn_probs * grad_probs, axis=-1, keepdims=True)
    grad_scores = (attn_probs * (grad_probs - settle)).astype(jnp.bfloat16)
    query_heads = query_rot.reshape(row_count, KV_HEADS, ratio_heads, HEAD_DIM)
    grad_query_rot = (
        jnp.einsum("grtk,kgd->tgrd", grad_scores, back_keys, preferred_element_type=jnp.float32)
        * scale_factor
    )
    grad_query_rot = grad_query_rot.astype(jnp.bfloat16)
    grad_keys = (
        jnp.einsum("grtk,tgrd->kgd", grad_scores, query_heads, preferred_element_type=jnp.float32)
        * scale_factor
    )
    grad_context = jnp.concatenate(
        [grad_keys.reshape(key_count, kv_width), grad_values.reshape(key_count, kv_width)], axis=1
    )
    grad_own = grad_context[reach_count * row_count :]
    for behind in range(1, reach_count + 1):
        start_row = (reach_count - behind) * row_count
        grad_own = grad_own + shifted(
            grad_context[start_row : start_row + row_count].astype(jnp.bfloat16), "ep", -behind
        ).astype(jnp.float32)
    grad_query_norm = rotate(
        grad_query_rot.astype(jnp.float32).reshape(row_count, HEADS, HEAD_DIM), cosine, -sine_part
    )
    grad_query_lin, grad_query_gain = norm_back(
        grad_query_norm.reshape(row_count, model_width), query_lin, scale_query, query_gain
    )
    grad_query_lin = grad_query_lin.astype(jnp.bfloat16)
    grad_key_rot = grad_own[:, :kv_width].astype(jnp.bfloat16)
    grad_key_norm = rotate(
        grad_key_rot.astype(jnp.float32).reshape(row_count, KV_HEADS, HEAD_DIM), cosine, -sine_part
    )
    grad_key_lin, grad_key_gain = norm_back(
        grad_key_norm.reshape(row_count, kv_width), key_lin, scale_key, key_gain
    )
    grad_key_lin = grad_key_lin.astype(jnp.bfloat16)
    grad_value_rows = grad_own[:, kv_width:].astype(jnp.bfloat16)
    grad_wquery = lax.dot_general(
        normed, grad_query_lin, contract_rows, preferred_element_type=jnp.float32
    )
    grad_wkey = lax.dot_general(
        normed, grad_key_lin, contract_rows, preferred_element_type=jnp.float32
    )
    grad_wvalue = lax.dot_general(
        normed, grad_value_rows, contract_rows, preferred_element_type=jnp.float32
    )
    grad_normed = lax.dot_general(
        grad_query_lin, back_query, contract_cols, preferred_element_type=jnp.float32
    )
    grad_normed = grad_normed + lax.dot_general(
        grad_key_lin, back_key, contract_cols, preferred_element_type=jnp.float32
    )
    grad_normed = grad_normed + lax.dot_general(
        grad_value_rows, back_value, contract_cols, preferred_element_type=jnp.float32
    )
    grad_input_norm, grad_attn_gain = norm_back(grad_normed, inputs, scale_first, attn_gain)
    input_grad = grad_hidden + grad_input_norm
    summed = (
        lax.psum_scatter(grad_wquery, ("rep", "ep"), scatter_dimension=0, tiled=True),
        lax.psum_scatter(grad_wkey, ("rep", "ep"), scatter_dimension=0, tiled=True),
        lax.psum_scatter(grad_wvalue, ("rep", "ep"), scatter_dimension=0, tiled=True),
        lax.psum_scatter(grad_wout, ("rep", "ep"), scatter_dimension=0, tiled=True),
        lax.psum_scatter(grad_router, ("rep", "ep"), scatter_dimension=0, tiled=True),
        lax.psum_scatter(grad_attn_gain, ("rep", "ep"), scatter_dimension=0, tiled=True),
        lax.psum_scatter(grad_query_gain, ("rep", "ep"), scatter_dimension=0, tiled=True),
        lax.psum_scatter(grad_key_gain, ("rep", "ep"), scatter_dimension=0, tiled=True),
        lax.psum_scatter(grad_ffn_gain, ("rep", "ep"), scatter_dimension=0, tiled=True),
    )
    return (
        output,
        input_grad,
        summed[0],
        summed[1],
        summed[2],
        summed[3],
        summed[4],
        summed[5],
        summed[6],
        summed[7],
        summed[8],
        expert_sums[0],
        expert_sums[1],
        expert_sums[2],
    )


def solution(mesh):
    placed = (
        P(("rep", "ep"), None),
        P("rep", None),
        P(("rep", "ep"), None),
        P(("rep", "ep"), None),
        P(("rep", "ep"), None),
        P(("rep", "ep"), None),
        P(("rep", "ep"), None),
        P(("rep", "ep"), None),
        P(("rep", "ep")),
        P(("rep", "ep")),
        P(("rep", "ep")),
        P(("rep", "ep")),
        P("ep", None, None),
        P("ep", None, None),
        P("ep", None, None),
        P(("rep", "ep"), None),
    )
    return jax.shard_map(
        body,
        mesh=mesh,
        in_specs=placed,
        out_specs=(
            P(("rep", "ep"), None),
            P(("rep", "ep"), None),
            P(("rep", "ep"), None),
            P(("rep", "ep"), None),
            P(("rep", "ep"), None),
            P(("rep", "ep"), None),
            P(("rep", "ep"), None),
            P(("rep", "ep")),
            P(("rep", "ep")),
            P(("rep", "ep")),
            P(("rep", "ep")),
            P("ep", "rep", None),
            P("ep", "rep", None),
            P("ep", "rep", None),
        ),
        check_vma=False,
    )
```

profile of v0, /device:TPU:1, one launch (start us, length us, event | category | flops | bytes accessed | tf_op | source)
XLA Modules:
  0.0 3497.6 jit_solution(9887803277376792689)
XLA Ops:
  16.5 69.3 %all-reduce.10 = (bf16[1024]{0:T(1024)(128)(2,1)S(1)}, bf16[512]{0:T(512)(128)(2,1)S(1)}, bf16[1024]{0:T(1024)(128)(2,1)}, bf16[1024]{0:T(1024)(128)(2,1)}) all-reduce(bf16[1024]{0:T(1024)(128)(2,1)S(1)} %dynamic-update-slice, bf16[512]{0:T(512)(128)(2,1)S(1)} %dynamic-update-slice.1, ...), channel_id=1, replica_groups=mesh['rep'=16,'ep'=8] {'rep','ep'}, use_global_device_ids=true, to_apply=%add | all-reduce | flops 3584 | bytes 14336
  86.1 9.1 reduce-window.6
  96.0 7.1 gather_fusion
  104.0 8.1 scatter_custom_fusion
  116.4 25.6 all-gather.7.cloned.1.call-done
  143.7 3.3 collective-permute-start.1
  151.1 3.0 collective-permute-start.2
  158.7 11.3 collective-permute-done
  170.2 16.3 collective-permute-done.2
  191.7 25.1 all-gather.9.cloned.1.call-done
  216.8 2.4 multiply_reduce_fusion.5
  221.4 2.5 copy.109
  225.3 3.2 fusion.114
  228.6 3.0 fusion.3
  231.6 4.0 copy-done.2
  235.5 3.9 fusion.61
  239.4 43.1 %all-gather.11.cloned.1.call-done = bf16[1024,1024]{1,0:T(8,128)(2,1)} async-done(((bf16[8,1024]{1,0:T(8,128)(2,1)}), bf16[1024,1024]{1,0:T(8,128)(2,1)}) %all-gather.11.cloned.1.call-update) | async-done | bytes 2097168 | tf_op jit(solution)/shard_map/all_gather | solution.py:115
  282.6 2.4 multiply_reduce_fusion.4
  286.1 9.7 gather_fusion.1
  295.8 3.6 broadcast_select_fusion.1
  299.5 69.7 %all_to_all.20 = bf16[32,88,1024]{2,1,0:T(8,128)(2,1)S(1)} all-to-all(bf16[32,88,1024]{2,1,0:T(8,128)(2,1)S(1)} %broadcast_select_fusion.1), channel_id=1, replica_groups=mesh['rep'=16,'ep'=8] {'ep'}, dimensions={0} | all-to-all | bytes 11534336 | tf_op jit(solution)/shard_map/all_to_all | solution.py:198
  369.2 5.0 fusion.28
  374.4 7.8 fusion.16
  382.2 5.2 convert_bitcast_fusion
  387.4 3.1 copy.118
  390.5 5.8 all-to-all-start.1
  396.4 92.2 %all_gather.35 = bf16[1024,32]{1,0:T(8,128)(2,1)S(1)} all-gather(bf16[8,32]{1,0:T(8,128)(2,1)S(1)} %copy-done.60), channel_id=1, replica_groups=mesh['rep'=16,'ep'=8] {'rep','ep'}, dimensions={0}, use_global_device_ids=true | all-gather | bytes 66048 | tf_op jit(solution)/shard_map/all_gather | solution.py:116
  488.9 14.3 gather_fusion.2
  503.3 4.5 fusion.39
  510.5 15.9 gather_fusion.3
  526.4 6.2 broadcast_select_fusion
  532.6 4.7 all-to-all-start.2
  539.0 65.2 %all-to-all-done.2 = bf16[32,88,1024]{2,1,0:T(8,128)(2,1)} async-done(((bf16[32,88,1024]{2,1,0:T(8,128)(2,1)}), bf16[32,88,1024]{2,1,0:T(8,128)(2,1)}, u32[]{:S(2)}, u32[]{:S(2)}) %all-to-all-start.2) | async-done | bytes 5767200 | tf_op jit(solution)/shard_map/all_to_all | solution.py:226
  604.3 9.0 bitcast_convert_fusion
  613.4 11.0 fusion.13
  625.9 5.0 bitcast_convert_fusion.2
  632.7 8.1 fusion.30
  640.8 9.6 fusion.10
  650.4 3.1 copy.121
  653.5 5.5 all-to-all-start.3
  659.3 4.6 fusion.41
  663.9 8.7 bitcast_convert_fusion.1
  672.6 53.0 %all-to-all-done.3 = bf16[32,88,1024]{2,1,0:T(8,128)(2,1)} async-done(((bf16[32,88,1024]{2,1,0:T(8,128)(2,1)}), bf16[32,88,1024]{2,1,0:T(8,128)(2,1)}, u32[]{:S(2)}, u32[]{:S(2)}) %all-to-all-start.3) | async-done | bytes 5767200 | tf_op jit(solution)/shard_map/all_to_all | solution.py:257
  725.6 14.3 gather_fusion.4
  739.9 5.7 convert_reduce_fusion
  748.5 13.4 fusion
  761.9 14.7 fusion.2
  776.7 3.9 copy-done.3
  780.6 3.3 fusion.45
  783.8 9.1 fusion.5
  793.4 3.0 collective-permute-start.4
  800.4 6.7 collective-permute-done.4
  807.1 6.4 collective-permute-done.7
  813.5 5.5 collective-permute-done.6
  826.7 2.7 fusion.79
  829.5 5.8 fusion.60
  841.3 2.8 fusion.104
  849.6 2.9 fusion.67
  852.5 79.3 %all-reduce.9 = (f32[1024]{0:T(1024)S(1)}, f32[1024]{0:T(1024)S(1)}, f32[512]{0:T(512)S(1)}, f32[1024]{0:T(1024)S(1)}) all-reduce(f32[1024]{0:T(1024)S(1)} %get-tuple-element.18, f32[1024]{0:T(1024)S(1)} %get-tuple-element.16, f32[512]{0:T(512)S(1)} %get-tuple-element.20, ...), channel_id=7, replica_groups=mesh['rep'=16,'ep'=8] {'rep','ep'}, use_global_device_ids=true, to_apply=%region_27.28.clone | all-reduce | flops 3584 | bytes 28672
  934.2 2.5 fusion.66
  942.1 630.3 %reduce-scatter.12.cloned.1.call-done = f32[8,512]{1,0:T(8,128)} async-done(((f32[1024,512]{1,0:T(8,128)}), f32[8,512]{1,0:T(8,128)}) %reduce-scatter.12.cloned.1.call-update) | async-done | bytes 16400 | tf_op jit(solution)/shard_map/reduce_scatter | solution.py:369
  1572.5 636.2 %reduce-scatter.10.cloned.1.call-done = f32[8,512]{1,0:T(8,128)} async-done(((f32[1024,512]{1,0:T(8,128)}), f32[8,512]{1,0:T(8,128)}) %reduce-scatter.10.cloned.1.call-update) | async-done | bytes 16400 | tf_op jit(solution)/shard_map/reduce_scatter | solution.py:368
  2208.7 640.9 %reduce-scatter.14.cloned.1.call-done = f32[8,1024]{1,0:T(8,128)} async-done(((f32[1024,1024]{1,0:T(8,128)}), f32[8,1024]{1,0:T(8,128)}) %reduce-scatter.14.cloned.1.call-update) | async-done | bytes 32784 | tf_op jit(solution)/shard_map/reduce_scatter | solution.py:370
  2849.6 640.9 %reduce-scatter.8.cloned.1.call-done = f32[8,1024]{1,0:T(8,128)} async-done(((f32[1024,1024]{1,0:T(8,128)}), f32[8,1024]{1,0:T(8,128)}) %reduce-scatter.8.cloned.1.call-update) | async-done | bytes 32784 | tf_op jit(solution)/shard_map/reduce_scatter | solution.py:367
  (281 shorter events, 78.3 us)
Async XLA Ops:
  7.2 88.8 %copy-start = (s32[1,2048]{1,0:T(1,128)S(1)}, s32[1,2048]{1,0:T(1,128)}, u32[]{:S(2)}) copy-start(s32[1,2048]{1,0:T(1,128)} %param.17) | copy-start | bytes 24580
  7.2 106.0 %all-gather.5.cloned.1.call-start = ((), (), s32[]{:S(2)}) async-start(), calls=%async_computation.11 | async-start | bytes 1056768 | tf_op jit(solution)/shard_map/all_gather | solution.py:113
  7.9 134.0 %all-gather.7.cloned.1.call-start = ((), (), s32[]{:S(2)}) async-start(), calls=%async_computation.12 | async-start | bytes 1056768 | tf_op jit(solution)/shard_map/all_gather | solution.py:114
  8.7 208.1 %all-gather.9.cloned.1.call-start = ((), (), s32[]{:S(2)}) async-start(), calls=%async_computation.13 | async-start | bytes 2113536 | tf_op jit(solution)/shard_map/all_gather | solution.py:112
  9.4 273.2 %all-gather.11.cloned.1.call-start = ((), (), s32[]{:S(2)}) async-start(), calls=%async_computation.14 | async-start | bytes 2113536 | tf_op jit(solution)/shard_map/all_gather | solution.py:115
  13.1 203.7 %copy-start.45 = (f32[256]{0:T(256)}, f32[256]{0:T(256)S(1)}, u32[]{:S(2)}) copy-start(f32[256]{0:T(256)S(1)} %add_rsqrt_fusion.3) | copy-start | bytes 3076
  85.8 131.0 %copy-start.36 = (f32[1024]{0:T(1024)}, f32[1024]{0:T(1024)S(1)}, u32[]{:S(2)}) copy-start(f32[1024]{0:T(1024)S(1)} %convert_element_type.161) | copy-start | bytes 12292
  85.8 29.2 copy-start.50
  96.0 17.3 copy-start.4
  103.9 120.0 %copy-start.34 = (f32[256,32]{0,1:T(8,128)}, f32[256,32]{0,1:T(8,128)S(1)}, u32[]{:S(2)}) copy-start(f32[256,32]{0,1:T(8,128)S(1)} %get-tuple-element.54) | copy-start | bytes 98308
  104.0 11.0 copy-start.52
  112.1 36.2 %copy-start.40 = (s32[2816]{0:T(1024)}, s32[2816]{0:T(1024)S(1)}, u32[]{:S(2)}) copy-start(s32[2816]{0:T(1024)S(1)} %scatter_custom_fusion) | copy-start | bytes 33796
  115.0 40.3 %copy-start.61 = (bf16[1024]{0:T(1024)(128)(2,1)S(1)}, bf16[1024]{0:T(1024)(128)(2,1)}, u32[]{:S(2)}) copy-start(bf16[1024]{0:T(1024)(128)(2,1)} %get-tuple-element.28) | copy-start | bytes 6148
  115.0 40.3 %copy-start.56 = (f32[256]{0:T(256)}, f32[256]{0:T(256)S(1)}, u32[]{:S(2)}) copy-start(f32[256]{0:T(256)S(1)} %add_rsqrt_fusion.2) | copy-start | bytes 3076
  143.7 26.4 collective-permute-start.1
  147.0 23.1 collective-permute-start
  148.9 38.6 %collective-permute-start.3 = (bf16[256,1024]{1,0:T(8,128)(2,1)S(1)}, bf16[256,1024]{1,0:T(8,128)(2,1)S(1)}, u32[]{:S(2)}, u32[]{:S(2)}) collective-permute-start(bf16[256,1024]{1,0:T(8,128)(2,1)S(1)} %pad_maximum_fusion.2), channel_id=1, source_target_pairs={{0,1},{1,2},{2,3},{3,4},{4,5},{5,6},{6,7},{8,9},{9,10},{10,11},{11... | collective-permute-start | bytes 1572872 | tf_op jit(solution)/shard_map/ppermute | solution.py:21
  151.1 35.4 %collective-permute-start.2 = (bf16[256,1024]{1,0:T(8,128)(2,1)S(1)}, bf16[256,1024]{1,0:T(8,128)(2,1)}, u32[]{:S(2)}, u32[]{:S(2)}) collective-permute-start(bf16[256,1024]{1,0:T(8,128)(2,1)S(1)} %pad_maximum_fusion.2), channel_id=1, source_target_pairs={{0,2},{1,3},{2,4},{3,5},{4,6},{5,7},{8,10},{9,11},{10,12},{11,13},... | collective-permute-start | bytes 1572872 | tf_op jit(solution)/shard_map/ppermute | solution.py:21
  155.3 63.9 %copy-start.41 = (f32[1024]{0:T(1024)}, f32[1024]{0:T(1024)S(1)}, u32[]{:S(2)}) copy-start(f32[1024]{0:T(1024)S(1)} %convert_element_type.167) | copy-start | bytes 12292
  156.0 129.0 %copy-start.43 = (f32[1024]{0:T(1024)}, f32[1024]{0:T(1024)S(1)}, u32[]{:S(2)}) copy-start(f32[1024]{0:T(1024)S(1)} %convert_element_type.172) | copy-start | bytes 12292
  189.6 35.7 %copy-start.6 = (bf16[1280,512]{0,1:T(8,128)(2,1)}, bf16[1280,512]{0,1:T(8,128)(2,1)S(1)}, u32[]{:S(2)}) copy-start(bf16[1280,512]{0,1:T(8,128)(2,1)S(1)} %copy.108) | copy-start | bytes 3932164
  191.7 39.9 %copy-start.13 = (bf16[1280,512]{0,1:T(8,128)(2,1)}, bf16[1280,512]{0,1:T(8,128)(2,1)S(1)}, u32[]{:S(2)}) copy-start(bf16[1280,512]{0,1:T(8,128)(2,1)S(1)} %copy.107) | copy-start | bytes 3932164
  219.3 9.2 copy-start.54
  228.5 7.0 copy-start.2
  239.4 56.4 %copy-start.32 = (bf16[8,64,2,256]{3,1,2,0:T(8,128)(2,1)}, bf16[8,64,2,256]{3,1,2,0:T(8,128)(2,1)S(1)}, u32[]{:S(2)}) copy-start(bf16[8,64,2,256]{3,1,2,0:T(8,128)(2,1)S(1)} %fusion.61) | copy-start | bytes 1572868
  239.4 46.7 %copy-start.48 = (s32[3072]{0:T(1024)S(1)}, s32[3072]{0:T(1024)}, u32[]{:S(2)}) copy-start(s32[3072]{0:T(1024)} %get-tuple-element.72) | copy-start | bytes 36868
  285.0 10.8 copy-start.58
  286.1 9.7 copy-start.49
  299.5 69.7 %copy-start.18 = (bf16[4,1024,512]{2,1,0:T(8,128)(2,1)S(1)}, bf16[4,1024,512]{2,1,0:T(8,128)(2,1)}, u32[]{:S(2)}) copy-start(bf16[4,1024,512]{2,1,0:T(8,128)(2,1)} %param.28) | copy-start | bytes 12582916
  369.2 5.3 copy-start.12
  369.2 5.3 copy-start.17
  374.4 7.8 copy-start.62
  390.5 5.8 copy-start.30
  390.5 5.9 copy-start.60
  390.5 98.1 %copy-start.53 = (s32[2048,1]{0,1:T(1,128)S(1)}, s32[2048,1]{0,1:T(1,128)}, u32[]{:S(2)}) copy-start(s32[2048,1]{0,1:T(1,128)} %copy-done.52) | copy-start | bytes 24580
  390.5 98.3 %copy-start.39 = (s32[256,8]{0,1:T(8,128)S(1)}, s32[256,8]{0,1:T(8,128)}, u32[]{:S(2)}) copy-start(s32[256,8]{0,1:T(8,128)} %param.18) | copy-start | bytes 24580
  390.5 98.4 %all-to-all-start.1 = ((bf16[32,88,1024]{2,1,0:T(8,128)(2,1)}), bf16[32,88,1024]{2,1,0:T(8,128)(2,1)}, u32[]{:S(2)}, u32[]{:S(2)}) async-start(bf16[32,88,1024]{2,1,0:T(8,128)(2,1)} %bitcast.230), calls=%async_computation.1 | async-start | bytes 11534336 | tf_op jit(solution)/shard_map/all_to_all | solution.py:208
  532.6 71.7 %all-to-all-start.2 = ((bf16[32,88,1024]{2,1,0:T(8,128)(2,1)}), bf16[32,88,1024]{2,1,0:T(8,128)(2,1)}, u32[]{:S(2)}, u32[]{:S(2)}) async-start(bf16[32,88,1024]{2,1,0:T(8,128)(2,1)} %broadcast_select_fusion), calls=%async_computation.2 | async-start | bytes 11534336 | tf_op jit(solution)/shard_map/all_to_all | solution.py:226
  537.3 306.9 %all-reduce.13.cloned.1.call-start = ((), (), s32[]{:S(2)}) async-start(), calls=%async_computation.22 | async-start | bytes 1048576
  539.0 397.7 %reduce-scatter.20.cloned.1.call-start = ((), (), s32[]{:S(2)}) async-start(), calls=%async_computation.21 | async-start | bytes 4456448 | tf_op jit(solution)/shard_map/reduce_scatter | solution.py:265
  613.3 12.6 slice-start
  613.3 325.2 %reduce-scatter.16.cloned.1.call-start = ((), (), s32[]{:S(2)}) async-start(), calls=%async_computation.19 | async-start | bytes 4456448 | tf_op jit(solution)/shard_map/reduce_scatter | solution.py:259
  613.4 12.5 slice-start.1
  653.5 72.1 %all-to-all-start.3 = ((bf16[32,88,1024]{2,1,0:T(8,128)(2,1)}), bf16[32,88,1024]{2,1,0:T(8,128)(2,1)}, u32[]{:S(2)}, u32[]{:S(2)}) async-start(bf16[32,88,1024]{2,1,0:T(8,128)(2,1)} %bitcast.229), calls=%async_computation.3 | async-start | bytes 11534336 | tf_op jit(solution)/shard_map/all_to_all | solution.py:257
  659.0 281.3 %reduce-scatter.18.cloned.1.call-start = ((), (), s32[]{:S(2)}) async-start(), calls=%async_computation.20 | async-start | bytes 4456448 | tf_op jit(solution)/shard_map/reduce_scatter | solution.py:262
  672.6 899.9 %reduce-scatter.12.cloned.1.call-start = ((), (), s32[]{:S(2)}) async-start(), calls=%async_computation.17 | async-start | bytes 2113536 | tf_op jit(solution)/shard_map/reduce_scatter | solution.py:369
  739.9 5.7 copy-start.9
  739.9 5.7 copy-start.44
  739.9 5.7 copy-start.59
  739.9 6.3 copy-start.19
  739.9 6.3 copy-start.31
  761.9 18.7 copy-start.25
  761.9 18.7 copy-start.27
  793.4 28.2 copy-start.5
  793.4 28.2 copy-start.37
  793.4 28.2 copy-start.46
  793.4 13.7 collective-permute-start.4
  796.5 17.0 collective-permute-start.7
  797.8 21.2 collective-permute-start.6
  799.1 22.2 collective-permute-start.5
  823.8 1384.9 %reduce-scatter.10.cloned.1.call-start = ((), (), s32[]{:S(2)}) async-start(), calls=%async_computation.16 | async-start | bytes 2113536 | tf_op jit(solution)/shard_map/reduce_scatter | solution.py:368
  826.7 2022.9 %reduce-scatter.14.cloned.1.call-start = ((), (), s32[]{:S(2)}) async-start(), calls=%async_computation.18 | async-start | bytes 4227072 | tf_op jit(solution)/shard_map/reduce_scatter | solution.py:370
  829.4 2661.1 %reduce-scatter.8.cloned.1.call-start = ((), (), s32[]{:S(2)}) async-start(), calls=%async_computation.15 | async-start | bytes 4227072 | tf_op jit(solution)/shard_map/reduce_scatter | solution.py:367
  847.8 2642.7 %copy-start.1 = (s32[1,2048]{1,0:T(1,128)S(1)}, s32[1,2048]{1,0:T(1,128)}, u32[]{:S(2)}) copy-start(s32[1,2048]{1,0:T(1,128)} %param.17) | copy-start | bytes 24580
  (24 other events, 59.2 us)
Sparse Core Ops, SparseCore 0:
  10.8 67.1 all-gather.4
  80.8 61.0 all-gather.6
  145.1 71.6 all-gather.8
  219.8 62.7 all-gather.10
  542.6 153.3 all-reduce.12
  699.5 74.5 reduce-scatter.19
  777.5 77.0 reduce-scatter.15
  858.3 77.6 reduce-scatter.17
  938.9 633.4 reduce-scatter.11
  1575.3 633.2 reduce-scatter.9
  2211.6 637.9 reduce-scatter.13
  2852.5 637.9 reduce-scatter.7
where the time goes:
time: 3510 us; the launch traced here: 3500 us
  waiting for transfers between devices  2810 us (80%)
  blocking collectives  311 us (9%)
  matrix products  145 us (4%)
  local copies, waits for them, and re-layouts  111 us (3%)
  other arithmetic  70.8 us (2%)
    reduce_scatter x1, waiting for transfers between devices, body(): lax.psum_scatter(grad_wquery, ('rep', 'ep'), scatter_dimension=0, tiled=T...  641 us
    reduce_scatter x1, waiting for transfers between devices, body(): lax.psum_scatter(grad_wout, ('rep', 'ep'), scatter_dimension=0, tiled=True)  641 us
    reduce_scatter x1, waiting for transfers between devices, body(): lax.psum_scatter(grad_wkey, ('rep', 'ep'), scatter_dimension=0, tiled=True)  636 us
    reduce_scatter x1, waiting for transfers between devices, body(): lax.psum_scatter(grad_wvalue, ('rep', 'ep'), scatter_dimension=0, tiled=T...  630 us
    unnamed x2, blocking collectives  149 us
    all_gather x1, blocking collectives, body(): lax.all_gather(shards[4], ('rep', 'ep'), axis=0, tiled=True)  92.2 us
  transfers between devices with their start and end apart: 23, of which 15 were waited for; matrix products, arithmetic and copies ran while one was open for 7% of the time, Pallas kernels for 0%

commit v1 on v0

v1 whole, which is shorter than its diff:
```python
import functools

import jax
import jax.numpy as jnp
import numpy as np
from jax import lax
from jax.experimental import pallas as pl
from jax.experimental.pallas import tpu as pltpu
from jax.sharding import PartitionSpec as P

BF = jnp.bfloat16
F32 = jnp.float32
MESH = pl.DeviceIdType.MESH
ANY = pl.BlockSpec(memory_space=pl.ANY)
VM = pl.BlockSpec(memory_space=pltpu.VMEM)
DMA = pltpu.SemaphoreType.DMA
MIB = 1 << 20

HEADS = 16
KV_HEADS = 8
HEAD_DIM = 64
TOP = 8
WINDOW = 1024
EPSILON = 1e-06
ROPE_BASE = 10000.0
MASKED = -1e30
EP = 8
REP = 16
TOK = 256
LENGTH = 2048
D = 1024
KV = 512
FF = 512
EXPERTS = 32
LOCAL = 4
CAP = 96
NT = (((1,), (1,)), ((), ()))
TN = (((0,), (0,)), ((), ()))
HIGH = lax.Precision.HIGHEST


def dot(a, b):
    return jnp.dot(a, b, preferred_element_type=F32)


def dot_nt(a, b, precision=None):
    return lax.dot_general(a, b, NT, preferred_element_type=F32, precision=precision)


def dot_tn(a, b):
    return lax.dot_general(a, b, TN, preferred_element_type=F32)


def iota(shape, dim):
    return lax.broadcasted_iota(jnp.int32, shape, dim)


def ep_device(x, c):
    return {"ep": x * 2 + c}


def greet(devices):
    barrier = pltpu.get_barrier_semaphore()
    for device in devices:
        pl.semaphore_signal(barrier, inc=1, device_id=device, device_id_type=MESH)
    pl.semaphore_wait(barrier, len(devices))


def remote(src, dst, sems, i, device):
    return pltpu.make_async_remote_copy(
        src_ref=src,
        dst_ref=dst,
        send_sem=sems[0].at[i],
        recv_sem=sems[1].at[i],
        device_id=device,
        device_id_type=MESH,
    )


def place():
    e = lax.axis_index("ep")
    return e, e // 2, e % 2


def ep_others(e):
    return [(e + k) % EP for k in range(1, EP)]


def rep_others(r):
    return [(r + k) % REP for k in range(1, REP)]


class RingGather:
    SEMS = 10

    def __init__(self, x_ref, o_ref, sems, lsem):
        e, x, c = place()
        self.n = n = x_ref.shape[0]
        h = n // 2
        self.o_ref = o_ref
        right, left = ep_device((x + 1) % 4, c), ep_device((x + 3) % 4, c)
        peer = ep_device(x, 1 - c)
        b_left, b_right, b_opp = (((x + 3) % 4) * 2 + c, ((x + 1) % 4) * 2 + c, ((x + 2) % 4) * 2 + c)

        def rows(b, off=0, size=n):
            return o_ref.at[pl.ds(pl.multiple_of(b * n + off, 16), size)]

        low, high = x_ref.at[pl.ds(0, h)], x_ref.at[pl.ds(h, h)]
        self.first = [
            remote(low, rows(e, 0, h), sems, 0, right),
            remote(high, rows(e, h, h), sems, 2, left),
            remote(high, rows(e, h, h), sems, 1, right),
            remote(low, rows(e, 0, h), sems, 3, left),
            remote(x_ref, rows(e), sems, 4, peer),
        ]
        self.fwd_right = remote(rows(b_left, 0, h), rows(b_left, 0, h), sems, 5, right)
        self.fwd_left = remote(rows(b_right, h, h), rows(b_right, h, h), sems, 6, left)
        self.to_peer = [
            remote(rows(b_left), rows(b_left), sems, 7, peer),
            remote(rows(b_right), rows(b_right), sems, 8, peer),
            remote(rows(b_opp), rows(b_opp), sems, 9, peer),
        ]
        self.own = pltpu.make_async_copy(x_ref, rows(e), lsem)

    def start(self):
        for copy in self.first:
            copy.start()
        self.own.start()

    def forward(self):
        self.first[0].wait_recv()
        self.fwd_right.start()
        self.first[1].wait_recv()
        self.fwd_left.start()
        self.first[2].wait_recv()
        self.to_peer[0].start()
        self.first[3].wait_recv()
        self.to_peer[1].start()

    def finish(self):
        self.fwd_right.wait_recv()
        self.fwd_left.wait_recv()
        self.to_peer[2].start()
        self.first[4].wait_recv()
        for copy in self.to_peer:
            copy.wait_recv()
        self.own.wait()
        for copy in self.first + [self.fwd_right, self.fwd_left] + self.to_peer:
            copy.wait_send()


class RingReduce:
    SEMS = 10
    STEP = 64

    def __init__(self, p_ref, n, pc, snd, rcv, hop, sems, lsems):
        e, x, c = place()
        self.n, self.h = n, n // 2
        h = n // 2
        self.pc, self.snd, self.rcv, self.hop = pc, snd, rcv, hop
        right, left = ep_device((x + 1) % 4, c), ep_device((x + 3) % 4, c)
        peer = ep_device(x, 1 - c)

        def rows(b):
            return p_ref.at[pl.ds(pl.multiple_of(b * n, 16), n)]

        chips = [(x + 2) % 4, (x + 1) % 4, (x + 3) % 4, x]
        self.swap = [remote(rows(b * 2 + 1 - c), pc.at[k], sems, k, peer) for k, b in enumerate(chips)]
        self.load = [
            pltpu.make_async_copy(rows(b * 2 + c), snd.at[k], lsems.at[k]) for k, b in enumerate(chips)
        ]
        low, high = pl.ds(0, h), pl.ds(h, h)
        self.opp = [
            remote(snd.at[0, low], hop.at[low], sems, 4, right),
            remote(snd.at[0, high], hop.at[high], sems, 5, left),
        ]
        self.near = [
            remote(snd.at[1, high], rcv.at[0, high], sems, 6, right),
            remote(snd.at[2, low], rcv.at[1, low], sems, 7, left),
        ]
        self.far = [
            remote(snd.at[1, low], rcv.at[0, low], sems, 8, right),
            remote(snd.at[2, high], rcv.at[1, high], sems, 9, left),
        ]

    def rows_loop(self, low, count, body):
        step = self.STEP

        def loop(i, carry):
            body(pl.ds(pl.multiple_of(low + i * step, 16), step))
            return carry

        lax.fori_loop(0, count // step, loop, 0)

    def merge(self, k):
        def body(s):
            self.snd[k, s] = (self.snd[k, s].astype(F32) + self.pc[k, s].astype(F32)).astype(BF)

        self.load[k].wait()
        self.swap[k].wait_recv()
        self.rows_loop(0, self.n, body)

    def merge_hop(self, k, low):
        def body(s):
            self.snd[k, s] = (self.snd[k, s].astype(F32) + self.hop[s].astype(F32)).astype(BF)

        self.rows_loop(low, self.h, body)

    def start(self):
        for copy in self.swap + self.load:
            copy.start()

    def middle(self):
        self.merge(0)
        for copy in self.opp:
            copy.start()
        self.merge(1)
        self.near[0].start()
        self.merge(2)
        self.near[1].start()
        self.merge(3)
        self.opp[0].wait_recv()
        self.merge_hop(1, 0)
        self.far[0].start()
        self.opp[1].wait_recv()
        self.merge_hop(2, self.h)
        self.far[1].start()

    def finish(self, out_ref):
        for copy in self.near + self.far:
            copy.wait_recv()

        def body(s):
            out_ref[s] = self.snd[3, s].astype(F32) + (
                self.rcv[0, s].astype(F32) + self.rcv[1, s].astype(F32)
            )

        self.rows_loop(0, self.n, body)
        for copy in self.swap + self.opp + self.near + self.far:
            copy.wait_send()


def reduce_scratch(n, w):
    return [
        pltpu.VMEM((4, n, w), BF),
        pltpu.VMEM((4, n, w), BF),
        pltpu.VMEM((2, n, w), BF),
        pltpu.VMEM((n, w), BF),
        DMA((RingReduce.SEMS,)),
        DMA((RingReduce.SEMS,)),
        DMA((4,)),
    ]


def comm_call(kernel, name, collective_id, out_shape, in_specs, out_specs, scratch, limit=48):
    return pl.pallas_call(
        kernel,
        out_shape=out_shape,
        in_specs=in_specs,
        out_specs=out_specs,
        scratch_shapes=scratch,
        compiler_params=pltpu.CompilerParams(
            collective_id=collective_id, has_side_effects=True, vmem_limit_bytes=limit * MIB
        ),
        name=name,
    )


def shape(dims, dtype=F32):
    return jax.ShapeDtypeStruct(dims, dtype)


def gather_first_kernel(
    tok, cot, wsl, wo, x_all, g_all, wg, wog, lsem, s_tok, r_tok, s_cot, r_cot, s_w, r_w, s_o, r_o
):
    r = lax.axis_index("rep")
    e, x, c = place()
    others = ep_others(e)
    copies = rep_others(r)
    greet([{"ep": d} for d in others] + [{"rep": d} for d in copies])
    stage = []
    for k, d in enumerate(others):
        stage.append(remote(wsl.at[d], wg.at[r, e], (s_w, r_w), k, {"ep": d}))
        stage.append(remote(wo, wog.at[r, e], (s_o, r_o), k, {"ep": d}))
    own = [
        pltpu.make_async_copy(wsl.at[e], wg.at[r, e], lsem.at[2]),
        pltpu.make_async_copy(wo, wog.at[r, e], lsem.at[3]),
    ]
    for copy in stage + own:
        copy.start()
    tokens = RingGather(tok, x_all, (s_tok, r_tok), lsem.at[0])
    grads = RingGather(cot, g_all, (s_cot, r_cot), lsem.at[1])
    tokens.start()
    for copy in own:
        copy.wait()
    for copy in stage:
        copy.wait_recv()
    spread = []
    for k, d in enumerate(copies):
        spread.append(remote(wg.at[r], wg.at[r], (s_w, r_w), 7 + k, {"rep": d}))
        spread.append(remote(wog.at[r], wog.at[r], (s_o, r_o), 7 + k, {"rep": d}))
    for copy in spread:
        copy.start()
    tokens.forward()
    grads.start()
    tokens.finish()
    grads.forward()
    grads.finish()
    for copy in spread:
        copy.wait_recv()
    for copy in stage + spread:
        copy.wait_send()


def gather_first(tok, cot, wsl, wo):
    return comm_call(
        gather_first_kernel,
        "gather_first",
        1,
        [
            shape((EP * TOK, D), BF),
            shape((EP * TOK, D), BF),
            shape((REP, EP, 32, 128), BF),
            shape((REP, EP, 64, 128), BF),
        ],
        [ANY] * 4,
        [ANY] * 4,
        [DMA((4,)), DMA((10,)), DMA((10,)), DMA((10,)), DMA((10,)), DMA((22,)), DMA((22,)), DMA((22,)), DMA((22,))],
    )(tok, cot, wsl, wo)


def sum_stats_kernel(x_ref, o_ref, held, ssem, rsem):
    e, _, _ = place()
    others = ep_others(e)
    greet([{"ep": d} for d in others])
    copies = [remote(x_ref, held.at[e], (ssem, rsem), k, {"ep": d}) for k, d in enumerate(others)]
    for copy in copies:
        copy.start()
    held[e] = x_ref[...]
    for copy in copies:
        copy.wait_recv()
    total = held[0]
    for k in range(1, EP):
        total = total + held[k]
    o_ref[...] = total
    for copy in copies:
        copy.wait_send()


def sum_stats(x, name, collective_id):
    return comm_call(
        sum_stats_kernel,
        name,
        collective_id,
        shape(x.shape),
        [VM],
        VM,
        [pltpu.VMEM((EP,) + x.shape, F32), DMA((7,)), DMA((7,))],
    )(x)


def swap_kernel(to_rows, x_ref, o_ref, lsem, ssem, rsem):
    e, _, _ = place()
    others = ep_others(e)
    greet([{"ep": d} for d in others])

    def rows(ref, b):
        return ref.at[pl.ds(pl.multiple_of(b * TOK, 16), TOK)]

    def cols(ref, b):
        return ref.at[:, pl.ds(pl.multiple_of(b * 128, 128), 128)]

    src, dst = (rows, cols) if to_rows else (cols, rows)
    own = pltpu.make_async_copy(src(x_ref, e), dst(o_ref, e), lsem)
    copies = [
        remote(src(x_ref, d), dst(o_ref, e), (ssem, rsem), k, {"ep": d}) for k, d in enumerate(others)
    ]
    for copy in copies:
        copy.start()
    own.start()
    own.wait()
    for copy in copies:
        copy.wait_recv()
    for copy in copies:
        copy.wait_send()


def swap_heads(x, to_rows, name, collective_id):
    out = (TOK, D) if to_rows else (LENGTH, 128)
    return comm_call(
        functools.partial(swap_kernel, to_rows),
        name,
        collective_id,
        shape(out, BF),
        [ANY],
        ANY,
        [DMA(()), DMA((7,)), DMA((7,))],
    )(x)


def gather_rows_kernel(x_ref, t_ref, o_ref, ot_ref, lsem, s_x, r_x, s_t, r_t):
    e, _, _ = place()
    others = ep_others(e)
    greet([{"ep": d} for d in others])
    small = [remote(t_ref, ot_ref.at[e], (s_t, r_t), k, {"ep": d}) for k, d in enumerate(others)]
    own = pltpu.make_async_copy(t_ref, ot_ref.at[e], lsem.at[1])
    for copy in small:
        copy.start()
    own.start()
    ring = RingGather(x_ref, o_ref, (s_x, r_x), lsem.at[0])
    ring.start()
    ring.forward()
    ring.finish()
    own.wait()
    for copy in small:
        copy.wait_recv()
    for copy in small:
        copy.wait_send()


def gather_rows(x, t):
    return comm_call(
        gather_rows_kernel,
        "gather_rows",
        4,
        [shape((EP * TOK, D), BF), shape((EP,) + t.shape)],
        [ANY, ANY],
        [ANY, ANY],
        [DMA((2,)), DMA((10,)), DMA((10,)), DMA((7,)), DMA((7,))],
    )(x, t)


def reduce_rows_kernel(p_ref, t_ref, o_ref, ot_ref, pc, snd, rcv, hop, ssem, rsem, lsems, lsem, s_t, r_t):
    e, _, _ = place()
    others = ep_others(e)
    greet([{"ep": d} for d in others])
    ring = RingReduce(p_ref, TOK, pc, snd, rcv, hop, (ssem, rsem), lsems)
    ring.start()
    small = [remote(t_ref.at[d], ot_ref.at[e], (s_t, r_t), k, {"ep": d}) for k, d in enumerate(others)]
    own = pltpu.make_async_copy(t_ref.at[e], ot_ref.at[e], lsem)
    for copy in small:
        copy.start()
    own.start()
    ring.middle()
    ring.finish(o_ref)
    own.wait()
    for copy in small:
        copy.wait_recv()
    for copy in small:
        copy.wait_send()


def reduce_rows(p, t):
    w = p.shape[1]
    return comm_call(
        reduce_rows_kernel,
        "reduce_rows",
        5,
        [shape((TOK, w)), shape(t.shape)],
        [ANY, ANY],
        [VM, ANY],
        reduce_scratch(TOK, w) + [DMA(()), DMA((7,)), DMA((7,))],
    )(p, t)


WB = D + 128


def reduce_last_kernel(
    gn, wb, dw, o_gn, o_wb, o_dw,
    pc1, snd1, rcv1, hop1, ss1, rs1, ls1,
    pc2, snd2, rcv2, hop2, ss2, rs2, ls2,
    wsum, wheld, dheld, dsum, lsem, s_w, r_w, s_d, r_d, s_e, r_e,
):
    r = lax.axis_index("rep")
    e, _, _ = place()
    others = ep_others(e)
    copies = rep_others(r)
    greet([{"ep": d} for d in others] + [{"rep": d} for d in copies])
    ring_w = RingReduce(wb, 128, pc2, snd2, rcv2, hop2, (ss2, rs2), ls2)
    ring_g = RingReduce(gn, TOK, pc1, snd1, rcv1, hop1, (ss1, rs1), ls1)
    ring_w.start()
    ring_g.start()

    def part(ref, b, n):
        return ref.at[pl.ds(pl.multiple_of(b * n, 8), n)]

    spread_d = [remote(part(dw, d, 64), dheld.at[r], (s_d, r_d), k, {"rep": d}) for k, d in enumerate(copies)]
    own_d = pltpu.make_async_copy(part(dw, r, 64), dheld.at[r], lsem.at[0])
    for copy in spread_d + [own_d]:
        copy.start()
    ring_w.middle()
    ring_g.middle()
    ring_w.finish(wsum)
    spread_w = [remote(part(wsum, d, 8), wheld.at[r], (s_w, r_w), k, {"rep": d}) for k, d in enumerate(copies)]
    own_w = pltpu.make_async_copy(part(wsum, r, 8), wheld.at[r], lsem.at[1])
    for copy in spread_w + [own_w]:
        copy.start()
    own_d.wait()
    for copy in spread_d:
        copy.wait_recv()
    total = dheld[0]
    for k in range(1, REP):
        total = total + dheld[k]
    dsum[...] = total
    spread_e = [remote(part(dsum, d, 8), o_dw.at[e], (s_e, r_e), k, {"ep": d}) for k, d in enumerate(others)]
    own_e = pltpu.make_async_copy(part(dsum, e, 8), o_dw.at[e], lsem.at[2])
    for copy in spread_e + [own_e]:
        copy.start()
    ring_g.finish(o_gn)
    own_w.wait()
    for copy in spread_w:
        copy.wait_recv()
    total = wheld[0]
    for k in range(1, REP):
        total = total + wheld[k]
    o_wb[...] = total
    own_e.wait()
    for copy in spread_e:
        copy.wait_recv()
    for copy in spread_d + spread_w + spread_e:
        copy.wait_send()


def reduce_last(gn, wb, dw):
    return comm_call(
        reduce_last_kernel,
        "reduce_last",
        6,
        [shape((TOK, D)), shape((8, WB)), shape((EP, 8, 256))],
        [ANY] * 3,
        [VM, VM, ANY],
        reduce_scratch(TOK, D)
        + reduce_scratch(128, WB)
        + [
            pltpu.VMEM((128, WB), F32),
            pltpu.VMEM((REP, 8, WB), F32),
            pltpu.VMEM((REP, 64, 256), F32),
            pltpu.VMEM((64, 256), F32),
            DMA((3,)),
            DMA((15,)),
            DMA((15,)),
            DMA((15,)),
            DMA((15,)),
            DMA((7,)),
            DMA((7,)),
        ],
    )(gn, wb, dw)


def column(row):
    return jnp.transpose(jnp.broadcast_to(row, (128, row.shape[1])))


def lane_row(values):
    return dot_nt(jnp.ones((8, 128), F32), values, precision=HIGH)[0:1]


def project_kernel(x_ref, w_ref, gain_ref, o_ref, st_ref):
    i = pl.program_id(0)
    x = x_ref[...].astype(F32)
    r = lax.rsqrt(jnp.mean(x * x, axis=1, keepdims=True) + EPSILON)
    normed = (x * r * gain_ref[...]).astype(BF)
    lin = dot(normed, w_ref[...])
    o_ref[...] = lin
    keys = iota((TOK, 128), 1) < HEAD_DIM
    sq = lin * lin
    st_ref[pl.ds(2 * i, 1)] = lane_row(sq[:, :128])
    st_ref[pl.ds(2 * i + 1, 1)] = lane_row(jnp.where(keys, sq[:, 128:], 0.0))


def project(x_all, w, gain):
    return pl.pallas_call(
        project_kernel,
        grid=(EP,),
        out_shape=[shape((LENGTH, 256)), shape((2 * EP, 256))],
        in_specs=[
            pl.BlockSpec((TOK, D), lambda i: (i, 0)),
            pl.BlockSpec((D, 256), lambda i: (0, 0)),
            pl.BlockSpec((1, D), lambda i: (0, 0)),
        ],
        out_specs=[pl.BlockSpec((TOK, 256), lambda i: (i, 0)), pl.BlockSpec((16, 256), lambda i: (0, 0))],
        compiler_params=pltpu.CompilerParams(vmem_limit_bytes=32 * MIB),
        name="project",
    )(x_all, w, gain)


def turn_tables():
    half = HEAD_DIM // 2
    freq = np.float32(ROPE_BASE) ** (-(np.arange(half, dtype=np.float32) * np.float32(2.0) / np.float32(HEAD_DIM)))
    angles = np.arange(LENGTH, dtype=np.float32)[:, None] * freq.astype(np.float32)[None, :]
    c, s = np.cos(angles), np.sin(angles)
    cosine = np.concatenate([c, c, c, c], axis=1)
    sine = np.concatenate([-s, s, -s, s], axis=1)
    return cosine.astype(np.float32), sine.astype(np.float32)


def turn(u, cosine, sine):
    early = iota(u.shape, 1) % HEAD_DIM < HEAD_DIM // 2
    partner = jnp.where(early, pltpu.roll(u, 96, 1), pltpu.roll(u, 32, 1))
    return u * cosine + partner * sine


def block_rows(b):
    return pl.ds(pl.multiple_of(b * TOK, TOK), TOK)


def key_start(i):
    return jnp.maximum(i - WINDOW // TOK, 0)


def stack_heads(values):
    first = iota(values.shape, 1) < HEAD_DIM
    return jnp.concatenate([jnp.where(first, values, 0.0), jnp.where(first, 0.0, values)], axis=0)


def merge_heads(values):
    first = iota((TOK, 128), 1) < HEAD_DIM
    return jnp.where(first, values[:TOK], values[TOK:])


def attend_kernel(
    lin, st, lo, cos_ref, sin_ref, gain, q_o, k_o, v_o, a_o, lse_o, s_scr, q2_scr, lo_scr, m_scr, l_scr, acc
):
    first = iota((TOK, 128), 1) < HEAD_DIM

    def prepare(b, carry):
        rows = block_rows(b)
        cq = column(lax.rsqrt(st[pl.ds(2 * b, 1)] * (1.0 / D) + EPSILON))
        ck = column(lax.rsqrt(st[pl.ds(2 * b + 1, 1)] * (1.0 / KV) + EPSILON))
        cosine, sine = cos_ref[rows], sin_ref[rows]
        q_o[rows] = turn(lin[rows, :128] * cq * gain[:, :128], cosine, sine).astype(BF)
        kv = lin[rows, 128:]
        kv = jnp.where(first, turn(kv * ck * gain[:, 128:], cosine, sine), kv)
        other = pltpu.roll(kv, HEAD_DIM, 1)
        k_o[rows] = jnp.where(first, kv, other).astype(BF)
        v_o[rows] = jnp.where(first, other, kv).astype(BF)
        return carry

    lax.fori_loop(0, EP, prepare, 0)

    def queries(i, carry):
        rows = block_rows(i)
        q2_scr[...] = stack_heads(q_o[rows].astype(F32) * HEAD_DIM ** (-0.5)).astype(BF)
        lo_col = column(lo[pl.ds(i, 1)])
        lo_scr[...] = jnp.concatenate([lo_col, lo_col], axis=0)
        m_scr[...] = jnp.full((2 * TOK, 128), MASKED, F32)
        l_scr[...] = jnp.zeros((2 * TOK, 128), F32)
        acc[...] = jnp.zeros((2 * TOK, 128), F32)
        j0 = key_start(i)

        def score(j, inner):
            s = dot_nt(q2_scr[...], k_o[block_rows(j)])
            key = (iota((2 * TOK, TOK), 1) + j * TOK).astype(F32)
            query = (iota((2 * TOK, TOK), 0) % TOK + i * TOK).astype(F32)
            s = jnp.where((key >= lo_scr[:, :1]) & (key <= query), s, MASKED)
            s_scr[j - j0] = s
            m_scr[...] = jnp.maximum(m_scr[...], jnp.maximum(s[:, :128], s[:, 128:]))
            return inner

        lax.fori_loop(j0, i + 1, score, 0)
        m = jnp.max(m_scr[...], axis=1, keepdims=True)
        m_scr[...] = jnp.broadcast_to(m, (2 * TOK, 128))

        def weigh(j, inner):
            p = jnp.exp(s_scr[j - j0] - m_scr[:, :1])
            l_scr[...] += p[:, :128] + p[:, 128:]
            acc[...] += dot(p.astype(BF), v_o[block_rows(j)])
            return inner

        lax.fori_loop(j0, i + 1, weigh, 0)
        total = jnp.sum(l_scr[...], axis=1, keepdims=True)
        a_o[rows] = merge_heads(acc[...] / total).astype(BF)
        lse = jnp.broadcast_to(m_scr[:, :1] + jnp.log(total), (2 * TOK, 128))
        lse_o[i] = jnp.transpose(lse)[:8]
        return carry

    lax.fori_loop(0, EP, queries, 0)


def attend(lin, st, lo, cosine, sine, gain):
    return pl.pallas_call(
        attend_kernel,
        out_shape=[shape((LENGTH, 128), BF)] * 4 + [shape((EP, 8, 2 * TOK))],
        in_specs=[VM] * 6,
        out_specs=[VM] * 5,
        scratch_shapes=[
            pltpu.VMEM((5, 2 * TOK, TOK), F32),
            pltpu.VMEM((2 * TOK, 128), BF),
            pltpu.VMEM((2 * TOK, 128), F32),
            pltpu.VMEM((2 * TOK, 128), F32),
            pltpu.VMEM((2 * TOK, 128), F32),
            pltpu.VMEM((2 * TOK, 128), F32),
        ],
        compiler_params=pltpu.CompilerParams(vmem_limit_bytes=48 * MIB),
        name="attend",
    )(lin, st, lo, cosine, sine, gain)


def attend_back_kernel(
    q_i, k_i, v_i, a_i, lse, lo, go, lin, st, cos_ref, sin_ref, gain, u_o, st_o, q2_scr, do2_scr, row_scr, dq, dk, dv
):
    first = iota((TOK, 128), 1) < HEAD_DIM
    dk[...] = jnp.zeros((LENGTH, 128), F32)
    dv[...] = jnp.zeros((LENGTH, 128), F32)

    def queries(i, carry):
        rows = block_rows(i)
        q2_scr[...] = stack_heads(q_i[rows].astype(F32) * HEAD_DIM ** (-0.5)).astype(BF)
        grad = stack_heads(go[rows].astype(F32))
        do2_scr[...] = grad.astype(BF)
        out = a_i[rows].astype(F32)
        row_scr[0:1] = lane_row(grad * jnp.concatenate([out, out], axis=0))
        row_scr[1:2] = lse[i][0:1]
        row_scr[2:3] = jnp.concatenate([lo[pl.ds(i, 1)]] * 2, axis=1)
        dq[...] = jnp.zeros((128, 2 * TOK), F32)

        def keys(j, inner):
            key_rows = block_rows(j)
            kk = k_i[key_rows]
            key = (iota((TOK, 2 * TOK), 0) + j * TOK).astype(F32)
            query = (iota((TOK, 2 * TOK), 1) % TOK + i * TOK).astype(F32)
            allowed = (key >= row_scr[2:3]) & (key <= query)
            s = dot_nt(kk, q2_scr[...])
            p = jnp.where(allowed, jnp.exp(s - row_scr[1:2]), 0.0)
            dp = dot_nt(v_i[key_rows], do2_scr[...])
            ds = (p * (dp - row_scr[0:1])).astype(BF)
            dv[key_rows] += dot(p.astype(BF), do2_scr[...])
            dk[key_rows] += dot(ds, q2_scr[...])
            dq[...] += dot_tn(kk, ds)
            return inner

        lax.fori_loop(key_start(i), i + 1, keys, 0)
        grad_q = merge_heads(jnp.transpose(dq[...])) * HEAD_DIM ** (-0.5)
        grad_q = turn(grad_q.astype(BF).astype(F32), cos_ref[rows], -sin_ref[rows])
        u_o[rows, :128] = grad_q
        cq = column(lax.rsqrt(st[pl.ds(2 * i, 1)] * (1.0 / D) + EPSILON))
        st_o[pl.ds(2 * i, 1)] = lane_row(grad_q * gain[:, :128] * lin[rows, :128] * cq)
        return carry

    lax.fori_loop(0, EP, queries, 0)

    def close(b, carry):
        rows = block_rows(b)
        grad_k, grad_v = dk[rows], dv[rows]
        grad_k = grad_k + pltpu.roll(grad_k, HEAD_DIM, 1)
        grad_v = grad_v + pltpu.roll(grad_v, HEAD_DIM, 1)
        both = jnp.where(first, grad_k, grad_v).astype(BF).astype(F32)
        both = jnp.where(first, turn(both, cos_ref[rows], -sin_ref[rows]), both)
        u_o[rows, 128:] = both
        ck = column(lax.rsqrt(st[pl.ds(2 * b + 1, 1)] * (1.0 / KV) + EPSILON))
        st_o[pl.ds(2 * b + 1, 1)] = lane_row(
            jnp.where(first, both * gain[:, 128:] * lin[rows, 128:] * ck, 0.0)
        )
        return carry

    lax.fori_loop(0, EP, close, 0)


def attend_back(q, k, v, a, lse, lo, go, lin, st, cosine, sine, gain):
    return pl.pallas_call(
        attend_back_kernel,
        out_shape=[shape((LENGTH, 256)), shape((2 * EP, 256))],
        in_specs=[VM] * 12,
        out_specs=[VM] * 2,
        scratch_shapes=[
            pltpu.VMEM((2 * TOK, 128), BF),
            pltpu.VMEM((2 * TOK, 128), BF),
            pltpu.VMEM((8, 2 * TOK), F32),
            pltpu.VMEM((128, 2 * TOK), F32),
            pltpu.VMEM((LENGTH, 128), F32),
            pltpu.VMEM((LENGTH, 128), F32),
        ],
        compiler_params=pltpu.CompilerParams(vmem_limit_bytes=48 * MIB),
        name="attend_back",
    )(q, k, v, a, lse, lo, go, lin, st, cosine, sine, gain)


def project_back_kernel(x_ref, u_ref, lin_ref, st, st2, gain, attn_gain, w_ref, gn_o, dw_o, ga_o, gqk_o, dwt):
    i = pl.program_id(0)
    first = iota((TOK, 128), 1) < HEAD_DIM

    @pl.when(i == 0)
    def _():
        dwt[...] = jnp.zeros_like(dwt)
        ga_o[...] = jnp.zeros_like(ga_o)
        gqk_o[...] = jnp.zeros_like(gqk_o)

    x = x_ref[...].astype(F32)
    r1 = lax.rsqrt(jnp.mean(x * x, axis=1, keepdims=True) + EPSILON)
    n1 = x * r1
    normed = (n1 * attn_gain[...]).astype(BF)
    u = u_ref[...]
    lin = lin_ref[...]
    cq = column(lax.rsqrt(st[pl.ds(2 * i, 1)] * (1.0 / D) + EPSILON))
    ck = column(lax.rsqrt(st[pl.ds(2 * i + 1, 1)] * (1.0 / KV) + EPSILON))
    mq = column(st2[pl.ds(2 * i, 1)] * (1.0 / D))
    mk = column(st2[pl.ds(2 * i + 1, 1)] * (1.0 / KV))
    nq = lin[:, :128] * cq
    nk = lin[:, 128:] * ck
    gq = cq * (u[:, :128] * gain[:, :128] - nq * mq)
    gk = jnp.where(first, ck * (u[:, 128:] * gain[:, 128:] - nk * mk), u[:, 128:])
    glin = jnp.concatenate([gq, gk], axis=1).astype(BF)
    gqk_o[0:1] += jnp.concatenate(
        [
            jnp.sum(u[:, :128] * nq, axis=0, keepdims=True),
            jnp.sum(u[:, 128:] * nk, axis=0, keepdims=True),
        ],
        axis=1,
    )
    gn = dot_nt(glin, w_ref[...])
    ga_o[0:1] += jnp.sum(gn * n1, axis=0, keepdims=True)
    gn_o[...] = gn.astype(BF)
    dwt[...] += dot_tn(glin, normed)

    @pl.when(i == EP - 1)
    def _():
        dw_o[...] = jnp.transpose(dwt[...])


def project_back(x_all, u, lin, st, st2, gain, attn_gain, w):
    def whole(dims):
        return pl.BlockSpec(dims, lambda i: tuple(0 for _ in dims))

    return pl.pallas_call(
        project_back_kernel,
        grid=(EP,),
        out_shape=[shape((LENGTH, D), BF), shape((D, 256)), shape((8, D)), shape((8, 256))],
        in_specs=[
            pl.BlockSpec((TOK, D), lambda i: (i, 0)),
            pl.BlockSpec((TOK, 256), lambda i: (i, 0)),
            pl.BlockSpec((TOK, 256), lambda i: (i, 0)),
            whole((16, 256)),
            whole((16, 256)),
            whole((1, 256)),
            whole((1, D)),
            whole((D, 256)),
        ],
        out_specs=[pl.BlockSpec((TOK, D), lambda i: (i, 0)), whole((D, 256)), whole((8, D)), whole((8, 256))],
        scratch_shapes=[pltpu.VMEM((256, D), F32)],
        compiler_params=pltpu.CompilerParams(vmem_limit_bytes=48 * MIB),
        name="project_back",
    )(x_all, u, lin, st, st2, gain, attn_gain, w)


ROWS = EP * CAP
HALF = 256


def experts_kernel(
    m_ref, g_ref, slot, gate, slots, wg, wu, wd, p_o, gg_o, dwg_o, dwu_o, dwd_o,
    a_s, c_s, gate_s, gg_s, act_s, gp_s, dgu_s, y_s, z_s,
):
    step = pl.program_id(0)

    def hits(row):
        return iota((CAP, TOK), 0) == row

    @pl.when(step < LOCAL)
    def _():
        def pick(s, carry):
            hit = hits(slot[0, pl.ds(s, 1)])
            chosen = jnp.where(hit, 1.0, 0.0).astype(BF)
            rows = pl.ds(pl.multiple_of(s * CAP, 32), CAP)
            a_s[rows] = dot(chosen, m_ref[block_rows(s)]).astype(BF)
            c_s[rows] = dot(chosen, g_ref[block_rows(s)]).astype(BF)
            weight = jnp.sum(jnp.where(hit, gate[0, pl.ds(s, 1)], 0.0), axis=1, keepdims=True)
            gate_s[rows] = jnp.broadcast_to(weight, (CAP, 128))
            return carry

        lax.fori_loop(0, EP, pick, 0)

        def rows_part(k, carry):
            rows = pl.ds(pl.multiple_of(k * HALF, HALF), HALF)
            a = a_s[rows]
            gate_lin = dot(a, wg[0])
            up_lin = dot(a, wu[0])
            sig = jax.nn.sigmoid(gate_lin)
            silu = gate_lin * sig
            act = (silu * up_lin).astype(BF)
            act_s[rows] = act
            weight = gate_s[rows][:, :1]
            produced = dot(act, wd[0]).astype(BF).astype(F32)
            cot = c_s[rows].astype(F32)
            gg = jnp.sum(produced * cot, axis=1, keepdims=True)
            gg_s[rows] = jnp.broadcast_to(gg, (HALF, 128))
            y_s[step, rows] = (weight * produced).astype(BF)
            grad = (weight * cot).astype(BF)
            gp_s[rows] = grad
            grad_act = dot_nt(grad, wd[0])
            dgate = (grad_act * up_lin * sig * (1.0 + gate_lin * (1.0 - sig))).astype(BF)
            dup = (grad_act * silu).astype(BF)
            dgu_s[rows, :FF] = dgate
            dgu_s[rows, FF:] = dup
            z_s[step, rows] = (dot_nt(dgate, wg[0]) + dot_nt(dup, wu[0])).astype(BF)
            return carry

        lax.fori_loop(0, ROWS // HALF, rows_part, 0)

        def gates_back(s, carry):
            hit = hits(slot[0, pl.ds(s, 1)])
            rows = pl.ds(pl.multiple_of(s * CAP, 32), CAP)
            gg_o[0, pl.ds(s, 1)] = jnp.sum(jnp.where(hit, gg_s[rows][:, :1], 0.0), axis=0, keepdims=True)
            return carry

        lax.fori_loop(0, EP, gates_back, 0)
        dwd_o[0] = dot_tn(act_s[...], gp_s[...]).astype(BF)
        dwg_o[0] = dot_tn(a_s[...], dgu_s[:, :FF]).astype(BF)
        dwu_o[0] = dot_tn(a_s[...], dgu_s[:, FF:]).astype(BF)

    @pl.when(step >= LOCAL)
    def _():
        s = step - LOCAL
        rows = pl.ds(pl.multiple_of(s * CAP, 32), CAP)
        chosen = jnp.concatenate(
            [jnp.where(hits(slots[k, pl.ds(s, 1)]), 1.0, 0.0).astype(BF) for k in range(LOCAL)], axis=0
        )
        y = jnp.concatenate([y_s[k, rows] for k in range(LOCAL)], axis=0)
        p_o[:, :D] = dot_tn(chosen, y).astype(BF)
        z = jnp.concatenate([z_s[k, rows] for k in range(LOCAL)], axis=0)
        p_o[:, D:] = dot_tn(chosen, z).astype(BF)


def experts(m_all, g_all, slot, gate, wg, wu, wd):
    def cur(*rest):
        return lambda i: (jnp.minimum(i, LOCAL - 1),) + rest

    once = pl.Buffered(1)
    return pl.pallas_call(
        experts_kernel,
        grid=(LOCAL + EP,),
        out_shape=[
            shape((LENGTH, 2 * D), BF),
            shape((LOCAL, EP, TOK)),
            shape((LOCAL, D, FF), BF),
            shape((LOCAL, D, FF), BF),
            shape((LOCAL, FF, D), BF),
        ],
        in_specs=[
            pl.BlockSpec((LENGTH, D), lambda i: (0, 0), pipeline_mode=once),
            pl.BlockSpec((LENGTH, D), lambda i: (0, 0), pipeline_mode=once),
            pl.BlockSpec((1, EP, TOK), cur(0, 0)),
            pl.BlockSpec((1, EP, TOK), cur(0, 0)),
            pl.BlockSpec((LOCAL, EP, TOK), lambda i: (0, 0, 0)),
            pl.BlockSpec((1, D, FF), cur(0, 0)),
            pl.BlockSpec((1, D, FF), cur(0, 0)),
            pl.BlockSpec((1, FF, D), cur(0, 0)),
        ],
        out_specs=[
            pl.BlockSpec((TOK, 2 * D), lambda i: (jnp.maximum(i - LOCAL, 0), 0)),
            pl.BlockSpec((1, EP, TOK), cur(0, 0)),
            pl.BlockSpec((1, D, FF), cur(0, 0)),
            pl.BlockSpec((1, D, FF), cur(0, 0)),
            pl.BlockSpec((1, FF, D), cur(0, 0)),
        ],
        scratch_shapes=[
            pltpu.VMEM((ROWS, D), BF),
            pltpu.VMEM((ROWS, D), BF),
            pltpu.VMEM((ROWS, 128), F32),
            pltpu.VMEM((ROWS, 128), F32),
            pltpu.VMEM((ROWS, FF), BF),
            pltpu.VMEM((ROWS, D), BF),
            pltpu.VMEM((ROWS, D), BF),
            pltpu.VMEM((LOCAL, ROWS, D), BF),
            pltpu.VMEM((LOCAL, ROWS, D), BF),
        ],
        compiler_params=pltpu.CompilerParams(vmem_limit_bytes=60 * MIB),
        name="experts",
    )(m_all, g_all, slot, gate, slot, wg, wu, wd)


def hidden_kernel(x_ref, a_ref, w_ref, gain, router, hit, hid_o, m_o, gate_o):
    hidden = x_ref[...].astype(F32) + dot(a_ref[...], w_ref[...])
    hid_o[...] = hidden
    r2 = lax.rsqrt(jnp.mean(hidden * hidden, axis=1, keepdims=True) + EPSILON)
    moe_in = (hidden * r2 * gain[...]).astype(BF)
    m_o[...] = moe_in
    logits = dot_nt(router[...], moe_in)
    chosen = hit[...] >= 0
    logits = jnp.where(chosen, logits, MASKED)
    raised = jnp.where(chosen, jnp.exp(logits - jnp.max(logits, axis=0, keepdims=True)), 0.0)
    gate_o[...] = raised / jnp.sum(raised, axis=0, keepdims=True)


def hidden_call(x, a, w, gain, router, hit):
    return pl.pallas_call(
        hidden_kernel,
        out_shape=[shape((TOK, D)), shape((TOK, D), BF), shape((EXPERTS, TOK))],
        in_specs=[VM] * 6,
        out_specs=[VM] * 3,
        compiler_params=pltpu.CompilerParams(vmem_limit_bytes=32 * MIB),
        name="hidden",
    )(x, a, w, gain, router, hit)


def hidden_back_kernel(
    hid, red, gg, gate, m_ref, cot, gain, router, w_ref, a_ref, out_o, gh_o, ga_o, dwo_o, dr_o, gf_o
):
    hidden = hid[...]
    out_o[...] = (hidden + red[:, :D]).astype(BF)
    weights = gate[...]
    grads = gg[...]
    mean = jnp.sum(weights * grads, axis=0, keepdims=True)
    grad_logits = (weights * (grads - mean)).astype(BF)
    dr_o[...] = dot(grad_logits, m_ref[...])
    grad_moe = red[:, D:] + dot_tn(grad_logits, router[...])
    r2 = lax.rsqrt(jnp.mean(hidden * hidden, axis=1, keepdims=True) + EPSILON)
    n = hidden * r2
    gf_o[...] = jnp.sum(grad_moe * n, axis=0, keepdims=True)
    u = grad_moe * gain[...]
    grad_hidden = cot[...].astype(F32) + r2 * (u - n * jnp.mean(u * n, axis=1, keepdims=True))
    gh_o[...] = grad_hidden
    branch = grad_hidden.astype(BF)
    ga_o[...] = dot_nt(branch, w_ref[...]).astype(BF)
    dwo_o[...] = dot_tn(a_ref[...], branch).astype(BF)


def hidden_back(hid, red, gg, gate, m, cot, gain, router, w, a):
    return pl.pallas_call(
        hidden_back_kernel,
        out_shape=[
            shape((TOK, D), BF),
            shape((TOK, D)),
            shape((TOK, D), BF),
            shape((D, D), BF),
            shape((EXPERTS, D)),
            shape((1, D)),
        ],
        in_specs=[VM] * 10,
        out_specs=[VM] * 6,
        compiler_params=pltpu.CompilerParams(vmem_limit_bytes=48 * MIB),
        name="hidden_back",
    )(hid, red, gg, gate, m, cot, gain, router, w, a)


def body(
    tokens,
    segments,
    routes,
    w_query,
    w_key,
    w_value,
    w_out,
    w_router,
    gain_attn,
    gain_query,
    gain_key,
    gain_ffn,
    w_gate,
    w_up,
    w_down,
    out_grad,
):
    r = lax.axis_index("rep")
    e = lax.axis_index("ep")
    cols = jnp.concatenate(
        [w_query.reshape(8, EP, 128), w_key.reshape(8, EP, 64), w_value.reshape(8, EP, 64)], axis=2
    )
    cols = cols.reshape(8, EP, 2, 128).transpose(1, 2, 0, 3).reshape(EP, 16, 128)
    small = jnp.concatenate([gain_attn, gain_query, gain_key, gain_ffn, w_router.reshape(-1)])
    small = jnp.pad(small, (0, 2048 - small.shape[0])).reshape(1, 16, 128)
    wsl = jnp.concatenate([cols, jnp.broadcast_to(small, (EP, 16, 128))], axis=1)
    wo = w_out.reshape(8, 8, 128).transpose(1, 0, 2).reshape(64, 128)

    expert_ids = jnp.arange(EXPERTS, dtype=jnp.int32)
    routed = jnp.sum((routes[:, :, None] == expert_ids[None, None, :]).astype(BF), axis=1)
    before = (jnp.arange(TOK)[:, None] < jnp.arange(TOK)[None, :]).astype(BF)
    rank = lax.dot_general(routed, before, TN, preferred_element_type=F32)
    slot_own = jnp.where(routed.T > 0, rank, -1.0)

    seg = segments[0]
    positions = jnp.arange(LENGTH, dtype=jnp.int32)
    zeros = jnp.sum((seg == 0).astype(jnp.int32))
    ones = jnp.sum((seg <= 1).astype(jnp.int32))
    opening = jnp.where(seg == 0, 0, jnp.where(seg == 1, zeros, ones))
    lo = jnp.maximum(opening, positions - (WINDOW - 1)).astype(F32).reshape(EP, TOK)
    cosine, sine = turn_tables()

    x_all, g_all, wg_all, wo_all = gather_first(tokens, out_grad, wsl, wo)

    w_cols = wg_all[:, :, :16].reshape(128, 2, 8, 128).transpose(0, 2, 1, 3).reshape(D, 256)
    small_all = wg_all[:, :, 16:].reshape(128, 2048)
    attn_gain = small_all[:, :8].reshape(1, D).astype(F32)
    query_gain = small_all[:, 8:16].reshape(1, D).astype(F32)
    key_gain = small_all[:, 16:20].reshape(1, KV).astype(F32)
    ffn_gain = small_all[:, 20:28].reshape(1, D).astype(F32)
    router = small_all[:, 28:284].reshape(D, EXPERTS).T
    whole_out = wo_all.reshape(128, 8, 8, 128).transpose(0, 2, 1, 3).reshape(D, D)
    qk_gain = jnp.concatenate(
        [
            lax.dynamic_slice_in_dim(query_gain, e * 128, 128, 1),
            lax.dynamic_slice_in_dim(key_gain, e * 64, 64, 1),
            jnp.ones((1, 64), F32),
        ],
        axis=1,
    )

    lin, sums = project(x_all, w_cols, attn_gain)
    st = sum_stats(sums, "sum_stats", 2)
    q, k, v, att, lse = attend(lin, st, lo, cosine, sine, qk_gain)
    attended = swap_heads(att, True, "swap_heads", 3)
    hidden, moe_in, gates = hidden_call(tokens, attended, whole_out, ffn_gain, router, slot_own)
    m_all, tables = gather_rows(moe_in, jnp.concatenate([slot_own, gates], axis=0))
    slot = lax.dynamic_slice_in_dim(tables, e * LOCAL, LOCAL, 1).transpose(1, 0, 2).astype(jnp.int32)
    gate = lax.dynamic_slice_in_dim(tables, EXPERTS + e * LOCAL, LOCAL, 1).transpose(1, 0, 2)
    part, gg, dwg, dwu, dwd = experts(m_all, g_all, slot, gate, w_gate, w_up, w_down)
    expert_sums = [
        lax.psum_scatter(value, "rep", scatter_dimension=1, tiled=True).astype(F32) for value in (dwg, dwu, dwd)
    ]
    gg = jnp.pad(gg.transpose(1, 0, 2), ((0, 0), (0, 4), (0, 0)))
    red, gg = reduce_rows(part, gg)
    gg = gg[:, :LOCAL].reshape(EXPERTS, TOK)
    attended_t = attended.reshape(TOK, REP, EP, 8).transpose(0, 2, 1, 3).reshape(TOK, D)
    output, grad_hidden, grad_att, dwo, drouter, dffn = hidden_back(
        hidden, red, gg, gates, moe_in, out_grad, ffn_gain, router, whole_out, attended_t
    )
    go = swap_heads(grad_att, False, "swap_heads_back", 7)
    u, sums2 = attend_back(q, k, v, att, lse, lo, go, lin, st, cosine, sine, qk_gain)
    st2 = sum_stats(sums2, "sum_stats_back", 8)
    gn, dw, dattn, dqk = project_back(x_all, u, lin, st, st2, qk_gain, attn_gain, w_cols)

    dquery = lax.dynamic_update_slice(jnp.zeros((1, D), F32), dqk[0:1, :128], (0, e * 128))
    dkey = lax.dynamic_update_slice(jnp.zeros((1, KV), F32), dqk[0:1, 128:192], (0, e * 64))
    dkey = jnp.pad(dkey.reshape(128, 4), ((0, 0), (0, 4))).reshape(1, D)
    vectors = jnp.concatenate([drouter, dattn[0:1], dquery, dkey, dffn], axis=0)
    vectors = vectors.reshape(36, REP, EP, 8).transpose(2, 1, 3, 0).reshape(D, 36)
    wb = jnp.concatenate([dwo, jnp.pad(vectors, ((0, 0), (0, 128 - 36))).astype(BF)], axis=1)
    gn_sum, wb_sum, dw_sum = reduce_last(gn, wb, dw)

    x = tokens.astype(F32)
    r1 = lax.rsqrt(jnp.mean(x * x, axis=-1, keepdims=True) + EPSILON)
    n1 = x * r1
    z = gn_sum * attn_gain
    input_grad = grad_hidden + r1 * (z - n1 * jnp.mean(z * n1, axis=-1, keepdims=True))
    dw_rows = dw_sum.transpose(1, 0, 2)
    return (
        output,
        input_grad,
        dw_rows[:, :, :128].reshape(8, D),
        dw_rows[:, :, 128:192].reshape(8, KV),
        dw_rows[:, :, 192:].reshape(8, KV),
        wb_sum[:, :D],
        wb_sum[:, D : D + EXPERTS],
        wb_sum[:, D + 32],
        wb_sum[:, D + 33],
        wb_sum[:4, D + 34],
        wb_sum[:, D + 35],
        expert_sums[0],
        expert_sums[1],
        expert_sums[2],
    )


def solution(mesh):
    both = P(("rep", "ep"), None)
    line = P(("rep", "ep"))
    owner = P("ep", None, None)
    kept = P("ep", "rep", None)
    return jax.shard_map(
        body,
        mesh=mesh,
        in_specs=(both, P("rep", None)) + (both,) * 6 + (line,) * 4 + (owner,) * 3 + (both,),
        out_specs=(both,) * 7 + (line,) * 4 + (kept,) * 3,
        check_vma=False,
    )
```

time: 3510 us -> 494 us (0.14)
  waiting for transfers between devices: 2810 us -> 71.2 us
  Pallas kernels: 0 us -> 347 us
  blocking collectives: 311 us -> 0 us
  matrix products: 145 us -> 0.15 us
  local copies, waits for them, and re-layouts: 111 us -> 46.7 us
  other arithmetic: 70.8 us -> 11.9 us
    reduce_scatter x7 -> x3, waiting for transfers between devices: 2550 us -> 70 us  [body(): lax.psum_scatter(value, 'rep', scatter_dimension=1, tiled=True).astype(F32)]
    pallas_call x0 -> x15, Pallas kernels: none -> 347 us  [the longest x1 65.8 us: gather_first(): comm_call(gather_first_kernel, 'gather_first', 1, [shape((EP * TOK, D), B...]
    unnamed x2 -> x0, blocking collectives: 149 us -> none
    dot_general x32 -> x1, matrix products: 145 us -> 0.15 us  [body(): rank = lax.dot_general(routed, before, TN, preferred_element_type=F32)]
    all_to_all x3 -> x0, waiting for transfers between devices: 118 us -> none  [the longest x1 65.2 us: body(): lax.all_to_all(grad_send, 'ep', split_axis=0, concat_axis=0, tiled=True)]
    all_gather x4 -> x0, waiting for transfers between devices: 93.8 us -> none  [the longest x1 43.1 us: body(): lax.all_gather(shards[3], ('rep', 'ep'), axis=0, tiled=True)]
    all_gather x1 -> x0, blocking collectives: 92.2 us -> none  [body(): lax.all_gather(shards[4], ('rep', 'ep'), axis=0, tiled=True)]
    all_to_all x1 -> x0, blocking collectives: 69.7 us -> none  [body(): lax.all_to_all(send_rows, 'ep', split_axis=0, concat_axis=0, tiled=True)]
  transfers between devices with their start and end apart: 23 -> 3, of which waited for: 15 -> 1; matrix products, arithmetic and copies ran while one was open for 7% -> 4% of each run, Pallas kernels for 0% -> 28%
where the time goes in v1:
time: 494 us; the launch traced here: 492 us
  Pallas kernels  347 us (70%)
  waiting for transfers between devices  71.2 us (14%)
  local copies, waits for them, and re-layouts  46.7 us (9%)
  between operations  14.3 us (3%)
  other arithmetic  11.9 us (2%)
    reduce_scatter x3, waiting for transfers between devices, body(): lax.psum_scatter(value, 'rep', scatter_dimension=1, tiled=True).astype(F32)  70 us
    pallas_call x1, Pallas kernels, gather_first(): comm_call(gather_first_kernel, 'gather_first', 1, [shape((EP * TOK, D), B...  65.8 us
    pallas_call x1, Pallas kernels, experts(): pl.pallas_call(experts_kernel, grid=(LOCAL + EP,), out_shape=[shape((LENG...  63.7 us
    pallas_call x1, Pallas kernels, reduce_rows(): comm_call(reduce_rows_kernel, 'reduce_rows', 5, [shape((TOK, w)), shape(t...  41.5 us
    pallas_call x1, Pallas kernels, reduce_last(): comm_call(reduce_last_kernel, 'reduce_last', 6, [shape((TOK, D)), shape((...  34.7 us
    pallas_call x1, Pallas kernels, attend_back(): pl.pallas_call(attend_back_kernel, out_shape=[shape((LENGTH, 256)), shape...  31.3 us
    pallas_call x1, Pallas kernels, gather_rows(): comm_call(gather_rows_kernel, 'gather_rows', 4, [shape((EP * TOK, D), BF)...  28.6 us
    unnamed x82, local copies, waits for them, and re-layouts  26.7 us
  transfers between devices with their start and end apart: 3, of which 1 were waited for; matrix products, arithmetic and copies ran while one was open for 4% of the time, Pallas kernels for 28%

profile of v1, /device:TPU:1, one launch (start us, length us, event | category | flops | bytes accessed | tf_op | source)
XLA Modules:
  0.0 491.9 jit_solution(10714801866587150048)
XLA Ops:
  7.2 0.8 reshape.210
  8.0 2.8 concatenate.34
  10.8 0.8 reshape.206
  11.6 0.8 reshape.207
  12.4 0.8 maximum_bitcast_fusion
  13.2 1.0 copy-done.3
  14.2 1.0 copy-done.14
  15.3 0.7 copy-done.35
  16.0 65.8 %gather_first.1 = (bf16[2048,1024]{1,0:T(8,128)(2,1)}, bf16[2048,1024]{1,0:T(8,128)(2,1)}, bf16[16,8,32,128]{3,2,1,0:T(8,128)(2,1)S(1)}, bf16[16,8,64,128]{3,2,1,0:T(8,128)(2,1)S(1)}) custom-call(bf16[256,1024]{1,0:T(8,128)(2,1)S(1)} %copy-done.3, bf16[256,1024]{1,0:T(8,128)(2,1)S(1)} %copy-done.14, bf16[8,32,128]{2,1,0:T(8,128)(2,1)S(1)} %pad_maximum_fusion.wsl, ...), custom_call_target="tpu_custom_call" | custom-call | tf_op jit(solution)/shard_map/gather_first/pallas_call | solution.py:316
  82.3 1.0 slice_convert_fusion
  83.3 0.7 fusion.11
  83.9 1.3 fusion.12
  85.6 0.9 reshape.230.gain
  87.0 2.2 copy-done.2
  89.2 7.6 %project.1 = (f32[2048,256]{1,0:T(8,128)S(1)}, f32[16,256]{1,0:T(8,128)S(1)}) custom-call(bf16[2048,1024]{1,0:T(8,128)(2,1)S(1)} %copy-done.2, bf16[1024,256]{1,0:T(8,128)(2,1)S(1)} %bitcast.56, f32[1,1024]{1,0:T(1,128)S(1)} %reshape.227.gain_ref.attn_gain), custom_call_target="tpu_custom_call" | custom-call | tf_op jit(solution)/shard_map/project/pallas_call | solution.py:573
  96.8 1.3 copy-done
  98.1 6.2 %sum_stats.1.st = f32[16,256]{1,0:T(8,128)S(1)} custom-call(f32[16,256]{1,0:T(8,128)S(1)} %get-tuple-element.55.x_ref), custom_call_target="tpu_custom_call" | custom-call | tf_op jit(solution)/shard_map/sum_stats/pallas_call | solution.py:351
  104.5 1.2 copy-done.9
  105.7 1.2 copy-done.11
  106.9 25.6 %attend.1 = (bf16[2048,128]{1,0:T(8,128)(2,1)S(1)}, bf16[2048,128]{1,0:T(8,128)(2,1)S(1)}, bf16[2048,128]{1,0:T(8,128)(2,1)S(1)}, bf16[2048,128]{1,0:T(8,128)(2,1)S(1)}, f32[8,8,512]{2,1,0:T(8,128)S(1)}) custom-call(f32[2048,256]{1,0:T(8,128)} %copy-done, f32[16,256]{1,0:T(8,128)S(1)} %sum_stats.1.st, f32[8,256]{1,0:T(8,128)S(1)} %maximum_convert_fusion.lo, ...), custom_call_target="tpu_custom_call" | custom-call | tf_op jit(solution)/shard_map/attend/pallas_call | solution.py:682
  132.6 10.0 %swap_heads.1.a_ref = bf16[256,1024]{1,0:T(8,128)(2,1)S(1)} custom-call(bf16[2048,128]{1,0:T(8,128)(2,1)S(1)} %get-tuple-element.56.x_ref.a_i), custom_call_target="tpu_custom_call" | custom-call | tf_op jit(solution)/shard_map/swap_heads/pallas_call | solution.py:390
  142.7 1.2 hidden.1
  143.9 1.0 copy-done.23
  144.9 28.6 %gather_rows.1 = (bf16[2048,1024]{1,0:T(8,128)(2,1)S(1)}, f32[8,64,256]{2,1,0:T(8,128)S(1)}) custom-call(bf16[256,1024]{1,0:T(8,128)(2,1)S(1)} %get-tuple-element.59.x_ref.m_ref, f32[64,256]{1,0:T(8,128)S(1)} %pad_maximum_fusion.1.t_ref), custom_call_target="tpu_custom_call" | custom-call | tf_op jit(solution)/shard_map/gather_rows/pallas_call | solution.py:422
  173.5 1.9 copy-done.8
  175.8 0.6 dynamic-slice_bitcast_fusion
  176.4 63.7 %experts.1 = (bf16[2048,2048]{1,0:T(8,128)(2,1)}, f32[4,8,256]{2,1,0:T(8,128)}, bf16[4,1024,512]{2,1,0:T(8,128)(2,1)}, bf16[4,1024,512]{2,1,0:T(8,128)(2,1)}, bf16[4,512,1024]{2,1,0:T(8,128)(2,1)}) custom-call(bf16[2048,1024]{1,0:T(8,128)(2,1)} %copy-done.8, bf16[2048,1024]{1,0:T(8,128)(2,1)} %get-tuple-element.62.g_ref, ...), custom_call_target="tpu_custom_call" | custom-call | tf_op jit(solution)/shard_map/experts/pallas_call | solution.py:929
  240.2 0.7 reduce-scatter.6.cloned.1.call-update
  242.2 41.5 %reduce_rows.1 = (f32[256,2048]{1,0:T(8,128)S(1)}, f32[8,8,256]{2,1,0:T(8,128)S(1)}) custom-call(bf16[2048,2048]{1,0:T(8,128)(2,1)} %get-tuple-element.64.p_ref, f32[8,8,256]{2,1,0:T(8,128)S(1)} %pad.19.t_ref), custom_call_target="tpu_custom_call" | custom-call | tf_op jit(solution)/shard_map/reduce_rows/pallas_call | solution.py:455
  283.8 1.3 copy-done.13
  285.2 1.2 copy-done.24
  286.4 5.5 %hidden_back.1 = (bf16[256,1024]{1,0:T(8,128)(2,1)}, f32[256,1024]{1,0:T(8,128)S(1)}, bf16[256,1024]{1,0:T(8,128)(2,1)S(1)}, bf16[1024,1024]{1,0:T(8,128)(2,1)},...) custom-call(f32[256,1024]{1,0:T(8,128)S(1)} %copy-done.24, f32[256,2048]{1,0:T(8,128)} %copy-done.13, ...), custom_call_target="tpu_custom_call" | custom-call | tf_op jit(solution)/shard_map/hidden_back/pallas_call | solution.py:1019
  291.9 1.0 copy-done.21
  292.9 0.8 copy-done.33
  293.7 0.9 copy.70
  294.6 1.2 concatenate.47
  295.8 1.0 copy-done.34
  296.8 10.3 %swap_heads_back.1.go = bf16[2048,128]{1,0:T(8,128)(2,1)S(1)} custom-call(bf16[256,1024]{1,0:T(8,128)(2,1)S(1)} %copy-done.34), custom_call_target="tpu_custom_call" | custom-call | tf_op jit(solution)/shard_map/swap_heads_back/pallas_call | solution.py:390
  307.2 1.2 copy-done.10
  308.4 1.2 copy-done.12
  309.6 1.0 copy-done.17
  310.7 1.0 copy-done.28
  311.7 1.1 copy-done.30
  312.8 1.0 copy-done.32
  313.8 31.3 %attend_back.1 = (f32[2048,256]{1,0:T(8,128)}, f32[16,256]{1,0:T(8,128)S(1)}) custom-call(bf16[2048,128]{1,0:T(8,128)(2,1)S(1)} %copy-done.28, bf16[2048,128]{1,0:T(8,128)(2,1)S(1)} %copy-done.30, bf16[2048,128]{1,0:T(8,128)(2,1)S(1)} %copy-done.32, bf16[2048,128]{1,0:T(8,128)(2,1)S(1)} %copy-done.17, f32[8,8,512]{2,1,0:T(8,128)S(1)} %get-tuple-element.73.lse, ...), custom_call_target="tpu_custom_call" | custom-call | tf_op jit(solution)/shard_map/attend_back/pallas_call | solution.py:761
  345.1 5.6 %sum_stats_back.1.st2 = f32[16,256]{1,0:T(8,128)S(1)} custom-call(f32[16,256]{1,0:T(8,128)S(1)} %get-tuple-element.76.x_ref), custom_call_target="tpu_custom_call" | custom-call | tf_op jit(solution)/shard_map/sum_stats_back/pallas_call | solution.py:351
  350.8 1.6 copy-done.20
  352.4 9.6 %project_back.1 = (bf16[2048,1024]{1,0:T(8,128)(2,1)}, f32[1024,256]{1,0:T(8,128)S(1)}, f32[8,1024]{1,0:T(8,128)S(1)}, f32[8,256]{1,0:T(8,128)S(1)}) custom-call(bf16[2048,1024]{1,0:T(8,128)(2,1)} %get-tuple-element.52.x_ref, f32[2048,256]{1,0:T(8,128)S(1)} %copy-done.20, f32[2048,256]{1,0:T(8,128)S(1)} %copy-done.1, f32[16,256]{1,0:T(8,128)S(1)} %sum_stats.1.st, ...), custom_call_target="tpu_custom_call" | custom-call | tf_op jit(solution)/shard_map/project_back/pallas_call | solution.py:825
  362.0 1.0 copy-done.25
  363.5 0.8 copy.74
  365.3 2.1 concatenate.43
  367.4 1.1 copy.76
  368.8 34.7 %reduce_last.1 = (f32[256,1024]{1,0:T(8,128)S(1)}, f32[8,1152]{1,0:T(8,128)S(1)}, f32[8,8,256]{2,1,0:T(8,128)S(1)}) custom-call(bf16[2048,1024]{1,0:T(8,128)(2,1)} %get-tuple-element.77.gn, bf16[1024,1152]{1,0:T(8,128)(2,1)S(1)} %fusion.1.wb, f32[1024,256]{1,0:T(8,128)S(1)} %copy-done.26), custom_call_target="tpu_custom_call" | custom-call | tf_op jit(solution)/shard_map/reduce_last/pallas_call | solution.py:526
  404.1 0.6 slice.75
  404.8 0.7 reshape.226
  405.4 0.7 reshape.225
  406.1 0.7 slice_reduce_fusion.3
  406.8 0.7 slice_reduce_fusion
  408.1 0.6 slice_bitcast_fusion.1
  408.7 1.3 fusion.7
  410.0 1.8 convert_element_type.105
  411.8 1.8 convert_element_type.104
  413.6 70.0 %reduce-scatter.4.cloned.1.call-done = bf16[4,64,512]{2,1,0:T(8,128)(2,1)} async-done(((bf16[4,1024,512]{2,1,0:T(8,128)(2,1)}), bf16[4,64,512]{2,1,0:T(8,128)(2,1)}) %reduce-scatter.4.cloned.1.call-update) | async-done | bytes 262160 | tf_op jit(solution)/shard_map/reduce_scatter | solution.py:1108
  483.5 1.8 convert_element_type.103
  (121 shorter events, 6.1 us)
Async XLA Ops:
  7.2 76.1 %copy-start.38 = (s32[1,2048]{1,0:T(1,128)S(1)}, s32[1,2048]{1,0:T(1,128)}, u32[]{:S(2)}) copy-start(s32[1,2048]{1,0:T(1,128)} %param.19) | copy-start | bytes 24580
  7.2 78.1 %copy-start.39 = (s32[256,8]{0,1:T(8,128)S(1)}, s32[256,8]{0,1:T(8,128)}, u32[]{:S(2)}) copy-start(s32[256,8]{0,1:T(8,128)} %param.20) | copy-start | bytes 24580
  7.2 402.8 %reduce-scatter.8.cloned.1.call-start = ((), (), s32[]{:S(2)}) async-start(), calls=%async_computation.5 | async-start | bytes 4456448 | tf_op jit(solution)/shard_map/reduce_scatter | solution.py:1108
  13.2 1.0 copy-start.3
  14.2 1.0 copy-start.14
  15.3 0.7 copy-start.35
  81.8 60.9 %copy-start.5 = (bf16[16,8,64,128]{3,2,1,0:T(8,128)(2,1)}, bf16[16,8,64,128]{3,2,1,0:T(8,128)(2,1)S(1)}, u32[]{:S(2)}) copy-start(bf16[16,8,64,128]{3,2,1,0:T(8,128)(2,1)S(1)} %get-tuple-element.57) | copy-start | bytes 6291460
  82.0 50.6 %copy-start.6 = (bf16[16,8,16,128]{3,2,1,0:T(8,128)(2,1)}, bf16[16,8,16,128]{3,2,1,0:T(8,128)(2,1)S(1)}, u32[]{:S(2)}) copy-start(bf16[16,8,16,128]{3,2,1,0:T(8,128)(2,1)S(1)} %get-tuple-element.96) | copy-start | bytes 1572868
  87.0 2.2 copy-start.2
  89.2 53.4 %copy-start.4 = (bf16[256,1024]{1,0:T(8,128)(2,1)S(1)}, bf16[256,1024]{1,0:T(8,128)(2,1)}, u32[]{:S(2)}) copy-start(bf16[256,1024]{1,0:T(8,128)(2,1)} %x_ref.1) | copy-start | bytes 1572868
  96.8 1.3 copy-start
  104.5 1.2 copy-start.9
  105.7 1.2 copy-start.11
  132.6 12.3 %copy-start.16 = (bf16[2048,128]{1,0:T(8,128)(2,1)}, bf16[2048,128]{1,0:T(8,128)(2,1)S(1)}, u32[]{:S(2)}) copy-start(bf16[2048,128]{1,0:T(8,128)(2,1)S(1)} %get-tuple-element.56.x_ref.a_i) | copy-start | bytes 1572868
  132.6 12.3 %copy-start.27 = (bf16[2048,128]{1,0:T(8,128)(2,1)}, bf16[2048,128]{1,0:T(8,128)(2,1)S(1)}, u32[]{:S(2)}) copy-start(bf16[2048,128]{1,0:T(8,128)(2,1)S(1)} %get-tuple-element.70.q_i) | copy-start | bytes 1572868
  132.6 12.3 %copy-start.29 = (bf16[2048,128]{1,0:T(8,128)(2,1)}, bf16[2048,128]{1,0:T(8,128)(2,1)S(1)}, u32[]{:S(2)}) copy-start(bf16[2048,128]{1,0:T(8,128)(2,1)S(1)} %get-tuple-element.71.k_i) | copy-start | bytes 1572868
  132.6 12.3 %copy-start.31 = (bf16[2048,128]{1,0:T(8,128)(2,1)}, bf16[2048,128]{1,0:T(8,128)(2,1)S(1)}, u32[]{:S(2)}) copy-start(bf16[2048,128]{1,0:T(8,128)(2,1)S(1)} %get-tuple-element.72.v_i) | copy-start | bytes 1572868
  143.9 1.0 copy-start.23
  144.8 28.7 %copy-start.18 = (bf16[256,1024]{1,0:T(8,128)(2,1)}, bf16[256,1024]{1,0:T(8,128)(2,1)S(1)}, u32[]{:S(2)}) copy-start(bf16[256,1024]{1,0:T(8,128)(2,1)S(1)} %get-tuple-element.59.x_ref.m_ref) | copy-start | bytes 1572868
  173.5 1.9 copy-start.8
  240.1 171.6 %reduce-scatter.6.cloned.1.call-start = ((), (), s32[]{:S(2)}) async-start(), calls=%async_computation.4 | async-start | bytes 4456448 | tf_op jit(solution)/shard_map/reduce_scatter | solution.py:1108
  240.9 1.3 copy-start.37
  240.9 242.7 %reduce-scatter.4.cloned.1.call-start = ((), (), s32[]{:S(2)}) async-start(), calls=%async_computation.3 | async-start | bytes 4456448 | tf_op jit(solution)/shard_map/reduce_scatter | solution.py:1108
  242.2 42.9 %copy-start.15 = (bf16[256,1024]{1,0:T(8,128)(2,1)S(1)}, bf16[256,1024]{1,0:T(8,128)(2,1)}, u32[]{:S(2)}) copy-start(bf16[256,1024]{1,0:T(8,128)(2,1)} %cot.3) | copy-start | bytes 1572868
  242.2 42.9 %copy-start.19 = (bf16[256,1024]{1,0:T(8,128)(2,1)S(1)}, bf16[256,1024]{1,0:T(8,128)(2,1)}, u32[]{:S(2)}) copy-start(bf16[256,1024]{1,0:T(8,128)(2,1)} %copy-done.18) | copy-start | bytes 1572868
  283.8 1.3 copy-start.13
  285.2 1.2 copy-start.24
  291.9 1.0 copy-start.21
  292.9 0.8 copy-start.33
  294.6 56.2 %copy-start.1 = (f32[2048,256]{1,0:T(8,128)S(1)}, f32[2048,256]{1,0:T(8,128)}, u32[]{:S(2)}) copy-start(f32[2048,256]{1,0:T(8,128)} %copy-done) | copy-start | bytes 6291460
  294.6 56.2 %copy-start.7 = (bf16[16,8,16,128]{3,2,1,0:T(8,128)(2,1)S(1)}, bf16[16,8,16,128]{3,2,1,0:T(8,128)(2,1)}, u32[]{:S(2)}) copy-start(bf16[16,8,16,128]{3,2,1,0:T(8,128)(2,1)} %copy-done.6) | copy-start | bytes 1572868
  295.8 1.0 copy-start.34
  307.1 1.2 copy-start.10
  308.4 1.2 copy-start.12
  309.6 1.0 copy-start.17
  310.7 1.0 copy-start.28
  311.7 1.1 copy-start.30
  312.8 1.0 copy-start.32
  350.8 1.6 copy-start.20
  362.0 1.0 copy-start.25
  363.0 5.5 %copy-start.36 = (bf16[1024,1024]{1,0:T(8,128)(2,1)S(1)}, bf16[1024,1024]{1,0:T(8,128)(2,1)}, u32[]{:S(2)}) copy-start(bf16[1024,1024]{1,0:T(8,128)(2,1)} %get-tuple-element.78) | copy-start | bytes 6291460
  367.4 1.3 copy-start.26
  368.8 39.9 %copy-start.22 = (f32[256,1024]{1,0:T(8,128)S(1)}, f32[256,1024]{1,0:T(8,128)}, u32[]{:S(2)}) copy-start(f32[256,1024]{1,0:T(8,128)} %copy-done.21) | copy-start | bytes 3145732
Sparse Core Ops, SparseCore 0:
  240.2 72.2 reduce-scatter.7
  316.2 87.3 reduce-scatter.5
  406.9 76.5 reduce-scatter.3

commit v2 on v1

--- a/solution.py
+++ b/solution.py
@@ -398,71 +398,6 @@
     )(x)
 
 
-def gather_rows_kernel(x_ref, t_ref, o_ref, ot_ref, lsem, s_x, r_x, s_t, r_t):
-    e, _, _ = place()
-    others = ep_others(e)
-    greet([{"ep": d} for d in others])
-    small = [remote(t_ref, ot_ref.at[e], (s_t, r_t), k, {"ep": d}) for k, d in enumerate(others)]
-    own = pltpu.make_async_copy(t_ref, ot_ref.at[e], lsem.at[1])
-    for copy in small:
-        copy.start()
-    own.start()
-    ring = RingGather(x_ref, o_ref, (s_x, r_x), lsem.at[0])
-    ring.start()
-    ring.forward()
-    ring.finish()
-    own.wait()
-    for copy in small:
-        copy.wait_recv()
-    for copy in small:
-        copy.wait_send()
-
-
-def gather_rows(x, t):
-    return comm_call(
-        gather_rows_kernel,
-        "gather_rows",
-        4,
-        [shape((EP * TOK, D), BF), shape((EP,) + t.shape)],
-        [ANY, ANY],
-        [ANY, ANY],
-        [DMA((2,)), DMA((10,)), DMA((10,)), DMA((7,)), DMA((7,))],
-    )(x, t)
-
-
-def reduce_rows_kernel(p_ref, t_ref, o_ref, ot_ref, pc, snd, rcv, hop, ssem, rsem, lsems, lsem, s_t, r_t):
-    e, _, _ = place()
-    others = ep_others(e)
-    greet([{"ep": d} for d in others])
-    ring = RingReduce(p_ref, TOK, pc, snd, rcv, hop, (ssem, rsem), lsems)
-    ring.start()
-    small = [remote(t_ref.at[d], ot_ref.at[e], (s_t, r_t), k, {"ep": d}) for k, d in enumerate(others)]
-    own = pltpu.make_async_copy(t_ref.at[e], ot_ref.at[e], lsem)
-    for copy in small:
-        copy.start()
-    own.start()
-    ring.middle()
-    ring.finish(o_ref)
-    own.wait()
-    for copy in small:
-        copy.wait_recv()
-    for copy in small:
-        copy.wait_send()
-
-
-def reduce_rows(p, t):
-    w = p.shape[1]
-    return comm_call(
-        reduce_rows_kernel,
-        "reduce_rows",
-        5,
-        [shape((TOK, w)), shape(t.shape)],
-        [ANY, ANY],
-        [VM, ANY],
-        reduce_scratch(TOK, w) + [DMA(()), DMA((7,)), DMA((7,))],
-    )(p, t)
-
-
 WB = D + 128
 
 
@@ -843,130 +778,325 @@
     )(x_all, u, lin, st, st2, gain, attn_gain, w)
 
 
+class ChipReduce:
+    SEMS = 10
+    STEP = 64
+
+    def __init__(self, n, swo, snd, pc, rcv, hop, sems):
+        e, x, c = place()
+        self.n, self.h = n, n // 2
+        h = n // 2
+        self.snd, self.pc, self.rcv, self.hop = snd, pc, rcv, hop
+        right, left = ep_device((x + 1) % 4, c), ep_device((x + 3) % 4, c)
+        peer = ep_device(x, 1 - c)
+        self.swap = lambda k: remote(swo.at[k], pc.at[k], sems, k, peer)
+        low, high = pl.ds(0, h), pl.ds(h, h)
+        self.opp = [
+            remote(snd.at[0, low], hop.at[low], sems, 4, right),
+            remote(snd.at[0, high], hop.at[high], sems, 5, left),
+        ]
+        self.near = [
+            remote(snd.at[2, high], rcv.at[0, high], sems, 6, right),
+            remote(snd.at[1, low], rcv.at[1, low], sems, 7, left),
+        ]
+        self.far = [
+            remote(snd.at[2, low], rcv.at[0, low], sems, 8, right),
+            remote(snd.at[1, high], rcv.at[1, high], sems, 9, left),
+        ]
+
+    def rows_loop(self, low, count, body):
+        step = self.STEP
+
+        def loop(i, carry):
+            body(pl.ds(pl.multiple_of(low + i * step, 16), step))
+            return carry
+
+        lax.fori_loop(0, count // step, loop, 0)
+
+    def merge(self, k):
+        def body(s):
+            self.snd[k, s] = (self.snd[k, s].astype(F32) + self.pc[k, s].astype(F32)).astype(BF)
+
+        self.swap(k).wait_recv()
+        self.rows_loop(0, self.n, body)
+
+    def merge_hop(self, k, low):
+        def body(s):
+            self.snd[k, s] = (self.snd[k, s].astype(F32) + self.hop[s].astype(F32)).astype(BF)
+
+        self.rows_loop(low, self.h, body)
+
+    def send_opp(self):
+        self.merge(0)
+        for copy in self.opp:
+            copy.start()
+
+    def send_near(self):
+        self.merge(2)
+        self.near[0].start()
+        self.merge(1)
+        self.near[1].start()
+
+    def send_far(self):
+        self.opp[0].wait_recv()
+        self.merge_hop(2, 0)
+        self.far[0].start()
+        self.opp[1].wait_recv()
+        self.merge_hop(1, self.h)
+        self.far[1].start()
+
+    def finish(self, out_ref):
+        for copy in self.near + self.far:
+            copy.wait_recv()
+
+        def body(s):
+            out_ref[s] = self.snd[3, s].astype(F32) + (
+                self.rcv[0, s].astype(F32) + self.rcv[1, s].astype(F32)
+            )
+
+        self.rows_loop(0, self.n, body)
+        for copy in [self.swap(k) for k in range(4)] + self.opp + self.near + self.far:
+            copy.wait_send()
+
+
 ROWS = EP * CAP
 HALF = 256
+BLOCK = 96
 
 
 def experts_kernel(
-    m_ref, g_ref, slot, gate, slots, wg, wu, wd, p_o, gg_o, dwg_o, dwu_o, dwd_o,
-    a_s, c_s, gate_s, gg_s, act_s, gp_s, dgu_s, y_s, z_s,
+    m_in, t_in, g_in, wg_in, wu_in, wd_in, out_o, gm_o, gg_o, eg_o,
+    m_ref, tab, g_ref, wg, wu, wd, a_s, c_s, gl_s, up_s, act_s, dgu_s, y_s, gate_s, gg_s, ggt, eg,
+    swo, snd, pc1, rcv1, hop1, pc2, rcv2, hop2,
+    s_m, r_m, s_t, r_t, s_1, r_1, s_2, r_2, s_g, r_g, lsem, esem,
 ):
-    step = pl.program_id(0)
-
-    def hits(row):
-        return iota((CAP, TOK), 0) == row
-
-    @pl.when(step < LOCAL)
-    def _():
-        def pick(s, carry):
-            hit = hits(slot[0, pl.ds(s, 1)])
-            chosen = jnp.where(hit, 1.0, 0.0).astype(BF)
-            rows = pl.ds(pl.multiple_of(s * CAP, 32), CAP)
+    e, x, c = place()
+    others = ep_others(e)
+    greet([{"ep": d} for d in others])
+    ring = RingGather(m_in, m_ref, (s_m, r_m), lsem.at[0])
+    ring.start()
+    tables = [remote(t_in, tab.at[e], (s_t, r_t), k, {"ep": d}) for k, d in enumerate(others)]
+    for copy in tables:
+        copy.start()
+    loads = [
+        pltpu.make_async_copy(t_in, tab.at[e], lsem.at[1]),
+        pltpu.make_async_copy(wg_in, wg, lsem.at[2]),
+        pltpu.make_async_copy(wu_in, wu, lsem.at[3]),
+        pltpu.make_async_copy(wd_in, wd, lsem.at[4]),
+        pltpu.make_async_copy(g_in, g_ref, lsem.at[5]),
+    ]
+    for copy in loads:
+        copy.start()
+    red1 = ChipReduce(TOK, swo, snd, pc1, rcv1, hop1, (s_1, r_1))
+    red2 = ChipReduce(TOK, swo, snd, pc2, rcv2, hop2, (s_2, r_2))
+
+    def hits(s, k):
+        return iota((CAP, TOK), 0).astype(F32) == tab[s, pl.ds(e * LOCAL + k, 1)]
+
+    def slot_rows(s):
+        return pl.ds(pl.multiple_of(s * CAP, 32), CAP)
+
+    def gate_column(s, k, hit):
+        row = tab[s, pl.ds(EXPERTS + e * LOCAL + k, 1)]
+        return jnp.sum(jnp.where(hit, row, 0.0), axis=1, keepdims=True)
+
+    def one_hot(hit):
+        return jnp.where(hit, 1.0, 0.0).astype(BF)
+
+    def combine(s):
+        chosen = jnp.concatenate([one_hot(hits(s, k)) for k in range(LOCAL)], axis=0)
+        rows = slot_rows(s)
+        return dot_tn(chosen, jnp.concatenate([y_s[k, rows] for k in range(LOCAL)], axis=0)).astype(BF)
+
+    def forward(k, carry):
+        @pl.when(k == 0)
+        def _():
+            ring.first[0].wait_recv()
+            ring.fwd_right.start()
+            ring.first[1].wait_recv()
+            ring.fwd_left.start()
+            ring.first[4].wait_recv()
+            ring.own.wait()
+            for copy in tables:
+                copy.wait_recv()
+            for copy in loads[:4]:
+                copy.wait()
+
+        @pl.when(k == 1)
+        def _():
+            ring.first[3].wait_recv()
+            ring.to_peer[1].start()
+            ring.first[2].wait_recv()
+            ring.to_peer[0].start()
+            ring.to_peer[1].wait_recv()
+
+        @pl.when(k == 2)
+        def _():
+            ring.fwd_right.wait_recv()
+            ring.fwd_left.wait_recv()
+            ring.to_peer[2].start()
+            ring.to_peer[0].wait_recv()
+
+        @pl.when(k == 3)
+        def _():
+            ring.to_peer[2].wait_recv()
+
+        q = (x + k + k // 2 - 2 * (k // 3)) % 4
+        rows = pl.ds(pl.multiple_of(q * 2 * CAP, 64), 2 * CAP)
+
+        def expert(n, inner):
+            for core in range(2):
+                s = q * 2 + core
+                hit = hits(s, n)
+                a_s[core * CAP : (core + 1) * CAP] = dot(one_hot(hit), m_ref[block_rows(s)]).astype(BF)
+                gate_s[core * CAP : (core + 1) * CAP] = jnp.broadcast_to(gate_column(s, n, hit), (CAP, 128))
+            a = a_s[: 2 * CAP]
+            gate_lin = dot(a, wg[n])
+            up_lin = dot(a, wu[n])
+            gl_s[n, rows] = gate_lin.astype(BF)
+            up_s[n, rows] = up_lin.astype(BF)
+            act = (gate_lin * jax.nn.sigmoid(gate_lin) * up_lin).astype(BF)
+            produced = dot(act, wd[n]).astype(BF).astype(F32)
+            y_s[n, rows] = (gate_s[: 2 * CAP, :1] * produced).astype(BF)
+            return inner
+
+        lax.fori_loop(0, LOCAL, expert, 0)
+        slot = 3 - k
+        swo[slot] = combine(q * 2 + 1 - c)
+        red1.swap(slot).start()
+        snd[slot] = combine(q * 2 + c)
+        return carry
+
+    lax.fori_loop(0, 4, forward, 0)
+    red1.send_opp()
+    red1.send_near()
+    loads[4].wait()
+
+    def backward(n, carry):
+        def pick(s, inner):
+            hit = hits(s, n)
+            chosen = one_hot(hit)
+            rows = slot_rows(s)
             a_s[rows] = dot(chosen, m_ref[block_rows(s)]).astype(BF)
             c_s[rows] = dot(chosen, g_ref[block_rows(s)]).astype(BF)
-            weight = jnp.sum(jnp.where(hit, gate[0, pl.ds(s, 1)], 0.0), axis=1, keepdims=True)
-            gate_s[rows] = jnp.broadcast_to(weight, (CAP, 128))
-            return carry
+            gate_s[rows] = jnp.broadcast_to(gate_column(s, n, hit), (CAP, 128))
+            return inner
 
         lax.fori_loop(0, EP, pick, 0)
 
-        def rows_part(k, carry):
+        def rows_part(k, inner):
             rows = pl.ds(pl.multiple_of(k * HALF, HALF), HALF)
-            a = a_s[rows]
-            gate_lin = dot(a, wg[0])
-            up_lin = dot(a, wu[0])
+            cot = c_s[rows]
+            weight = gate_s[rows][:, :1]
+            back = dot_nt(cot, wd[n])
+            c_s[rows] = (weight * cot.astype(F32)).astype(BF)
+            gate_lin, up_lin = gl_s[n, rows].astype(F32), up_s[n, rows].astype(F32)
             sig = jax.nn.sigmoid(gate_lin)
             silu = gate_lin * sig
-            act = (silu * up_lin).astype(BF)
-            act_s[rows] = act
-            weight = gate_s[rows][:, :1]
-            produced = dot(act, wd[0]).astype(BF).astype(F32)
-            cot = c_s[rows].astype(F32)
-            gg = jnp.sum(produced * cot, axis=1, keepdims=True)
-            gg_s[rows] = jnp.broadcast_to(gg, (HALF, 128))
-            y_s[step, rows] = (weight * produced).astype(BF)
-            grad = (weight * cot).astype(BF)
-            gp_s[rows] = grad
-            grad_act = dot_nt(grad, wd[0])
-            dgate = (grad_act * up_lin * sig * (1.0 + gate_lin * (1.0 - sig))).astype(BF)
-            dup = (grad_act * silu).astype(BF)
+            act = silu * up_lin
+            act_s[rows] = act.astype(BF)
+            gg_s[rows] = jnp.broadcast_to(jnp.sum(act * back, axis=1, keepdims=True), (HALF, 128))
+            back = back * weight
+            dgate = (back * up_lin * sig * (1.0 + gate_lin * (1.0 - sig))).astype(BF)
+            dup = (back * silu).astype(BF)
             dgu_s[rows, :FF] = dgate
             dgu_s[rows, FF:] = dup
-            z_s[step, rows] = (dot_nt(dgate, wg[0]) + dot_nt(dup, wu[0])).astype(BF)
-            return carry
+            y_s[n, rows] = (dot_nt(dgate, wg[n]) + dot_nt(dup, wu[n])).astype(BF)
+            return inner
 
         lax.fori_loop(0, ROWS // HALF, rows_part, 0)
 
-        def gates_back(s, carry):
-            hit = hits(slot[0, pl.ds(s, 1)])
-            rows = pl.ds(pl.multiple_of(s * CAP, 32), CAP)
-            gg_o[0, pl.ds(s, 1)] = jnp.sum(jnp.where(hit, gg_s[rows][:, :1], 0.0), axis=0, keepdims=True)
-            return carry
+        def gates_back(s, inner):
+            column_ = gg_s[slot_rows(s)][:, :1]
+            ggt[s, pl.ds(n, 1)] = jnp.sum(jnp.where(hits(s, n), column_, 0.0), axis=0, keepdims=True)
+            return inner
 
         lax.fori_loop(0, EP, gates_back, 0)
-        dwd_o[0] = dot_tn(act_s[...], gp_s[...]).astype(BF)
-        dwg_o[0] = dot_tn(a_s[...], dgu_s[:, :FF]).astype(BF)
-        dwu_o[0] = dot_tn(a_s[...], dgu_s[:, FF:]).astype(BF)
-
-    @pl.when(step >= LOCAL)
-    def _():
-        s = step - LOCAL
-        rows = pl.ds(pl.multiple_of(s * CAP, 32), CAP)
-        chosen = jnp.concatenate(
-            [jnp.where(hits(slots[k, pl.ds(s, 1)]), 1.0, 0.0).astype(BF) for k in range(LOCAL)], axis=0
-        )
-        y = jnp.concatenate([y_s[k, rows] for k in range(LOCAL)], axis=0)
-        p_o[:, :D] = dot_tn(chosen, y).astype(BF)
-        z = jnp.concatenate([z_s[k, rows] for k in range(LOCAL)], axis=0)
-        p_o[:, D:] = dot_tn(chosen, z).astype(BF)
-
-
-def experts(m_all, g_all, slot, gate, wg, wu, wd):
-    def cur(*rest):
-        return lambda i: (jnp.minimum(i, LOCAL - 1),) + rest
-
-    once = pl.Buffered(1)
-    return pl.pallas_call(
+
+        @pl.when(n == 0)
+        def _():
+            red1.merge(3)
+            red1.send_far()
+
+        @pl.when(n == 2)
+        def _():
+            red1.finish(out_o)
+
+        @pl.when(n > 0)
+        def _():
+            pltpu.make_async_copy(eg, eg_o.at[n - 1], esem).wait()
+
+        eg[:, :64, :FF] = dot_tn(a_s[...], dgu_s[:, :FF]).astype(BF).reshape(REP, 64, FF)
+        eg[:, :64, FF:] = dot_tn(a_s[...], dgu_s[:, FF:]).astype(BF).reshape(REP, 64, FF)
+        eg[:, 64:] = dot_tn(act_s[...], c_s[...]).astype(BF).reshape(REP, 32, D)
+        pltpu.make_async_copy(eg, eg_o.at[n], esem).start()
+        return carry
+
+    lax.fori_loop(0, LOCAL, backward, 0)
+    gates = [remote(ggt.at[d], gg_o.at[e], (s_g, r_g), k, {"ep": d}) for k, d in enumerate(others)]
+    own = pltpu.make_async_copy(ggt.at[e], gg_o.at[e], lsem.at[1])
+    for copy in gates + [own]:
+        copy.start()
+    for slot, q in enumerate([(x + 2) % 4, (x + 3) % 4, (x + 1) % 4, x]):
+        swo[slot] = combine(q * 2 + 1 - c)
+        red2.swap(slot).start()
+        snd[slot] = combine(q * 2 + c)
+        if slot == 0:
+            red2.send_opp()
+    red2.send_near()
+    red2.merge(3)
+    red2.send_far()
+    red2.finish(gm_o)
+    own.wait()
+    pltpu.make_async_copy(eg, eg_o.at[LOCAL - 1], esem).wait()
+    for copy in gates:
+        copy.wait_recv()
+    for copy in ring.first + [ring.fwd_right, ring.fwd_left] + ring.to_peer + tables + gates:
+        copy.wait_send()
+
+
+def experts(m, t, g_all, wg, wu, wd):
+    return comm_call(
         experts_kernel,
-        grid=(LOCAL + EP,),
-        out_shape=[
-            shape((LENGTH, 2 * D), BF),
-            shape((LOCAL, EP, TOK)),
-            shape((LOCAL, D, FF), BF),
-            shape((LOCAL, D, FF), BF),
-            shape((LOCAL, FF, D), BF),
+        "experts",
+        4,
+        [
+            shape((TOK, D)),
+            shape((TOK, D)),
+            shape((EP, 8, TOK)),
+            shape((LOCAL, REP, BLOCK, D), BF),
         ],
-        in_specs=[
-            pl.BlockSpec((LENGTH, D), lambda i: (0, 0), pipeline_mode=once),
-            pl.BlockSpec((LENGTH, D), lambda i: (0, 0), pipeline_mode=once),
-            pl.BlockSpec((1, EP, TOK), cur(0, 0)),
-            pl.BlockSpec((1, EP, TOK), cur(0, 0)),
-            pl.BlockSpec((LOCAL, EP, TOK), lambda i: (0, 0, 0)),
-            pl.BlockSpec((1, D, FF), cur(0, 0)),
-            pl.BlockSpec((1, D, FF), cur(0, 0)),
-            pl.BlockSpec((1, FF, D), cur(0, 0)),
-        ],
-        out_specs=[
-            pl.BlockSpec((TOK, 2 * D), lambda i: (jnp.maximum(i - LOCAL, 0), 0)),
-            pl.BlockSpec((1, EP, TOK), cur(0, 0)),
-            pl.BlockSpec((1, D, FF), cur(0, 0)),
-            pl.BlockSpec((1, D, FF), cur(0, 0)),
-            pl.BlockSpec((1, FF, D), cur(0, 0)),
-        ],
-        scratch_shapes=[
+        [ANY] * 6,
+        [VM, VM, ANY, ANY],
+        [
+            pltpu.VMEM((LENGTH, D), BF),
+            pltpu.VMEM((EP, 2 * EXPERTS, TOK), F32),
+            pltpu.VMEM((LENGTH, D), BF),
+            pltpu.VMEM((LOCAL, D, FF), BF),
+            pltpu.VMEM((LOCAL, D, FF), BF),
+            pltpu.VMEM((LOCAL, FF, D), BF),
             pltpu.VMEM((ROWS, D), BF),
             pltpu.VMEM((ROWS, D), BF),
+            pltpu.VMEM((LOCAL, ROWS, FF), BF),
+            pltpu.VMEM((LOCAL, ROWS, FF), BF),
+            pltpu.VMEM((ROWS, FF), BF),
+            pltpu.VMEM((ROWS, D), BF),
+            pltpu.VMEM((LOCAL, ROWS, D), BF),
             pltpu.VMEM((ROWS, 128), F32),
             pltpu.VMEM((ROWS, 128), F32),
-            pltpu.VMEM((ROWS, FF), BF),
-            pltpu.VMEM((ROWS, D), BF),
-            pltpu.VMEM((ROWS, D), BF),
-            pltpu.VMEM((LOCAL, ROWS, D), BF),
-            pltpu.VMEM((LOCAL, ROWS, D), BF),
-        ],
-        compiler_params=pltpu.CompilerParams(vmem_limit_bytes=60 * MIB),
-        name="experts",
-    )(m_all, g_all, slot, gate, slot, wg, wu, wd)
+            pltpu.VMEM((EP, 8, TOK), F32),
+            pltpu.VMEM((REP, BLOCK, D), BF),
+            pltpu.VMEM((4, TOK, D), BF),
+            pltpu.VMEM((4, TOK, D), BF),
+        ]
+        + [pltpu.VMEM((4, TOK, D), BF), pltpu.VMEM((2, TOK, D), BF), pltpu.VMEM((TOK, D), BF)] * 2
+        + [DMA((10,))] * 2
+        + [DMA((7,))] * 2
+        + [DMA((10,))] * 4
+        + [DMA((7,))] * 2
+        + [DMA((6,)), DMA(())],
+        limit=63,
+    )(m, t, g_all, wg, wu, wd)
 
 
 def hidden_kernel(x_ref, a_ref, w_ref, gain, router, hit, hid_o, m_o, gate_o):
@@ -994,16 +1124,16 @@
 
 
 def hidden_back_kernel(
-    hid, red, gg, gate, m_ref, cot, gain, router, w_ref, a_ref, out_o, gh_o, ga_o, dwo_o, dr_o, gf_o
+    hid, mixed, gmoe, gg, gate, m_ref, cot, gain, router, w_ref, a_ref, out_o, gh_o, ga_o, dwo_o, dr_o, gf_o
 ):
     hidden = hid[...]
-    out_o[...] = (hidden + red[:, :D]).astype(BF)
+    out_o[...] = (hidden + mixed[...]).astype(BF)
     weights = gate[...]
     grads = gg[...]
     mean = jnp.sum(weights * grads, axis=0, keepdims=True)
     grad_logits = (weights * (grads - mean)).astype(BF)
     dr_o[...] = dot(grad_logits, m_ref[...])
-    grad_moe = red[:, D:] + dot_tn(grad_logits, router[...])
+    grad_moe = gmoe[...] + dot_tn(grad_logits, router[...])
     r2 = lax.rsqrt(jnp.mean(hidden * hidden, axis=1, keepdims=True) + EPSILON)
     n = hidden * r2
     gf_o[...] = jnp.sum(grad_moe * n, axis=0, keepdims=True)
@@ -1015,7 +1145,7 @@
     dwo_o[...] = dot_tn(a_ref[...], branch).astype(BF)
 
 
-def hidden_back(hid, red, gg, gate, m, cot, gain, router, w, a):
+def hidden_back(hid, mixed, grad_moe, gg, gate, m, cot, gain, router, w, a):
     return pl.pallas_call(
         hidden_back_kernel,
         out_shape=[
@@ -1026,11 +1156,11 @@
             shape((EXPERTS, D)),
             shape((1, D)),
         ],
-        in_specs=[VM] * 10,
+        in_specs=[VM] * 11,
         out_specs=[VM] * 6,
         compiler_params=pltpu.CompilerParams(vmem_limit_bytes=48 * MIB),
         name="hidden_back",
-    )(hid, red, gg, gate, m, cot, gain, router, w, a)
+    )(hid, mixed, grad_moe, gg, gate, m, cot, gain, router, w, a)
 
 
 def body(
@@ -1100,19 +1230,14 @@
     q, k, v, att, lse = attend(lin, st, lo, cosine, sine, qk_gain)
     attended = swap_heads(att, True, "swap_heads", 3)
     hidden, moe_in, gates = hidden_call(tokens, attended, whole_out, ffn_gain, router, slot_own)
-    m_all, tables = gather_rows(moe_in, jnp.concatenate([slot_own, gates], axis=0))
-    slot = lax.dynamic_slice_in_dim(tables, e * LOCAL, LOCAL, 1).transpose(1, 0, 2).astype(jnp.int32)
-    gate = lax.dynamic_slice_in_dim(tables, EXPERTS + e * LOCAL, LOCAL, 1).transpose(1, 0, 2)
-    part, gg, dwg, dwu, dwd = experts(m_all, g_all, slot, gate, w_gate, w_up, w_down)
-    expert_sums = [
-        lax.psum_scatter(value, "rep", scatter_dimension=1, tiled=True).astype(F32) for value in (dwg, dwu, dwd)
-    ]
-    gg = jnp.pad(gg.transpose(1, 0, 2), ((0, 0), (0, 4), (0, 0)))
-    red, gg = reduce_rows(part, gg)
+    tables = jnp.concatenate([slot_own, gates], axis=0)
+    mixed, grad_moe, gg, grads = experts(moe_in, tables, g_all, w_gate, w_up, w_down)
+    grads = grads.reshape(LOCAL, REP * BLOCK, D)
+    expert_sums = lax.psum_scatter(grads, "rep", scatter_dimension=1, tiled=True).astype(F32)
     gg = gg[:, :LOCAL].reshape(EXPERTS, TOK)
     attended_t = attended.reshape(TOK, REP, EP, 8).transpose(0, 2, 1, 3).reshape(TOK, D)
     output, grad_hidden, grad_att, dwo, drouter, dffn = hidden_back(
-        hidden, red, gg, gates, moe_in, out_grad, ffn_gain, router, whole_out, attended_t
+        hidden, mixed, grad_moe, gg, gates, moe_in, out_grad, ffn_gain, router, whole_out, attended_t
     )
     go = swap_heads(grad_att, False, "swap_heads_back", 7)
     u, sums2 = attend_back(q, k, v, att, lse, lo, go, lin, st, cosine, sine, qk_gain)
@@ -1145,9 +1270,9 @@
         wb_sum[:, D + 33],
         wb_sum[:4, D + 34],
         wb_sum[:, D + 35],
-        expert_sums[0],
-        expert_sums[1],
-        expert_sums[2],
+        expert_sums[:, :64, :FF],
+        expert_sums[:, :64, FF:],
+        expert_sums[:, 64:],
     )
 
 

time: 494 us -> 401 us (0.81)
  waiting for transfers between devices: 71.2 us -> 0.02 us
  Pallas kernels: 347 us -> 324 us
  local copies, waits for them, and re-layouts: 46.7 us -> 55.7 us
  other arithmetic: 11.9 us -> 5.65 us
    reduce_scatter x3 -> x1, waiting for transfers between devices: 70 us -> 0.01 us  [body(): lax.psum_scatter(grads, 'rep', scatter_dimension=1, tiled=True).astype(F32)]
    pallas_call x3 -> x1, Pallas kernels: 134 us -> 109 us  [experts(): comm_call(experts_kernel, 'experts', 4, [shape((TOK, D)), shape((TOK, D))...]
    convert_element_type x3 -> x0, other arithmetic: 5.4 us -> none  [body(): lax.psum_scatter(value, 'rep', scatter_dimension=1, tiled=True).astype(F32)]
    unnamed x82 -> x86, local copies, waits for them, and re-layouts: 26.7 us -> 29.7 us
  transfers between devices with their start and end apart: 3 -> 1, of which waited for: 1 -> 0; matrix products, arithmetic and copies ran while one was open for 4% -> 5% of each run, Pallas kernels for 28% -> 25%
where the time goes in v2:
time: 401 us; the launch traced here: 400 us
  Pallas kernels  324 us (81%)
  local copies, waits for them, and re-layouts  55.7 us (14%)
  between operations  14.5 us (4%)
  other arithmetic  5.65 us (1%)
    pallas_call x1, Pallas kernels, experts(): comm_call(experts_kernel, 'experts', 4, [shape((TOK, D)), shape((TOK, D))...  109 us
    pallas_call x1, Pallas kernels, gather_first(): comm_call(gather_first_kernel, 'gather_first', 1, [shape((EP * TOK, D), B...  65.8 us
    pallas_call x1, Pallas kernels, reduce_last(): comm_call(reduce_last_kernel, 'reduce_last', 6, [shape((TOK, D)), shape((...  35 us
    pallas_call x1, Pallas kernels, attend_back(): pl.pallas_call(attend_back_kernel, out_shape=[shape((LENGTH, 256)), shape...  31.4 us
    unnamed x86, local copies, waits for them, and re-layouts  29.7 us
    pallas_call x1, Pallas kernels, attend(): pl.pallas_call(attend_kernel, out_shape=[shape((LENGTH, 128), BF)] * 4 +...  25.6 us
    pallas_call x2, Pallas kernels, swap_heads(): comm_call(functools.partial(swap_kernel, to_rows), name, collective_id, s...  20.9 us
    pallas_call x2, Pallas kernels, sum_stats(): comm_call(sum_stats_kernel, name, collective_id, shape(x.shape), [VM], VM...  11.8 us
  transfers between devices with their start and end apart: 1, of which 0 were waited for; matrix products, arithmetic and copies ran while one was open for 5% of the time, Pallas kernels for 25%

profile of v2, /device:TPU:1, one launch (start us, length us, event | category | flops | bytes accessed | tf_op | source)
XLA Modules:
  0.0 399.7 jit_solution(2237541107440279388)
XLA Ops:
  7.2 0.8 reshape.213
  8.0 2.8 concatenate.34
  10.8 0.8 reshape.209
  11.6 0.8 reshape.210
  12.4 0.8 maximum_bitcast_fusion
  13.2 1.0 copy-done.3
  14.2 1.0 copy-done.16
  15.3 0.7 copy-done.36
  16.0 65.8 %gather_first.1 = (bf16[2048,1024]{1,0:T(8,128)(2,1)}, bf16[2048,1024]{1,0:T(8,128)(2,1)}, bf16[16,8,32,128]{3,2,1,0:T(8,128)(2,1)S(1)}, bf16[16,8,64,128]{3,2,1,0:T(8,128)(2,1)S(1)}) custom-call(bf16[256,1024]{1,0:T(8,128)(2,1)S(1)} %copy-done.3, bf16[256,1024]{1,0:T(8,128)(2,1)S(1)} %copy-done.16, bf16[8,32,128]{2,1,0:T(8,128)(2,1)S(1)} %pad_maximum_fusion.wsl, ...), custom_call_target="tpu_custom_call" | custom-call | tf_op jit(solution)/shard_map/gather_first/pallas_call | solution.py:316
  81.8 1.4 slice_bitcast_fusion
  83.6 0.7 fusion.11
  84.3 1.3 fusion.12
  86.5 2.2 copy-done.2
  88.7 1.0 copy-done.8
  89.8 7.5 %project.1 = (f32[2048,256]{1,0:T(8,128)S(1)}, f32[16,256]{1,0:T(8,128)S(1)}) custom-call(bf16[2048,1024]{1,0:T(8,128)(2,1)S(1)} %copy-done.2, bf16[1024,256]{1,0:T(8,128)(2,1)S(1)} %bitcast.50, f32[1,1024]{1,0:T(1,128)S(1)} %reshape.231.gain_ref.attn_gain), custom_call_target="tpu_custom_call" | custom-call | tf_op jit(solution)/shard_map/project/pallas_call | solution.py:508
  97.3 1.4 copy-done
  98.7 6.2 %sum_stats.1.st = f32[16,256]{1,0:T(8,128)S(1)} custom-call(f32[16,256]{1,0:T(8,128)S(1)} %get-tuple-element.50.x_ref), custom_call_target="tpu_custom_call" | custom-call | tf_op jit(solution)/shard_map/sum_stats/pallas_call | solution.py:351
  105.0 1.2 copy-done.10
  106.2 1.2 copy-done.12
  107.4 25.6 %attend.1 = (bf16[2048,128]{1,0:T(8,128)(2,1)S(1)}, bf16[2048,128]{1,0:T(8,128)(2,1)S(1)}, bf16[2048,128]{1,0:T(8,128)(2,1)S(1)}, bf16[2048,128]{1,0:T(8,128)(2,1)S(1)}, f32[8,8,512]{2,1,0:T(8,128)S(1)}) custom-call(f32[2048,256]{1,0:T(8,128)} %copy-done, f32[16,256]{1,0:T(8,128)S(1)} %sum_stats.1.st, f32[8,256]{1,0:T(8,128)S(1)} %maximum_convert_fusion.lo, ...), custom_call_target="tpu_custom_call" | custom-call | tf_op jit(solution)/shard_map/attend/pallas_call | solution.py:617
  133.1 10.0 %swap_heads.1.a_ref = bf16[256,1024]{1,0:T(8,128)(2,1)S(1)} custom-call(bf16[2048,128]{1,0:T(8,128)(2,1)S(1)} %get-tuple-element.51.x_ref.a_i), custom_call_target="tpu_custom_call" | custom-call | tf_op jit(solution)/shard_map/swap_heads/pallas_call | solution.py:390
  143.2 1.2 hidden.1
  144.4 0.8 copy-done.14
  145.2 1.0 copy-done.23
  146.2 0.6 pad_maximum_fusion.1.t_in
  146.8 109.0 %experts.1 = (f32[256,1024]{1,0:T(8,128)}, f32[256,1024]{1,0:T(8,128)}, f32[8,8,256]{2,1,0:T(8,128)}, bf16[4,16,96,1024]{3,2,1,0:T(8,128)(2,1)}) custom-call(bf16[256,1024]{1,0:T(8,128)(2,1)} %copy-done.14, f32[64,256]{1,0:T(8,128)} %pad_maximum_fusion.1.t_in, bf16[2048,1024]{1,0:T(8,128)(2,1)} %get-tuple-element.56.g_in, bf16[4,1024,512]{2,1,0:T(8,128)(2,1)} %wg_in.1, ...), custom_call_target="tpu_custom_call" | custom-call | tf_op jit(solution)/shard_map/experts/pallas_call | solution.py:1059
  256.0 0.9 copy-done.7
  257.1 0.8 copy.59
  257.9 1.2 copy.60.a_ref
  259.3 1.2 copy-done.24
  260.5 1.2 copy-done.25
  261.7 5.7 %hidden_back.1 = (bf16[256,1024]{1,0:T(8,128)(2,1)}, f32[256,1024]{1,0:T(8,128)S(1)}, bf16[256,1024]{1,0:T(8,128)(2,1)S(1)}, bf16[1024,1024]{1,0:T(8,128)(2,1)},...) custom-call(f32[256,1024]{1,0:T(8,128)S(1)} %copy-done.24, f32[256,1024]{1,0:T(8,128)S(1)} %copy-done.25, ...), custom_call_target="tpu_custom_call" | custom-call | tf_op jit(solution)/shard_map/hidden_back/pallas_call | solution.py:1149
  267.4 1.0 copy-done.21
  268.4 0.8 copy-done.34
  269.4 1.1 concatenate.47
  270.5 1.0 copy-done.35
  271.6 10.8 %swap_heads_back.1.go = bf16[2048,128]{1,0:T(8,128)(2,1)S(1)} custom-call(bf16[256,1024]{1,0:T(8,128)(2,1)S(1)} %copy-done.35), custom_call_target="tpu_custom_call" | custom-call | tf_op jit(solution)/shard_map/swap_heads_back/pallas_call | solution.py:390
  282.4 1.2 copy-done.11
  283.7 1.2 copy-done.13
  284.9 1.1 copy-done.19
  286.0 1.1 copy-done.29
  287.0 1.0 copy-done.31
  288.1 1.1 copy-done.33
  289.1 31.4 %attend_back.1 = (f32[2048,256]{1,0:T(8,128)}, f32[16,256]{1,0:T(8,128)S(1)}) custom-call(bf16[2048,128]{1,0:T(8,128)(2,1)S(1)} %copy-done.29, bf16[2048,128]{1,0:T(8,128)(2,1)S(1)} %copy-done.31, bf16[2048,128]{1,0:T(8,128)(2,1)S(1)} %copy-done.33, bf16[2048,128]{1,0:T(8,128)(2,1)S(1)} %copy-done.19, f32[8,8,512]{2,1,0:T(8,128)S(1)} %get-tuple-element.65.lse, ...), custom_call_target="tpu_custom_call" | custom-call | tf_op jit(solution)/shard_map/attend_back/pallas_call | solution.py:696
  320.6 5.6 %sum_stats_back.1.st2 = f32[16,256]{1,0:T(8,128)S(1)} custom-call(f32[16,256]{1,0:T(8,128)S(1)} %get-tuple-element.68.x_ref), custom_call_target="tpu_custom_call" | custom-call | tf_op jit(solution)/shard_map/sum_stats_back/pallas_call | solution.py:351
  326.2 1.0 copy-done.9
  327.2 1.6 copy-done.20
  328.8 9.7 %project_back.1 = (bf16[2048,1024]{1,0:T(8,128)(2,1)}, f32[1024,256]{1,0:T(8,128)S(1)}, f32[8,1024]{1,0:T(8,128)S(1)}, f32[8,256]{1,0:T(8,128)S(1)}) custom-call(bf16[2048,1024]{1,0:T(8,128)(2,1)} %get-tuple-element.47.x_ref, f32[2048,256]{1,0:T(8,128)S(1)} %copy-done.20, f32[2048,256]{1,0:T(8,128)S(1)} %copy-done.1, f32[16,256]{1,0:T(8,128)S(1)} %sum_stats.1.st, ...), custom_call_target="tpu_custom_call" | custom-call | tf_op jit(solution)/shard_map/project_back/pallas_call | solution.py:760
  338.5 1.0 copy-done.26
  339.9 1.5 copy.65
  341.5 1.1 concatenate.45
  342.7 1.1 concatenate.46
  343.8 2.2 concatenate.43
  346.0 1.1 copy.67
  347.4 35.0 %reduce_last.1 = (f32[256,1024]{1,0:T(8,128)S(1)}, f32[8,1152]{1,0:T(8,128)S(1)}, f32[8,8,256]{2,1,0:T(8,128)S(1)}) custom-call(bf16[2048,1024]{1,0:T(8,128)(2,1)} %get-tuple-element.69.gn, bf16[1024,1152]{1,0:T(8,128)(2,1)S(1)} %fusion.1.wb, f32[1024,256]{1,0:T(8,128)S(1)} %copy-done.27), custom_call_target="tpu_custom_call" | custom-call | tf_op jit(solution)/shard_map/reduce_last/pallas_call | solution.py:461
  383.0 0.6 slice.84
  383.7 0.7 reshape.229
  384.4 0.7 reshape.228
  385.1 0.7 slice_reduce_fusion.3
  385.7 0.7 slice_reduce_fusion
  387.0 0.6 slice_bitcast_fusion.1
  387.6 1.3 fusion.7
  388.9 1.8 slice.104
  390.7 2.1 fusion.15
  (112 shorter events, 4.1 us)
Async XLA Ops:
  7.2 76.4 %copy-start.39 = (s32[1,2048]{1,0:T(1,128)S(1)}, s32[1,2048]{1,0:T(1,128)}, u32[]{:S(2)}) copy-start(s32[1,2048]{1,0:T(1,128)} %param.19) | copy-start | bytes 24580
  7.2 78.4 %copy-start.41 = (s32[256,8]{0,1:T(8,128)S(1)}, s32[256,8]{0,1:T(8,128)}, u32[]{:S(2)}) copy-start(s32[256,8]{0,1:T(8,128)} %param.20) | copy-start | bytes 24580
  7.2 381.7 %reduce-scatter.2.cloned.1.call-start = ((), (), s32[]{:S(2)}) async-start(), calls=%async_computation.1 | async-start | bytes 13369344 | tf_op jit(solution)/shard_map/reduce_scatter | solution.py:1236
  13.2 1.0 copy-start.3
  14.2 1.0 copy-start.16
  15.3 0.7 copy-start.36
  81.8 61.4 %copy-start.5 = (bf16[16,8,64,128]{3,2,1,0:T(8,128)(2,1)}, bf16[16,8,64,128]{3,2,1,0:T(8,128)(2,1)S(1)}, u32[]{:S(2)}) copy-start(bf16[16,8,64,128]{3,2,1,0:T(8,128)(2,1)S(1)} %get-tuple-element.52) | copy-start | bytes 6291460
  86.5 2.2 copy-start.2
  88.7 1.0 copy-start.8
  89.8 53.4 %copy-start.4 = (bf16[256,1024]{1,0:T(8,128)(2,1)S(1)}, bf16[256,1024]{1,0:T(8,128)(2,1)}, u32[]{:S(2)}) copy-start(bf16[256,1024]{1,0:T(8,128)(2,1)} %x_ref.1) | copy-start | bytes 1572868
  97.3 1.4 copy-start
  105.0 1.2 copy-start.10
  106.2 1.2 copy-start.12
  133.1 13.1 %copy-start.18 = (bf16[2048,128]{1,0:T(8,128)(2,1)}, bf16[2048,128]{1,0:T(8,128)(2,1)S(1)}, u32[]{:S(2)}) copy-start(bf16[2048,128]{1,0:T(8,128)(2,1)S(1)} %get-tuple-element.51.x_ref.a_i) | copy-start | bytes 1572868
  133.1 13.7 %copy-start.28 = (bf16[2048,128]{1,0:T(8,128)(2,1)}, bf16[2048,128]{1,0:T(8,128)(2,1)S(1)}, u32[]{:S(2)}) copy-start(bf16[2048,128]{1,0:T(8,128)(2,1)S(1)} %get-tuple-element.62.q_i) | copy-start | bytes 1572868
  133.1 13.7 %copy-start.30 = (bf16[2048,128]{1,0:T(8,128)(2,1)}, bf16[2048,128]{1,0:T(8,128)(2,1)S(1)}, u32[]{:S(2)}) copy-start(bf16[2048,128]{1,0:T(8,128)(2,1)S(1)} %get-tuple-element.63.k_i) | copy-start | bytes 1572868
  133.1 13.7 %copy-start.32 = (bf16[2048,128]{1,0:T(8,128)(2,1)}, bf16[2048,128]{1,0:T(8,128)(2,1)S(1)}, u32[]{:S(2)}) copy-start(bf16[2048,128]{1,0:T(8,128)(2,1)S(1)} %get-tuple-element.64.v_i) | copy-start | bytes 1572868
  143.2 1.2 copy-start.6
  144.4 0.8 copy-start.14
  145.2 1.0 copy-start.23
  255.8 1.0 copy-start.7
  255.9 3.3 copy-start.40
  255.9 3.4 copy-start.15
  255.9 3.4 copy-start.17
  259.2 1.2 copy-start.24
  260.5 1.2 copy-start.25
  267.4 1.0 copy-start.21
  268.4 0.8 copy-start.34
  269.4 56.8 %copy-start.1 = (f32[2048,256]{1,0:T(8,128)S(1)}, f32[2048,256]{1,0:T(8,128)}, u32[]{:S(2)}) copy-start(f32[2048,256]{1,0:T(8,128)} %copy-done) | copy-start | bytes 6291460
  270.5 1.0 copy-start.35
  282.4 1.3 copy-start.11
  283.7 1.2 copy-start.13
  284.9 1.1 copy-start.19
  286.0 1.1 copy-start.29
  287.0 1.1 copy-start.31
  288.1 1.1 copy-start.33
  326.2 1.0 copy-start.9
  327.2 1.6 copy-start.20
  328.8 15.0 %copy-start.38 = (bf16[1,16,8,8]{0,3,2,1:T(8,128)(2,1)S(1)}, bf16[1,16,8,8]{0,3,2,1:T(8,128)(2,1)}, u32[]{:S(2)}) copy-start(bf16[1,16,8,8]{0,3,2,1:T(8,128)(2,1)} %concatenate.47) | copy-start | bytes 6148
  338.5 1.0 copy-start.26
  339.5 7.6 %copy-start.37 = (bf16[1024,1024]{1,0:T(8,128)(2,1)S(1)}, bf16[1024,1024]{1,0:T(8,128)(2,1)}, u32[]{:S(2)}) copy-start(bf16[1024,1024]{1,0:T(8,128)(2,1)} %get-tuple-element.70) | copy-start | bytes 6291460
  346.0 1.3 copy-start.27
  347.4 40.3 %copy-start.22 = (f32[256,1024]{1,0:T(8,128)S(1)}, f32[256,1024]{1,0:T(8,128)}, u32[]{:S(2)}) copy-start(f32[256,1024]{1,0:T(8,128)} %copy-done.21) | copy-start | bytes 3145732
Sparse Core Ops, SparseCore 0:
  256.0 91.8 reduce-scatter.1

commit v3 on v2

--- a/solution.py
+++ b/solution.py
@@ -268,65 +268,6 @@
 
 def shape(dims, dtype=F32):
     return jax.ShapeDtypeStruct(dims, dtype)
-
-
-def gather_first_kernel(
-    tok, cot, wsl, wo, x_all, g_all, wg, wog, lsem, s_tok, r_tok, s_cot, r_cot, s_w, r_w, s_o, r_o
-):
-    r = lax.axis_index("rep")
-    e, x, c = place()
-    others = ep_others(e)
-    copies = rep_others(r)
-    greet([{"ep": d} for d in others] + [{"rep": d} for d in copies])
-    stage = []
-    for k, d in enumerate(others):
-        stage.append(remote(wsl.at[d], wg.at[r, e], (s_w, r_w), k, {"ep": d}))
-        stage.append(remote(wo, wog.at[r, e], (s_o, r_o), k, {"ep": d}))
-    own = [
-        pltpu.make_async_copy(wsl.at[e], wg.at[r, e], lsem.at[2]),
-        pltpu.make_async_copy(wo, wog.at[r, e], lsem.at[3]),
-    ]
-    for copy in stage + own:
-        copy.start()
-    tokens = RingGather(tok, x_all, (s_tok, r_tok), lsem.at[0])
-    grads = RingGather(cot, g_all, (s_cot, r_cot), lsem.at[1])
-    tokens.start()
-    for copy in own:
-        copy.wait()
-    for copy in stage:
-        copy.wait_recv()
-    spread = []
-    for k, d in enumerate(copies):
-        spread.append(remote(wg.at[r], wg.at[r], (s_w, r_w), 7 + k, {"rep": d}))
-        spread.append(remote(wog.at[r], wog.at[r], (s_o, r_o), 7 + k, {"rep": d}))
-    for copy in spread:
-        copy.start()
-    tokens.forward()
-    grads.start()
-    tokens.finish()
-    grads.forward()
-    grads.finish()
-    for copy in spread:
-        copy.wait_recv()
-    for copy in stage + spread:
-        copy.wait_send()
-
-
-def gather_first(tok, cot, wsl, wo):
-    return comm_call(
-        gather_first_kernel,
-        "gather_first",
-        1,
-        [
-            shape((EP * TOK, D), BF),
-            shape((EP * TOK, D), BF),
-            shape((REP, EP, 32, 128), BF),
-            shape((REP, EP, 64, 128), BF),
-        ],
-        [ANY] * 4,
-        [ANY] * 4,
-        [DMA((4,)), DMA((10,)), DMA((10,)), DMA((10,)), DMA((10,)), DMA((22,)), DMA((22,)), DMA((22,)), DMA((22,))],
-    )(tok, cot, wsl, wo)
 
 
 def sum_stats_kernel(x_ref, o_ref, held, ssem, rsem):
@@ -491,35 +432,6 @@
     return dot_nt(jnp.ones((8, 128), F32), values, precision=HIGH)[0:1]
 
 
-def project_kernel(x_ref, w_ref, gain_ref, o_ref, st_ref):
-    i = pl.program_id(0)
-    x = x_ref[...].astype(F32)
-    r = lax.rsqrt(jnp.mean(x * x, axis=1, keepdims=True) + EPSILON)
-    normed = (x * r * gain_ref[...]).astype(BF)
-    lin = dot(normed, w_ref[...])
-    o_ref[...] = lin
-    keys = iota((TOK, 128), 1) < HEAD_DIM
-    sq = lin * lin
-    st_ref[pl.ds(2 * i, 1)] = lane_row(sq[:, :128])
-    st_ref[pl.ds(2 * i + 1, 1)] = lane_row(jnp.where(keys, sq[:, 128:], 0.0))
-
-
-def project(x_all, w, gain):
-    return pl.pallas_call(
-        project_kernel,
-        grid=(EP,),
-        out_shape=[shape((LENGTH, 256)), shape((2 * EP, 256))],
-        in_specs=[
-            pl.BlockSpec((TOK, D), lambda i: (i, 0)),
-            pl.BlockSpec((D, 256), lambda i: (0, 0)),
-            pl.BlockSpec((1, D), lambda i: (0, 0)),
-        ],
-        out_specs=[pl.BlockSpec((TOK, 256), lambda i: (i, 0)), pl.BlockSpec((16, 256), lambda i: (0, 0))],
-        compiler_params=pltpu.CompilerParams(vmem_limit_bytes=32 * MIB),
-        name="project",
-    )(x_all, w, gain)
-
-
 def turn_tables():
     half = HEAD_DIM // 2
     freq = np.float32(ROPE_BASE) ** (-(np.arange(half, dtype=np.float32) * np.float32(2.0) / np.float32(HEAD_DIM)))
@@ -554,10 +466,147 @@
     return jnp.where(first, values[:TOK], values[TOK:])
 
 
-def attend_kernel(
-    lin, st, lo, cos_ref, sin_ref, gain, q_o, k_o, v_o, a_o, lse_o, s_scr, q2_scr, lo_scr, m_scr, l_scr, acc
+def front_kernel(
+    tok, cot, wq, wk, wv, wo_in, small, seg, rts, cos_in, sin_in,
+    x_all, g_all, lin, st, lo, q_o, k_o, v_o, a_o, lse_o, hid_o, m_o, tab_o, att_o, gain_a, gain_f, gain, rout_o, whole, wcol,
+    x_s, wsl, wos, wg, wog, w32, gains_s, cos_ref, sin_ref, sums, held,
+    s_scr, q2_scr, lo_scr, m_scr, l_scr, acc,
+    s_tok, r_tok, s_cot, r_cot, s_w, r_w, s_o, r_o, s_st, r_st, s_a, r_a, lsem,
 ):
+    r = lax.axis_index("rep")
+    e, x, c = place()
+    others = ep_others(e)
+    copies = rep_others(r)
     first = iota((TOK, 128), 1) < HEAD_DIM
+    greet([{"ep": d} for d in others] + [{"rep": d} for d in copies])
+
+    low_lanes = iota((8, 128), 1) < HEAD_DIM
+    for d in range(EP):
+        k_t = wk[:, (d // 2) * 128 : (d // 2 + 1) * 128].astype(F32)
+        v_t = wv[:, (d // 2) * 128 : (d // 2 + 1) * 128].astype(F32)
+        if d % 2:
+            k_t = pltpu.roll(k_t, HEAD_DIM, 1)
+        else:
+            v_t = pltpu.roll(v_t, HEAD_DIM, 1)
+        q_t = wq[:, d * 128 : (d + 1) * 128].astype(F32)
+        wsl[d, :16] = jnp.concatenate([q_t, jnp.where(low_lanes, k_t, v_t)], axis=0).astype(BF)
+        wsl[d, 16:] = small[...]
+    wos[...] = jnp.concatenate(
+        [wo_in[:, j * 128 : (j + 1) * 128].astype(F32) for j in range(8)], axis=0
+    ).astype(BF)
+    stage_w = [remote(wsl.at[d], wg.at[r, e], (s_w, r_w), k, {"ep": d}) for k, d in enumerate(others)]
+    stage_o = [remote(wos, wog.at[r, e], (s_o, r_o), k, {"ep": d}) for k, d in enumerate(others)]
+    spread_w = [remote(wg.at[r], wg.at[r], (s_w, r_w), 7 + k, {"rep": d}) for k, d in enumerate(copies)]
+    spread_o = [remote(wog.at[r], wog.at[r], (s_o, r_o), 7 + k, {"rep": d}) for k, d in enumerate(copies)]
+    tokens = RingGather(tok, x_s, (s_tok, r_tok), lsem.at[0])
+    grads = RingGather(cot, g_all, (s_cot, r_cot), lsem.at[1])
+    for copy in stage_w:
+        copy.start()
+    tokens.start()
+    for copy in stage_o:
+        copy.start()
+    tables = [
+        pltpu.make_async_copy(cos_in, cos_ref, lsem.at[2]),
+        pltpu.make_async_copy(sin_in, sin_ref, lsem.at[3]),
+    ]
+    for copy in tables:
+        copy.start()
+    wg[r, e] = wsl[e]
+    wog[r, e] = wos[...]
+    for copy in stage_w:
+        copy.wait_recv()
+    for copy in spread_w:
+        copy.start()
+    tokens.forward()
+
+    hit = jnp.zeros((EXPERTS, TOK), F32)
+    for k in range(TOP):
+        hit = jnp.where(iota((EXPERTS, TOK), 0) == rts[k : k + 1], 1.0, hit)
+    before = jnp.where(iota((TOK, TOK), 0) < iota((TOK, TOK), 1), 1.0, 0.0).astype(BF)
+    tab_o[:EXPERTS] = jnp.where(hit > 0.0, dot(hit.astype(BF), before), -1.0)
+    segs = seg[...]
+    opening = jnp.zeros((EP, TOK), F32)
+    for value in range(2):
+        count = jnp.sum(jnp.where(segs == value, 1.0, 0.0), axis=1, keepdims=True)
+        opening = opening + jnp.where(segs > value, jnp.sum(count, axis=0, keepdims=True), 0.0)
+    places = (iota((EP, TOK), 0) * TOK + iota((EP, TOK), 1)).astype(F32)
+    lo[...] = jnp.maximum(opening, places - (WINDOW - 1))
+
+    tokens.fwd_right.wait_recv()
+    tokens.fwd_left.wait_recv()
+    tokens.to_peer[2].start()
+    for copy in spread_w:
+        copy.wait_recv()
+    for copy in stage_o:
+        copy.wait_recv()
+    for copy in spread_o:
+        copy.start()
+
+    def unpack(b, carry):
+        tile = wg[b // EP, b % EP].astype(F32)
+        rows = pl.ds(pl.multiple_of(b * 8, 8), 8)
+        w32[rows, 0:128] = tile[0:8]
+        w32[rows, 128:256] = tile[8:16]
+        w32[rows, 256:384] = tile[16:24]
+        gains_s[pl.ds(b, 1)] = tile[24:25]
+        return carry
+
+    lax.fori_loop(0, 128, unpack, 0)
+    wcol[...] = w32[:, :256].astype(BF)
+    rout_o[...] = jnp.transpose(w32[:, 256:384])[:EXPERTS].astype(BF)
+    packed = gains_s[...].astype(BF)
+
+    def spread_gain(width, group, base, shift):
+        lane = base + iota((128, width), 1) % group
+        picked = dot(packed, jnp.where(iota((128, width), 0) == lane, 1.0, 0.0).astype(BF))
+        mine = iota((128, width), 0) == shift + iota((128, width), 1) // group
+        return jnp.sum(jnp.where(mine, picked, 0.0), axis=0, keepdims=True)
+
+    gain_a[...] = spread_gain(D, 8, 0, 0)
+    gain_f[...] = spread_gain(D, 8, 20, 0)
+    key_part = spread_gain(128, 4, 16, e * 16)
+    gain[:, :128] = spread_gain(128, 8, 8, e * 16)
+    gain[:, 128:] = jnp.where(iota((1, 128), 1) < HEAD_DIM, key_part, 1.0)
+
+    tokens.first[4].wait_recv()
+    tokens.own.wait()
+    tokens.to_peer[1].wait_recv()
+    tokens.to_peer[0].wait_recv()
+
+    def project(k, carry):
+        @pl.when(k == 6)
+        def _():
+            tokens.to_peer[2].wait_recv()
+
+        g = k // 2
+        b = (2 * (x + g + g // 2 - 2 * (g // 3)) + k % 2) % EP
+        rows = block_rows(b)
+        values = x_s[rows].astype(F32)
+        r1 = lax.rsqrt(jnp.mean(values * values, axis=1, keepdims=True) + EPSILON)
+        normed = (values * r1 * gain_a[...]).astype(BF)
+        out = dot(normed, wcol[...])
+        lin[rows] = out
+        sq = out * out
+        sums[pl.ds(2 * b, 1)] = lane_row(sq[:, :128])
+        sums[pl.ds(2 * b + 1, 1)] = lane_row(jnp.where(first, sq[:, 128:], 0.0))
+        return carry
+
+    lax.fori_loop(0, EP, project, 0)
+    stats = [remote(sums, held.at[e], (s_st, r_st), k, {"ep": d}) for k, d in enumerate(others)]
+    for copy in stats:
+        copy.start()
+    held[e] = sums[...]
+    keep = pltpu.make_async_copy(x_s, x_all, lsem.at[4])
+    keep.start()
+    for copy in tables:
+        copy.wait()
+    for copy in stats:
+        copy.wait_recv()
+    total = held[0]
+    for k in range(1, EP):
+        total = total + held[k]
+    st[...] = total
+    grads.start()
 
     def prepare(b, carry):
         rows = block_rows(b)
@@ -574,6 +623,17 @@
 
     lax.fori_loop(0, EP, prepare, 0)
 
+    def heads(i, source):
+        cols = pl.ds(pl.multiple_of(source * 128, 128), 128)
+        return pltpu.make_async_remote_copy(
+            src_ref=a_o.at[block_rows(i)],
+            dst_ref=att_o.at[:, cols],
+            send_sem=s_a.at[i],
+            recv_sem=r_a.at[source],
+            device_id={"ep": i},
+            device_id_type=MESH,
+        )
+
     def queries(i, carry):
         rows = block_rows(i)
         q2_scr[...] = stack_heads(q_o[rows].astype(F32) * HEAD_DIM ** (-0.5)).astype(BF)
@@ -608,28 +668,124 @@
         a_o[rows] = merge_heads(acc[...] / total).astype(BF)
         lse = jnp.broadcast_to(m_scr[:, :1] + jnp.log(total), (2 * TOK, 128))
         lse_o[i] = jnp.transpose(lse)[:8]
+
+        @pl.when(i != e)
+        def _():
+            heads(i, e).start()
+
+        @pl.when(i == e)
+        def _():
+            att_o[:, pl.ds(pl.multiple_of(e * 128, 128), 128)] = a_o[rows]
+
+        @pl.when(i == 4)
+        def _():
+            grads.forward()
+
+        @pl.when(i == 6)
+        def _():
+            grads.fwd_right.wait_recv()
+            grads.fwd_left.wait_recv()
+            grads.to_peer[2].start()
+
         return carry
 
     lax.fori_loop(0, EP, queries, 0)
 
-
-def attend(lin, st, lo, cosine, sine, gain):
-    return pl.pallas_call(
-        attend_kernel,
-        out_shape=[shape((LENGTH, 128), BF)] * 4 + [shape((EP, 8, 2 * TOK))],
-        in_specs=[VM] * 6,
-        out_specs=[VM] * 5,
-        scratch_shapes=[
+    for copy in spread_o:
+        copy.wait_recv()
+
+    def unpack_out(b, carry):
+        tile = wog[b // EP, b % EP].astype(F32)
+        rows = pl.ds(pl.multiple_of(b * 8, 8), 8)
+        for j in range(8):
+            w32[rows, j * 128 : (j + 1) * 128] = tile[j * 8 : (j + 1) * 8]
+        return carry
+
+    lax.fori_loop(0, 128, unpack_out, 0)
+    whole[...] = w32[...].astype(BF)
+    for d in others:
+        heads(d, d).wait_recv()
+
+    hidden = x_s[block_rows(e)].astype(F32) + dot(att_o[...], whole[...])
+    hid_o[...] = hidden
+    r2 = lax.rsqrt(jnp.mean(hidden * hidden, axis=1, keepdims=True) + EPSILON)
+    moe_in = (hidden * r2 * gain_f[...]).astype(BF)
+    m_o[...] = moe_in
+    logits = dot_nt(rout_o[...], moe_in)
+    chosen = hit > 0.0
+    logits = jnp.where(chosen, logits, MASKED)
+    raised = jnp.where(chosen, jnp.exp(logits - jnp.max(logits, axis=0, keepdims=True)), 0.0)
+    tab_o[EXPERTS:] = raised / jnp.sum(raised, axis=0, keepdims=True)
+
+    grads.first[4].wait_recv()
+    for copy in grads.to_peer:
+        copy.wait_recv()
+    grads.own.wait()
+    keep.wait()
+    for d in others:
+        heads(d, d).wait_send()
+    for ring in (tokens, grads):
+        for copy in ring.first + [ring.fwd_right, ring.fwd_left] + ring.to_peer:
+            copy.wait_send()
+    for copy in stage_w + stage_o + spread_w + spread_o + stats:
+        copy.wait_send()
+
+
+def front(*args):
+    return comm_call(
+        front_kernel,
+        "front",
+        1,
+        [
+            shape((LENGTH, D), BF),
+            shape((LENGTH, D), BF),
+            shape((LENGTH, 256)),
+            shape((16, 256)),
+            shape((EP, TOK)),
+            shape((LENGTH, 128), BF),
+            shape((LENGTH, 128), BF),
+            shape((LENGTH, 128), BF),
+            shape((LENGTH, 128), BF),
+            shape((EP, 8, 2 * TOK)),
+            shape((TOK, D)),
+            shape((TOK, D), BF),
+            shape((2 * EXPERTS, TOK)),
+            shape((TOK, D), BF),
+            shape((1, D)),
+            shape((1, D)),
+            shape((1, 256)),
+            shape((EXPERTS, D), BF),
+            shape((D, D), BF),
+            shape((D, 256), BF),
+        ],
+        [ANY, ANY] + [VM] * 7 + [ANY, ANY],
+        [ANY, ANY] + [VM] * 18,
+        [
+            pltpu.VMEM((LENGTH, D), BF),
+            pltpu.VMEM((EP, 32, 128), BF),
+            pltpu.VMEM((64, 128), BF),
+            pltpu.VMEM((REP, EP, 32, 128), BF),
+            pltpu.VMEM((REP, EP, 64, 128), BF),
+            pltpu.VMEM((D, D), F32),
+            pltpu.VMEM((128, 128), F32),
+            pltpu.VMEM((LENGTH, 128), F32),
+            pltpu.VMEM((LENGTH, 128), F32),
+            pltpu.VMEM((16, 256), F32),
+            pltpu.VMEM((EP, 16, 256), F32),
             pltpu.VMEM((5, 2 * TOK, TOK), F32),
             pltpu.VMEM((2 * TOK, 128), BF),
             pltpu.VMEM((2 * TOK, 128), F32),
             pltpu.VMEM((2 * TOK, 128), F32),
             pltpu.VMEM((2 * TOK, 128), F32),
             pltpu.VMEM((2 * TOK, 128), F32),
-        ],
-        compiler_params=pltpu.CompilerParams(vmem_limit_bytes=48 * MIB),
-        name="attend",
-    )(lin, st, lo, cosine, sine, gain)
+        ]
+        + [DMA((10,))] * 4
+        + [DMA((22,))] * 4
+        + [DMA((7,))] * 2
+        + [DMA((8,))] * 2
+        + [DMA((5,))],
+        limit=60,
+    )(*args)
 
 
 def attend_back_kernel(
@@ -1099,30 +1255,6 @@
     )(m, t, g_all, wg, wu, wd)
 
 
-def hidden_kernel(x_ref, a_ref, w_ref, gain, router, hit, hid_o, m_o, gate_o):
-    hidden = x_ref[...].astype(F32) + dot(a_ref[...], w_ref[...])
-    hid_o[...] = hidden
-    r2 = lax.rsqrt(jnp.mean(hidden * hidden, axis=1, keepdims=True) + EPSILON)
-    moe_in = (hidden * r2 * gain[...]).astype(BF)
-    m_o[...] = moe_in
-    logits = dot_nt(router[...], moe_in)
-    chosen = hit[...] >= 0
-    logits = jnp.where(chosen, logits, MASKED)
-    raised = jnp.where(chosen, jnp.exp(logits - jnp.max(logits, axis=0, keepdims=True)), 0.0)
-    gate_o[...] = raised / jnp.sum(raised, axis=0, keepdims=True)
-
-
-def hidden_call(x, a, w, gain, router, hit):
-    return pl.pallas_call(
-        hidden_kernel,
-        out_shape=[shape((TOK, D)), shape((TOK, D), BF), shape((EXPERTS, TOK))],
-        in_specs=[VM] * 6,
-        out_specs=[VM] * 3,
-        compiler_params=pltpu.CompilerParams(vmem_limit_bytes=32 * MIB),
-        name="hidden",
-    )(x, a, w, gain, router, hit)
-
-
 def hidden_back_kernel(
     hid, mixed, gmoe, gg, gate, m_ref, cot, gain, router, w_ref, a_ref, out_o, gh_o, ga_o, dwo_o, dr_o, gf_o
 ):
@@ -1181,56 +1313,19 @@
     w_down,
     out_grad,
 ):
-    r = lax.axis_index("rep")
     e = lax.axis_index("ep")
-    cols = jnp.concatenate(
-        [w_query.reshape(8, EP, 128), w_key.reshape(8, EP, 64), w_value.reshape(8, EP, 64)], axis=2
+    gains = jnp.concatenate([gain_attn, gain_query, gain_key, gain_ffn]).reshape(1, 28)
+    small = jnp.concatenate(
+        [jnp.pad(w_router, ((0, 0), (0, 128 - EXPERTS))), jnp.pad(gains, ((0, 7), (0, 100)))], axis=0
     )
-    cols = cols.reshape(8, EP, 2, 128).transpose(1, 2, 0, 3).reshape(EP, 16, 128)
-    small = jnp.concatenate([gain_attn, gain_query, gain_key, gain_ffn, w_router.reshape(-1)])
-    small = jnp.pad(small, (0, 2048 - small.shape[0])).reshape(1, 16, 128)
-    wsl = jnp.concatenate([cols, jnp.broadcast_to(small, (EP, 16, 128))], axis=1)
-    wo = w_out.reshape(8, 8, 128).transpose(1, 0, 2).reshape(64, 128)
-
-    expert_ids = jnp.arange(EXPERTS, dtype=jnp.int32)
-    routed = jnp.sum((routes[:, :, None] == expert_ids[None, None, :]).astype(BF), axis=1)
-    before = (jnp.arange(TOK)[:, None] < jnp.arange(TOK)[None, :]).astype(BF)
-    rank = lax.dot_general(routed, before, TN, preferred_element_type=F32)
-    slot_own = jnp.where(routed.T > 0, rank, -1.0)
-
-    seg = segments[0]
-    positions = jnp.arange(LENGTH, dtype=jnp.int32)
-    zeros = jnp.sum((seg == 0).astype(jnp.int32))
-    ones = jnp.sum((seg <= 1).astype(jnp.int32))
-    opening = jnp.where(seg == 0, 0, jnp.where(seg == 1, zeros, ones))
-    lo = jnp.maximum(opening, positions - (WINDOW - 1)).astype(F32).reshape(EP, TOK)
     cosine, sine = turn_tables()
-
-    x_all, g_all, wg_all, wo_all = gather_first(tokens, out_grad, wsl, wo)
-
-    w_cols = wg_all[:, :, :16].reshape(128, 2, 8, 128).transpose(0, 2, 1, 3).reshape(D, 256)
-    small_all = wg_all[:, :, 16:].reshape(128, 2048)
-    attn_gain = small_all[:, :8].reshape(1, D).astype(F32)
-    query_gain = small_all[:, 8:16].reshape(1, D).astype(F32)
-    key_gain = small_all[:, 16:20].reshape(1, KV).astype(F32)
-    ffn_gain = small_all[:, 20:28].reshape(1, D).astype(F32)
-    router = small_all[:, 28:284].reshape(D, EXPERTS).T
-    whole_out = wo_all.reshape(128, 8, 8, 128).transpose(0, 2, 1, 3).reshape(D, D)
-    qk_gain = jnp.concatenate(
-        [
-            lax.dynamic_slice_in_dim(query_gain, e * 128, 128, 1),
-            lax.dynamic_slice_in_dim(key_gain, e * 64, 64, 1),
-            jnp.ones((1, 64), F32),
-        ],
-        axis=1,
+    (
+        x_all, g_all, lin, st, lo, q, k, v, att, lse, hidden, moe_in, tables, attended,
+        attn_gain, ffn_gain, qk_gain, router, whole_out, w_cols,
+    ) = front(
+        tokens, out_grad, w_query, w_key, w_value, w_out, small, segments.reshape(EP, TOK), routes.T, cosine, sine
     )
-
-    lin, sums = project(x_all, w_cols, attn_gain)
-    st = sum_stats(sums, "sum_stats", 2)
-    q, k, v, att, lse = attend(lin, st, lo, cosine, sine, qk_gain)
-    attended = swap_heads(att, True, "swap_heads", 3)
-    hidden, moe_in, gates = hidden_call(tokens, attended, whole_out, ffn_gain, router, slot_own)
-    tables = jnp.concatenate([slot_own, gates], axis=0)
+    gates = tables[EXPERTS:]
     mixed, grad_moe, gg, grads = experts(moe_in, tables, g_all, w_gate, w_up, w_down)
     grads = grads.reshape(LOCAL, REP * BLOCK, D)
     expert_sums = lax.psum_scatter(grads, "rep", scatter_dimension=1, tiled=True).astype(F32)

time: 401 us -> 348 us (0.87)
  Pallas kernels: 324 us -> 290 us
  local copies, waits for them, and re-layouts: 55.7 us -> 33.2 us
    pallas_call x4 -> x1, Pallas kernels: 100 us -> 80.5 us  [front(): comm_call(front_kernel, 'front', 1, [shape((LENGTH, D), BF), shape((LENGT...]
    unnamed x86 -> x57, local copies, waits for them, and re-layouts: 29.7 us -> 13.9 us
    pallas_call x2 -> x1, Pallas kernels: 20.9 us -> 11.1 us  [swap_heads(): comm_call(functools.partial(swap_kernel, to_rows), name, collective_id, s...]
    pallas_call x2 -> x1, Pallas kernels: 11.8 us -> 5.62 us  [sum_stats(): comm_call(sum_stats_kernel, name, collective_id, shape(x.shape), [VM], VM...]
  transfers between devices with their start and end apart: 1 -> 1, of which waited for: 0 -> 0; matrix products, arithmetic and copies ran while one was open for 5% -> 6% of each run, Pallas kernels for 25% -> 28%
where the time goes in v3:
time: 348 us; the launch traced here: 347 us
  Pallas kernels  290 us (83%)
  local copies, waits for them, and re-layouts  33.2 us (10%)
  between operations  14.4 us (4%)
  other arithmetic  8.55 us (2%)
    pallas_call x1, Pallas kernels, experts(): comm_call(experts_kernel, 'experts', 4, [shape((TOK, D)), shape((TOK, D))...  112 us
    pallas_call x1, Pallas kernels, front(): comm_call(front_kernel, 'front', 1, [shape((LENGTH, D), BF), shape((LENGT...  80.5 us
    pallas_call x1, Pallas kernels, reduce_last(): comm_call(reduce_last_kernel, 'reduce_last', 6, [shape((TOK, D)), shape((...  34.9 us
    pallas_call x1, Pallas kernels, attend_back(): pl.pallas_call(attend_back_kernel, out_shape=[shape((LENGTH, 256)), shape...  31.6 us
    unnamed x57, local copies, waits for them, and re-layouts  13.9 us
    pallas_call x1, Pallas kernels, swap_heads(): comm_call(functools.partial(swap_kernel, to_rows), name, collective_id, s...  11.1 us
    pallas_call x1, Pallas kernels, project_back(): pl.pallas_call(project_back_kernel, grid=(EP,), out_shape=[shape((LENGTH,...  9.65 us
    concatenate x6, local copies, waits for them, and re-layouts, body(): vectors = jnp.concatenate([drouter, dattn[0:1], dquery, dkey, dffn], axis=0)  7.31 us
  transfers between devices with their start and end apart: 1, of which 0 were waited for; matrix products, arithmetic and copies ran while one was open for 6% of the time, Pallas kernels for 28%

profile of v3, /device:TPU:1, one launch (start us, length us, event | category | flops | bytes accessed | tf_op | source)
XLA Modules:
  0.0 346.6 jit_solution(4715547499907729745)
XLA Ops:
  7.2 0.0 reduce-scatter.2.cloned.1.call-start
  7.2 0.5 broadcast.52
  7.7 1.4 reduce.19
  9.1 0.6 reshape.89.seg
  9.7 0.8 maximum_bitcast_fusion
  10.5 1.3 fusion.11.small
  11.8 80.5 %front.1 = (bf16[2048,1024]{1,0:T(8,128)(2,1)}, bf16[2048,1024]{1,0:T(8,128)(2,1)}, f32[2048,256]{1,0:T(8,128)}, f32[16,256]{1,0:T(8,128)}, f32[8,256]{1,0:T(8,1...) custom-call(bf16[256,1024]{1,0:T(8,128)(2,1)} %tok.1, ...), custom_call_target="tpu_custom_call" | custom-call | tf_op jit(solution)/shard_map/front/pallas_call | solution.py:735
  92.3 111.8 %experts.1 = (f32[256,1024]{1,0:T(8,128)}, f32[256,1024]{1,0:T(8,128)}, f32[8,8,256]{2,1,0:T(8,128)}, bf16[4,16,96,1024]{3,2,1,0:T(8,128)(2,1)}) custom-call(bf16[256,1024]{1,0:T(8,128)(2,1)} %get-tuple-element.54.m_in.m_ref, f32[64,256]{1,0:T(8,128)} %get-tuple-element.55.t_in, bf16[2048,1024]{1,0:T(8,128)(2,1)} %get-tuple-element.56.g_in, ...), custom_call_target="tpu_custom_call" | custom-call | tf_op jit(solution)/shard_map/experts/pallas_call | solution.py:1215
  204.1 0.0 copy-start.26
  204.1 0.0 copy-start.25
  204.1 0.0 copy-start.27
  204.1 0.0 copy-start.3
  204.1 0.0 reduce-scatter.2.cloned.1.call-update
  204.2 0.7 copy-done.26
  204.9 0.2 copy-done.25
  205.2 0.2 copy.36
  205.4 0.2 copy.38.a_ref
  205.7 0.0 copy-done.3
  205.7 0.0 copy-done.4
  205.7 0.0 copy-done.18
  205.7 0.0 copy-done.22
  205.7 0.0 copy-start.8
  205.7 1.2 copy-done.8
  206.9 1.2 copy-done.9
  208.2 5.3 %hidden_back.1 = (bf16[256,1024]{1,0:T(8,128)(2,1)}, f32[256,1024]{1,0:T(8,128)S(1)}, bf16[256,1024]{1,0:T(8,128)(2,1)S(1)}, bf16[1024,1024]{1,0:T(8,128)(2,1)},...) custom-call(f32[256,1024]{1,0:T(8,128)S(1)} %copy-done.8, f32[256,1024]{1,0:T(8,128)S(1)} %copy-done.9, ...), custom_call_target="tpu_custom_call" | custom-call | tf_op jit(solution)/shard_map/hidden_back/pallas_call | solution.py:1281
  213.4 1.0 copy-done.6
  214.4 0.8 copy-done.15
  215.2 0.8 copy.39
  216.1 1.1 concatenate.35
  217.2 1.1 copy-done.16
  218.3 11.1 %swap_heads_back.1.go = bf16[2048,128]{1,0:T(8,128)(2,1)S(1)} custom-call(bf16[256,1024]{1,0:T(8,128)(2,1)S(1)} %copy-done.16), custom_call_target="tpu_custom_call" | custom-call | tf_op jit(solution)/shard_map/swap_heads_back/pallas_call | solution.py:331
  229.4 0.0 copy-start.2
  229.4 1.2 copy-done.2
  230.7 1.1 copy-done.11
  231.7 1.1 copy-done.12
  232.8 1.1 copy-done.13
  233.8 1.1 copy-done.14
  234.9 31.6 %attend_back.1 = (f32[2048,256]{1,0:T(8,128)}, f32[16,256]{1,0:T(8,128)S(1)}) custom-call(bf16[2048,128]{1,0:T(8,128)(2,1)S(1)} %copy-done.11, bf16[2048,128]{1,0:T(8,128)(2,1)S(1)} %copy-done.12, bf16[2048,128]{1,0:T(8,128)(2,1)S(1)} %copy-done.13, bf16[2048,128]{1,0:T(8,128)(2,1)S(1)} %copy-done.14, f32[8,8,512]{2,1,0:T(8,128)S(1)} %copy-done.17, ...), custom_call_target="tpu_custom_call" | custom-call | tf_op jit(solution)/shard_map/attend_back/pallas_call | solution.py:852
  266.4 5.6 %sum_stats_back.1.st2 = f32[16,256]{1,0:T(8,128)S(1)} custom-call(f32[16,256]{1,0:T(8,128)S(1)} %get-tuple-element.78.x_ref), custom_call_target="tpu_custom_call" | custom-call | tf_op jit(solution)/shard_map/sum_stats_back/pallas_call | solution.py:292
  272.1 1.6 copy-done.5
  273.7 9.7 %project_back.1 = (bf16[2048,1024]{1,0:T(8,128)(2,1)}, f32[1024,256]{1,0:T(8,128)S(1)}, f32[8,1024]{1,0:T(8,128)S(1)}, f32[8,256]{1,0:T(8,128)S(1)}) custom-call(bf16[2048,1024]{1,0:T(8,128)(2,1)} %get-tuple-element.66.x_ref, f32[2048,256]{1,0:T(8,128)S(1)} %copy-done.5, f32[2048,256]{1,0:T(8,128)S(1)} %copy-done, f32[16,256]{1,0:T(8,128)S(1)} %copy-done.19, ...), custom_call_target="tpu_custom_call" | custom-call | tf_op jit(solution)/shard_map/project_back/pallas_call | solution.py:916
  283.4 0.3 dynamic_update_slice.7
  283.7 0.1 reshape.93
  283.8 1.5 copy.43
  285.4 1.1 concatenate.33
  286.5 1.1 concatenate.34
  287.7 2.3 concatenate.31
  290.0 1.0 copy.45
  291.0 0.2 fusion.1.wb
  291.3 0.0 copy-start.7
  291.3 34.9 %reduce_last.1 = (f32[256,1024]{1,0:T(8,128)S(1)}, f32[8,1152]{1,0:T(8,128)S(1)}, f32[8,8,256]{2,1,0:T(8,128)S(1)}) custom-call(bf16[2048,1024]{1,0:T(8,128)(2,1)} %get-tuple-element.81.gn, bf16[1024,1152]{1,0:T(8,128)(2,1)S(1)} %fusion.1.wb, f32[1024,256]{1,0:T(8,128)S(1)} %get-tuple-element.87.dw), custom_call_target="tpu_custom_call" | custom-call | tf_op jit(solution)/shard_map/reduce_last/pallas_call | solution.py:402
  326.2 0.6 slice.61
  326.8 0.6 slice.60
  327.4 0.1 fusion.14
  327.5 0.7 reshape.97
  328.2 0.7 reshape.96
  328.9 0.7 slice_reduce_fusion.3
  329.6 0.7 slice_reduce_fusion
  330.3 1.2 fusion.8
  331.6 1.3 fusion.4
  332.9 0.6 slice_bitcast_fusion
  333.5 2.3 fusion.7
  335.8 1.8 slice.75
  337.6 2.1 fusion.13
  (51 shorter events, 0.3 us)
Async XLA Ops:
  7.2 328.7 %reduce-scatter.2.cloned.1.call-start = ((), (), s32[]{:S(2)}) async-start(), calls=%async_computation.1 | async-start | bytes 13369344 | tf_op jit(solution)/shard_map/reduce_scatter | solution.py:1331
  204.1 0.8 copy-start.26
  204.1 1.1 copy-start.25
  204.1 1.5 copy-start.27
  204.1 1.6 copy-start.3
  204.1 1.6 copy-start.4
  204.1 1.6 copy-start.18
  204.1 1.6 copy-start.22
  205.7 1.2 copy-start.8
  206.9 1.2 copy-start.9
  208.2 21.2 %copy-start.1 = (f32[2048,128]{1,0:T(8,128)S(1)}, f32[2048,128]{1,0:T(8,128)}, u32[]{:S(2)}) copy-start(f32[2048,128]{1,0:T(8,128)} %constant.33.clone.sin_in.sin_ref) | copy-start | bytes 3145732
  208.2 21.2 %copy-start.17 = (f32[8,8,512]{2,1,0:T(8,128)S(1)}, f32[8,8,512]{2,1,0:T(8,128)}, u32[]{:S(2)}) copy-start(f32[8,8,512]{2,1,0:T(8,128)} %get-tuple-element.71.lse) | copy-start | bytes 393220
  208.2 21.2 %copy-start.19 = (f32[16,256]{1,0:T(8,128)S(1)}, f32[16,256]{1,0:T(8,128)}, u32[]{:S(2)}) copy-start(f32[16,256]{1,0:T(8,128)} %get-tuple-element.75.st) | copy-start | bytes 49156
  208.2 21.2 %copy-start.21 = (f32[8,256]{1,0:T(8,128)S(1)}, f32[8,256]{1,0:T(8,128)}, u32[]{:S(2)}) copy-start(f32[8,256]{1,0:T(8,128)} %get-tuple-element.72.lo) | copy-start | bytes 24580
  208.2 21.2 %copy-start.23 = (f32[1,256]{1,0:T(1,128)S(1)}, f32[1,256]{1,0:T(1,128)}, u32[]{:S(2)}) copy-start(f32[1,256]{1,0:T(1,128)} %get-tuple-element.76.gain) | copy-start | bytes 3076
  213.4 1.0 copy-start.6
  214.4 0.8 copy-start.15
  215.2 56.9 %copy-start.20 = (f32[1,1024]{1,0:T(1,128)S(1)}, f32[1,1024]{1,0:T(1,128)}, u32[]{:S(2)}) copy-start(f32[1,1024]{1,0:T(1,128)} %get-tuple-element.79.attn_gain) | copy-start | bytes 12292
  216.1 56.0 %copy-start = (f32[2048,256]{1,0:T(8,128)S(1)}, f32[2048,256]{1,0:T(8,128)}, u32[]{:S(2)}) copy-start(f32[2048,256]{1,0:T(8,128)} %get-tuple-element.74.lin.lin_ref) | copy-start | bytes 6291460
  217.2 1.1 copy-start.16
  229.4 1.3 copy-start.2
  230.7 1.1 copy-start.11
  231.7 1.1 copy-start.12
  232.8 1.1 copy-start.13
  233.8 1.1 copy-start.14
  234.9 37.2 %copy-start.10 = (bf16[1024,256]{1,0:T(8,128)(2,1)S(1)}, bf16[1024,256]{1,0:T(8,128)(2,1)}, u32[]{:S(2)}) copy-start(bf16[1024,256]{1,0:T(8,128)(2,1)} %get-tuple-element.80.w_ref) | copy-start | bytes 1572868
  272.1 1.6 copy-start.5
  283.4 7.7 %copy-start.24 = (bf16[1024,1024]{1,0:T(8,128)(2,1)S(1)}, bf16[1024,1024]{1,0:T(8,128)(2,1)}, u32[]{:S(2)}) copy-start(bf16[1024,1024]{1,0:T(8,128)(2,1)} %get-tuple-element.82) | copy-start | bytes 6291460
  291.3 42.3 %copy-start.7 = (f32[256,1024]{1,0:T(8,128)S(1)}, f32[256,1024]{1,0:T(8,128)}, u32[]{:S(2)}) copy-start(f32[256,1024]{1,0:T(8,128)} %copy-done.6) | copy-start | bytes 3145732
Sparse Core Ops, SparseCore 0:
  204.3 92.0 reduce-scatter.1

commit v4 on v3

--- a/solution.py
+++ b/solution.py
@@ -210,15 +210,19 @@
         for copy in self.swap + self.load:
             copy.start()
 
-    def middle(self):
+    def push_opp(self):
         self.merge(0)
         for copy in self.opp:
             copy.start()
+
+    def push_near(self):
         self.merge(1)
         self.near[0].start()
         self.merge(2)
         self.near[1].start()
         self.merge(3)
+
+    def relay(self):
         self.opp[0].wait_recv()
         self.merge_hop(1, 0)
         self.far[0].start()
@@ -238,18 +242,6 @@
         self.rows_loop(0, self.n, body)
         for copy in self.swap + self.opp + self.near + self.far:
             copy.wait_send()
-
-
-def reduce_scratch(n, w):
-    return [
-        pltpu.VMEM((4, n, w), BF),
-        pltpu.VMEM((4, n, w), BF),
-        pltpu.VMEM((2, n, w), BF),
-        pltpu.VMEM((n, w), BF),
-        DMA((RingReduce.SEMS,)),
-        DMA((RingReduce.SEMS,)),
-        DMA((4,)),
-    ]
 
 
 def comm_call(kernel, name, collective_id, out_shape, in_specs, out_specs, scratch, limit=48):
@@ -270,158 +262,7 @@
     return jax.ShapeDtypeStruct(dims, dtype)
 
 
-def sum_stats_kernel(x_ref, o_ref, held, ssem, rsem):
-    e, _, _ = place()
-    others = ep_others(e)
-    greet([{"ep": d} for d in others])
-    copies = [remote(x_ref, held.at[e], (ssem, rsem), k, {"ep": d}) for k, d in enumerate(others)]
-    for copy in copies:
-        copy.start()
-    held[e] = x_ref[...]
-    for copy in copies:
-        copy.wait_recv()
-    total = held[0]
-    for k in range(1, EP):
-        total = total + held[k]
-    o_ref[...] = total
-    for copy in copies:
-        copy.wait_send()
-
-
-def sum_stats(x, name, collective_id):
-    return comm_call(
-        sum_stats_kernel,
-        name,
-        collective_id,
-        shape(x.shape),
-        [VM],
-        VM,
-        [pltpu.VMEM((EP,) + x.shape, F32), DMA((7,)), DMA((7,))],
-    )(x)
-
-
-def swap_kernel(to_rows, x_ref, o_ref, lsem, ssem, rsem):
-    e, _, _ = place()
-    others = ep_others(e)
-    greet([{"ep": d} for d in others])
-
-    def rows(ref, b):
-        return ref.at[pl.ds(pl.multiple_of(b * TOK, 16), TOK)]
-
-    def cols(ref, b):
-        return ref.at[:, pl.ds(pl.multiple_of(b * 128, 128), 128)]
-
-    src, dst = (rows, cols) if to_rows else (cols, rows)
-    own = pltpu.make_async_copy(src(x_ref, e), dst(o_ref, e), lsem)
-    copies = [
-        remote(src(x_ref, d), dst(o_ref, e), (ssem, rsem), k, {"ep": d}) for k, d in enumerate(others)
-    ]
-    for copy in copies:
-        copy.start()
-    own.start()
-    own.wait()
-    for copy in copies:
-        copy.wait_recv()
-    for copy in copies:
-        copy.wait_send()
-
-
-def swap_heads(x, to_rows, name, collective_id):
-    out = (TOK, D) if to_rows else (LENGTH, 128)
-    return comm_call(
-        functools.partial(swap_kernel, to_rows),
-        name,
-        collective_id,
-        shape(out, BF),
-        [ANY],
-        ANY,
-        [DMA(()), DMA((7,)), DMA((7,))],
-    )(x)
-
-
 WB = D + 128
-
-
-def reduce_last_kernel(
-    gn, wb, dw, o_gn, o_wb, o_dw,
-    pc1, snd1, rcv1, hop1, ss1, rs1, ls1,
-    pc2, snd2, rcv2, hop2, ss2, rs2, ls2,
-    wsum, wheld, dheld, dsum, lsem, s_w, r_w, s_d, r_d, s_e, r_e,
-):
-    r = lax.axis_index("rep")
-    e, _, _ = place()
-    others = ep_others(e)
-    copies = rep_others(r)
-    greet([{"ep": d} for d in others] + [{"rep": d} for d in copies])
-    ring_w = RingReduce(wb, 128, pc2, snd2, rcv2, hop2, (ss2, rs2), ls2)
-    ring_g = RingReduce(gn, TOK, pc1, snd1, rcv1, hop1, (ss1, rs1), ls1)
-    ring_w.start()
-    ring_g.start()
-
-    def part(ref, b, n):
-        return ref.at[pl.ds(pl.multiple_of(b * n, 8), n)]
-
-    spread_d = [remote(part(dw, d, 64), dheld.at[r], (s_d, r_d), k, {"rep": d}) for k, d in enumerate(copies)]
-    own_d = pltpu.make_async_copy(part(dw, r, 64), dheld.at[r], lsem.at[0])
-    for copy in spread_d + [own_d]:
-        copy.start()
-    ring_w.middle()
-    ring_g.middle()
-    ring_w.finish(wsum)
-    spread_w = [remote(part(wsum, d, 8), wheld.at[r], (s_w, r_w), k, {"rep": d}) for k, d in enumerate(copies)]
-    own_w = pltpu.make_async_copy(part(wsum, r, 8), wheld.at[r], lsem.at[1])
-    for copy in spread_w + [own_w]:
-        copy.start()
-    own_d.wait()
-    for copy in spread_d:
-        copy.wait_recv()
-    total = dheld[0]
-    for k in range(1, REP):
-        total = total + dheld[k]
-    dsum[...] = total
-    spread_e = [remote(part(dsum, d, 8), o_dw.at[e], (s_e, r_e), k, {"ep": d}) for k, d in enumerate(others)]
-    own_e = pltpu.make_async_copy(part(dsum, e, 8), o_dw.at[e], lsem.at[2])
-    for copy in spread_e + [own_e]:
-        copy.start()
-    ring_g.finish(o_gn)
-    own_w.wait()
-    for copy in spread_w:
-        copy.wait_recv()
-    total = wheld[0]
-    for k in range(1, REP):
-        total = total + wheld[k]
-    o_wb[...] = total
-    own_e.wait()
-    for copy in spread_e:
-        copy.wait_recv()
-    for copy in spread_d + spread_w + spread_e:
-        copy.wait_send()
-
-
-def reduce_last(gn, wb, dw):
-    return comm_call(
-        reduce_last_kernel,
-        "reduce_last",
-        6,
-        [shape((TOK, D)), shape((8, WB)), shape((EP, 8, 256))],
-        [ANY] * 3,
-        [VM, VM, ANY],
-        reduce_scratch(TOK, D)
-        + reduce_scratch(128, WB)
-        + [
-            pltpu.VMEM((128, WB), F32),
-            pltpu.VMEM((REP, 8, WB), F32),
-            pltpu.VMEM((REP, 64, 256), F32),
-            pltpu.VMEM((64, 256), F32),
-            DMA((3,)),
-            DMA((15,)),
-            DMA((15,)),
-            DMA((15,)),
-            DMA((15,)),
-            DMA((7,)),
-            DMA((7,)),
-        ],
-    )(gn, wb, dw)
 
 
 def column(row):
@@ -468,7 +309,7 @@
 
 def front_kernel(
     tok, cot, wq, wk, wv, wo_in, small, seg, rts, cos_in, sin_in,
-    x_all, g_all, lin, st, lo, q_o, k_o, v_o, a_o, lse_o, hid_o, m_o, tab_o, att_o, gain_a, gain_f, gain, rout_o, whole, wcol,
+    x_all, g_all, lin, q_o, k_o, v_o, a_o, lse_o, hid_o, m_o, tab_o, att_o, misc, rout_o, whole, wcol,
     x_s, wsl, wos, wg, wog, w32, gains_s, cos_ref, sin_ref, sums, held,
     s_scr, q2_scr, lo_scr, m_scr, l_scr, acc,
     s_tok, r_tok, s_cot, r_cot, s_w, r_w, s_o, r_o, s_st, r_st, s_a, r_a, lsem,
@@ -478,7 +319,10 @@
     others = ep_others(e)
     copies = rep_others(r)
     first = iota((TOK, 128), 1) < HEAD_DIM
+    gain_a, gain_f, gain = misc.at[0:1], misc.at[1:2], misc.at[2:3, 0:256]
+    lo, st = misc.at[8:16, 0:256], misc.at[16:32, 0:256]
     greet([{"ep": d} for d in others] + [{"rep": d} for d in copies])
+    misc[...] = jnp.zeros((32, D), F32)
 
     low_lanes = iota((8, 128), 1) < HEAD_DIM
     for d in range(EP):
@@ -740,8 +584,6 @@
             shape((LENGTH, D), BF),
             shape((LENGTH, D), BF),
             shape((LENGTH, 256)),
-            shape((16, 256)),
-            shape((EP, TOK)),
             shape((LENGTH, 128), BF),
             shape((LENGTH, 128), BF),
             shape((LENGTH, 128), BF),
@@ -751,15 +593,13 @@
             shape((TOK, D), BF),
             shape((2 * EXPERTS, TOK)),
             shape((TOK, D), BF),
-            shape((1, D)),
-            shape((1, D)),
-            shape((1, 256)),
+            shape((32, D)),
             shape((EXPERTS, D), BF),
             shape((D, D), BF),
             shape((D, 256), BF),
         ],
         [ANY, ANY] + [VM] * 7 + [ANY, ANY],
-        [ANY, ANY] + [VM] * 18,
+        [ANY, ANY] + [VM] * 14,
         [
             pltpu.VMEM((LENGTH, D), BF),
             pltpu.VMEM((EP, 32, 128), BF),
@@ -788,152 +628,6 @@
     )(*args)
 
 
-def attend_back_kernel(
-    q_i, k_i, v_i, a_i, lse, lo, go, lin, st, cos_ref, sin_ref, gain, u_o, st_o, q2_scr, do2_scr, row_scr, dq, dk, dv
-):
-    first = iota((TOK, 128), 1) < HEAD_DIM
-    dk[...] = jnp.zeros((LENGTH, 128), F32)
-    dv[...] = jnp.zeros((LENGTH, 128), F32)
-
-    def queries(i, carry):
-        rows = block_rows(i)
-        q2_scr[...] = stack_heads(q_i[rows].astype(F32) * HEAD_DIM ** (-0.5)).astype(BF)
-        grad = stack_heads(go[rows].astype(F32))
-        do2_scr[...] = grad.astype(BF)
-        out = a_i[rows].astype(F32)
-        row_scr[0:1] = lane_row(grad * jnp.concatenate([out, out], axis=0))
-        row_scr[1:2] = lse[i][0:1]
-        row_scr[2:3] = jnp.concatenate([lo[pl.ds(i, 1)]] * 2, axis=1)
-        dq[...] = jnp.zeros((128, 2 * TOK), F32)
-
-        def keys(j, inner):
-            key_rows = block_rows(j)
-            kk = k_i[key_rows]
-            key = (iota((TOK, 2 * TOK), 0) + j * TOK).astype(F32)
-            query = (iota((TOK, 2 * TOK), 1) % TOK + i * TOK).astype(F32)
-            allowed = (key >= row_scr[2:3]) & (key <= query)
-            s = dot_nt(kk, q2_scr[...])
-            p = jnp.where(allowed, jnp.exp(s - row_scr[1:2]), 0.0)
-            dp = dot_nt(v_i[key_rows], do2_scr[...])
-            ds = (p * (dp - row_scr[0:1])).astype(BF)
-            dv[key_rows] += dot(p.astype(BF), do2_scr[...])
-            dk[key_rows] += dot(ds, q2_scr[...])
-            dq[...] += dot_tn(kk, ds)
-            return inner
-
-        lax.fori_loop(key_start(i), i + 1, keys, 0)
-        grad_q = merge_heads(jnp.transpose(dq[...])) * HEAD_DIM ** (-0.5)
-        grad_q = turn(grad_q.astype(BF).astype(F32), cos_ref[rows], -sin_ref[rows])
-        u_o[rows, :128] = grad_q
-        cq = column(lax.rsqrt(st[pl.ds(2 * i, 1)] * (1.0 / D) + EPSILON))
-        st_o[pl.ds(2 * i, 1)] = lane_row(grad_q * gain[:, :128] * lin[rows, :128] * cq)
-        return carry
-
-    lax.fori_loop(0, EP, queries, 0)
-
-    def close(b, carry):
-        rows = block_rows(b)
-        grad_k, grad_v = dk[rows], dv[rows]
-        grad_k = grad_k + pltpu.roll(grad_k, HEAD_DIM, 1)
-        grad_v = grad_v + pltpu.roll(grad_v, HEAD_DIM, 1)
-        both = jnp.where(first, grad_k, grad_v).astype(BF).astype(F32)
-        both = jnp.where(first, turn(both, cos_ref[rows], -sin_ref[rows]), both)
-        u_o[rows, 128:] = both
-        ck = column(lax.rsqrt(st[pl.ds(2 * b + 1, 1)] * (1.0 / KV) + EPSILON))
-        st_o[pl.ds(2 * b + 1, 1)] = lane_row(
-            jnp.where(first, both * gain[:, 128:] * lin[rows, 128:] * ck, 0.0)
-        )
-        return carry
-
-    lax.fori_loop(0, EP, close, 0)
-
-
-def attend_back(q, k, v, a, lse, lo, go, lin, st, cosine, sine, gain):
-    return pl.pallas_call(
-        attend_back_kernel,
-        out_shape=[shape((LENGTH, 256)), shape((2 * EP, 256))],
-        in_specs=[VM] * 12,
-        out_specs=[VM] * 2,
-        scratch_shapes=[
-            pltpu.VMEM((2 * TOK, 128), BF),
-            pltpu.VMEM((2 * TOK, 128), BF),
-            pltpu.VMEM((8, 2 * TOK), F32),
-            pltpu.VMEM((128, 2 * TOK), F32),
-            pltpu.VMEM((LENGTH, 128), F32),
-            pltpu.VMEM((LENGTH, 128), F32),
-        ],
-        compiler_params=pltpu.CompilerParams(vmem_limit_bytes=48 * MIB),
-        name="attend_back",
-    )(q, k, v, a, lse, lo, go, lin, st, cosine, sine, gain)
-
-
-def project_back_kernel(x_ref, u_ref, lin_ref, st, st2, gain, attn_gain, w_ref, gn_o, dw_o, ga_o, gqk_o, dwt):
-    i = pl.program_id(0)
-    first = iota((TOK, 128), 1) < HEAD_DIM
-
-    @pl.when(i == 0)
-    def _():
-        dwt[...] = jnp.zeros_like(dwt)
-        ga_o[...] = jnp.zeros_like(ga_o)
-        gqk_o[...] = jnp.zeros_like(gqk_o)
-
-    x = x_ref[...].astype(F32)
-    r1 = lax.rsqrt(jnp.mean(x * x, axis=1, keepdims=True) + EPSILON)
-    n1 = x * r1
-    normed = (n1 * attn_gain[...]).astype(BF)
-    u = u_ref[...]
-    lin = lin_ref[...]
-    cq = column(lax.rsqrt(st[pl.ds(2 * i, 1)] * (1.0 / D) + EPSILON))
-    ck = column(lax.rsqrt(st[pl.ds(2 * i + 1, 1)] * (1.0 / KV) + EPSILON))
-    mq = column(st2[pl.ds(2 * i, 1)] * (1.0 / D))
-    mk = column(st2[pl.ds(2 * i + 1, 1)] * (1.0 / KV))
-    nq = lin[:, :128] * cq
-    nk = lin[:, 128:] * ck
-    gq = cq * (u[:, :128] * gain[:, :128] - nq * mq)
-    gk = jnp.where(first, ck * (u[:, 128:] * gain[:, 128:] - nk * mk), u[:, 128:])
-    glin = jnp.concatenate([gq, gk], axis=1).astype(BF)
-    gqk_o[0:1] += jnp.concatenate(
-        [
-            jnp.sum(u[:, :128] * nq, axis=0, keepdims=True),
-            jnp.sum(u[:, 128:] * nk, axis=0, keepdims=True),
-        ],
-        axis=1,
-    )
-    gn = dot_nt(glin, w_ref[...])
-    ga_o[0:1] += jnp.sum(gn * n1, axis=0, keepdims=True)
-    gn_o[...] = gn.astype(BF)
-    dwt[...] += dot_tn(glin, normed)
-
-    @pl.when(i == EP - 1)
-    def _():
-        dw_o[...] = jnp.transpose(dwt[...])
-
-
-def project_back(x_all, u, lin, st, st2, gain, attn_gain, w):
-    def whole(dims):
-        return pl.BlockSpec(dims, lambda i: tuple(0 for _ in dims))
-
-    return pl.pallas_call(
-        project_back_kernel,
-        grid=(EP,),
-        out_shape=[shape((LENGTH, D), BF), shape((D, 256)), shape((8, D)), shape((8, 256))],
-        in_specs=[
-            pl.BlockSpec((TOK, D), lambda i: (i, 0)),
-            pl.BlockSpec((TOK, 256), lambda i: (i, 0)),
-            pl.BlockSpec((TOK, 256), lambda i: (i, 0)),
-            whole((16, 256)),
-            whole((16, 256)),
-            whole((1, 256)),
-            whole((1, D)),
-            whole((D, 256)),
-        ],
-        out_specs=[pl.BlockSpec((TOK, D), lambda i: (i, 0)), whole((D, 256)), whole((8, D)), whole((8, 256))],
-        scratch_shapes=[pltpu.VMEM((256, D), F32)],
-        compiler_params=pltpu.CompilerParams(vmem_limit_bytes=48 * MIB),
-        name="project_back",
-    )(x_all, u, lin, st, st2, gain, attn_gain, w)
-
-
 class ChipReduce:
     SEMS = 10
     STEP = 64
@@ -1023,8 +717,8 @@
 def experts_kernel(
     m_in, t_in, g_in, wg_in, wu_in, wd_in, out_o, gm_o, gg_o, eg_o,
     m_ref, tab, g_ref, wg, wu, wd, a_s, c_s, gl_s, up_s, act_s, dgu_s, y_s, gate_s, gg_s, ggt, eg,
-    swo, snd, pc1, rcv1, hop1, pc2, rcv2, hop2,
-    s_m, r_m, s_t, r_t, s_1, r_1, s_2, r_2, s_g, r_g, lsem, esem,
+    swo, snd, pc1, rcv1, hop1,
+    s_m, r_m, s_t, r_t, s_1, r_1, s_g, r_g, lsem, esem,
 ):
     e, x, c = place()
     others = ep_others(e)
@@ -1044,7 +738,6 @@
     for copy in loads:
         copy.start()
     red1 = ChipReduce(TOK, swo, snd, pc1, rcv1, hop1, (s_1, r_1))
-    red2 = ChipReduce(TOK, swo, snd, pc2, rcv2, hop2, (s_2, r_2))
 
     def hits(s, k):
         return iota((CAP, TOK), 0).astype(F32) == tab[s, pl.ds(e * LOCAL + k, 1)]
@@ -1190,19 +883,17 @@
 
     lax.fori_loop(0, LOCAL, backward, 0)
     gates = [remote(ggt.at[d], gg_o.at[e], (s_g, r_g), k, {"ep": d}) for k, d in enumerate(others)]
-    own = pltpu.make_async_copy(ggt.at[e], gg_o.at[e], lsem.at[1])
+    own = pltpu.make_async_copy(ggt.at[e], gg_o.at[e], lsem.at[8])
     for copy in gates + [own]:
         copy.start()
-    for slot, q in enumerate([(x + 2) % 4, (x + 3) % 4, (x + 1) % 4, x]):
-        swo[slot] = combine(q * 2 + 1 - c)
-        red2.swap(slot).start()
-        snd[slot] = combine(q * 2 + c)
-        if slot == 0:
-            red2.send_opp()
-    red2.send_near()
-    red2.merge(3)
-    red2.send_far()
-    red2.finish(gm_o)
+    spill = []
+    for k, q in enumerate([(x + 2) % 4, (x + 3) % 4, (x + 1) % 4, x]):
+        for core, buffer in ((1 - c, swo), (c, snd)):
+            buffer[k] = combine(q * 2 + core)
+            spill.append(pltpu.make_async_copy(buffer.at[k], gm_o.at[block_rows(q * 2 + core)], lsem.at[len(spill)]))
+            spill[-1].start()
+    for copy in spill:
+        copy.wait()
     own.wait()
     pltpu.make_async_copy(eg, eg_o.at[LOCAL - 1], esem).wait()
     for copy in gates:
@@ -1218,12 +909,12 @@
         4,
         [
             shape((TOK, D)),
-            shape((TOK, D)),
+            shape((LENGTH, D), BF),
             shape((EP, 8, TOK)),
             shape((LOCAL, REP, BLOCK, D), BF),
         ],
         [ANY] * 6,
-        [VM, VM, ANY, ANY],
+        [VM, ANY, ANY, ANY],
         [
             pltpu.VMEM((LENGTH, D), BF),
             pltpu.VMEM((EP, 2 * EXPERTS, TOK), F32),
@@ -1245,54 +936,368 @@
             pltpu.VMEM((4, TOK, D), BF),
             pltpu.VMEM((4, TOK, D), BF),
         ]
-        + [pltpu.VMEM((4, TOK, D), BF), pltpu.VMEM((2, TOK, D), BF), pltpu.VMEM((TOK, D), BF)] * 2
+        + [pltpu.VMEM((4, TOK, D), BF), pltpu.VMEM((2, TOK, D), BF), pltpu.VMEM((TOK, D), BF)]
         + [DMA((10,))] * 2
         + [DMA((7,))] * 2
-        + [DMA((10,))] * 4
+        + [DMA((10,))] * 2
         + [DMA((7,))] * 2
-        + [DMA((6,)), DMA(())],
+        + [DMA((9,)), DMA(())],
         limit=63,
     )(m, t, g_all, wg, wu, wd)
 
 
-def hidden_back_kernel(
-    hid, mixed, gmoe, gg, gate, m_ref, cot, gain, router, w_ref, a_ref, out_o, gh_o, ga_o, dwo_o, dr_o, gf_o
+def back_kernel(
+    gm_in, mixed_in, gg_in, tab_in, hid_in, m_in, cot_in, att_in, misc_in, rout_in, whole_in, wcol_in, x_in, lin_in,
+    q_in, k_in, v_in, a_in, lse_in, cos_in, sin_in,
+    out_o, ig_o, wb_o, dw_o, vec_o,
+    mixed, gg, tab, hid, m_s, cot, att, misc, rout, whole, wcol, x_s, lin, q_s, k_s, v_s, a_s, lse, cos_ref, sin_ref,
+    gm, gh, ga_s, go, q2_s, p_s, do2, row_s, dq, dk, dv, u_s, sums, st2, held, wb, wsum, wheld,
+    dwt, dws, dheld, dsum, vec, vheld, vtot, vheld2, swo, snd, pc1, rcv1, hop1, pc2, rcv2, hop2, snd3, pc3, rcv3, hop3,
+    s_1, r_1, s_2, r_2, s_3, r_3, s_go, r_go, s_st, r_st, s_w, r_w, s_d, r_d, s_e, r_e, s_v, r_v, s_v2, r_v2, lsem, l_1, l_3,
 ):
+    r = lax.axis_index("rep")
+    e, x, c = place()
+    others = ep_others(e)
+    copies = rep_others(r)
+    first = iota((TOK, 128), 1) < HEAD_DIM
+    gain_a, gain_f, gain = misc.at[0:1], misc.at[1:2], misc.at[2:3, 0:256]
+    lo, st = misc.at[8:16, 0:256], misc.at[16:32, 0:256]
+    greet([{"ep": d} for d in others] + [{"rep": d} for d in copies])
+    red1 = RingReduce(gm_in, TOK, pc1, snd, rcv1, hop1, (s_1, r_1), l_1)
+    red2 = ChipReduce(TOK, swo, snd, pc2, rcv2, hop2, (s_2, r_2))
+    red3 = RingReduce(wb, 128, pc3, snd3, rcv3, hop3, (s_3, r_3), l_3)
+    red1.start()
+    loads = [
+        pltpu.make_async_copy(src, dst, lsem.at[k])
+        for k, (src, dst) in enumerate(
+            [
+                (q_in, q_s), (k_in, k_s), (misc_in, misc), (lse_in, lse), (mixed_in, mixed), (gg_in, gg),
+                (tab_in, tab), (hid_in, hid), (m_in, m_s), (cot_in, cot), (att_in, att), (rout_in, rout),
+                (whole_in, whole), (v_in, v_s), (a_in, a_s), (cos_in, cos_ref), (sin_in, sin_ref),
+                (lin_in, lin), (x_in, x_s), (wcol_in, wcol),
+            ]
+        )
+    ]
+    for copy in loads:
+        copy.start()
+    for copy in loads[:4]:
+        copy.wait()
+
+    def tile(i, j):
+        cut = jnp.minimum(i, 4)
+        return cut * (cut + 1) // 2 + 5 * jnp.maximum(i - 4, 0) + j - key_start(i)
+
+    def probabilities(i, carry):
+        q2_s[i] = stack_heads(q_s[block_rows(i)].astype(F32) * HEAD_DIM ** (-0.5)).astype(BF)
+        row_s[1:2] = lse[i][0:1]
+        row_s[2:3] = jnp.concatenate([lo[pl.ds(i, 1)]] * 2, axis=1)
+
+        def keys(j, inner):
+            key = (iota((TOK, 2 * TOK), 0) + j * TOK).astype(F32)
+            query = (iota((TOK, 2 * TOK), 1) % TOK + i * TOK).astype(F32)
+            allowed = (key >= row_s[2:3]) & (key <= query)
+            s = dot_nt(k_s[block_rows(j)], q2_s[i])
+            p_s[tile(i, j)] = jnp.where(allowed, jnp.exp(s - row_s[1:2]), 0.0).astype(BF)
+            return inner
+
+        lax.fori_loop(key_start(i), i + 1, keys, 0)
+
+        @pl.when(i == 1)
+        def _():
+            red1.push_opp()
+
+        @pl.when(i == 3)
+        def _():
+            red1.push_near()
+
+        @pl.when(i == 5)
+        def _():
+            red1.relay()
+
+        return carry
+
+    lax.fori_loop(0, EP, probabilities, 0)
+    for copy in loads[4:]:
+        copy.wait()
+    red1.finish(gm)
+
     hidden = hid[...]
-    out_o[...] = (hidden + mixed[...]).astype(BF)
-    weights = gate[...]
-    grads = gg[...]
+    weights = tab[EXPERTS:]
+    grads = jnp.concatenate([gg[d][:LOCAL] for d in range(EP)], axis=0)
     mean = jnp.sum(weights * grads, axis=0, keepdims=True)
-    grad_logits = (weights * (grads - mean)).astype(BF)
-    dr_o[...] = dot(grad_logits, m_ref[...])
-    grad_moe = gmoe[...] + dot_tn(grad_logits, router[...])
+    grad_logits = weights * (grads - mean)
+    grad_moe = gm[...] + dot_tn(grad_logits.astype(BF), rout[...])
     r2 = lax.rsqrt(jnp.mean(hidden * hidden, axis=1, keepdims=True) + EPSILON)
     n = hidden * r2
-    gf_o[...] = jnp.sum(grad_moe * n, axis=0, keepdims=True)
-    u = grad_moe * gain[...]
+    u = grad_moe * gain_f[...]
     grad_hidden = cot[...].astype(F32) + r2 * (u - n * jnp.mean(u * n, axis=1, keepdims=True))
-    gh_o[...] = grad_hidden
+    gh[...] = grad_hidden
     branch = grad_hidden.astype(BF)
-    ga_o[...] = dot_nt(branch, w_ref[...]).astype(BF)
-    dwo_o[...] = dot_tn(a_ref[...], branch).astype(BF)
-
-
-def hidden_back(hid, mixed, grad_moe, gg, gate, m, cot, gain, router, w, a):
-    return pl.pallas_call(
-        hidden_back_kernel,
-        out_shape=[
-            shape((TOK, D), BF),
-            shape((TOK, D)),
-            shape((TOK, D), BF),
-            shape((D, D), BF),
-            shape((EXPERTS, D)),
-            shape((1, D)),
-        ],
-        in_specs=[VM] * 11,
-        out_specs=[VM] * 6,
-        compiler_params=pltpu.CompilerParams(vmem_limit_bytes=48 * MIB),
-        name="hidden_back",
-    )(hid, mixed, grad_moe, gg, gate, m, cot, gain, router, w, a)
+    ga_s[...] = dot_nt(branch, whole[...]).astype(BF)
+
+    def own_cols(ref, b):
+        return ref.at[:, pl.ds(pl.multiple_of(b * 128, 128), 128)]
+
+    heads = [
+        remote(own_cols(ga_s, d), go.at[block_rows(e)], (s_go, r_go), k, {"ep": d}) for k, d in enumerate(others)
+    ]
+    for copy in heads:
+        copy.start()
+    go[block_rows(e)] = own_cols(ga_s, e)[...]
+    out_o[...] = (hidden + mixed[...]).astype(BF)
+    ffn = jnp.sum(grad_moe * n, axis=0, keepdims=True)
+    logit_rows = jnp.transpose(jnp.concatenate([grad_logits, jnp.zeros((96, TOK), F32)], axis=0)).astype(BF)
+    router_rows = dot_tn(m_s[...], logit_rows)
+    lane = iota((D, 128), 1)
+    router_rows = jnp.where(lane == EXPERTS, column(ffn), router_rows).reshape(REP, EP, 8, 128)
+    out_rows = dot_tn(att[...], branch).reshape(REP, EP, 8, D)
+    for d in range(EP):
+        wb[d * 128 : (d + 1) * 128, :D] = out_rows[:, d].reshape(128, D).astype(BF)
+        wb[d * 128 : (d + 1) * 128, D:] = router_rows[:, d].reshape(128, 128).astype(BF)
+    red3.start()
+    dk[...] = jnp.zeros((LENGTH, 128), F32)
+    dv[...] = jnp.zeros((LENGTH, 128), F32)
+    for copy in heads:
+        copy.wait_recv()
+
+    def part(ref, b, size):
+        return ref.at[pl.ds(pl.multiple_of(b * size, 8), size)]
+
+    spread_w = [remote(part(wsum, d, 8), wheld.at[r], (s_w, r_w), k, {"rep": d}) for k, d in enumerate(copies)]
+
+    def queries(i, carry):
+        rows = block_rows(i)
+        grad = stack_heads(go[rows].astype(F32))
+        do2[...] = grad.astype(BF)
+        out = a_s[rows].astype(F32)
+        row_s[0:1] = lane_row(grad * jnp.concatenate([out, out], axis=0))
+        dq[...] = jnp.zeros((128, 2 * TOK), F32)
+
+        def keys(j, inner):
+            key_rows = block_rows(j)
+            p = p_s[tile(i, j)]
+            dp = dot_nt(v_s[key_rows], do2[...])
+            ds = (p.astype(F32) * (dp - row_s[0:1])).astype(BF)
+            dv[key_rows] += dot(p, do2[...])
+            dk[key_rows] += dot(ds, q2_s[i])
+            dq[...] += dot_tn(k_s[key_rows], ds)
+            return inner
+
+        lax.fori_loop(key_start(i), i + 1, keys, 0)
+        grad_q = merge_heads(jnp.transpose(dq[...])) * HEAD_DIM ** (-0.5)
+        grad_q = turn(grad_q.astype(BF).astype(F32), cos_ref[rows], -sin_ref[rows])
+        u_s[rows, :128] = grad_q
+        cq = column(lax.rsqrt(st[pl.ds(2 * i, 1)] * (1.0 / D) + EPSILON))
+        sums[pl.ds(2 * i, 1)] = lane_row(grad_q * gain[:, :128] * lin[rows, :128] * cq)
+
+        @pl.when(i == 2)
+        def _():
+            red3.push_opp()
+            red3.push_near()
+
+        @pl.when(i == 4)
+        def _():
+            red3.relay()
+
+        @pl.when(i == 6)
+        def _():
+            red3.finish(wsum)
+            for copy in spread_w:
+                copy.start()
+            wheld[r] = part(wsum, r, 8)[...]
+
+        return carry
+
+    lax.fori_loop(0, EP, queries, 0)
+
+    def close(b, carry):
+        rows = block_rows(b)
+        grad_k, grad_v = dk[rows], dv[rows]
+        grad_k = grad_k + pltpu.roll(grad_k, HEAD_DIM, 1)
+        grad_v = grad_v + pltpu.roll(grad_v, HEAD_DIM, 1)
+        both = jnp.where(first, grad_k, grad_v).astype(BF).astype(F32)
+        both = jnp.where(first, turn(both, cos_ref[rows], -sin_ref[rows]), both)
+        u_s[rows, 128:] = both
+        ck = column(lax.rsqrt(st[pl.ds(2 * b + 1, 1)] * (1.0 / KV) + EPSILON))
+        sums[pl.ds(2 * b + 1, 1)] = lane_row(jnp.where(first, both * gain[:, 128:] * lin[rows, 128:] * ck, 0.0))
+        return carry
+
+    lax.fori_loop(0, EP, close, 0)
+    stats = [remote(sums, held.at[e], (s_st, r_st), k, {"ep": d}) for k, d in enumerate(others)]
+    for copy in stats:
+        copy.start()
+    held[e] = sums[...]
+    dwt[...] = jnp.zeros((256, D), F32)
+    vec[...] = jnp.zeros((8, D), F32)
+    for copy in stats:
+        copy.wait_recv()
+    total = held[0]
+    for k in range(1, EP):
+        total = total + held[k]
+    st2[...] = total
+
+    def project_back(b):
+        rows = block_rows(b)
+        values = x_s[rows].astype(F32)
+        r1 = lax.rsqrt(jnp.mean(values * values, axis=1, keepdims=True) + EPSILON)
+        n1 = values * r1
+        normed = (n1 * gain_a[...]).astype(BF)
+        cq = column(lax.rsqrt(st[pl.ds(2 * b, 1)] * (1.0 / D) + EPSILON))
+        ck = column(lax.rsqrt(st[pl.ds(2 * b + 1, 1)] * (1.0 / KV) + EPSILON))
+        mq = column(st2[pl.ds(2 * b, 1)] * (1.0 / D))
+        mk = column(st2[pl.ds(2 * b + 1, 1)] * (1.0 / KV))
+        uq, uk = u_s[rows, :128], u_s[rows, 128:]
+        nq = lin[rows, :128] * cq
+        nk = lin[rows, 128:] * ck
+        gq = cq * (uq * gain[:, :128] - nq * mq)
+        gk = jnp.where(first, ck * (uk * gain[:, 128:] - nk * mk), uk)
+        glin = jnp.concatenate([gq, gk], axis=1).astype(BF)
+        vec[1:2, :128] += jnp.sum(uq * nq, axis=0, keepdims=True)
+        vec[2:3, :128] += jnp.sum(uk * nk, axis=0, keepdims=True)
+        gn = dot_nt(glin, wcol[...])
+        vec[0:1] += jnp.sum(gn * n1, axis=0, keepdims=True)
+        dwt[...] += dot_tn(glin, normed)
+        return gn.astype(BF)
+
+    def chips(k, carry):
+        q = (x + 2 + k - (k // 2) * (2 * k - 1)) % 4
+        swo[k] = project_back(q * 2 + 1 - c)
+        red2.swap(k).start()
+        snd[k] = project_back(q * 2 + c)
+
+        @pl.when(k == 1)
+        def _():
+            red2.send_opp()
+
+        @pl.when(k == 2)
+        def _():
+            red2.send_near()
+
+        return carry
+
+    lax.fori_loop(0, 4, chips, 0)
+    dws[...] = jnp.transpose(dwt[...])
+    spread_d = [remote(part(dws, d, 64), dheld.at[r], (s_d, r_d), k, {"rep": d}) for k, d in enumerate(copies)]
+    for copy in spread_d:
+        copy.start()
+    dheld[r] = part(dws, r, 64)[...]
+    gain_q, gain_k = vec[1:2, :128], jnp.where(iota((1, 128), 1) < HEAD_DIM, vec[2:3, :128], 0.0)
+    gain_k = jnp.where(e % 2 == 1, pltpu.roll(gain_k, HEAD_DIM, 1), gain_k)
+    vec[1:3, :128] = jnp.zeros((2, 128), F32)
+    vec[1:2, pl.ds(pl.multiple_of(e * 128, 128), 128)] = gain_q
+    vec[2:3, pl.ds(pl.multiple_of(e // 2 * 128, 128), 128)] = gain_k
+    spread_v = [remote(vec, vheld.at[e], (s_v, r_v), k, {"ep": d}) for k, d in enumerate(others)]
+    for copy in spread_v:
+        copy.start()
+    vheld[e] = vec[...]
+    red2.merge(3)
+    for copy in spread_v:
+        copy.wait_recv()
+    total = vheld[0]
+    for k in range(1, EP):
+        total = total + vheld[k]
+    vtot[...] = total
+    spread_v2 = [remote(vtot, vheld2.at[r], (s_v2, r_v2), k, {"rep": d}) for k, d in enumerate(copies)]
+    for copy in spread_v2:
+        copy.start()
+    vheld2[r] = vtot[...]
+    red2.send_far()
+    for copy in spread_w:
+        copy.wait_recv()
+    total = wheld[0]
+    for k in range(1, REP):
+        total = total + wheld[k]
+    wb_o[...] = total
+    for copy in spread_d:
+        copy.wait_recv()
+    total = dheld[0]
+    for k in range(1, REP):
+        total = total + dheld[k]
+    dsum[...] = total
+    spread_e = [remote(part(dsum, d, 8), dw_o.at[e], (s_e, r_e), k, {"ep": d}) for k, d in enumerate(others)]
+    for copy in spread_e:
+        copy.start()
+    dw_o[e] = part(dsum, e, 8)[...]
+    for copy in spread_v2:
+        copy.wait_recv()
+    total = vheld2[0]
+    for k in range(1, REP):
+        total = total + vheld2[k]
+    start = r * EP + e
+    rows_d, lanes_d = iota((D, 128), 0), iota((D, 128), 1)
+    eight = jnp.where((rows_d == start * 8 + lanes_d) & (lanes_d < 8), 1.0, 0.0)
+    four = jnp.where((rows_d == start * 4 + lanes_d) & (lanes_d < 4), 1.0, 0.0)
+
+    def pick(sel):
+        return jnp.dot(total, sel, preferred_element_type=F32, precision=HIGH)
+
+    vec_o[...] = jnp.where(iota((8, 128), 0) == 2, pick(four), pick(eight))
+    red2.finish(gm)
+    values = x_s[block_rows(e)].astype(F32)
+    r1 = lax.rsqrt(jnp.mean(values * values, axis=1, keepdims=True) + EPSILON)
+    n1 = values * r1
+    z = gm[...] * gain_a[...]
+    ig_o[...] = gh[...] + r1 * (z - n1 * jnp.mean(z * n1, axis=1, keepdims=True))
+    for copy in spread_e:
+        copy.wait_recv()
+    for copy in heads + stats + spread_w + spread_d + spread_e + spread_v + spread_v2:
+        copy.wait_send()
+
+
+def back(*args):
+    def vm(dims, dtype=F32):
+        return pltpu.VMEM(dims, dtype)
+
+    held = [vm(a.shape, a.dtype) for a in args[1:12]] + [vm(args[12].shape, BF)] + [vm(a.shape, a.dtype) for a in args[13:]]
+    landing = [vm((4, TOK, D), BF), vm((2, TOK, D), BF), vm((TOK, D), BF)]
+    return comm_call(
+        back_kernel,
+        "back",
+        6,
+        [shape((TOK, D), BF), shape((TOK, D)), shape((8, WB)), shape((EP, 8, 256)), shape((8, 128))],
+        [ANY] * 21,
+        [VM] * 5,
+        held
+        + [
+            vm((TOK, D)),
+            vm((TOK, D)),
+            vm((TOK, D), BF),
+            vm((LENGTH, 128), BF),
+            vm((EP, 2 * TOK, 128), BF),
+            vm((30, TOK, 2 * TOK), BF),
+            vm((2 * TOK, 128), BF),
+            vm((8, 2 * TOK)),
+            vm((128, 2 * TOK)),
+            vm((LENGTH, 128)),
+            vm((LENGTH, 128)),
+            vm((LENGTH, 256)),
+            vm((16, 256)),
+            vm((16, 256)),
+            vm((EP, 16, 256)),
+            vm((D, WB), BF),
+            vm((128, WB)),
+            vm((REP, 8, WB)),
+            vm((256, D)),
+            vm((D, 256)),
+            vm((REP, 64, 256)),
+            vm((64, 256)),
+            vm((8, D)),
+            vm((EP, 8, D)),
+            vm((8, D)),
+            vm((REP, 8, D)),
+            vm((4, TOK, D), BF),
+            vm((4, TOK, D), BF),
+        ]
+        + landing * 2
+        + [vm((4, 128, WB), BF), vm((4, 128, WB), BF), vm((2, 128, WB), BF), vm((128, WB), BF)]
+        + [DMA((10,))] * 6
+        + [DMA((7,))] * 4
+        + [DMA((15,))] * 4
+        + [DMA((7,))] * 4
+        + [DMA((15,))] * 2
+        + [DMA((20,)), DMA((4,)), DMA((4,))],
+        limit=63,
+    )(*args)
 
 
 def body(
@@ -1313,45 +1318,23 @@
     w_down,
     out_grad,
 ):
-    e = lax.axis_index("ep")
     gains = jnp.concatenate([gain_attn, gain_query, gain_key, gain_ffn]).reshape(1, 28)
     small = jnp.concatenate(
         [jnp.pad(w_router, ((0, 0), (0, 128 - EXPERTS))), jnp.pad(gains, ((0, 7), (0, 100)))], axis=0
     )
     cosine, sine = turn_tables()
     (
-        x_all, g_all, lin, st, lo, q, k, v, att, lse, hidden, moe_in, tables, attended,
-        attn_gain, ffn_gain, qk_gain, router, whole_out, w_cols,
+        x_all, g_all, lin, q, k, v, att, lse, hidden, moe_in, tables, attended, misc, router, whole_out, w_cols,
     ) = front(
         tokens, out_grad, w_query, w_key, w_value, w_out, small, segments.reshape(EP, TOK), routes.T, cosine, sine
     )
-    gates = tables[EXPERTS:]
-    mixed, grad_moe, gg, grads = experts(moe_in, tables, g_all, w_gate, w_up, w_down)
+    mixed, grad_rows, gg, grads = experts(moe_in, tables, g_all, w_gate, w_up, w_down)
     grads = grads.reshape(LOCAL, REP * BLOCK, D)
     expert_sums = lax.psum_scatter(grads, "rep", scatter_dimension=1, tiled=True).astype(F32)
-    gg = gg[:, :LOCAL].reshape(EXPERTS, TOK)
-    attended_t = attended.reshape(TOK, REP, EP, 8).transpose(0, 2, 1, 3).reshape(TOK, D)
-    output, grad_hidden, grad_att, dwo, drouter, dffn = hidden_back(
-        hidden, mixed, grad_moe, gg, gates, moe_in, out_grad, ffn_gain, router, whole_out, attended_t
+    output, input_grad, wb_sum, dw_sum, vec = back(
+        grad_rows, mixed, gg, tables, hidden, moe_in, out_grad, attended, misc, router, whole_out, w_cols, x_all, lin,
+        q, k, v, att, lse, cosine, sine,
     )
-    go = swap_heads(grad_att, False, "swap_heads_back", 7)
-    u, sums2 = attend_back(q, k, v, att, lse, lo, go, lin, st, cosine, sine, qk_gain)
-    st2 = sum_stats(sums2, "sum_stats_back", 8)
-    gn, dw, dattn, dqk = project_back(x_all, u, lin, st, st2, qk_gain, attn_gain, w_cols)
-
-    dquery = lax.dynamic_update_slice(jnp.zeros((1, D), F32), dqk[0:1, :128], (0, e * 128))
-    dkey = lax.dynamic_update_slice(jnp.zeros((1, KV), F32), dqk[0:1, 128:192], (0, e * 64))
-    dkey = jnp.pad(dkey.reshape(128, 4), ((0, 0), (0, 4))).reshape(1, D)
-    vectors = jnp.concatenate([drouter, dattn[0:1], dquery, dkey, dffn], axis=0)
-    vectors = vectors.reshape(36, REP, EP, 8).transpose(2, 1, 3, 0).reshape(D, 36)
-    wb = jnp.concatenate([dwo, jnp.pad(vectors, ((0, 0), (0, 128 - 36))).astype(BF)], axis=1)
-    gn_sum, wb_sum, dw_sum = reduce_last(gn, wb, dw)
-
-    x = tokens.astype(F32)
-    r1 = lax.rsqrt(jnp.mean(x * x, axis=-1, keepdims=True) + EPSILON)
-    n1 = x * r1
-    z = gn_sum * attn_gain
-    input_grad = grad_hidden + r1 * (z - n1 * jnp.mean(z * n1, axis=-1, keepdims=True))
     dw_rows = dw_sum.transpose(1, 0, 2)
     return (
         output,
@@ -1361,10 +1344,10 @@
         dw_rows[:, :, 192:].reshape(8, KV),
         wb_sum[:, :D],
         wb_sum[:, D : D + EXPERTS],
-        wb_sum[:, D + 32],
-        wb_sum[:, D + 33],
-        wb_sum[:4, D + 34],
-        wb_sum[:, D + 35],
+        vec[0, :8],
+        vec[1, :8],
+        vec[2, :4],
+        wb_sum[:, D + EXPERTS],
         expert_sums[:, :64, :FF],
         expert_sums[:, :64, FF:],
         expert_sums[:, 64:],

time: 348 us -> 308 us (0.89)
  Pallas kernels: 290 us -> 271 us
  local copies, waits for them, and re-layouts: 33.2 us -> 18.1 us
  other arithmetic: 8.55 us -> 3.43 us
    pallas_call x7 -> x2, Pallas kernels: 210 us -> 191 us  [the longest x1 96.5 us: back(): comm_call(back_kernel, 'back', 6, [shape((TOK, D), BF), shape((TOK, D)),...]
    unnamed x57 -> x5, local copies, waits for them, and re-layouts: 13.9 us -> 3.35 us
    concatenate x6 -> x0, local copies, waits for them, and re-layouts: 7.31 us -> none  [body(): vectors = jnp.concatenate([drouter, dattn[0:1], dquery, dkey, dffn], axis=0)]
  transfers between devices with their start and end apart: 1 -> 1, of which waited for: 0 -> 0; matrix products, arithmetic and copies ran while one was open for 6% -> 3% of each run, Pallas kernels for 28% -> 31%
where the time goes in v4:
time: 308 us; the launch traced here: 307 us
  Pallas kernels  271 us (88%)
  local copies, waits for them, and re-layouts  18.1 us (6%)
  between operations  14.1 us (5%)
  other arithmetic  3.43 us (1%)
    pallas_call x1, Pallas kernels, back(): comm_call(back_kernel, 'back', 6, [shape((TOK, D), BF), shape((TOK, D)),...  96.5 us
    pallas_call x1, Pallas kernels, experts(): comm_call(experts_kernel, 'experts', 4, [shape((TOK, D)), shape((LENGTH,...  94.4 us
    pallas_call x1, Pallas kernels, front(): comm_call(front_kernel, 'front', 1, [shape((LENGTH, D), BF), shape((LENGT...  80.5 us
  transfers between devices with their start and end apart: 1, of which 0 were waited for; matrix products, arithmetic and copies ran while one was open for 3% of the time, Pallas kernels for 31%

profile of v4, /device:TPU:1, one launch (start us, length us, event | category | flops | bytes accessed | tf_op | source)
XLA Modules:
  0.0 307.1 jit_solution(1623227598459280964)
XLA Ops:
  7.2 0.0 reduce-scatter.2.cloned.1.call-start
  7.2 0.5 broadcast.14
  7.7 1.4 reduce.5
  9.1 0.6 reshape.47.seg
  9.7 0.8 maximum_bitcast_fusion
  10.5 1.3 fusion.2.small
  11.8 80.5 %front.1 = (bf16[2048,1024]{1,0:T(8,128)(2,1)}, bf16[2048,1024]{1,0:T(8,128)(2,1)}, f32[2048,256]{1,0:T(8,128)}, bf16[2048,128]{1,0:T(8,128)(2,1)}, bf16[2048,12...) custom-call(bf16[256,1024]{1,0:T(8,128)(2,1)} %tok.1, ...), custom_call_target="tpu_custom_call" | custom-call | tf_op jit(solution)/shard_map/front/pallas_call | solution.py:579
  92.3 94.4 %experts.1 = (f32[256,1024]{1,0:T(8,128)}, bf16[2048,1024]{1,0:T(8,128)(2,1)}, f32[8,8,256]{2,1,0:T(8,128)}, bf16[4,16,96,1024]{3,2,1,0:T(8,128)(2,1)}) custom-call(bf16[256,1024]{1,0:T(8,128)(2,1)} %get-tuple-element.39.m_in, f32[64,256]{1,0:T(8,128)} %get-tuple-element.40.t_in.tab_in, bf16[2048,1024]{1,0:T(8,128)(2,1)} %get-tuple-element.41.g_in, ...), custom_call_target="tpu_custom_call" | custom-call | tf_op jit(solution)/shard_map/experts/pallas_call | solution.py:906
  186.7 0.0 reduce-scatter.2.cloned.1.call-update
  186.7 96.5 %back.1 = (bf16[256,1024]{1,0:T(8,128)(2,1)}, f32[256,1024]{1,0:T(8,128)}, f32[8,1152]{1,0:T(8,128)}, f32[8,8,256]{2,1,0:T(8,128)}, f32[8,128]{1,0:T(8,128)}) custom-call(bf16[2048,1024]{1,0:T(8,128)(2,1)} %get-tuple-element.42.gm_in, f32[256,1024]{1,0:T(8,128)} %get-tuple-element.43.mixed_in, f32[8,8,256]{2,1,0:T(8,128)} %get-tuple-element.44.gg_in, ...), custom_call_target="tpu_custom_call" | custom-call | tf_op jit(solution)/shard_map/back/pallas_call | solution.py:1253
  283.3 0.0 copy-start
  283.3 1.4 slice.40
  284.6 1.4 slice.39
  286.0 0.9 fusion.4
  286.9 0.7 reshape.50
  287.6 0.7 reshape.49
  288.3 1.4 slice_reduce_fusion
  289.7 1.2 slice_bitcast_fusion.1
  290.9 1.3 slice_bitcast_fusion.2
  292.1 1.4 slice_bitcast_fusion
  293.5 0.0 reduce-scatter.2.cloned.1.call-done
  293.5 1.8 slice.53
  295.3 2.1 fusion.3
  297.4 1.9 copy.36
  299.3 0.0 copy-done
  299.3 1.0 copy.37
  (2 shorter events, 0.0 us)
Async XLA Ops:
  7.2 286.3 %reduce-scatter.2.cloned.1.call-start = ((), (), s32[]{:S(2)}) async-start(), calls=%async_computation.1 | async-start | bytes 13369344 | tf_op jit(solution)/shard_map/reduce_scatter | solution.py:1333
  283.3 16.0 %copy-start = (f32[256,1024]{1,0:T(8,128)S(1)}, f32[256,1024]{1,0:T(8,128)}, u32[]{:S(2)}) copy-start(f32[256,1024]{1,0:T(8,128)} %get-tuple-element.85) | copy-start | bytes 3145732
Sparse Core Ops, SparseCore 0:
  186.8 104.8 reduce-scatter.1

commit v5 on v4

v5 whole, which is shorter than its diff:
```python
import functools

import jax
import jax.numpy as jnp
import numpy as np
from jax import lax
from jax.experimental import pallas as pl
from jax.experimental.pallas import tpu as pltpu
from jax.sharding import PartitionSpec as P

BF = jnp.bfloat16
F32 = jnp.float32
MESH = pl.DeviceIdType.MESH
ANY = pl.BlockSpec(memory_space=pl.ANY)
VM = pl.BlockSpec(memory_space=pltpu.VMEM)
DMA = pltpu.SemaphoreType.DMA
MIB = 1 << 20

HEADS = 16
KV_HEADS = 8
HEAD_DIM = 64
TOP = 8
WINDOW = 1024
EPSILON = 1e-06
ROPE_BASE = 10000.0
MASKED = -1e30
EP = 8
REP = 16
TOK = 256
LENGTH = 2048
D = 1024
KV = 512
FF = 512
EXPERTS = 32
LOCAL = 4
CAP = 88
NT = (((1,), (1,)), ((), ()))
TN = (((0,), (0,)), ((), ()))
HIGH = lax.Precision.HIGHEST


def dot(a, b):
    return jnp.dot(a, b, preferred_element_type=F32)


def dot_nt(a, b, precision=None):
    return lax.dot_general(a, b, NT, preferred_element_type=F32, precision=precision)


def dot_tn(a, b):
    return lax.dot_general(a, b, TN, preferred_element_type=F32)


def iota(shape, dim):
    return lax.broadcasted_iota(jnp.int32, shape, dim)


def ep_device(x, c):
    return {"ep": x * 2 + c}


def greet(devices):
    barrier = pltpu.get_barrier_semaphore()
    for device in devices:
        pl.semaphore_signal(barrier, inc=1, device_id=device, device_id_type=MESH)
    pl.semaphore_wait(barrier, len(devices))


def remote(src, dst, sems, i, device):
    return pltpu.make_async_remote_copy(
        src_ref=src,
        dst_ref=dst,
        send_sem=sems[0].at[i],
        recv_sem=sems[1].at[i],
        device_id=device,
        device_id_type=MESH,
    )


def place():
    e = lax.axis_index("ep")
    return e, e // 2, e % 2


def ep_others(e):
    return [(e + k) % EP for k in range(1, EP)]


def rep_others(r):
    return [(r + k) % REP for k in range(1, REP)]


class RingGather:
    SEMS = 10

    def __init__(self, x_ref, o_ref, sems, lsem):
        e, x, c = place()
        self.n = n = x_ref.shape[0]
        h = n // 2
        self.o_ref = o_ref
        right, left = ep_device((x + 1) % 4, c), ep_device((x + 3) % 4, c)
        peer = ep_device(x, 1 - c)
        b_left, b_right, b_opp = (((x + 3) % 4) * 2 + c, ((x + 1) % 4) * 2 + c, ((x + 2) % 4) * 2 + c)

        def rows(b, off=0, size=n):
            return o_ref.at[pl.ds(pl.multiple_of(b * n + off, 16), size)]

        low, high = x_ref.at[pl.ds(0, h)], x_ref.at[pl.ds(h, h)]
        self.first = [
            remote(low, rows(e, 0, h), sems, 0, right),
            remote(high, rows(e, h, h), sems, 2, left),
            remote(high, rows(e, h, h), sems, 1, right),
            remote(low, rows(e, 0, h), sems, 3, left),
            remote(x_ref, rows(e), sems, 4, peer),
        ]
        self.fwd_right = remote(rows(b_left, 0, h), rows(b_left, 0, h), sems, 5, right)
        self.fwd_left = remote(rows(b_right, h, h), rows(b_right, h, h), sems, 6, left)
        self.to_peer = [
            remote(rows(b_left), rows(b_left), sems, 7, peer),
            remote(rows(b_right), rows(b_right), sems, 8, peer),
            remote(rows(b_opp), rows(b_opp), sems, 9, peer),
        ]
        self.own = pltpu.make_async_copy(x_ref, rows(e), lsem)

    def start(self):
        for copy in self.first:
            copy.start()
        self.own.start()

    def forward_half(self):
        self.first[0].wait_recv()
        self.fwd_right.start()
        self.first[1].wait_recv()
        self.fwd_left.start()

    def forward_rest(self):
        self.first[2].wait_recv()
        self.to_peer[0].start()
        self.first[3].wait_recv()
        self.to_peer[1].start()

    def finish(self):
        self.fwd_right.wait_recv()
        self.fwd_left.wait_recv()
        self.to_peer[2].start()
        self.first[4].wait_recv()
        for copy in self.to_peer:
            copy.wait_recv()
        self.own.wait()
        for copy in self.first + [self.fwd_right, self.fwd_left] + self.to_peer:
            copy.wait_send()


class RingReduce:
    SEMS = 10
    STEP = 64

    def __init__(self, p_ref, n, pc, snd, rcv, hop, sems, lsems):
        e, x, c = place()
        self.n, self.h = n, n // 2
        h = n // 2
        self.pc, self.snd, self.rcv, self.hop = pc, snd, rcv, hop
        right, left = ep_device((x + 1) % 4, c), ep_device((x + 3) % 4, c)
        peer = ep_device(x, 1 - c)

        def rows(b):
            return p_ref.at[pl.ds(pl.multiple_of(b * n, 16), n)]

        chips = [(x + 2) % 4, (x + 1) % 4, (x + 3) % 4, x]
        self.swap = [remote(rows(b * 2 + 1 - c), pc.at[k], sems, k, peer) for k, b in enumerate(chips)]
        self.load = [
            pltpu.make_async_copy(rows(b * 2 + c), snd.at[k], lsems.at[k]) for k, b in enumerate(chips)
        ]
        low, high = pl.ds(0, h), pl.ds(h, h)
        self.opp = [
            remote(snd.at[0, low], hop.at[low], sems, 4, right),
            remote(snd.at[0, high], hop.at[high], sems, 5, left),
        ]
        self.near = [
            remote(snd.at[1, high], rcv.at[0, high], sems, 6, right),
            remote(snd.at[2, low], rcv.at[1, low], sems, 7, left),
        ]
        self.far = [
            remote(snd.at[1, low], rcv.at[0, low], sems, 8, right),
            remote(snd.at[2, high], rcv.at[1, high], sems, 9, left),
        ]

    def rows_loop(self, low, count, body):
        step = self.STEP

        def loop(i, carry):
            body(pl.ds(pl.multiple_of(low + i * step, 16), step))
            return carry

        lax.fori_loop(0, count // step, loop, 0)

    def merge(self, k):
        def body(s):
            self.snd[k, s] = (self.snd[k, s].astype(F32) + self.pc[k, s].astype(F32)).astype(BF)

        self.load[k].wait()
        self.swap[k].wait_recv()
        self.rows_loop(0, self.n, body)

    def merge_hop(self, k, low):
        def body(s):
            self.snd[k, s] = (self.snd[k, s].astype(F32) + self.hop[s].astype(F32)).astype(BF)

        self.rows_loop(low, self.h, body)

    def start(self):
        for copy in self.swap + self.load:
            copy.start()

    def push_opp(self):
        self.merge(0)
        for copy in self.opp:
            copy.start()

    def push_near(self):
        self.merge(1)
        self.near[0].start()
        self.merge(2)
        self.near[1].start()
        self.merge(3)

    def relay(self):
        self.opp[0].wait_recv()
        self.merge_hop(1, 0)
        self.far[0].start()
        self.opp[1].wait_recv()
        self.merge_hop(2, self.h)
        self.far[1].start()

    def finish(self, out_ref):
        for copy in self.near + self.far:
            copy.wait_recv()

        def body(s):
            out_ref[s] = self.snd[3, s].astype(F32) + (
                self.rcv[0, s].astype(F32) + self.rcv[1, s].astype(F32)
            )

        self.rows_loop(0, self.n, body)
        for copy in self.swap + self.opp + self.near + self.far:
            copy.wait_send()


class AxisReduce:
    def __init__(self, devices, snd, hop, rcv, sems, base):
        right, left = devices
        self.snd, self.hop, self.rcv = snd, hop, rcv
        self.opp = [
            remote(snd.at[0, 0], hop.at[0], sems, base, right),
            remote(snd.at[0, 1], hop.at[1], sems, base + 1, left),
        ]
        self.near = [
            remote(snd.at[2, 1], rcv.at[0, 1], sems, base + 2, right),
            remote(snd.at[1, 0], rcv.at[1, 0], sems, base + 3, left),
        ]
        self.far = [
            remote(snd.at[2, 0], rcv.at[0, 0], sems, base + 4, right),
            remote(snd.at[1, 1], rcv.at[1, 1], sems, base + 5, left),
        ]

    def push(self):
        for copy in self.opp + self.near:
            copy.start()

    def relay(self):
        for k, (slot, half) in enumerate(((2, 0), (1, 1))):
            self.opp[k].wait_recv()
            self.snd[slot, half] = (self.snd[slot, half].astype(F32) + self.hop[half].astype(F32)).astype(BF)
            self.far[k].start()

    def arrive(self):
        for copy in self.near + self.far:
            copy.wait_recv()

    def total(self, *index):
        return self.snd[(3,) + index].astype(F32) + (
            self.rcv[(0,) + index].astype(F32) + self.rcv[(1,) + index].astype(F32)
        )

    def leave(self):
        for copy in self.opp + self.near + self.far:
            copy.wait_send()


class GridReduce:
    def __init__(self, along_z, src, cols, snd, hop, rcv, snd2, hop2, rcv2, sems, lsems):
        r = lax.axis_index("rep")
        z, y = r // 4, r % 4
        along = (lambda k: {"rep": (z + k) % 4 * 4 + y}, lambda k: {"rep": z * 4 + (y + k) % 4})
        one, two = along if along_z else along[::-1]
        here, self.there = (z, y) if along_z else (y, z)
        offsets = (2, 3, 1, 0)
        cut = pl.ds(cols, FF)
        self.load = []
        for k, off in enumerate(offsets):
            b = (here + off) % 4
            block = src.at[:, b, :, :, cut] if along_z else src.at[:, :, b, :, cut]
            self.load.append(pltpu.make_async_copy(block, snd.at[k], lsems.at[k]))
        self.offsets, self.snd2 = offsets, snd2
        self.stage = AxisReduce((one(1), one(3)), snd, hop, rcv, sems, 0)
        self.last = AxisReduce((two(1), two(3)), snd2, hop2, rcv2, sems, 6)

    def push(self):
        for copy in self.load:
            copy.wait()
        self.stage.push()

    def turn(self):
        self.stage.arrive()
        for k, off in enumerate(self.offsets):
            b = (self.there + off) % 4
            for n in range(PAIR):
                self.snd2[k, n] = self.stage.total(n, b).astype(BF)
        self.last.push()

    def finish(self, out_ref, cols):
        self.last.arrive()
        for n in range(PAIR):
            out_ref[n, :, cols : cols + FF] = self.last.total(n).astype(BF)
        self.stage.leave()
        self.last.leave()


def grid_scratch():
    blocks = [(4, PAIR, 4, BLOCK, FF), (PAIR, 4, BLOCK, FF), (2, PAIR, 4, BLOCK, FF)]
    blocks += [(4, PAIR, BLOCK, FF), (PAIR, BLOCK, FF), (2, PAIR, BLOCK, FF)]
    return [pltpu.VMEM(dims, BF) for dims in blocks]


def comm_call(kernel, name, collective_id, out_shape, in_specs, out_specs, scratch, limit=48):
    return pl.pallas_call(
        kernel,
        out_shape=out_shape,
        in_specs=in_specs,
        out_specs=out_specs,
        scratch_shapes=scratch,
        compiler_params=pltpu.CompilerParams(
            collective_id=collective_id, has_side_effects=True, vmem_limit_bytes=limit * MIB
        ),
        name=name,
    )


def shape(dims, dtype=F32):
    return jax.ShapeDtypeStruct(dims, dtype)


WB = D + 128


def column(row):
    return jnp.transpose(jnp.broadcast_to(row, (128, row.shape[1])))


def lane_row(values):
    return dot_nt(jnp.ones((8, 128), F32), values, precision=HIGH)[0:1]


def turn_tables():
    half = HEAD_DIM // 2
    freq = np.float32(ROPE_BASE) ** (-(np.arange(half, dtype=np.float32) * np.float32(2.0) / np.float32(HEAD_DIM)))
    angles = np.arange(LENGTH, dtype=np.float32)[:, None] * freq.astype(np.float32)[None, :]
    c, s = np.cos(angles), np.sin(angles)
    cosine = np.concatenate([c, c, c, c], axis=1)
    sine = np.concatenate([-s, s, -s, s], axis=1)
    return cosine.astype(np.float32), sine.astype(np.float32)


def turn(u, cosine, sine):
    early = iota(u.shape, 1) % HEAD_DIM < HEAD_DIM // 2
    partner = jnp.where(early, pltpu.roll(u, 96, 1), pltpu.roll(u, 32, 1))
    return u * cosine + partner * sine


def block_rows(b):
    return pl.ds(pl.multiple_of(b * TOK, TOK), TOK)


def stack_heads(values):
    first = iota(values.shape, 1) < HEAD_DIM
    return jnp.concatenate([jnp.where(first, values, 0.0), jnp.where(first, 0.0, values)], axis=0)


def merge_heads(values):
    first = iota((TOK, 128), 1) < HEAD_DIM
    return jnp.where(first, values[:TOK], values[TOK:])


def front_kernel(
    tok, cot, wq, wk, wv, wo_in, router_in, ga_in, gq_in, gk_in, gf_in, seg, rts_in, cos_in, sin_in,
    x_all, g_all, lin, q_o, k_o, v_o, a_o, lse_o, hid_o, m_o, tab_o, att_o, misc, rout_o, whole, wcol,
    x_s, cot_s, tiny, tiny_b, smalls, wsl, wos, wg, wog, wog2, w32, gains_s, cos_ref, sin_ref, sums, held,
    s_tok, r_tok, s_cot, r_cot, s_w, r_w, s_o, r_o, s_st, r_st, s_t, r_t, s_a, r_a, lsem,
):
    r = lax.axis_index("rep")
    e, x, c = place()
    others = ep_others(e)
    copies = rep_others(r)
    first = iota((TOK, 128), 1) < HEAD_DIM
    gain_a, gain_f, gain = misc.at[0:1], misc.at[1:2], misc.at[2:3, 0:256]
    lo, st = misc.at[8:16, 0:256], misc.at[16:32, 0:256]
    greet([{"ep": d} for d in others] + [{"rep": d} for d in copies])
    misc[...] = jnp.zeros((32, D), F32)

    tiny[...] = jnp.zeros((16, 128), F32)
    tiny[0:8, 0:EXPERTS] = router_in[...].astype(F32)
    for lane, ref in ((0, ga_in), (8, gq_in), (16, gk_in), (20, gf_in)):
        tiny[8:9, lane : lane + ref.shape[1]] = ref[...].astype(F32)
    tiny_b[...] = tiny[...].astype(BF)
    low_lanes = iota((8, 128), 1) < HEAD_DIM
    for d in range(EP):
        k_t = wk[:, (d // 2) * 128 : (d // 2 + 1) * 128].astype(F32)
        v_t = wv[:, (d // 2) * 128 : (d // 2 + 1) * 128].astype(F32)
        if d % 2:
            k_t = pltpu.roll(k_t, HEAD_DIM, 1)
        else:
            v_t = pltpu.roll(v_t, HEAD_DIM, 1)
        q_t = wq[:, d * 128 : (d + 1) * 128].astype(F32)
        wsl[d] = jnp.concatenate([q_t, jnp.where(low_lanes, k_t, v_t)], axis=0).astype(BF)
    for half in range(2):
        wos[half] = jnp.concatenate(
            [wo_in[:, j * 128 : (j + 1) * 128].astype(F32) for j in range(half * 4, half * 4 + 4)], axis=0
        ).astype(BF)

    def cols_of(b):
        return wg.at[r, pl.ds(pl.multiple_of(b * 16, 16), 16)]

    stage_w = [remote(wsl.at[d], cols_of(e), (s_w, r_w), k, {"ep": d}) for k, d in enumerate(others)]
    stage_t = [remote(tiny_b, smalls.at[e], (s_t, r_t), k, {"ep": d}) for k, d in enumerate(others)]
    stage_o = [remote(wos.at[d % 2], wog.at[r, e], (s_o, r_o), k, {"ep": d}) for k, d in enumerate(others)]
    spread_w = [remote(wg.at[r], wg.at[r], (s_w, r_w), 7 + k, {"rep": d}) for k, d in enumerate(copies)]
    spread_o = [remote(wog.at[r], wog.at[r], (s_o, r_o), 7 + k, {"rep": d}) for k, d in enumerate(copies)]
    other_half = remote(wog, wog2, (s_o, r_o), 22, ep_device(x, 1 - c))
    tokens = RingGather(tok, x_s, (s_tok, r_tok), lsem.at[0])
    grads = RingGather(cot_s, g_all, (s_cot, r_cot), lsem.at[1])
    for copy in stage_w + stage_t:
        copy.start()
    tokens.start()
    for copy in stage_o:
        copy.start()
    tables = [
        pltpu.make_async_copy(cos_in, cos_ref, lsem.at[2]),
        pltpu.make_async_copy(sin_in, sin_ref, lsem.at[3]),
        pltpu.make_async_copy(cot, cot_s, lsem.at[5]),
    ]
    for copy in tables:
        copy.start()
    cols_of(e)[...] = wsl[e]
    smalls[e] = tiny_b[...]
    wog[r, e] = wos[c]
    for copy in stage_w + stage_t:
        copy.wait_recv()
    router_tiles = [
        sum(pltpu.roll(smalls[4 * a + b][:8].astype(F32), 32 * b, 1) if b else smalls[4 * a][:8].astype(F32) for b in range(4))
        for a in range(2)
    ]
    gain_rows = [smalls[d][8:9].astype(F32) for d in range(EP)]
    wg[r, 128:160] = jnp.concatenate(router_tiles + gain_rows + [jnp.zeros((8, 128), F32)], axis=0).astype(BF)
    for copy in spread_w:
        copy.start()
    tokens.forward_half()
    tokens.forward_rest()

    routed = rts_in[...]
    hit = jnp.zeros((EXPERTS, TOK), F32)
    for k in range(TOP):
        hit = jnp.where(iota((EXPERTS, TOK), 0) == routed[k : k + 1], 1.0, hit)
    before = jnp.where(iota((TOK, TOK), 0) < iota((TOK, TOK), 1), 1.0, 0.0).astype(BF)
    tab_o[:EXPERTS] = jnp.where(hit > 0.0, dot(hit.astype(BF), before), -1.0)
    segs = jnp.concatenate([seg[:, b * TOK : (b + 1) * TOK] for b in range(EP)], axis=0)
    opening = jnp.zeros((EP, TOK), F32)
    for value in range(2):
        count = jnp.sum(jnp.where(segs == value, 1.0, 0.0), axis=1, keepdims=True)
        opening = opening + jnp.where(segs > value, jnp.sum(count, axis=0, keepdims=True), 0.0)
    places = (iota((EP, TOK), 0) * TOK + iota((EP, TOK), 1)).astype(F32)
    lo[...] = jnp.maximum(opening, places - (WINDOW - 1))

    for copy in spread_w:
        copy.wait_recv()
    for copy in stage_o:
        copy.wait_recv()
    for copy in spread_o:
        copy.start()

    def unpack(b, carry):
        for d in range(EP):
            tile = wg[b, d * 16 : d * 16 + 16].astype(F32)
            rows = pl.ds(pl.multiple_of(b * 64 + d * 8, 8), 8)
            w32[rows, 0:128] = tile[0:8]
            w32[rows, 128:256] = tile[8:16]
        extra = wg[b, 128:160].astype(F32)
        for d in range(EP):
            tile = extra[d // 4 * 8 : d // 4 * 8 + 8]
            if d % 4:
                tile = pltpu.roll(tile, 128 - 32 * (d % 4), 1)
            w32[pl.ds(pl.multiple_of(b * 64 + d * 8, 8), 8), 256:384] = tile
        gains_s[pl.ds(pl.multiple_of(b * 8, 8), 8)] = extra[16:24]
        return carry

    lax.fori_loop(0, REP, unpack, 0)
    wcol[...] = w32[:, :256].astype(BF)
    rout_o[...] = jnp.transpose(w32[:, 256:384])[:EXPERTS].astype(BF)
    packed = gains_s[...].astype(BF)

    def spread_gain(width, group, base, shift):
        lane = base + iota((128, width), 1) % group
        picked = dot(packed, jnp.where(iota((128, width), 0) == lane, 1.0, 0.0).astype(BF))
        mine = iota((128, width), 0) == shift + iota((128, width), 1) // group
        return jnp.sum(jnp.where(mine, picked, 0.0), axis=0, keepdims=True)

    gain_a[...] = spread_gain(D, 8, 0, 0)
    gain_f[...] = spread_gain(D, 8, 20, 0)
    key_part = spread_gain(128, 4, 16, e * 16)
    gain[:, :128] = spread_gain(128, 8, 8, e * 16)
    gain[:, 128:] = jnp.where(iota((1, 128), 1) < HEAD_DIM, key_part, 1.0)

    tokens.first[4].wait_recv()
    tokens.own.wait()

    def project(k, carry):
        @pl.when(k == 2)
        def _():
            tokens.fwd_right.wait_recv()
            tokens.fwd_left.wait_recv()
            tokens.to_peer[2].start()
            tokens.to_peer[1].wait_recv()

        @pl.when(k == 4)
        def _():
            tokens.to_peer[0].wait_recv()

        @pl.when(k == 6)
        def _():
            tokens.to_peer[2].wait_recv()

        g = k // 2
        b = (2 * (x + g + g // 2 - 2 * (g // 3)) + k % 2) % EP
        rows = block_rows(b)
        values = x_s[rows].astype(F32)
        r1 = lax.rsqrt(jnp.mean(values * values, axis=1, keepdims=True) + EPSILON)
        normed = (values * r1 * gain_a[...]).astype(BF)
        out = dot(normed, wcol[...])
        lin[rows] = out
        sq = out * out
        sums[pl.ds(2 * b, 1)] = lane_row(sq[:, :128])
        sums[pl.ds(2 * b + 1, 1)] = lane_row(jnp.where(first, sq[:, 128:], 0.0))
        return carry

    lax.fori_loop(0, EP, project, 0)
    stats = [remote(sums, held.at[e], (s_st, r_st), k, {"ep": d}) for k, d in enumerate(others)]
    for copy in stats:
        copy.start()
    held[e] = sums[...]
    keep = pltpu.make_async_copy(x_s, x_all, lsem.at[4])
    keep.start()
    for copy in tables:
        copy.wait()
    for copy in stats:
        copy.wait_recv()
    total = held[0]
    for k in range(1, EP):
        total = total + held[k]
    st[...] = total
    grads.start()

    def prepare(b, carry):
        rows = block_rows(b)
        cq = column(lax.rsqrt(st[pl.ds(2 * b, 1)] * (1.0 / D) + EPSILON))
        ck = column(lax.rsqrt(st[pl.ds(2 * b + 1, 1)] * (1.0 / KV) + EPSILON))
        cosine, sine = cos_ref[rows], sin_ref[rows]
        q_o[rows] = turn(lin[rows, :128] * cq * gain[:, :128], cosine, sine).astype(BF)
        kv = lin[rows, 128:]
        kv = jnp.where(first, turn(kv * ck * gain[:, 128:], cosine, sine), kv)
        other = pltpu.roll(kv, HEAD_DIM, 1)
        k_o[rows] = jnp.where(first, kv, other).astype(BF)
        v_o[rows] = jnp.where(first, other, kv).astype(BF)
        return carry

    lax.fori_loop(0, EP, prepare, 0)

    def heads(i, source):
        cols = pl.ds(pl.multiple_of(source * 128, 128), 128)
        return pltpu.make_async_remote_copy(
            src_ref=a_o.at[block_rows(i)],
            dst_ref=att_o.at[:, cols],
            send_sem=s_a.at[i],
            recv_sem=r_a.at[source],
            device_id={"ep": i},
            device_id_type=MESH,
        )

    def attend_block(i, n):
        rows = block_rows(i)
        past = (n - 1) * TOK
        q2 = stack_heads(q_o[rows].astype(F32) * HEAD_DIM ** (-0.5)).astype(BF)
        lo_col = column(lo[pl.ds(i, 1)])[:, :1]
        low = jnp.concatenate([lo_col, lo_col], axis=0)
        own_key = (iota((2 * TOK, TOK), 1) + i * TOK).astype(F32)
        query = (iota((2 * TOK, TOK), 0) % TOK + i * TOK).astype(F32)
        s_own = jnp.where((own_key >= low) & (own_key <= query), dot_nt(q2, k_o[rows]), MASKED)
        m = jnp.max(s_own, axis=1, keepdims=True)
        if past:
            early = pl.ds(pl.multiple_of((i - n + 1) * TOK, TOK), past)
            key = (iota((2 * TOK, past), 1) + (i - n + 1) * TOK).astype(F32)
            s = jnp.where(key >= low, dot_nt(q2, k_o[early]), MASKED)
            m = jnp.maximum(m, jnp.max(s, axis=1, keepdims=True))
        p_own = jnp.exp(s_own - m)
        total = jnp.sum(p_own, axis=1, keepdims=True)
        out = dot(p_own.astype(BF), v_o[rows])
        if past:
            p = jnp.exp(s - m)
            total = total + jnp.sum(p, axis=1, keepdims=True)
            out = out + dot(p.astype(BF), v_o[early])
        a_o[rows] = merge_heads(out / total).astype(BF)
        lse = jnp.broadcast_to(m + jnp.log(total), (2 * TOK, 128))
        lse_o[i] = jnp.transpose(lse)[:8]

        @pl.when(i != e)
        def _():
            heads(i, e).start()

        @pl.when(i == e)
        def _():
            att_o[:, pl.ds(pl.multiple_of(e * 128, 128), 128)] = a_o[rows]

    def later(i, carry):
        attend_block(i, 5)

        @pl.when(i == 5)
        def _():
            grads.forward_rest()

        return carry

    for i in range(4):
        attend_block(i, i + 1)
    grads.forward_half()
    for copy in spread_o:
        copy.wait_recv()
    other_half.start()
    lax.fori_loop(4, EP, later, 0)

    other_half.wait_recv()
    grads.fwd_right.wait_recv()
    grads.fwd_left.wait_recv()
    grads.to_peer[2].start()

    def unpack_out(b, carry):
        rows = pl.ds(pl.multiple_of(b * 8, 8), 8)
        for half, held_half in ((c, wog), (1 - c, wog2)):
            tile = held_half[b // EP, b % EP].astype(F32)
            for j in range(4):
                w32[rows, pl.ds(pl.multiple_of(half * 512 + j * 128, 128), 128)] = tile[j * 8 : (j + 1) * 8]
        return carry

    lax.fori_loop(0, 128, unpack_out, 0)
    whole[...] = w32[...].astype(BF)
    for d in others:
        heads(d, d).wait_recv()

    hidden = x_s[block_rows(e)].astype(F32) + dot(att_o[...], whole[...])
    hid_o[...] = hidden
    r2 = lax.rsqrt(jnp.mean(hidden * hidden, axis=1, keepdims=True) + EPSILON)
    moe_in = (hidden * r2 * gain_f[...]).astype(BF)
    m_o[...] = moe_in
    logits = dot_nt(rout_o[...], moe_in)
    chosen = hit > 0.0
    logits = jnp.where(chosen, logits, MASKED)
    raised = jnp.where(chosen, jnp.exp(logits - jnp.max(logits, axis=0, keepdims=True)), 0.0)
    tab_o[EXPERTS:] = raised / jnp.sum(raised, axis=0, keepdims=True)

    grads.first[4].wait_recv()
    for copy in grads.to_peer:
        copy.wait_recv()
    grads.own.wait()
    keep.wait()
    for d in others:
        heads(d, d).wait_send()
    for ring in (tokens, grads):
        for copy in ring.first + [ring.fwd_right, ring.fwd_left] + ring.to_peer:
            copy.wait_send()
    for copy in stage_w + stage_t + stage_o + spread_w + spread_o + stats + [other_half]:
        copy.wait_send()


def front(*args):
    return comm_call(
        front_kernel,
        "front",
        1,
        [
            shape((LENGTH, D), BF),
            shape((LENGTH, D), BF),
            shape((LENGTH, 256)),
            shape((LENGTH, 128), BF),
            shape((LENGTH, 128), BF),
            shape((LENGTH, 128), BF),
            shape((LENGTH, 128), BF),
            shape((EP, 8, 2 * TOK)),
            shape((TOK, D)),
            shape((TOK, D), BF),
            shape((2 * EXPERTS, TOK)),
            shape((TOK, D), BF),
            shape((32, D)),
            shape((EXPERTS, D), BF),
            shape((D, D), BF),
            shape((D, 256), BF),
        ],
        [ANY, ANY] + [VM] * 11 + [ANY, ANY],
        [ANY, ANY] + [VM] * 14,
        [
            pltpu.VMEM((LENGTH, D), BF),
            pltpu.VMEM((TOK, D), BF),
            pltpu.VMEM((16, 128), F32),
            pltpu.VMEM((16, 128), BF),
            pltpu.VMEM((EP, 16, 128), BF),
            pltpu.VMEM((EP, 16, 128), BF),
            pltpu.VMEM((2, 32, 128), BF),
            pltpu.VMEM((REP, 160, 128), BF),
            pltpu.VMEM((REP, EP, 32, 128), BF),
            pltpu.VMEM((REP, EP, 32, 128), BF),
            pltpu.VMEM((D, D), F32),
            pltpu.VMEM((128, 128), F32),
            pltpu.VMEM((LENGTH, 128), F32),
            pltpu.VMEM((LENGTH, 128), F32),
            pltpu.VMEM((16, 256), F32),
            pltpu.VMEM((EP, 16, 256), F32),
        ]
        + [DMA((10,))] * 4
        + [DMA((23,))] * 4
        + [DMA((7,))] * 4
        + [DMA((8,))] * 2
        + [DMA((6,))],
        limit=60,
    )(*args)


class ChipReduce:
    SEMS = 10
    STEP = 64

    def __init__(self, n, swo, snd, pc, rcv, hop, sems):
        e, x, c = place()
        self.n, self.h = n, n // 2
        h = n // 2
        self.snd, self.pc, self.rcv, self.hop = snd, pc, rcv, hop
        right, left = ep_device((x + 1) % 4, c), ep_device((x + 3) % 4, c)
        peer = ep_device(x, 1 - c)
        self.swap = lambda k: remote(swo.at[k], pc.at[k], sems, k, peer)
        low, high = pl.ds(0, h), pl.ds(h, h)
        self.opp = [
            remote(snd.at[0, low], hop.at[low], sems, 4, right),
            remote(snd.at[0, high], hop.at[high], sems, 5, left),
        ]
        self.near = [
            remote(snd.at[2, high], rcv.at[0, high], sems, 6, right),
            remote(snd.at[1, low], rcv.at[1, low], sems, 7, left),
        ]
        self.far = [
            remote(snd.at[2, low], rcv.at[0, low], sems, 8, right),
            remote(snd.at[1, high], rcv.at[1, high], sems, 9, left),
        ]

    def rows_loop(self, low, count, body):
        step = self.STEP

        def loop(i, carry):
            body(pl.ds(pl.multiple_of(low + i * step, 16), step))
            return carry

        lax.fori_loop(0, count // step, loop, 0)

    def merge(self, k):
        def body(s):
            self.snd[k, s] = (self.snd[k, s].astype(F32) + self.pc[k, s].astype(F32)).astype(BF)

        self.swap(k).wait_recv()
        self.rows_loop(0, self.n, body)

    def merge_hop(self, k, low):
        def body(s):
            self.snd[k, s] = (self.snd[k, s].astype(F32) + self.hop[s].astype(F32)).astype(BF)

        self.rows_loop(low, self.h, body)

    def send_opp(self):
        self.merge(0)
        for copy in self.opp:
            copy.start()

    def send_near(self):
        self.merge(2)
        self.near[0].start()
        self.merge(1)
        self.near[1].start()

    def send_far(self):
        self.opp[0].wait_recv()
        self.merge_hop(2, 0)
        self.far[0].start()
        self.opp[1].wait_recv()
        self.merge_hop(1, self.h)
        self.far[1].start()

    def finish(self, out_ref):
        for copy in self.near + self.far:
            copy.wait_recv()

        def body(s):
            out_ref[s] = self.snd[3, s].astype(F32) + (
                self.rcv[0, s].astype(F32) + self.rcv[1, s].astype(F32)
            )

        self.rows_loop(0, self.n, body)
        for copy in [self.swap(k) for k in range(4)] + self.opp + self.near + self.far:
            copy.wait_send()


PAIR = 2
ROWS = EP * CAP
CHIP = 2 * CAP
BLOCK = 96


def chip_rows(q):
    return pl.ds(pl.multiple_of(q * CHIP, 16), CHIP)


def chip_tokens(q):
    return pl.ds(pl.multiple_of(q * 2 * TOK, 2 * TOK), 2 * TOK)


def expert_hits(tab, e, n, q):
    row = pl.ds(e * LOCAL + n, 1)
    second = tab[2 * q + 1, row]
    slots = jnp.concatenate([tab[2 * q, row], jnp.where(second >= 0.0, second + CAP, -1.0)], axis=1)
    return iota((CHIP, 2 * TOK), 0).astype(F32) == slots


def one_hot(hit):
    return jnp.where(hit, 1.0, 0.0).astype(BF)


def expert_chip(q, e, start, tab, m_ref, g_ref, wgu, wd, a_s, act_s, gp_s, dgu_s, y_s, z_s, ggt):
    hits = [expert_hits(tab, e, start + n, q) for n in range(PAIR)]
    chosen = jnp.concatenate([one_hot(hit) for hit in hits], axis=0)
    rows = chip_rows(q)
    a_both = dot(chosen, m_ref[chip_tokens(q)]).astype(BF)
    c_both = dot(chosen, g_ref[chip_tokens(q)]).astype(BF)
    for n in range(PAIR):
        part = slice(n * CHIP, (n + 1) * CHIP)
        row = pl.ds(EXPERTS + e * LOCAL + start + n, 1)
        gates = jnp.concatenate([tab[2 * q, row], tab[2 * q + 1, row]], axis=1)
        weight = jnp.sum(jnp.where(hits[n], gates, 0.0), axis=1, keepdims=True)
        a, cot = a_both[part], c_both[part]
        lin = dot(a, wgu[n])
        back = dot_nt(cot, wd[n])
        gate_lin, up_lin = lin[:, :FF], lin[:, FF:]
        sig = jax.nn.sigmoid(gate_lin)
        silu = gate_lin * sig
        act = silu * up_lin
        act_low = act.astype(BF)
        produced = dot(act_low, wd[n]).astype(BF).astype(F32)
        gg = jnp.sum(act * back, axis=1, keepdims=True)
        back = back * weight
        dgate = (back * up_lin * sig * (1.0 + gate_lin * (1.0 - sig))).astype(BF)
        dup = (back * silu).astype(BF)
        dgu = jnp.concatenate([dgate, dup], axis=1)
        a_s[n, rows] = a
        act_s[n, rows] = act_low
        gp_s[n, rows] = (weight * cot.astype(F32)).astype(BF)
        dgu_s[n, rows] = dgu
        y_s[n, rows] = (weight * produced).astype(BF)
        z_s[n, rows] = dot_nt(dgu, wgu[n]).astype(BF)
        gg_row = jnp.sum(jnp.where(hits[n], gg, 0.0), axis=0, keepdims=True)
        ggt[2 * q, n : n + 1] = gg_row[:, :TOK]
        ggt[2 * q + 1, n : n + 1] = gg_row[:, TOK:]


def expert_grads(n, a_s, act_s, gp_s, dgu_s, eg):
    eg[n, :, :64] = dot_tn(a_s[n], dgu_s[n]).astype(BF).reshape(REP, 64, D)
    eg[n, :, 64:] = dot_tn(act_s[n], gp_s[n]).astype(BF).reshape(REP, 32, D)


def load_weights(start, wg_in, wu_in, wd_in, wgu, wd, sems):
    some = pl.ds(start, PAIR)
    return [
        pltpu.make_async_copy(wg_in.at[some], wgu.at[:, :, pl.ds(0, FF)], sems.at[0]),
        pltpu.make_async_copy(wu_in.at[some], wgu.at[:, :, pl.ds(FF, FF)], sems.at[1]),
        pltpu.make_async_copy(wd_in.at[some], wd, sems.at[2]),
    ]


def send_gates(ggt, gg_o, e, sems, lsem):
    copies = [remote(ggt.at[d], gg_o.at[e], sems, k, {"ep": d}) for k, d in enumerate(ep_others(e))]
    return copies, pltpu.make_async_copy(ggt.at[e], gg_o.at[e], lsem)


def experts_first_kernel(
    m_in, t_in, g_in, wg_in, wu_in, wd_in, m_o, tab_o, y_o, z_o, gg_o, eg_o,
    m_ref, tab, g_ref, wgu, wd, a_s, act_s, gp_s, dgu_s, y_s, z_s, ggt, eg,
    s_m, r_m, s_t, r_t, s_g, r_g, lsem, wsem, gsem, esem,
):
    e, x, c = place()
    others = ep_others(e)
    greet([{"ep": d} for d in others])
    ring = RingGather(m_in, m_ref, (s_m, r_m), lsem.at[0])
    tables = [remote(t_in, tab.at[e], (s_t, r_t), k, {"ep": d}) for k, d in enumerate(others)]
    for copy in tables:
        copy.start()
    ring.start()
    own = pltpu.make_async_copy(t_in, tab.at[e], lsem.at[1])
    loads = load_weights(0, wg_in, wu_in, wd_in, wgu, wd, wsem)
    cots = [
        pltpu.make_async_copy(g_in.at[chip_tokens(q)], g_ref.at[chip_tokens(q)], gsem.at[k])
        for k, q in enumerate([x, (x + 1) % 4, (x + 3) % 4, (x + 2) % 4])
    ]
    for copy in [own] + loads + cots:
        copy.start()
    ggt[...] = jnp.zeros((EP, 8, TOK), F32)
    kept = pltpu.make_async_copy(m_ref, m_o, lsem.at[2])

    def chips(k, carry):
        @pl.when(k == 0)
        def _():
            ring.first[0].wait_recv()
            ring.fwd_right.start()
            ring.first[1].wait_recv()
            ring.fwd_left.start()
            ring.first[4].wait_recv()
            ring.own.wait()
            own.wait()
            for copy in tables:
                copy.wait_recv()
            for copy in loads:
                copy.wait()
            cots[0].wait()

        @pl.when(k == 1)
        def _():
            ring.first[3].wait_recv()
            ring.to_peer[1].start()
            ring.first[2].wait_recv()
            ring.to_peer[0].start()
            ring.to_peer[1].wait_recv()
            cots[1].wait()

        @pl.when(k == 2)
        def _():
            ring.fwd_right.wait_recv()
            ring.fwd_left.wait_recv()
            ring.to_peer[2].start()
            ring.to_peer[0].wait_recv()
            cots[2].wait()

        @pl.when(k == 3)
        def _():
            ring.to_peer[2].wait_recv()
            cots[3].wait()
            kept.start()

        q = (x + k + k // 2 - 2 * (k // 3)) % 4
        expert_chip(q, e, 0, tab, m_ref, g_ref, wgu, wd, a_s, act_s, gp_s, dgu_s, y_s, z_s, ggt)
        return carry

    lax.fori_loop(0, 4, chips, 0)
    gates, own_gates = send_gates(ggt, gg_o, e, (s_g, r_g), lsem.at[3])
    states = [
        pltpu.make_async_copy(tab, tab_o, lsem.at[4]),
        pltpu.make_async_copy(y_s, y_o, lsem.at[5]),
        pltpu.make_async_copy(z_s, z_o, lsem.at[6]),
    ]
    for copy in gates + [own_gates] + states:
        copy.start()
    for n in range(PAIR):
        expert_grads(n, a_s, act_s, gp_s, dgu_s, eg)
        states.append(pltpu.make_async_copy(eg.at[n], eg_o.at[n], esem.at[n]))
        states[-1].start()
    for copy in states + [kept, own_gates]:
        copy.wait()
    for copy in gates:
        copy.wait_recv()
    for copy in ring.first + [ring.fwd_right, ring.fwd_left] + ring.to_peer + tables + gates:
        copy.wait_send()


def pair_scratch():
    return [
        pltpu.VMEM((LENGTH, D), BF),
        pltpu.VMEM((EP, 2 * EXPERTS, TOK), F32),
        pltpu.VMEM((LENGTH, D), BF),
        pltpu.VMEM((PAIR, D, 2 * FF), BF),
        pltpu.VMEM((PAIR, FF, D), BF),
        pltpu.VMEM((PAIR, ROWS, D), BF),
        pltpu.VMEM((PAIR, ROWS, FF), BF),
        pltpu.VMEM((PAIR, ROWS, D), BF),
        pltpu.VMEM((PAIR, ROWS, D), BF),
        pltpu.VMEM((PAIR, ROWS, D), BF),
        pltpu.VMEM((PAIR, ROWS, D), BF),
        pltpu.VMEM((EP, 8, TOK), F32),
        pltpu.VMEM((PAIR, REP, BLOCK, D), BF),
    ]


def experts_first(m, t, g_all, wg, wu, wd):
    return comm_call(
        experts_first_kernel,
        "experts_first",
        2,
        [
            shape((LENGTH, D), BF),
            shape((EP, 2 * EXPERTS, TOK)),
            shape((PAIR, ROWS, D), BF),
            shape((PAIR, ROWS, D), BF),
            shape((EP, 8, TOK)),
            shape((PAIR, REP, BLOCK, D), BF),
        ],
        [ANY] * 6,
        [ANY] * 6,
        pair_scratch()
        + [DMA((10,))] * 2
        + [DMA((7,))] * 4
        + [DMA((7,)), DMA((3,)), DMA((4,)), DMA((2,))],
        limit=60,
    )(m, t, g_all, wg, wu, wd)


def experts_last_kernel(
    m_in, t_in, y_in, z_in, g_in, wg_in, wu_in, wd_in, gm_o, mix_o, gg_o, eg_o,
    m_ref, tab, g_ref, wgu, wd, a_s, act_s, gp_s, dgu_s, y_s, z_s, ggt, eg,
    y_f, z_f, gm, swo, snd, pc, rcv, hop, mix,
    s_r, r_r, s_g, r_g, lsem, wsem, gsem, msem, esem, osem,
):
    e, x, c = place()
    order = [(x + 2) % 4, (x + 3) % 4, (x + 1) % 4, x]
    loads = [pltpu.make_async_copy(t_in, tab, lsem.at[0])] + load_weights(2, wg_in, wu_in, wd_in, wgu, wd, wsem)
    rows = [
        (
            pltpu.make_async_copy(m_in.at[chip_tokens(q)], m_ref.at[chip_tokens(q)], msem.at[k]),
            pltpu.make_async_copy(g_in.at[chip_tokens(q)], g_ref.at[chip_tokens(q)], gsem.at[k]),
        )
        for k, q in enumerate(order)
    ]
    firsts = [pltpu.make_async_copy(z_in, z_f, lsem.at[1]), pltpu.make_async_copy(y_in, y_f, lsem.at[2])]
    for copy in loads + list(rows[0]) + [firsts[0]] + list(rows[1] + rows[2] + rows[3]) + [firsts[1]]:
        copy.start()
    greet([{"ep": d} for d in ep_others(e)])
    red = ChipReduce(TOK, swo, snd, pc, rcv, hop, (s_r, r_r))
    ggt[...] = jnp.zeros((EP, 8, TOK), F32)

    def combine(q, early, late):
        chosen = jnp.concatenate([one_hot(expert_hits(tab, e, n, q)) for n in range(LOCAL)], axis=0)
        part = chip_rows(q)
        values = [ref[n, part] for ref in (early, late) for n in range(PAIR)]
        return dot_tn(chosen, jnp.concatenate(values, axis=0)).astype(BF)

    for copy in loads:
        copy.wait()

    def chips(k, carry):
        for step in range(4):

            @pl.when(k == step)
            def _(step=step):
                for copy in rows[step]:
                    copy.wait()
                if step == 0:
                    firsts[0].wait()

        q = (x + 2 + k - (k // 2) * (2 * k - 1)) % 4
        expert_chip(q, e, 2, tab, m_ref, g_ref, wgu, wd, a_s, act_s, gp_s, dgu_s, y_s, z_s, ggt)
        mix[...] = combine(q, z_f, z_s)
        swo[k] = mix[pl.ds(pl.multiple_of((1 - c) * TOK, TOK), TOK)]
        red.swap(k).start()
        snd[k] = mix[pl.ds(pl.multiple_of(c * TOK, TOK), TOK)]

        @pl.when(k == 1)
        def _():
            red.send_opp()

        @pl.when(k == 3)
        def _():
            red.send_near()

        return carry

    lax.fori_loop(0, 4, chips, 0)
    gates, own_gates = send_gates(ggt, gg_o, e, (s_g, r_g), lsem.at[3])
    for copy in gates + [own_gates]:
        copy.start()
    states = []

    def grads(n):
        expert_grads(n, a_s, act_s, gp_s, dgu_s, eg)
        states.append(pltpu.make_async_copy(eg.at[n], eg_o.at[n], esem.at[n]))
        states[-1].start()

    grads(0)
    red.merge(3)
    red.send_far()
    grads(1)
    firsts[1].wait()

    def mixture(q, carry):
        @pl.when(q > 0)
        def _():
            pltpu.make_async_copy(mix, mix_o.at[chip_tokens(q)], osem).wait()

        mix[...] = combine(q, y_f, y_s)
        pltpu.make_async_copy(mix, mix_o.at[chip_tokens(q)], osem).start()
        return carry

    lax.fori_loop(0, 4, mixture, 0)
    red.finish(gm)
    last = pltpu.make_async_copy(gm, gm_o, lsem.at[4])
    last.start()
    pltpu.make_async_copy(mix, mix_o.at[chip_tokens(3)], osem).wait()
    for copy in states + [own_gates, last]:
        copy.wait()
    for copy in gates:
        copy.wait_recv()
    for copy in gates:
        copy.wait_send()


def experts_last(m, t, y, z, g_all, wg, wu, wd):
    return comm_call(
        experts_last_kernel,
        "experts_last",
        4,
        [
            shape((TOK, D)),
            shape((LENGTH, D), BF),
            shape((EP, 8, TOK)),
            shape((PAIR, REP, BLOCK, D), BF),
        ],
        [ANY] * 8,
        [ANY] * 4,
        pair_scratch()
        + [
            pltpu.VMEM((PAIR, ROWS, D), BF),
            pltpu.VMEM((PAIR, ROWS, D), BF),
            pltpu.VMEM((TOK, D), F32),
            pltpu.VMEM((4, TOK, D), BF),
            pltpu.VMEM((4, TOK, D), BF),
            pltpu.VMEM((4, TOK, D), BF),
            pltpu.VMEM((2, TOK, D), BF),
            pltpu.VMEM((TOK, D), BF),
            pltpu.VMEM((2 * TOK, D), BF),
        ]
        + [DMA((10,))] * 2
        + [DMA((7,))] * 2
        + [DMA((5,)), DMA((3,)), DMA((4,)), DMA((4,)), DMA((2,)), DMA(())],
        limit=63,
    )(m, t, y, z, g_all, wg, wu, wd)


KEPT = 8


def back_kernel(
    eg_in, mix_in, gm_in, gg1_in, gg2_in, tab_in, hid_in, m_in, cot_in, att_in, misc_in, rout_in, whole_in, wcol_in, x_in, lin_in,
    q_in, k_in, v_in, a_in, lse_in, cos_in, sin_in,
    out_o, ig_o, gq_o, gk_o, gv_o, go_o, pack_o, eg_o,
    gm, gg1, gg2, tab, hid, m_s, cot, att, misc, rout, wcol, x_s, lin, q_s, k_s, v_s, a_s, lse, cos_ref, sin_ref,
    gh, ga_s, go, q2_s, p_s, dk, dv, u_s, sums, st2, held, wb, wsum, wheld,
    dwt, dws, dheld, dsum, dw_o, vec, vheld, vtot, vheld2, swo, snd, pc1, rcv1, hop1, snd3, pc3, rcv3, hop3,
    s_1, r_1, s_2, r_2, s_3, r_3, s_go, r_go, s_st, r_st, s_w, r_w, s_d, r_d, s_e, r_e, s_v, r_v, s_v2, r_v2, lsem, l_1, l_3, esem, xsem,
    out_s, gq_s, gk_s, gv_s, go_s, pack_s, eg_s,
    za, zb, zc, zd, ze, zf, ya, yb, yc, yd, ye, yf, s_z, r_z, s_y, r_y, l_z, l_y,
):
    r = lax.axis_index("rep")
    e, x, c = place()
    others = ep_others(e)
    copies = rep_others(r)
    first = iota((TOK, 128), 1) < HEAD_DIM
    gain_a, gain_f, gain = misc.at[0:1], misc.at[1:2], misc.at[2:3, 0:256]
    lo, st = misc.at[8:16, 0:256], misc.at[16:32, 0:256]
    greet([{"ep": d} for d in others] + [{"rep": d} for d in copies])
    red1 = RingReduce(mix_in, TOK, pc1, snd, rcv1, hop1, (s_1, r_1), l_1)
    red2 = ChipReduce(TOK, swo, snd, pc1, rcv1, hop1, (s_2, r_2))
    red3 = RingReduce(wb, 128, pc3, snd3, rcv3, hop3, (s_3, r_3), l_3)
    by_z = GridReduce(True, eg_in, 0, za, zb, zc, zd, ze, zf, (s_z, r_z), l_z)
    by_y = GridReduce(False, eg_in, FF, ya, yb, yc, yd, ye, yf, (s_y, r_y), l_y)
    for copy in by_z.load + by_y.load:
        copy.start()
    red1.start()
    loads = [
        pltpu.make_async_copy(src, dst, lsem.at[k])
        for k, (src, dst) in enumerate(
            [
                (misc_in, misc), (gm_in, gm), (gg1_in, gg1), (gg2_in, gg2), (tab_in, tab), (hid_in, hid),
                (cot_in, cot), (rout_in, rout), (whole_in, wb.at[:, pl.ds(0, D)]), (q_in, q_s), (k_in, k_s), (lse_in, lse),
                (m_in, m_s), (att_in, att), (v_in, v_s), (a_in, a_s), (cos_in, cos_ref), (sin_in, sin_ref),
                (lin_in, lin), (wcol_in, wcol),
            ]
        )
    ]
    chips_order = [(x + 2) % 4, (x + 3) % 4, (x + 1) % 4, x]

    def x_load(k):
        return pltpu.make_async_copy(x_in.at[chip_tokens(chips_order[k])], x_s.at[k % 2], xsem.at[k % 2])

    for copy in loads + [x_load(0), x_load(1)]:
        copy.start()
    for copy in loads[:9]:
        copy.wait()

    def base(i):
        cut = jnp.minimum(i, 4)
        return cut * (cut + 1) // 2 + 5 * jnp.maximum(i - 4, 0)

    def spans(i, n):
        keys = pl.ds(pl.multiple_of((i - n + 1) * TOK, TOK), n * TOK)
        return keys, pl.ds(pl.multiple_of(base(i) * TOK, TOK), n * TOK)

    def probabilities(i, n):
        _, held_rows = spans(i, n)
        p_s[held_rows] = make_probabilities(i, n)

    def make_probabilities(i, n):
        keys, _ = spans(i, n)
        q2 = stack_heads(q_s[block_rows(i)].astype(F32) * HEAD_DIM ** (-0.5)).astype(BF)
        q2_s[i] = q2
        top = lse[i][0:1]
        low = jnp.concatenate([lo[pl.ds(i, 1)]] * 2, axis=1)
        key = (iota((n * TOK, 2 * TOK), 0) + (i - n + 1) * TOK).astype(F32)
        query = (iota((n * TOK, 2 * TOK), 1) % TOK + i * TOK).astype(F32)
        allowed = (key >= low) & (key <= query)
        return jnp.where(allowed, jnp.exp(dot_nt(k_s[keys], q2) - top), 0.0).astype(BF)

    def probabilities_later(i, carry):
        probabilities(i, 5)

        @pl.when(i == 4)
        def _():
            red1.push_opp()

        @pl.when(i == 5)
        def _():
            red1.push_near()

        return carry


    hidden = hid[...]
    weights = tab[EXPERTS:]
    grads = jnp.concatenate([ref[d][:PAIR] for d in range(EP) for ref in (gg1, gg2)], axis=0)
    mean = jnp.sum(weights * grads, axis=0, keepdims=True)
    grad_logits = weights * (grads - mean)
    grad_moe = gm[...] + dot_tn(grad_logits.astype(BF), rout[...])
    r2 = lax.rsqrt(jnp.mean(hidden * hidden, axis=1, keepdims=True) + EPSILON)
    n = hidden * r2
    u = grad_moe * gain_f[...]
    grad_hidden = cot[...].astype(F32) + r2 * (u - n * jnp.mean(u * n, axis=1, keepdims=True))
    gh[...] = grad_hidden
    branch = grad_hidden.astype(BF)
    ga_s[...] = dot_nt(branch, wb[:, :D]).astype(BF)

    def own_cols(ref, b):
        return ref.at[:, pl.ds(pl.multiple_of(b * 128, 128), 128)]

    heads = [
        remote(own_cols(ga_s, d), go.at[block_rows(e)], (s_go, r_go), k, {"ep": d}) for k, d in enumerate(others)
    ]
    for copy in heads:
        copy.start()
    by_z.push()
    by_y.push()
    go[block_rows(e)] = own_cols(ga_s, e)[...]
    for copy in loads[9:]:
        copy.wait()
    for i in range(4):
        probabilities(i, i + 1)
    lax.fori_loop(4, KEPT, probabilities_later, 0)
    for copy in heads:
        copy.wait_recv()
    ffn = jnp.sum(grad_moe * n, axis=0, keepdims=True)
    logit_rows = jnp.transpose(jnp.concatenate([grad_logits, jnp.zeros((96, TOK), F32)], axis=0)).astype(BF)
    router_rows = dot_tn(m_s[...], logit_rows)
    vec[...] = jnp.zeros((8, D), F32)
    vec[3:4] = ffn
    router_rows = router_rows.reshape(REP, EP, 8, 128)
    for d in range(EP):
        wb[d * 128 : (d + 1) * 128, D:] = router_rows[:, d].reshape(128, 128).astype(BF)
    for cols in range(0, D, 256):
        out_rows = dot_tn(att[...], branch[:, cols : cols + 256]).reshape(REP, EP, 8, 256)
        for d in range(EP):
            wb[d * 128 : (d + 1) * 128, cols : cols + 256] = out_rows[:, d].reshape(128, 256).astype(BF)
    red3.start()
    by_z.stage.relay()
    by_y.stage.relay()
    dk[...] = jnp.zeros((LENGTH, 128), F32)
    dv[...] = jnp.zeros((LENGTH, 128), F32)

    def part(ref, b, size):
        return ref.at[pl.ds(pl.multiple_of(b * size, 8), size)]

    spread_w = [remote(part(wsum, d, 8), wheld.at[r], (s_w, r_w), k, {"rep": d}) for k, d in enumerate(copies)]

    def attend_back(i, n):
        keys, held_rows = spans(i, n)
        rows = block_rows(i)
        grad = stack_heads(go[rows].astype(F32))
        do2 = grad.astype(BF)
        out = a_s[rows].astype(F32)
        settle = lane_row(grad * jnp.concatenate([out, out], axis=0))
        p = p_s[held_rows]
        ds = (p.astype(F32) * (dot_nt(v_s[keys], do2) - settle)).astype(BF)
        dv[keys] += dot(p, do2)
        dk[keys] += dot(ds, q2_s[i])
        dq = dot_tn(k_s[keys], ds)
        grad_q = merge_heads(jnp.transpose(dq)) * HEAD_DIM ** (-0.5)
        grad_q = turn(grad_q.astype(BF).astype(F32), cos_ref[rows], -sin_ref[rows])
        u_s[rows, :128] = grad_q
        cq = column(lax.rsqrt(st[pl.ds(2 * i, 1)] * (1.0 / D) + EPSILON))
        sums[pl.ds(2 * i, 1)] = lane_row(grad_q * gain[:, :128] * lin[rows, :128] * cq)

    def attend_back_later(i, carry):
        attend_back(i, 5)
        return carry

    for i in range(4):
        attend_back(i, i + 1)
    red3.push_opp()
    red3.push_near()
    lax.fori_loop(4, 6, attend_back_later, 0)
    red1.relay()
    red3.relay()
    lax.fori_loop(6, EP, attend_back_later, 0)

    def close(b, carry):
        rows = block_rows(b)
        grad_k, grad_v = dk[rows], dv[rows]
        grad_k = grad_k + pltpu.roll(grad_k, HEAD_DIM, 1)
        grad_v = grad_v + pltpu.roll(grad_v, HEAD_DIM, 1)
        both = jnp.where(first, grad_k, grad_v).astype(BF).astype(F32)
        both = jnp.where(first, turn(both, cos_ref[rows], -sin_ref[rows]), both)
        u_s[rows, 128:] = both
        ck = column(lax.rsqrt(st[pl.ds(2 * b + 1, 1)] * (1.0 / KV) + EPSILON))
        sums[pl.ds(2 * b + 1, 1)] = lane_row(jnp.where(first, both * gain[:, 128:] * lin[rows, 128:] * ck, 0.0))
        return carry

    lax.fori_loop(0, EP, close, 0)
    red1.finish(gm)
    stats = [remote(sums, held.at[e], (s_st, r_st), k, {"ep": d}) for k, d in enumerate(others)]
    for copy in stats:
        copy.start()
    held[e] = sums[...]
    out_s[...] = (hid[...] + gm[...]).astype(BF)
    ends = [pltpu.make_async_copy(out_s, out_o, esem.at[0])]
    ends[0].start()
    red3.finish(wsum)
    for copy in spread_w:
        copy.start()
    wheld[r] = part(wsum, r, 8)[...]
    by_z.turn()
    by_y.turn()
    dwt[...] = jnp.zeros((256, D), F32)
    for copy in stats:
        copy.wait_recv()
    total = held[0]
    for k in range(1, EP):
        total = total + held[k]
    st2[...] = total

    def project_back(b, slot):
        rows = block_rows(b)
        values = x_s[slot, pl.ds(pl.multiple_of(b % 2 * TOK, TOK), TOK)].astype(F32)
        r1 = lax.rsqrt(jnp.mean(values * values, axis=1, keepdims=True) + EPSILON)
        n1 = values * r1
        normed = (n1 * gain_a[...]).astype(BF)
        cq = column(lax.rsqrt(st[pl.ds(2 * b, 1)] * (1.0 / D) + EPSILON))
        ck = column(lax.rsqrt(st[pl.ds(2 * b + 1, 1)] * (1.0 / KV) + EPSILON))
        mq = column(st2[pl.ds(2 * b, 1)] * (1.0 / D))
        mk = column(st2[pl.ds(2 * b + 1, 1)] * (1.0 / KV))
        uq, uk = u_s[rows, :128], u_s[rows, 128:]
        nq = lin[rows, :128] * cq
        nk = lin[rows, 128:] * ck
        gq = cq * (uq * gain[:, :128] - nq * mq)
        gk = jnp.where(first, ck * (uk * gain[:, 128:] - nk * mk), uk)
        glin = jnp.concatenate([gq, gk], axis=1).astype(BF)
        vec[1:2, :128] += jnp.sum(uq * nq, axis=0, keepdims=True)
        vec[2:3, :128] += jnp.sum(uk * nk, axis=0, keepdims=True)
        gn = dot_nt(glin, wcol[...])
        vec[0:1] += jnp.sum(gn * n1, axis=0, keepdims=True)
        dwt[...] += dot_tn(glin, normed)
        return gn.astype(BF)

    def chips(k, carry):
        q = (x + 2 + k - (k // 2) * (2 * k - 1)) % 4
        for step in range(4):

            @pl.when(k == step)
            def _(step=step):
                x_load(step).wait()

        swo[k] = project_back(q * 2 + 1 - c, k % 2)
        red2.swap(k).start()
        snd[k] = project_back(q * 2 + c, k % 2)
        for step in range(2):

            @pl.when(k == step)
            def _(step=step):
                x_load(step + 2).start()

        @pl.when(k == 1)
        def _():
            red2.send_opp()

        @pl.when(k == 2)
        def _():
            red2.send_near()

        return carry

    lax.fori_loop(0, 4, chips, 0)
    red2.merge(3)
    red2.send_far()
    dws[...] = jnp.transpose(dwt[...]).astype(BF)
    spread_d = [remote(part(dws, d, 64), dheld.at[r], (s_d, r_d), k, {"rep": d}) for k, d in enumerate(copies)]
    for copy in spread_d:
        copy.start()
    by_z.last.relay()
    by_y.last.relay()
    dheld[r] = part(dws, r, 64)[...]
    gain_q, gain_k = vec[1:2, :128], vec[2:3, :128]
    low, spread = iota((1, 128), 1) < 32, iota((1, 128), 1) // 32 == 2
    gain_k = jnp.where(low, gain_k, jnp.where(spread, pltpu.roll(gain_k, 32, 1), 0.0))
    vec[1:3, :128] = jnp.zeros((2, 128), F32)
    vec[1:2, pl.ds(pl.multiple_of(e * 128, 128), 128)] = gain_q
    vec[2:3, pl.ds(pl.multiple_of(e * 128, 128), 128)] = gain_k
    spread_v = [remote(vec, vheld.at[e], (s_v, r_v), k, {"ep": d}) for k, d in enumerate(others)]
    for copy in spread_v:
        copy.start()
    vheld[e] = vec[...]
    for copy in spread_v:
        copy.wait_recv()
    total = vheld[0]
    for k in range(1, EP):
        total = total + vheld[k]
    vtot[...] = total
    def lanes_of(d):
        return vtot.at[:, pl.ds(pl.multiple_of(d // 2 * 128, 128), 128)]

    spread_v2 = [remote(lanes_of(d), vheld2.at[r], (s_v2, r_v2), k, {"rep": d}) for k, d in enumerate(copies)]
    for copy in spread_v2:
        copy.start()
    vheld2[r] = lanes_of(r)[...]
    for copy in spread_w:
        copy.wait_recv()
    total = wheld[0]
    for k in range(1, REP):
        total = total + wheld[k]
    go_s[...] = total[:, :D]
    pack_s[0:8] = total[:, D:]
    for copy in spread_d:
        copy.wait_recv()
    total = dheld[0].astype(F32)
    for k in range(1, REP):
        total = total + dheld[k].astype(F32)
    dsum[...] = total
    spread_e = [remote(part(dsum, d, 8), dw_o.at[e], (s_e, r_e), k, {"ep": d}) for k, d in enumerate(others)]
    for copy in spread_e:
        copy.start()
    dw_o[e] = part(dsum, e, 8)[...]
    for copy in spread_v2:
        copy.wait_recv()
    total = vheld2[0]
    for k in range(1, REP):
        total = total + vheld2[k]
    start = r % 2 * 64
    rows_d, lanes_d = iota((128, 128), 0), iota((128, 128), 1)
    eight = jnp.where((rows_d == start + e * 8 + lanes_d) & (lanes_d < 8), 1.0, 0.0)
    four = jnp.where((rows_d == start + e * 4 + lanes_d) & (lanes_d < 4), 1.0, 0.0)

    def pick(sel):
        return jnp.dot(total, sel, preferred_element_type=F32, precision=HIGH)

    eights, fours = pick(eight), pick(four)
    pack_s[8:16] = jnp.where(iota((8, 128), 0) == 2, fours, eights)
    by_z.finish(eg_s, 0)
    by_y.finish(eg_s, FF)
    red2.finish(gm)
    values = x_s[1, pl.ds(pl.multiple_of(c * TOK, TOK), TOK)].astype(F32)
    r1 = lax.rsqrt(jnp.mean(values * values, axis=1, keepdims=True) + EPSILON)
    n1 = values * r1
    z = gm[...] * gain_a[...]
    gh[...] = gh[...] + r1 * (z - n1 * jnp.mean(z * n1, axis=1, keepdims=True))
    for copy in spread_e:
        copy.wait_recv()
    low_lanes = iota((8, 128), 1) < HEAD_DIM
    for d in range(EP):
        gq_s[:, d * 128 : (d + 1) * 128] = dw_o[d][:, :128]
    for d in range(EP // 2):
        even, odd = dw_o[2 * d][:, 128:], dw_o[2 * d + 1][:, 128:]
        gk_s[:, d * 128 : (d + 1) * 128] = jnp.where(low_lanes, even, pltpu.roll(odd, HEAD_DIM, 1))
        gv_s[:, d * 128 : (d + 1) * 128] = jnp.where(low_lanes, pltpu.roll(even, HEAD_DIM, 1), odd)
    pairs = [(gh, ig_o), (gq_s, gq_o), (gk_s, gk_o), (gv_s, gv_o), (go_s, go_o), (pack_s, pack_o), (eg_s, eg_o)]
    for k, (src, dst) in enumerate(pairs):
        ends.append(pltpu.make_async_copy(src, dst, esem.at[1 + k]))
        ends[-1].start()
    for copy in ends:
        copy.wait()
    for copy in heads + stats + spread_w + spread_d + spread_e + spread_v + spread_v2:
        copy.wait_send()


W_OUT = 12
X_ALL = 14


def back(*args):
    def vm(dims, dtype=F32):
        return pltpu.VMEM(dims, dtype)

    held = [vm((2, 2 * TOK, D), BF) if k == X_ALL else vm(a.shape, a.dtype) for k, a in enumerate(args) if k > 1 and k != W_OUT]
    results = [((TOK, D), BF), ((TOK, D), F32), ((8, D), F32), ((8, KV), F32), ((8, KV), F32), ((8, D), F32), ((16, 128), F32)]
    results.append(((PAIR, BLOCK, D), BF))
    landing = [vm((4, TOK, D), BF), vm((2, TOK, D), BF), vm((TOK, D), BF)]
    return comm_call(
        back_kernel,
        "back",
        6,
        [shape(*result) for result in results],
        [ANY] * 23,
        [ANY] * 8,
        held
        + [
            vm((TOK, D)),
            vm((TOK, D), BF),
            vm((LENGTH, 128), BF),
            vm((EP, 2 * TOK, 128), BF),
            vm(((10 + 5 * (KEPT - 4)) * TOK, 2 * TOK), BF),
            vm((LENGTH, 128)),
            vm((LENGTH, 128)),
            vm((LENGTH, 256)),
            vm((16, 256)),
            vm((16, 256)),
            vm((EP, 16, 256)),
            vm((D, WB), BF),
            vm((128, WB)),
            vm((REP, 8, WB)),
            vm((256, D)),
            vm((D, 256), BF),
            vm((REP, 64, 256), BF),
            vm((64, 256)),
            vm((EP, 8, 256)),
            vm((8, D)),
            vm((EP, 8, D)),
            vm((8, D)),
            vm((REP, 8, 128)),
            vm((4, TOK, D), BF),
            vm((4, TOK, D), BF),
        ]
        + landing
        + [vm((4, 128, WB), BF), vm((4, 128, WB), BF), vm((2, 128, WB), BF), vm((128, WB), BF)]
        + [DMA((10,))] * 6
        + [DMA((7,))] * 4
        + [DMA((15,))] * 4
        + [DMA((7,))] * 4
        + [DMA((15,))] * 2
        + [DMA((20,)), DMA((4,)), DMA((4,)), DMA((8,)), DMA((2,))]
        + [vm(*result) for k, result in enumerate(results) if k != 1]
        + grid_scratch() * 2
        + [DMA((12,))] * 4
        + [DMA((4,))] * 2,
        limit=64,
    )(*args)


def finish_kernel(
    xa_in, xb_in, out_in, ig_in, gq_in, gk_in, gv_in, go_in, pack,
    out_o, ig_o, gq_o, gk_o, gv_o, go_o, gr_o, va_o, vq_o, vk_o, vf_o, gate_o, up_o, down_o,
    x_s, gate_s, up_s, down_s, out_s, ig_s, gq_s, gk_s, gv_s, go_s, sem,
):
    loads = [
        pltpu.make_async_copy(xa_in, x_s.at[pl.ds(0, PAIR)], sem.at[9]),
        pltpu.make_async_copy(xb_in, x_s.at[pl.ds(PAIR, PAIR)], sem.at[10]),
    ]
    for load in loads:
        load.start()
    stages = [out_s, ig_s, gq_s, gk_s, gv_s, go_s]
    fetch = [
        pltpu.make_async_copy(src, dst, sem.at[k])
        for k, (src, dst) in enumerate(zip([out_in, ig_in, gq_in, gk_in, gv_in, go_in], stages))
    ]
    copies = [
        pltpu.make_async_copy(src, dst, sem.at[k])
        for k, (src, dst) in enumerate(zip(stages, [out_o, ig_o, gq_o, gk_o, gv_o, go_o]))
    ]
    for copy in fetch:
        copy.start()
    gr_o[...] = pack[0:8, :EXPERTS]
    va_o[...] = pack[8:9, :8]
    vq_o[...] = pack[9:10, :8]
    vk_o[...] = pack[10:11, :4]
    vf_o[...] = pack[11:12, :8]
    for load, copy in zip(fetch, copies):
        load.wait()
        copy.start()
    for load in loads:
        load.wait()
    gate_s[...] = x_s[:, :64, :FF].astype(F32)
    up_s[...] = x_s[:, :64, FF:].astype(F32)
    down_s[...] = x_s[:, 64:].astype(F32)
    pairs = [(gate_s, gate_o), (up_s, up_o), (down_s, down_o)]
    for k, (src, dst) in enumerate(pairs):
        copies.append(pltpu.make_async_copy(src, dst, sem.at[6 + k]))
        copies[-1].start()
    for copy in copies:
        copy.wait()


def finish(xa, xb, out, ig, gq, gk, gv, go, pack):
    gate, down = shape((LOCAL, 64, FF)), shape((LOCAL, 32, D))
    return pl.pallas_call(
        finish_kernel,
        out_shape=[shape(a.shape, a.dtype) for a in (out, ig, gq, gk, gv, go)]
        + [shape((8, EXPERTS)), shape((1, 8)), shape((1, 8)), shape((1, 4)), shape((1, 8)), gate, gate, down],
        in_specs=[ANY] * 8 + [VM],
        out_specs=[ANY] * 6 + [VM] * 5 + [ANY] * 3,
        scratch_shapes=[
            pltpu.VMEM((LOCAL, BLOCK, D), BF),
            pltpu.VMEM(gate.shape, F32),
            pltpu.VMEM(gate.shape, F32),
            pltpu.VMEM(down.shape, F32),
        ]
        + [pltpu.VMEM(a.shape, a.dtype) for a in (out, ig, gq, gk, gv, go)]
        + [
            DMA((11,)),
        ],
        compiler_params=pltpu.CompilerParams(vmem_limit_bytes=62 * MIB),
        name="finish",
    )(xa, xb, out, ig, gq, gk, gv, go, pack)


def body(
    tokens,
    segments,
    routes,
    w_query,
    w_key,
    w_value,
    w_out,
    w_router,
    gain_attn,
    gain_query,
    gain_key,
    gain_ffn,
    w_gate,
    w_up,
    w_down,
    out_grad,
):
    gains = [gain.reshape(1, -1) for gain in (gain_attn, gain_query, gain_key, gain_ffn)]
    cosine, sine = turn_tables()
    (
        x_all, g_all, lin, q, k, v, att, lse, hidden, moe_in, tables, attended, misc, router, whole_out, w_cols,
    ) = front(
        tokens, out_grad, w_query, w_key, w_value, w_out, w_router, *gains, segments, routes.T, cosine, sine
    )
    def over_copies(grads):
        grads = grads.reshape(PAIR, REP * BLOCK, D)
        return lax.psum_scatter(grads, "rep", scatter_dimension=1, tiled=True)

    m_all, tabs, y, z, gg_first, grads = experts_first(moe_in, tables, g_all, w_gate, w_up, w_down)
    sums_first = over_copies(grads)
    grad_moe, mixture, gg_last, grads = experts_last(m_all, tabs, y, z, g_all, w_gate, w_up, w_down)
    *rows, sums_last = back(
        grads.reshape(PAIR, 4, 4, BLOCK, D), mixture, grad_moe, gg_first, gg_last, tables, hidden, moe_in, out_grad, attended, misc, router, whole_out,
        w_cols, x_all, lin, q, k, v, att, lse, cosine, sine,
    )
    out, ig, gq, gk, gv, go, gr, va, vq, vk, vf, gate, up, down = finish(sums_first, sums_last, *rows)
    return out, ig, gq, gk, gv, go, gr, va.reshape(8), vq.reshape(8), vk.reshape(4), vf.reshape(8), gate, up, down


def solution(mesh):
    both = P(("rep", "ep"), None)
    line = P(("rep", "ep"))
    owner = P("ep", None, None)
    kept = P("ep", "rep", None)
    return jax.shard_map(
        body,
        mesh=mesh,
        in_specs=(both, P("rep", None)) + (both,) * 6 + (line,) * 4 + (owner,) * 3 + (both,),
        out_specs=(both,) * 7 + (line,) * 4 + (kept,) * 3,
        check_vma=False,
    )
```

time: 308 us -> 264 us (0.86); the launches traced: 307 us -> 260 us
  Pallas kernels: 271 us -> 245 us
  local copies, waits for them, and re-layouts: 18.1 us -> 0 us
  other arithmetic: 3.43 us -> 0 us
    pallas_call x2 -> x4, Pallas kernels: 191 us -> 171 us  [the longest x1 79.4 us: back(): comm_call(back_kernel, 'back', 6, [shape(*result) for result in results],...]
    slice x8 -> x0, local copies, waits for them, and re-layouts: 8.94 us -> none  [the longest x1 2.13 us: body(): expert_sums[:, :64, FF:]]
    pallas_call x1, Pallas kernels: 80.5 us -> 73.9 us  [front(): comm_call(front_kernel, 'front', 1, [shape((LENGTH, D), BF), shape((LENGT...]
    unnamed x5 -> x0, local copies, waits for them, and re-layouts: 3.35 us -> none
    reshape x4 -> x0, local copies, waits for them, and re-layouts: 3.33 us -> none  [the longest x1 1.37 us: body(): dw_rows[:, :, :128].reshape(8, D)]
  transfers between devices with their start and end apart: 1 -> 1, of which waited for: 0 -> 0; matrix products, arithmetic and copies ran while one was open for 3% -> 0% of each run, Pallas kernels for 31% -> 47%
where the time goes in v5:
time: 264 us; the launch traced here: 260 us
  Pallas kernels  245 us (93%)
  between operations  14.3 us (5%)
    pallas_call x1, Pallas kernels, back(): comm_call(back_kernel, 'back', 6, [shape(*result) for result in results],...  79.4 us
    pallas_call x1, Pallas kernels, front(): comm_call(front_kernel, 'front', 1, [shape((LENGTH, D), BF), shape((LENGT...  73.9 us
    pallas_call x1, Pallas kernels, experts_first(): comm_call(experts_first_kernel, 'experts_first', 2, [shape((LENGTH, D), B...  43.7 us
    pallas_call x1, Pallas kernels, experts_last(): comm_call(experts_last_kernel, 'experts_last', 4, [shape((TOK, D)), shape...  43.7 us
  transfers between devices with their start and end apart: 1, of which 0 were waited for; matrix products, arithmetic and copies ran while one was open for 0% of the time, Pallas kernels for 47%

profile of v5, /device:TPU:1, one launch (start us, length us, event | category | flops | bytes accessed | tf_op | source)
XLA Modules:
  0.0 259.6 jit_solution(2791493488672915805)
XLA Ops:
  7.2 0.0 reduce-scatter.2.cloned.1.call-start
  7.2 73.9 %front.1 = (bf16[2048,1024]{1,0:T(8,128)(2,1)}, bf16[2048,1024]{1,0:T(8,128)(2,1)}, f32[2048,256]{1,0:T(8,128)}, bf16[2048,128]{1,0:T(8,128)(2,1)}, bf16[2048,12...) custom-call(bf16[256,1024]{1,0:T(8,128)(2,1)} %tok.1, ...), custom_call_target="tpu_custom_call" | custom-call | tf_op jit(solution)/shard_map/front/pallas_call | solution.py:692
  81.1 43.7 %experts_first.1 = (bf16[2048,1024]{1,0:T(8,128)(2,1)}, f32[8,64,256]{2,1,0:T(8,128)}, bf16[2,704,1024]{2,1,0:T(8,128)(2,1)}, bf16[2,704,1024]{2,1,0:T(8,128)(2,...) custom-call(bf16[256,1024]{1,0:T(8,128)(2,1)} %get-tuple-element.62.m_in, ...), custom_call_target="tpu_custom_call" | custom-call | tf_op jit(solution)/shard_map/experts_first/pallas_call | solution.py:1011
  124.9 0.0 reduce-scatter.2.cloned.1.call-update
  124.9 43.7 %experts_last.1 = (f32[256,1024]{1,0:T(8,128)}, bf16[2048,1024]{1,0:T(8,128)(2,1)}, f32[8,8,256]{2,1,0:T(8,128)}, bf16[2,16,96,1024]{3,2,1,0:T(8,128)(2,1)}) custom-call(bf16[2048,1024]{1,0:T(8,128)(2,1)} %get-tuple-element.66.m_in, f32[8,64,256]{2,1,0:T(8,128)} %get-tuple-element.67.t_in, bf16[2,704,1024]{2,1,0:T(8,128)(2,1)} %get-tuple-element.68.y_in, ...), custom_call_target="tpu_custom_call" | custom-call | tf_op jit(solution)/shard_map/experts_last/pallas_call | solution.py:1132
  168.6 79.4 %back.1 = (bf16[256,1024]{1,0:T(8,128)(2,1)}, f32[256,1024]{1,0:T(8,128)}, f32[8,1024]{1,0:T(8,128)}, f32[8,512]{1,0:T(8,128)}, f32[8,512]{1,0:T(8,128)}, /*inde...) custom-call(bf16[2,4,4,96,1024]{4,3,2,1,0:T(8,128)(2,1)} %bitcast.12, ...), custom_call_target="tpu_custom_call" | custom-call | tf_op jit(solution)/shard_map/back/pallas_call | solution.py:1526
  248.0 0.0 reduce-scatter.2.cloned.1.call-done.xa_in
  248.0 4.5 %finish.1 = (bf16[256,1024]{1,0:T(8,128)(2,1)}, f32[256,1024]{1,0:T(8,128)}, f32[8,1024]{1,0:T(8,128)}, f32[8,512]{1,0:T(8,128)}, f32[8,512]{1,0:T(8,128)}, /*in...) custom-call(bf16[2,96,1024]{2,1,0:T(8,128)(2,1)} %reduce-scatter.2.c, ...), custom_call_target="tpu_custom_call" | custom-call | tf_op jit(solution)/shard_map/finish/pallas_call | solution.py:1622
Async XLA Ops:
  7.2 240.8 %reduce-scatter.2.cloned.1.call-start = ((), (), s32[]{:S(2)}) async-start(), calls=%async_computation.1 | async-start | bytes 6684672 | tf_op jit(solution)/shard_map/reduce_scatter | solution.py:1670
Sparse Core Ops, SparseCore 0:
  125.0 83.3 reduce-scatter.1

commit v6 on v5

--- a/solution.py
+++ b/solution.py
@@ -353,12 +353,25 @@
 WB = D + 128
 
 
-def column(row):
-    return jnp.transpose(jnp.broadcast_to(row, (128, row.shape[1])))
-
-
-def lane_row(values):
-    return dot_nt(jnp.ones((8, 128), F32), values, precision=HIGH)[0:1]
+def columns(*rows):
+    pad = jnp.zeros((128 - len(rows), rows[0].shape[1]), F32)
+    turned = jnp.transpose(jnp.concatenate(list(rows) + [pad], axis=0))
+    return [turned[:, k : k + 1] for k in range(len(rows))]
+
+
+def row_sums(values, bounds):
+    width = values.shape[1]
+    high = values.astype(BF)
+    low = (values - high.astype(F32)).astype(BF)
+    lane, row = iota((8, width), 1), iota((8, width), 0)
+    chosen = jnp.zeros((8, width), F32)
+    for k, (first, last) in enumerate(bounds):
+        chosen = jnp.where((row == k) & (lane >= first) & (lane < last), 1.0, chosen)
+    chosen = chosen.astype(BF)
+    return dot_nt(jnp.concatenate([chosen, chosen], axis=1), jnp.concatenate([high, low], axis=1))
+
+
+PARTS = ((0, 128), (128, 192))
 
 
 def turn_tables():
@@ -393,7 +406,8 @@
 
 def front_kernel(
     tok, cot, wq, wk, wv, wo_in, router_in, ga_in, gq_in, gk_in, gf_in, seg, rts_in, cos_in, sin_in,
-    x_all, g_all, lin, q_o, k_o, v_o, a_o, lse_o, hid_o, m_o, tab_o, att_o, misc, rout_o, whole, wcol,
+    x_all, g_all, lin_h, q_h, k_h, v_h, a_h, lse_h, hid_h, m_h, tab_h, att_h, misc_h, rout_h, whole_h, wcol_h,
+    lin, q_o, k_o, v_o, a_o, lse_o, hid_o, m_o, tab_o, att_o, misc, rout_o, whole, wcol, hsem,
     x_s, cot_s, tiny, tiny_b, smalls, wsl, wos, wg, wog, wog2, w32, gains_s, cos_ref, sin_ref, sums, held,
     s_tok, r_tok, s_cot, r_cot, s_w, r_w, s_o, r_o, s_st, r_st, s_t, r_t, s_a, r_a, lsem,
 ):
@@ -405,6 +419,13 @@
     gain_a, gain_f, gain = misc.at[0:1], misc.at[1:2], misc.at[2:3, 0:256]
     lo, st = misc.at[8:16, 0:256], misc.at[16:32, 0:256]
     greet([{"ep": d} for d in others] + [{"rep": d} for d in copies])
+    leaving = []
+
+    def leave(*pairs):
+        for src, dst in pairs:
+            leaving.append(pltpu.make_async_copy(src, dst, hsem.at[len(leaving)]))
+            leaving[-1].start()
+
     misc[...] = jnp.zeros((32, D), F32)
 
     tiny[...] = jnp.zeros((16, 128), F32)
@@ -464,6 +485,8 @@
     for copy in spread_w:
         copy.start()
     tokens.forward_half()
+    tables[2].wait()
+    grads.start()
     tokens.forward_rest()
 
     routed = rts_in[...]
@@ -471,7 +494,7 @@
     for k in range(TOP):
         hit = jnp.where(iota((EXPERTS, TOK), 0) == routed[k : k + 1], 1.0, hit)
     before = jnp.where(iota((TOK, TOK), 0) < iota((TOK, TOK), 1), 1.0, 0.0).astype(BF)
-    tab_o[:EXPERTS] = jnp.where(hit > 0.0, dot(hit.astype(BF), before), -1.0)
+    slots = jnp.where(hit > 0.0, dot(hit.astype(BF), before), -1.0)
     segs = jnp.concatenate([seg[:, b * TOK : (b + 1) * TOK] for b in range(EP)], axis=0)
     opening = jnp.zeros((EP, TOK), F32)
     for value in range(2):
@@ -519,6 +542,7 @@
     gain[:, :128] = spread_gain(128, 8, 8, e * 16)
     gain[:, 128:] = jnp.where(iota((1, 128), 1) < HEAD_DIM, key_part, 1.0)
 
+    leave((wcol, wcol_h), (rout_o, rout_h))
     tokens.first[4].wait_recv()
     tokens.own.wait()
 
@@ -546,9 +570,9 @@
         normed = (values * r1 * gain_a[...]).astype(BF)
         out = dot(normed, wcol[...])
         lin[rows] = out
-        sq = out * out
-        sums[pl.ds(2 * b, 1)] = lane_row(sq[:, :128])
-        sums[pl.ds(2 * b + 1, 1)] = lane_row(jnp.where(first, sq[:, 128:], 0.0))
+        both = row_sums(out * out, PARTS)
+        sums[pl.ds(2 * b, 1)] = both[0:1]
+        sums[pl.ds(2 * b + 1, 1)] = both[1:2]
         return carry
 
     lax.fori_loop(0, EP, project, 0)
@@ -558,7 +582,7 @@
     held[e] = sums[...]
     keep = pltpu.make_async_copy(x_s, x_all, lsem.at[4])
     keep.start()
-    for copy in tables:
+    for copy in tables[:2]:
         copy.wait()
     for copy in stats:
         copy.wait_recv()
@@ -566,12 +590,15 @@
     for k in range(1, EP):
         total = total + held[k]
     st[...] = total
-    grads.start()
+    grads.forward_half()
+    leave((lin, lin_h), (misc, misc_h))
 
     def prepare(b, carry):
         rows = block_rows(b)
-        cq = column(lax.rsqrt(st[pl.ds(2 * b, 1)] * (1.0 / D) + EPSILON))
-        ck = column(lax.rsqrt(st[pl.ds(2 * b + 1, 1)] * (1.0 / KV) + EPSILON))
+        cq, ck = columns(
+            lax.rsqrt(st[pl.ds(2 * b, 1)] * (1.0 / D) + EPSILON),
+            lax.rsqrt(st[pl.ds(2 * b + 1, 1)] * (1.0 / KV) + EPSILON),
+        )
         cosine, sine = cos_ref[rows], sin_ref[rows]
         q_o[rows] = turn(lin[rows, :128] * cq * gain[:, :128], cosine, sine).astype(BF)
         kv = lin[rows, 128:]
@@ -581,7 +608,8 @@
         v_o[rows] = jnp.where(first, other, kv).astype(BF)
         return carry
 
-    lax.fori_loop(0, EP, prepare, 0)
+    lax.fori_loop(0, EP, prepare, 0, unroll=2)
+    leave((q_o, q_h), (k_o, k_h), (v_o, v_h))
 
     def heads(i, source):
         cols = pl.ds(pl.multiple_of(source * 128, 128), 128)
@@ -598,7 +626,7 @@
         rows = block_rows(i)
         past = (n - 1) * TOK
         q2 = stack_heads(q_o[rows].astype(F32) * HEAD_DIM ** (-0.5)).astype(BF)
-        lo_col = column(lo[pl.ds(i, 1)])[:, :1]
+        (lo_col,) = columns(lo[pl.ds(i, 1)])
         low = jnp.concatenate([lo_col, lo_col], axis=0)
         own_key = (iota((2 * TOK, TOK), 1) + i * TOK).astype(F32)
         query = (iota((2 * TOK, TOK), 0) % TOK + i * TOK).astype(F32)
@@ -633,52 +661,62 @@
 
         @pl.when(i == 5)
         def _():
-            grads.forward_rest()
+            grads.fwd_right.wait_recv()
+            grads.fwd_left.wait_recv()
+            grads.to_peer[2].start()
 
         return carry
 
     for i in range(4):
         attend_block(i, i + 1)
-    grads.forward_half()
+    grads.forward_rest()
     for copy in spread_o:
         copy.wait_recv()
     other_half.start()
     lax.fori_loop(4, EP, later, 0)
 
+    leave((a_o, a_h), (lse_o, lse_h))
     other_half.wait_recv()
-    grads.fwd_right.wait_recv()
-    grads.fwd_left.wait_recv()
-    grads.to_peer[2].start()
 
     def unpack_out(b, carry):
-        rows = pl.ds(pl.multiple_of(b * 8, 8), 8)
-        for half, held_half in ((c, wog), (1 - c, wog2)):
-            tile = held_half[b // EP, b % EP].astype(F32)
-            for j in range(4):
-                w32[rows, pl.ds(pl.multiple_of(half * 512 + j * 128, 128), 128)] = tile[j * 8 : (j + 1) * 8]
+        for d in range(EP):
+            rows = pl.ds(pl.multiple_of(b * 64 + d * 8, 8), 8)
+            for half, held_half in ((c, wog), (1 - c, wog2)):
+                tile = held_half[b, d].astype(F32)
+                for j in range(4):
+                    w32[rows, pl.ds(pl.multiple_of(half * 512 + j * 128, 128), 128)] = tile[j * 8 : (j + 1) * 8]
         return carry
 
-    lax.fori_loop(0, 128, unpack_out, 0)
+    lax.fori_loop(0, REP, unpack_out, 0)
     whole[...] = w32[...].astype(BF)
+    leave((whole, whole_h))
     for d in others:
         heads(d, d).wait_recv()
+    leave((att_o, att_h))
 
     hidden = x_s[block_rows(e)].astype(F32) + dot(att_o[...], whole[...])
     hid_o[...] = hidden
     r2 = lax.rsqrt(jnp.mean(hidden * hidden, axis=1, keepdims=True) + EPSILON)
     moe_in = (hidden * r2 * gain_f[...]).astype(BF)
     m_o[...] = moe_in
+    leave((hid_o, hid_h), (m_o, m_h))
     logits = dot_nt(rout_o[...], moe_in)
     chosen = hit > 0.0
     logits = jnp.where(chosen, logits, MASKED)
     raised = jnp.where(chosen, jnp.exp(logits - jnp.max(logits, axis=0, keepdims=True)), 0.0)
-    tab_o[EXPERTS:] = raised / jnp.sum(raised, axis=0, keepdims=True)
+    gates = raised / jnp.sum(raised, axis=0, keepdims=True)
+    for d in range(EP):
+        part = slice(d * LOCAL, (d + 1) * LOCAL)
+        tab_o[d] = jnp.concatenate([slots[part], gates[part]], axis=0)
+    leave((tab_o, tab_h))
 
     grads.first[4].wait_recv()
     for copy in grads.to_peer:
         copy.wait_recv()
     grads.own.wait()
     keep.wait()
+    for copy in leaving:
+        copy.wait()
     for d in others:
         heads(d, d).wait_send()
     for ring in (tokens, grads):
@@ -689,31 +727,34 @@
 
 
 def front(*args):
+    results = [
+        shape((LENGTH, D), BF),
+        shape((LENGTH, D), BF),
+        shape((LENGTH, 256)),
+        shape((LENGTH, 128), BF),
+        shape((LENGTH, 128), BF),
+        shape((LENGTH, 128), BF),
+        shape((LENGTH, 128), BF),
+        shape((EP, 8, 2 * TOK)),
+        shape((TOK, D)),
+        shape((TOK, D), BF),
+        shape((EP, 2 * LOCAL, TOK)),
+        shape((TOK, D), BF),
+        shape((32, D)),
+        shape((EXPERTS, D), BF),
+        shape((D, D), BF),
+        shape((D, 256), BF),
+    ]
     return comm_call(
         front_kernel,
         "front",
         1,
-        [
-            shape((LENGTH, D), BF),
-            shape((LENGTH, D), BF),
-            shape((LENGTH, 256)),
-            shape((LENGTH, 128), BF),
-            shape((LENGTH, 128), BF),
-            shape((LENGTH, 128), BF),
-            shape((LENGTH, 128), BF),
-            shape((EP, 8, 2 * TOK)),
-            shape((TOK, D)),
-            shape((TOK, D), BF),
-            shape((2 * EXPERTS, TOK)),
-            shape((TOK, D), BF),
-            shape((32, D)),
-            shape((EXPERTS, D), BF),
-            shape((D, D), BF),
-            shape((D, 256), BF),
-        ],
+        results,
         [ANY, ANY] + [VM] * 11 + [ANY, ANY],
-        [ANY, ANY] + [VM] * 14,
-        [
+        [ANY] * len(results),
+        [pltpu.VMEM(a.shape, a.dtype) for a in results[2:]]
+        + [
+            DMA((14,)),
             pltpu.VMEM((LENGTH, D), BF),
             pltpu.VMEM((TOK, D), BF),
             pltpu.VMEM((16, 128), F32),
@@ -793,11 +834,17 @@
         for copy in self.opp:
             copy.start()
 
-    def send_near(self):
+    def near_right(self):
         self.merge(2)
         self.near[0].start()
+
+    def near_left(self):
         self.merge(1)
         self.near[1].start()
+
+    def send_near(self):
+        self.near_right()
+        self.near_left()
 
     def send_far(self):
         self.opp[0].wait_recv()
@@ -836,7 +883,7 @@
 
 
 def expert_hits(tab, e, n, q):
-    row = pl.ds(e * LOCAL + n, 1)
+    row = slice(n, n + 1)
     second = tab[2 * q + 1, row]
     slots = jnp.concatenate([tab[2 * q, row], jnp.where(second >= 0.0, second + CAP, -1.0)], axis=1)
     return iota((CHIP, 2 * TOK), 0).astype(F32) == slots
@@ -854,7 +901,7 @@
     c_both = dot(chosen, g_ref[chip_tokens(q)]).astype(BF)
     for n in range(PAIR):
         part = slice(n * CHIP, (n + 1) * CHIP)
-        row = pl.ds(EXPERTS + e * LOCAL + start + n, 1)
+        row = slice(LOCAL + start + n, LOCAL + start + n + 1)
         gates = jnp.concatenate([tab[2 * q, row], tab[2 * q + 1, row]], axis=1)
         weight = jnp.sum(jnp.where(hits[n], gates, 0.0), axis=1, keepdims=True)
         a, cot = a_both[part], c_both[part]
@@ -910,11 +957,11 @@
     others = ep_others(e)
     greet([{"ep": d} for d in others])
     ring = RingGather(m_in, m_ref, (s_m, r_m), lsem.at[0])
-    tables = [remote(t_in, tab.at[e], (s_t, r_t), k, {"ep": d}) for k, d in enumerate(others)]
+    tables = [remote(t_in.at[d], tab.at[e], (s_t, r_t), k, {"ep": d}) for k, d in enumerate(others)]
     for copy in tables:
         copy.start()
     ring.start()
-    own = pltpu.make_async_copy(t_in, tab.at[e], lsem.at[1])
+    own = pltpu.make_async_copy(t_in.at[e], tab.at[e], lsem.at[1])
     loads = load_weights(0, wg_in, wu_in, wd_in, wgu, wd, wsem)
     cots = [
         pltpu.make_async_copy(g_in.at[chip_tokens(q)], g_ref.at[chip_tokens(q)], gsem.at[k])
@@ -992,7 +1039,7 @@
 def pair_scratch():
     return [
         pltpu.VMEM((LENGTH, D), BF),
-        pltpu.VMEM((EP, 2 * EXPERTS, TOK), F32),
+        pltpu.VMEM((EP, 2 * LOCAL, TOK), F32),
         pltpu.VMEM((LENGTH, D), BF),
         pltpu.VMEM((PAIR, D, 2 * FF), BF),
         pltpu.VMEM((PAIR, FF, D), BF),
@@ -1014,7 +1061,7 @@
         2,
         [
             shape((LENGTH, D), BF),
-            shape((EP, 2 * EXPERTS, TOK)),
+            shape((EP, 2 * LOCAL, TOK)),
             shape((PAIR, ROWS, D), BF),
             shape((PAIR, ROWS, D), BF),
             shape((EP, 8, TOK)),
@@ -1033,7 +1080,7 @@
 def experts_last_kernel(
     m_in, t_in, y_in, z_in, g_in, wg_in, wu_in, wd_in, gm_o, mix_o, gg_o, eg_o,
     m_ref, tab, g_ref, wgu, wd, a_s, act_s, gp_s, dgu_s, y_s, z_s, ggt, eg,
-    y_f, z_f, gm, swo, snd, pc, rcv, hop, mix,
+    y_f, z_f, gm, swo, snd, pc, rcv, hop, mix_z, mix_y,
     s_r, r_r, s_g, r_g, lsem, wsem, gsem, msem, esem, osem,
 ):
     e, x, c = place()
@@ -1074,22 +1121,28 @@
 
         q = (x + 2 + k - (k // 2) * (2 * k - 1)) % 4
         expert_chip(q, e, 2, tab, m_ref, g_ref, wgu, wd, a_s, act_s, gp_s, dgu_s, y_s, z_s, ggt)
-        mix[...] = combine(q, z_f, z_s)
-        swo[k] = mix[pl.ds(pl.multiple_of((1 - c) * TOK, TOK), TOK)]
+
+        @pl.when(k == 2)
+        def _():
+            red.near_left()
+
+        @pl.when(k == 3)
+        def _():
+            red.near_right()
+
+        mix_z[...] = combine(q, z_f, z_s)
+        swo[k] = mix_z[pl.ds(pl.multiple_of((1 - c) * TOK, TOK), TOK)]
         red.swap(k).start()
-        snd[k] = mix[pl.ds(pl.multiple_of(c * TOK, TOK), TOK)]
-
-        @pl.when(k == 1)
+        snd[k] = mix_z[pl.ds(pl.multiple_of(c * TOK, TOK), TOK)]
+
+        @pl.when(k == 0)
         def _():
             red.send_opp()
 
-        @pl.when(k == 3)
-        def _():
-            red.send_near()
-
         return carry
 
     lax.fori_loop(0, 4, chips, 0)
+    red.send_far()
     gates, own_gates = send_gates(ggt, gg_o, e, (s_g, r_g), lsem.at[3])
     for copy in gates + [own_gates]:
         copy.start()
@@ -1101,25 +1154,26 @@
         states[-1].start()
 
     grads(0)
+    grads(1)
     red.merge(3)
-    red.send_far()
-    grads(1)
     firsts[1].wait()
 
     def mixture(q, carry):
+        values = combine(q, y_f, y_s)
+
         @pl.when(q > 0)
         def _():
-            pltpu.make_async_copy(mix, mix_o.at[chip_tokens(q)], osem).wait()
-
-        mix[...] = combine(q, y_f, y_s)
-        pltpu.make_async_copy(mix, mix_o.at[chip_tokens(q)], osem).start()
+            pltpu.make_async_copy(mix_y, mix_o.at[chip_tokens(q)], osem).wait()
+
+        mix_y[...] = values
+        pltpu.make_async_copy(mix_y, mix_o.at[chip_tokens(q)], osem).start()
         return carry
 
     lax.fori_loop(0, 4, mixture, 0)
     red.finish(gm)
     last = pltpu.make_async_copy(gm, gm_o, lsem.at[4])
     last.start()
-    pltpu.make_async_copy(mix, mix_o.at[chip_tokens(3)], osem).wait()
+    pltpu.make_async_copy(mix_y, mix_o.at[chip_tokens(3)], osem).wait()
     for copy in states + [own_gates, last]:
         copy.wait()
     for copy in gates:
@@ -1152,6 +1206,7 @@
             pltpu.VMEM((2, TOK, D), BF),
             pltpu.VMEM((TOK, D), BF),
             pltpu.VMEM((2 * TOK, D), BF),
+            pltpu.VMEM((2 * TOK, D), BF),
         ]
         + [DMA((10,))] * 2
         + [DMA((7,))] * 2
@@ -1187,9 +1242,6 @@
     red3 = RingReduce(wb, 128, pc3, snd3, rcv3, hop3, (s_3, r_3), l_3)
     by_z = GridReduce(True, eg_in, 0, za, zb, zc, zd, ze, zf, (s_z, r_z), l_z)
     by_y = GridReduce(False, eg_in, FF, ya, yb, yc, yd, ye, yf, (s_y, r_y), l_y)
-    for copy in by_z.load + by_y.load:
-        copy.start()
-    red1.start()
     loads = [
         pltpu.make_async_copy(src, dst, lsem.at[k])
         for k, (src, dst) in enumerate(
@@ -1206,8 +1258,9 @@
     def x_load(k):
         return pltpu.make_async_copy(x_in.at[chip_tokens(chips_order[k])], x_s.at[k % 2], xsem.at[k % 2])
 
-    for copy in loads + [x_load(0), x_load(1)]:
-        copy.start()
+    for copy in loads + [x_load(0), x_load(1)] + by_z.load + by_y.load:
+        copy.start()
+    red1.start()
     for copy in loads[:9]:
         copy.wait()
 
@@ -1249,7 +1302,7 @@
 
 
     hidden = hid[...]
-    weights = tab[EXPERTS:]
+    weights = jnp.concatenate([tab[d][LOCAL:] for d in range(EP)], axis=0)
     grads = jnp.concatenate([ref[d][:PAIR] for d in range(EP) for ref in (gg1, gg2)], axis=0)
     mean = jnp.sum(weights * grads, axis=0, keepdims=True)
     grad_logits = weights * (grads - mean)
@@ -1273,11 +1326,13 @@
     by_z.push()
     by_y.push()
     go[block_rows(e)] = own_cols(ga_s, e)[...]
-    for copy in loads[9:]:
+    for copy in loads[9:12]:
         copy.wait()
     for i in range(4):
         probabilities(i, i + 1)
     lax.fori_loop(4, KEPT, probabilities_later, 0)
+    for copy in loads[12:]:
+        copy.wait()
     for copy in heads:
         copy.wait_recv()
     ffn = jnp.sum(grad_moe * n, axis=0, keepdims=True)
@@ -1309,17 +1364,13 @@
         grad = stack_heads(go[rows].astype(F32))
         do2 = grad.astype(BF)
         out = a_s[rows].astype(F32)
-        settle = lane_row(grad * jnp.concatenate([out, out], axis=0))
+        settle = row_sums(grad * jnp.concatenate([out, out], axis=0), ((0, 128),))[0:1]
         p = p_s[held_rows]
         ds = (p.astype(F32) * (dot_nt(v_s[keys], do2) - settle)).astype(BF)
         dv[keys] += dot(p, do2)
         dk[keys] += dot(ds, q2_s[i])
         dq = dot_tn(k_s[keys], ds)
-        grad_q = merge_heads(jnp.transpose(dq)) * HEAD_DIM ** (-0.5)
-        grad_q = turn(grad_q.astype(BF).astype(F32), cos_ref[rows], -sin_ref[rows])
-        u_s[rows, :128] = grad_q
-        cq = column(lax.rsqrt(st[pl.ds(2 * i, 1)] * (1.0 / D) + EPSILON))
-        sums[pl.ds(2 * i, 1)] = lane_row(grad_q * gain[:, :128] * lin[rows, :128] * cq)
+        u_s[rows, :128] = merge_heads(jnp.transpose(dq)) * HEAD_DIM ** (-0.5)
 
     def attend_back_later(i, carry):
         attend_back(i, 5)
@@ -1329,10 +1380,10 @@
         attend_back(i, i + 1)
     red3.push_opp()
     red3.push_near()
-    lax.fori_loop(4, 6, attend_back_later, 0)
+    lax.fori_loop(4, 6, attend_back_later, 0, unroll=True)
     red1.relay()
     red3.relay()
-    lax.fori_loop(6, EP, attend_back_later, 0)
+    lax.fori_loop(6, EP, attend_back_later, 0, unroll=True)
 
     def close(b, carry):
         rows = block_rows(b)
@@ -1340,13 +1391,22 @@
         grad_k = grad_k + pltpu.roll(grad_k, HEAD_DIM, 1)
         grad_v = grad_v + pltpu.roll(grad_v, HEAD_DIM, 1)
         both = jnp.where(first, grad_k, grad_v).astype(BF).astype(F32)
-        both = jnp.where(first, turn(both, cos_ref[rows], -sin_ref[rows]), both)
+        cosine, sine = cos_ref[rows], -sin_ref[rows]
+        both = jnp.where(first, turn(both, cosine, sine), both)
+        grad_q = turn(u_s[rows, :128].astype(BF).astype(F32), cosine, sine)
+        u_s[rows, :128] = grad_q
         u_s[rows, 128:] = both
-        ck = column(lax.rsqrt(st[pl.ds(2 * b + 1, 1)] * (1.0 / KV) + EPSILON))
-        sums[pl.ds(2 * b + 1, 1)] = lane_row(jnp.where(first, both * gain[:, 128:] * lin[rows, 128:] * ck, 0.0))
+        cq, ck = columns(
+            lax.rsqrt(st[pl.ds(2 * b, 1)] * (1.0 / D) + EPSILON),
+            lax.rsqrt(st[pl.ds(2 * b + 1, 1)] * (1.0 / KV) + EPSILON),
+        )
+        products = jnp.concatenate([grad_q * cq, both * ck], axis=1) * gain[...] * lin[rows]
+        pair = row_sums(products, PARTS)
+        sums[pl.ds(2 * b, 1)] = pair[0:1]
+        sums[pl.ds(2 * b + 1, 1)] = pair[1:2]
         return carry
 
-    lax.fori_loop(0, EP, close, 0)
+    lax.fori_loop(0, EP, close, 0, unroll=2)
     red1.finish(gm)
     stats = [remote(sums, held.at[e], (s_st, r_st), k, {"ep": d}) for k, d in enumerate(others)]
     for copy in stats:
@@ -1375,10 +1435,12 @@
         r1 = lax.rsqrt(jnp.mean(values * values, axis=1, keepdims=True) + EPSILON)
         n1 = values * r1
         normed = (n1 * gain_a[...]).astype(BF)
-        cq = column(lax.rsqrt(st[pl.ds(2 * b, 1)] * (1.0 / D) + EPSILON))
-        ck = column(lax.rsqrt(st[pl.ds(2 * b + 1, 1)] * (1.0 / KV) + EPSILON))
-        mq = column(st2[pl.ds(2 * b, 1)] * (1.0 / D))
-        mk = column(st2[pl.ds(2 * b + 1, 1)] * (1.0 / KV))
+        cq, ck, mq, mk = columns(
+            lax.rsqrt(st[pl.ds(2 * b, 1)] * (1.0 / D) + EPSILON),
+            lax.rsqrt(st[pl.ds(2 * b + 1, 1)] * (1.0 / KV) + EPSILON),
+            st2[pl.ds(2 * b, 1)] * (1.0 / D),
+            st2[pl.ds(2 * b + 1, 1)] * (1.0 / KV),
+        )
         uq, uk = u_s[rows, :128], u_s[rows, 128:]
         nq = lin[rows, :128] * cq
         nk = lin[rows, 128:] * ck
@@ -1402,6 +1464,19 @@
 
         swo[k] = project_back(q * 2 + 1 - c, k % 2)
         red2.swap(k).start()
+
+        @pl.when(k == 1)
+        def _():
+            red2.send_opp()
+
+        @pl.when(k == 2)
+        def _():
+            red2.near_left()
+
+        @pl.when(k == 3)
+        def _():
+            red2.near_right()
+
         snd[k] = project_back(q * 2 + c, k % 2)
         for step in range(2):
 
@@ -1409,25 +1484,13 @@
             def _(step=step):
                 x_load(step + 2).start()
 
-        @pl.when(k == 1)
-        def _():
-            red2.send_opp()
-
-        @pl.when(k == 2)
-        def _():
-            red2.send_near()
-
         return carry
 
     lax.fori_loop(0, 4, chips, 0)
-    red2.merge(3)
-    red2.send_far()
     dws[...] = jnp.transpose(dwt[...]).astype(BF)
     spread_d = [remote(part(dws, d, 64), dheld.at[r], (s_d, r_d), k, {"rep": d}) for k, d in enumerate(copies)]
     for copy in spread_d:
         copy.start()
-    by_z.last.relay()
-    by_y.last.relay()
     dheld[r] = part(dws, r, 64)[...]
     gain_q, gain_k = vec[1:2, :128], vec[2:3, :128]
     low, spread = iota((1, 128), 1) < 32, iota((1, 128), 1) // 32 == 2
@@ -1439,6 +1502,10 @@
     for copy in spread_v:
         copy.start()
     vheld[e] = vec[...]
+    red2.merge(3)
+    red2.send_far()
+    by_z.last.relay()
+    by_y.last.relay()
     for copy in spread_v:
         copy.wait_recv()
     total = vheld[0]

time: 264 us -> 250 us (0.947)
  Pallas kernels: 245 us -> 231 us
    pallas_call x1, Pallas kernels: 73.9 us -> 64.7 us  [front(): comm_call(front_kernel, 'front', 1, results, [ANY, ANY] + [VM] * 11 + [AN...]
    pallas_call x1, Pallas kernels: 79.4 us -> 75.7 us  [back(): comm_call(back_kernel, 'back', 6, [shape(*result) for result in results],...]
  transfers between devices with their start and end apart: 1 -> 1, of which waited for: 0 -> 0; matrix products, arithmetic and copies ran while one was open for 0% -> 0% of each run, Pallas kernels for 47% -> 49%
where the time goes in v6:
time: 250 us; the launch traced here: 245 us
  Pallas kernels  231 us (92%)
  between operations  14.3 us (6%)
    pallas_call x1, Pallas kernels, back(): comm_call(back_kernel, 'back', 6, [shape(*result) for result in results],...  75.7 us
    pallas_call x1, Pallas kernels, front(): comm_call(front_kernel, 'front', 1, results, [ANY, ANY] + [VM] * 11 + [AN...  64.7 us
    pallas_call x1, Pallas kernels, experts_last(): comm_call(experts_last_kernel, 'experts_last', 4, [shape((TOK, D)), shape...  43.5 us
    pallas_call x1, Pallas kernels, experts_first(): comm_call(experts_first_kernel, 'experts_first', 2, [shape((LENGTH, D), B...  42.3 us
  transfers between devices with their start and end apart: 1, of which 0 were waited for; matrix products, arithmetic and copies ran while one was open for 0% of the time, Pallas kernels for 49%

profile of v6, /device:TPU:1, one launch (start us, length us, event | category | flops | bytes accessed | tf_op | source)
XLA Modules:
  0.0 245.2 jit_solution(14529841978067570253)
XLA Ops:
  7.2 0.0 reduce-scatter.2.cloned.1.call-start
  7.2 64.7 %front.1 = (bf16[2048,1024]{1,0:T(8,128)(2,1)}, bf16[2048,1024]{1,0:T(8,128)(2,1)}, f32[2048,256]{1,0:T(8,128)}, bf16[2048,128]{1,0:T(8,128)(2,1)}, bf16[2048,12...) custom-call(bf16[256,1024]{1,0:T(8,128)(2,1)} %tok.1, ...), custom_call_target="tpu_custom_call" | custom-call | tf_op jit(solution)/shard_map/front/pallas_call | solution.py:748
  71.9 42.3 %experts_first.1 = (bf16[2048,1024]{1,0:T(8,128)(2,1)}, f32[8,8,256]{2,1,0:T(8,128)}, bf16[2,704,1024]{2,1,0:T(8,128)(2,1)}, bf16[2,704,1024]{2,1,0:T(8,128)(2,1...) custom-call(bf16[256,1024]{1,0:T(8,128)(2,1)} %get-tuple-element.62.m_in, ...), custom_call_target="tpu_custom_call" | custom-call | tf_op jit(solution)/shard_map/experts_first/pallas_call | solution.py:1058
  114.2 0.0 reduce-scatter.2.cloned.1.call-update
  114.3 43.5 %experts_last.1 = (f32[256,1024]{1,0:T(8,128)}, bf16[2048,1024]{1,0:T(8,128)(2,1)}, f32[8,8,256]{2,1,0:T(8,128)}, bf16[2,16,96,1024]{3,2,1,0:T(8,128)(2,1)}) custom-call(bf16[2048,1024]{1,0:T(8,128)(2,1)} %get-tuple-element.66.m_in, f32[8,8,256]{2,1,0:T(8,128)} %get-tuple-element.67.t_in, bf16[2,704,1024]{2,1,0:T(8,128)(2,1)} %get-tuple-element.68.y_in, ...), custom_call_target="tpu_custom_call" | custom-call | tf_op jit(solution)/shard_map/experts_last/pallas_call | solution.py:1186
  157.7 75.7 %back.1 = (bf16[256,1024]{1,0:T(8,128)(2,1)}, f32[256,1024]{1,0:T(8,128)}, f32[8,1024]{1,0:T(8,128)}, f32[8,512]{1,0:T(8,128)}, f32[8,512]{1,0:T(8,128)}, /*inde...) custom-call(bf16[2,4,4,96,1024]{4,3,2,1,0:T(8,128)(2,1)} %bitcast.12, ...), custom_call_target="tpu_custom_call" | custom-call | tf_op jit(solution)/shard_map/back/pallas_call | solution.py:1593
  233.5 0.0 reduce-scatter.2.cloned.1.call-done.xa_in
  233.5 4.5 %finish.1 = (bf16[256,1024]{1,0:T(8,128)(2,1)}, f32[256,1024]{1,0:T(8,128)}, f32[8,1024]{1,0:T(8,128)}, f32[8,512]{1,0:T(8,128)}, f32[8,512]{1,0:T(8,128)}, /*in...) custom-call(bf16[2,96,1024]{2,1,0:T(8,128)(2,1)} %reduce-scatter.2.c, ...), custom_call_target="tpu_custom_call" | custom-call | tf_op jit(solution)/shard_map/finish/pallas_call | solution.py:1689
Async XLA Ops:
  7.2 226.3 %reduce-scatter.2.cloned.1.call-start = ((), (), s32[]{:S(2)}) async-start(), calls=%async_computation.1 | async-start | bytes 6684672 | tf_op jit(solution)/shard_map/reduce_scatter | solution.py:1737
Sparse Core Ops, SparseCore 0:
  114.4 82.2 reduce-scatter.1

commit v7 on v6

--- a/solution.py
+++ b/solution.py
@@ -59,10 +59,12 @@
     return {"ep": x * 2 + c}
 
 
-def greet(devices):
+def greet(devices, local_work=None):
     barrier = pltpu.get_barrier_semaphore()
     for device in devices:
         pl.semaphore_signal(barrier, inc=1, device_id=device, device_id_type=MESH)
+    if local_work is not None:
+        local_work()
     pl.semaphore_wait(barrier, len(devices))
 
 
@@ -408,7 +410,7 @@
     tok, cot, wq, wk, wv, wo_in, router_in, ga_in, gq_in, gk_in, gf_in, seg, rts_in, cos_in, sin_in,
     x_all, g_all, lin_h, q_h, k_h, v_h, a_h, lse_h, hid_h, m_h, tab_h, att_h, misc_h, rout_h, whole_h, wcol_h,
     lin, q_o, k_o, v_o, a_o, lse_o, hid_o, m_o, tab_o, att_o, misc, rout_o, whole, wcol, hsem,
-    x_s, cot_s, tiny, tiny_b, smalls, wsl, wos, wg, wog, wog2, w32, gains_s, cos_ref, sin_ref, sums, held,
+    x_s, cot_s, tiny, tiny_b, smalls, wsl, wo_f, wo_r, wg, w32, gains_s, cos_ref, sin_ref, sums, held,
     s_tok, r_tok, s_cot, r_cot, s_w, r_w, s_o, r_o, s_st, r_st, s_t, r_t, s_a, r_a, lsem,
 ):
     r = lax.axis_index("rep")
@@ -418,7 +420,6 @@
     first = iota((TOK, 128), 1) < HEAD_DIM
     gain_a, gain_f, gain = misc.at[0:1], misc.at[1:2], misc.at[2:3, 0:256]
     lo, st = misc.at[8:16, 0:256], misc.at[16:32, 0:256]
-    greet([{"ep": d} for d in others] + [{"rep": d} for d in copies])
     leaving = []
 
     def leave(*pairs):
@@ -426,54 +427,63 @@
             leaving.append(pltpu.make_async_copy(src, dst, hsem.at[len(leaving)]))
             leaving[-1].start()
 
-    misc[...] = jnp.zeros((32, D), F32)
-
-    tiny[...] = jnp.zeros((16, 128), F32)
-    tiny[0:8, 0:EXPERTS] = router_in[...].astype(F32)
-    for lane, ref in ((0, ga_in), (8, gq_in), (16, gk_in), (20, gf_in)):
-        tiny[8:9, lane : lane + ref.shape[1]] = ref[...].astype(F32)
-    tiny_b[...] = tiny[...].astype(BF)
-    low_lanes = iota((8, 128), 1) < HEAD_DIM
-    for d in range(EP):
-        k_t = wk[:, (d // 2) * 128 : (d // 2 + 1) * 128].astype(F32)
-        v_t = wv[:, (d // 2) * 128 : (d // 2 + 1) * 128].astype(F32)
-        if d % 2:
-            k_t = pltpu.roll(k_t, HEAD_DIM, 1)
-        else:
-            v_t = pltpu.roll(v_t, HEAD_DIM, 1)
-        q_t = wq[:, d * 128 : (d + 1) * 128].astype(F32)
-        wsl[d] = jnp.concatenate([q_t, jnp.where(low_lanes, k_t, v_t)], axis=0).astype(BF)
-    for half in range(2):
-        wos[half] = jnp.concatenate(
-            [wo_in[:, j * 128 : (j + 1) * 128].astype(F32) for j in range(half * 4, half * 4 + 4)], axis=0
-        ).astype(BF)
-
-    def cols_of(b):
-        return wg.at[r, pl.ds(pl.multiple_of(b * 16, 16), 16)]
-
-    stage_w = [remote(wsl.at[d], cols_of(e), (s_w, r_w), k, {"ep": d}) for k, d in enumerate(others)]
-    stage_t = [remote(tiny_b, smalls.at[e], (s_t, r_t), k, {"ep": d}) for k, d in enumerate(others)]
-    stage_o = [remote(wos.at[d % 2], wog.at[r, e], (s_o, r_o), k, {"ep": d}) for k, d in enumerate(others)]
-    spread_w = [remote(wg.at[r], wg.at[r], (s_w, r_w), 7 + k, {"rep": d}) for k, d in enumerate(copies)]
-    spread_o = [remote(wog.at[r], wog.at[r], (s_o, r_o), 7 + k, {"rep": d}) for k, d in enumerate(copies)]
-    other_half = remote(wog, wog2, (s_o, r_o), 22, ep_device(x, 1 - c))
-    tokens = RingGather(tok, x_s, (s_tok, r_tok), lsem.at[0])
-    grads = RingGather(cot_s, g_all, (s_cot, r_cot), lsem.at[1])
-    for copy in stage_w + stage_t:
-        copy.start()
-    tokens.start()
-    for copy in stage_o:
-        copy.start()
     tables = [
         pltpu.make_async_copy(cos_in, cos_ref, lsem.at[2]),
         pltpu.make_async_copy(sin_in, sin_ref, lsem.at[3]),
         pltpu.make_async_copy(cot, cot_s, lsem.at[5]),
     ]
-    for copy in tables:
+
+    def prepare_tiles():
+        misc[...] = jnp.zeros((32, D), F32)
+
+        tiny[...] = jnp.zeros((16, 128), F32)
+        tiny[0:8, 0:EXPERTS] = router_in[...].astype(F32)
+        for lane, ref in ((0, ga_in), (8, gq_in), (16, gk_in), (20, gf_in)):
+            tiny[8:9, lane : lane + ref.shape[1]] = ref[...].astype(F32)
+        tiny_b[...] = tiny[...].astype(BF)
+        low_lanes = iota((8, 128), 1) < HEAD_DIM
+        for d in range(EP):
+            k_t = wk[:, (d // 2) * 128 : (d // 2 + 1) * 128].astype(F32)
+            v_t = wv[:, (d // 2) * 128 : (d // 2 + 1) * 128].astype(F32)
+            if d % 2:
+                k_t = pltpu.roll(k_t, HEAD_DIM, 1)
+            else:
+                v_t = pltpu.roll(v_t, HEAD_DIM, 1)
+            q_t = wq[:, d * 128 : (d + 1) * 128].astype(F32)
+            wsl[d] = jnp.concatenate([q_t, jnp.where(low_lanes, k_t, v_t)], axis=0).astype(BF)
+        wo_f[...] = wo_in[...].astype(F32)
+        for copy in tables:
+            copy.start()
+
+    greet([{"ep": d} for d in others] + [{"rep": d} for d in copies], prepare_tiles)
+    half_cols = pl.ds(pl.multiple_of(c * 512, 512), 512)
+    other_cols = pl.ds(pl.multiple_of((1 - c) * 512, 512), 512)
+    peer = ep_device(x, 1 - c)
+
+    def whole_rows(start, size):
+        return whole.at[pl.ds(pl.multiple_of(start, 16), size), half_cols]
+
+    pairing = remote(wo_f.at[:, other_cols], wo_r, (s_o, r_o), 19, peer)
+    mine = whole_rows(r * 64 + x * 16, 16)
+    stage_o = [remote(mine, mine, (s_o, r_o), k, ep_device((x + 1 + k) % 4, c)) for k in range(3)]
+    mine = whole_rows(r * 64, 64)
+    spread_o = [remote(mine, mine, (s_o, r_o), 3 + k, {"rep": d}) for k, d in enumerate(copies)]
+    mine = whole_rows(0, D)
+    other_half = remote(mine, mine, (s_o, r_o), 18, peer)
+
+    def cols_of(b):
+        return wg.at[r, pl.ds(pl.multiple_of(b * 16, 16), 16)]
+
+    stage_w = [remote(wsl.at[d], cols_of(e), (s_w, r_w), k, {"ep": d}) for k, d in enumerate(others)]
+    stage_t = [remote(tiny_b, smalls.at[e], (s_t, r_t), k, {"ep": d}) for k, d in enumerate(others)]
+    spread_w = [remote(wg.at[r], wg.at[r], (s_w, r_w), 7 + k, {"rep": d}) for k, d in enumerate(copies)]
+    tokens = RingGather(tok, x_s, (s_tok, r_tok), lsem.at[0])
+    grads = RingGather(cot_s, g_all, (s_cot, r_cot), lsem.at[1])
+    for copy in stage_w + stage_t + [pairing]:
         copy.start()
+    tokens.start()
     cols_of(e)[...] = wsl[e]
     smalls[e] = tiny_b[...]
-    wog[r, e] = wos[c]
     for copy in stage_w + stage_t:
         copy.wait_recv()
     router_tiles = [
@@ -483,6 +493,12 @@
     gain_rows = [smalls[d][8:9].astype(F32) for d in range(EP)]
     wg[r, 128:160] = jnp.concatenate(router_tiles + gain_rows + [jnp.zeros((8, 128), F32)], axis=0).astype(BF)
     for copy in spread_w:
+        copy.start()
+    pairing.wait_recv()
+    own_half, peer_half = wo_f[:, half_cols], wo_r[...]
+    upper, lower = jnp.where(c == 0, own_half, peer_half), jnp.where(c == 0, peer_half, own_half)
+    whole[pl.ds(pl.multiple_of(r * 64 + x * 16, 16), 16), half_cols] = jnp.concatenate([upper, lower], axis=0).astype(BF)
+    for copy in stage_o:
         copy.start()
     tokens.forward_half()
     tables[2].wait()
@@ -664,8 +680,13 @@
             grads.fwd_right.wait_recv()
             grads.fwd_left.wait_recv()
             grads.to_peer[2].start()
+            other_half.wait_recv()
+            whole_out.start()
 
         return carry
+
+    whole_out = pltpu.make_async_copy(whole, whole_h, hsem.at[len(leaving)])
+    leaving.append(whole_out)
 
     for i in range(4):
         attend_block(i, i + 1)
@@ -676,20 +697,6 @@
     lax.fori_loop(4, EP, later, 0)
 
     leave((a_o, a_h), (lse_o, lse_h))
-    other_half.wait_recv()
-
-    def unpack_out(b, carry):
-        for d in range(EP):
-            rows = pl.ds(pl.multiple_of(b * 64 + d * 8, 8), 8)
-            for half, held_half in ((c, wog), (1 - c, wog2)):
-                tile = held_half[b, d].astype(F32)
-                for j in range(4):
-                    w32[rows, pl.ds(pl.multiple_of(half * 512 + j * 128, 128), 128)] = tile[j * 8 : (j + 1) * 8]
-        return carry
-
-    lax.fori_loop(0, REP, unpack_out, 0)
-    whole[...] = w32[...].astype(BF)
-    leave((whole, whole_h))
     for d in others:
         heads(d, d).wait_recv()
     leave((att_o, att_h))
@@ -722,7 +729,7 @@
     for ring in (tokens, grads):
         for copy in ring.first + [ring.fwd_right, ring.fwd_left] + ring.to_peer:
             copy.wait_send()
-    for copy in stage_w + stage_t + stage_o + spread_w + spread_o + stats + [other_half]:
+    for copy in stage_w + stage_t + stage_o + spread_w + spread_o + stats + [other_half, pairing]:
         copy.wait_send()
 
 
@@ -761,11 +768,10 @@
             pltpu.VMEM((16, 128), BF),
             pltpu.VMEM((EP, 16, 128), BF),
             pltpu.VMEM((EP, 16, 128), BF),
-            pltpu.VMEM((2, 32, 128), BF),
+            pltpu.VMEM((8, D), F32),
+            pltpu.VMEM((8, 512), F32),
             pltpu.VMEM((REP, 160, 128), BF),
-            pltpu.VMEM((REP, EP, 32, 128), BF),
-            pltpu.VMEM((REP, EP, 32, 128), BF),
-            pltpu.VMEM((D, D), F32),
+            pltpu.VMEM((D, 384), F32),
             pltpu.VMEM((128, 128), F32),
             pltpu.VMEM((LENGTH, 128), F32),
             pltpu.VMEM((LENGTH, 128), F32),
@@ -929,9 +935,15 @@
         ggt[2 * q + 1, n : n + 1] = gg_row[:, TOK:]
 
 
-def expert_grads(n, a_s, act_s, gp_s, dgu_s, eg):
-    eg[n, :, :64] = dot_tn(a_s[n], dgu_s[n]).astype(BF).reshape(REP, 64, D)
-    eg[n, :, 64:] = dot_tn(act_s[n], gp_s[n]).astype(BF).reshape(REP, 32, D)
+def expert_grads(n, a_s, act_s, gp_s, dgu_s, eg, eg_o, sems):
+    copies = []
+    for k, (first, size) in enumerate(((0, 64), (64, 32))):
+        left, right = ((a_s, dgu_s), (act_s, gp_s))[k]
+        eg[n, :, first : first + size] = dot_tn(left[n], right[n]).astype(BF).reshape(REP, size, D)
+        some = pl.ds(first, size)
+        copies.append(pltpu.make_async_copy(eg.at[n, :, some], eg_o.at[n, :, some], sems.at[2 * n + k]))
+        copies[-1].start()
+    return copies
 
 
 def load_weights(start, wg_in, wu_in, wd_in, wgu, wd, sems):
@@ -951,26 +963,36 @@
 def experts_first_kernel(
     m_in, t_in, g_in, wg_in, wu_in, wd_in, m_o, tab_o, y_o, z_o, gg_o, eg_o,
     m_ref, tab, g_ref, wgu, wd, a_s, act_s, gp_s, dgu_s, y_s, z_s, ggt, eg,
-    s_m, r_m, s_t, r_t, s_g, r_g, lsem, wsem, gsem, esem,
+    s_m, r_m, s_t, r_t, s_g, r_g, lsem, wsem, gsem, esem, ksem,
 ):
     e, x, c = place()
     others = ep_others(e)
-    greet([{"ep": d} for d in others])
     ring = RingGather(m_in, m_ref, (s_m, r_m), lsem.at[0])
     tables = [remote(t_in.at[d], tab.at[e], (s_t, r_t), k, {"ep": d}) for k, d in enumerate(others)]
-    for copy in tables:
-        copy.start()
-    ring.start()
     own = pltpu.make_async_copy(t_in.at[e], tab.at[e], lsem.at[1])
     loads = load_weights(0, wg_in, wu_in, wd_in, wgu, wd, wsem)
     cots = [
         pltpu.make_async_copy(g_in.at[chip_tokens(q)], g_ref.at[chip_tokens(q)], gsem.at[k])
         for k, q in enumerate([x, (x + 1) % 4, (x + 3) % 4, (x + 2) % 4])
     ]
-    for copy in [own] + loads + cots:
+
+    def fetch():
+        for copy in [own] + loads + cots:
+            copy.start()
+        ggt[...] = jnp.zeros((EP, 8, TOK), F32)
+
+    greet([{"ep": d} for d in others], fetch)
+    for copy in tables:
         copy.start()
-    ggt[...] = jnp.zeros((EP, 8, TOK), F32)
-    kept = pltpu.make_async_copy(m_ref, m_o, lsem.at[2])
+    ring.start()
+
+    def keep(k, q):
+        rows = chip_rows(q)
+        return [
+            pltpu.make_async_copy(m_ref.at[chip_tokens(q)], m_o.at[chip_tokens(q)], ksem.at[0, k]),
+            pltpu.make_async_copy(y_s.at[:, rows], y_o.at[:, rows], ksem.at[1, k]),
+            pltpu.make_async_copy(z_s.at[:, rows], z_o.at[:, rows], ksem.at[2, k]),
+        ]
 
     def chips(k, carry):
         @pl.when(k == 0)
@@ -1009,26 +1031,23 @@
         def _():
             ring.to_peer[2].wait_recv()
             cots[3].wait()
-            kept.start()
 
         q = (x + k + k // 2 - 2 * (k // 3)) % 4
         expert_chip(q, e, 0, tab, m_ref, g_ref, wgu, wd, a_s, act_s, gp_s, dgu_s, y_s, z_s, ggt)
+        for copy in keep(k, q):
+            copy.start()
         return carry
 
     lax.fori_loop(0, 4, chips, 0)
     gates, own_gates = send_gates(ggt, gg_o, e, (s_g, r_g), lsem.at[3])
-    states = [
-        pltpu.make_async_copy(tab, tab_o, lsem.at[4]),
-        pltpu.make_async_copy(y_s, y_o, lsem.at[5]),
-        pltpu.make_async_copy(z_s, z_o, lsem.at[6]),
-    ]
+    states = [pltpu.make_async_copy(tab, tab_o, lsem.at[2])]
     for copy in gates + [own_gates] + states:
         copy.start()
     for n in range(PAIR):
-        expert_grads(n, a_s, act_s, gp_s, dgu_s, eg)
-        states.append(pltpu.make_async_copy(eg.at[n], eg_o.at[n], esem.at[n]))
-        states[-1].start()
-    for copy in states + [kept, own_gates]:
+        states += expert_grads(n, a_s, act_s, gp_s, dgu_s, eg, eg_o, esem)
+    for k, q in enumerate([x, (x + 1) % 4, (x + 3) % 4, (x + 2) % 4]):
+        states += keep(k, q)
+    for copy in states + [own_gates]:
         copy.wait()
     for copy in gates:
         copy.wait_recv()
@@ -1072,7 +1091,7 @@
         pair_scratch()
         + [DMA((10,))] * 2
         + [DMA((7,))] * 4
-        + [DMA((7,)), DMA((3,)), DMA((4,)), DMA((2,))],
+        + [DMA((4,)), DMA((3,)), DMA((4,)), DMA((4,)), DMA((3, 4))],
         limit=60,
     )(m, t, g_all, wg, wu, wd)
 
@@ -1116,8 +1135,6 @@
             def _(step=step):
                 for copy in rows[step]:
                     copy.wait()
-                if step == 0:
-                    firsts[0].wait()
 
         q = (x + 2 + k - (k // 2) * (2 * k - 1)) % 4
         expert_chip(q, e, 2, tab, m_ref, g_ref, wgu, wd, a_s, act_s, gp_s, dgu_s, y_s, z_s, ggt)
@@ -1129,6 +1146,10 @@
         @pl.when(k == 3)
         def _():
             red.near_right()
+
+        @pl.when(k == 0)
+        def _():
+            firsts[0].wait()
 
         mix_z[...] = combine(q, z_f, z_s)
         swo[k] = mix_z[pl.ds(pl.multiple_of((1 - c) * TOK, TOK), TOK)]
@@ -1147,14 +1168,8 @@
     for copy in gates + [own_gates]:
         copy.start()
     states = []
-
-    def grads(n):
-        expert_grads(n, a_s, act_s, gp_s, dgu_s, eg)
-        states.append(pltpu.make_async_copy(eg.at[n], eg_o.at[n], esem.at[n]))
-        states[-1].start()
-
-    grads(0)
-    grads(1)
+    for n in range(PAIR):
+        states += expert_grads(n, a_s, act_s, gp_s, dgu_s, eg, eg_o, esem)
     red.merge(3)
     firsts[1].wait()
 
@@ -1210,7 +1225,7 @@
         ]
         + [DMA((10,))] * 2
         + [DMA((7,))] * 2
-        + [DMA((5,)), DMA((3,)), DMA((4,)), DMA((4,)), DMA((2,)), DMA(())],
+        + [DMA((5,)), DMA((3,)), DMA((4,)), DMA((4,)), DMA((4,)), DMA(())],
         limit=63,
     )(m, t, y, z, g_all, wg, wu, wd)
 
@@ -1222,9 +1237,9 @@
     eg_in, mix_in, gm_in, gg1_in, gg2_in, tab_in, hid_in, m_in, cot_in, att_in, misc_in, rout_in, whole_in, wcol_in, x_in, lin_in,
     q_in, k_in, v_in, a_in, lse_in, cos_in, sin_in,
     out_o, ig_o, gq_o, gk_o, gv_o, go_o, pack_o, eg_o,
-    gm, gg1, gg2, tab, hid, m_s, cot, att, misc, rout, wcol, x_s, lin, q_s, k_s, v_s, a_s, lse, cos_ref, sin_ref,
+    gm, gg1, gg2, tab, hid, cot, misc, rout, wcol, x_s, lin, q_s, k_s, v_s, a_s, lse, cos_ref, sin_ref,
     gh, ga_s, go, q2_s, p_s, dk, dv, u_s, sums, st2, held, wb, wsum, wheld,
-    dwt, dws, dheld, dsum, dw_o, vec, vheld, vtot, vheld2, swo, snd, pc1, rcv1, hop1, snd3, pc3, rcv3, hop3,
+    dwt, dws, dheld, dsum, dw_o, vec, vheld, vtot, vheld2, swo, snd, pc1, rcv1, hop1, rcv2, snd3, pc3, rcv3, hop3,
     s_1, r_1, s_2, r_2, s_3, r_3, s_go, r_go, s_st, r_st, s_w, r_w, s_d, r_d, s_e, r_e, s_v, r_v, s_v2, r_v2, lsem, l_1, l_3, esem, xsem,
     out_s, gq_s, gk_s, gv_s, go_s, pack_s, eg_s,
     za, zb, zc, zd, ze, zf, ya, yb, yc, yd, ye, yf, s_z, r_z, s_y, r_y, l_z, l_y,
@@ -1236,9 +1251,8 @@
     first = iota((TOK, 128), 1) < HEAD_DIM
     gain_a, gain_f, gain = misc.at[0:1], misc.at[1:2], misc.at[2:3, 0:256]
     lo, st = misc.at[8:16, 0:256], misc.at[16:32, 0:256]
-    greet([{"ep": d} for d in others] + [{"rep": d} for d in copies])
     red1 = RingReduce(mix_in, TOK, pc1, snd, rcv1, hop1, (s_1, r_1), l_1)
-    red2 = ChipReduce(TOK, swo, snd, pc1, rcv1, hop1, (s_2, r_2))
+    red2 = ChipReduce(TOK, swo, snd, pc1, rcv2, hop1, (s_2, r_2))
     red3 = RingReduce(wb, 128, pc3, snd3, rcv3, hop3, (s_3, r_3), l_3)
     by_z = GridReduce(True, eg_in, 0, za, zb, zc, zd, ze, zf, (s_z, r_z), l_z)
     by_y = GridReduce(False, eg_in, FF, ya, yb, yc, yd, ye, yf, (s_y, r_y), l_y)
@@ -1248,7 +1262,7 @@
             [
                 (misc_in, misc), (gm_in, gm), (gg1_in, gg1), (gg2_in, gg2), (tab_in, tab), (hid_in, hid),
                 (cot_in, cot), (rout_in, rout), (whole_in, wb.at[:, pl.ds(0, D)]), (q_in, q_s), (k_in, k_s), (lse_in, lse),
-                (m_in, m_s), (att_in, att), (v_in, v_s), (a_in, a_s), (cos_in, cos_ref), (sin_in, sin_ref),
+                (m_in, rcv2.at[0]), (att_in, rcv2.at[1]), (v_in, v_s), (a_in, a_s), (cos_in, cos_ref), (sin_in, sin_ref),
                 (lin_in, lin), (wcol_in, wcol),
             ]
         )
@@ -1258,8 +1272,12 @@
     def x_load(k):
         return pltpu.make_async_copy(x_in.at[chip_tokens(chips_order[k])], x_s.at[k % 2], xsem.at[k % 2])
 
-    for copy in loads + [x_load(0), x_load(1)] + by_z.load + by_y.load:
-        copy.start()
+
+    def fetch():
+        for copy in loads + [x_load(0), x_load(1)] + by_z.load + by_y.load:
+            copy.start()
+
+    greet([{"ep": d} for d in others] + [{"rep": d} for d in copies], fetch)
     red1.start()
     for copy in loads[:9]:
         copy.wait()
@@ -1337,14 +1355,14 @@
         copy.wait_recv()
     ffn = jnp.sum(grad_moe * n, axis=0, keepdims=True)
     logit_rows = jnp.transpose(jnp.concatenate([grad_logits, jnp.zeros((96, TOK), F32)], axis=0)).astype(BF)
-    router_rows = dot_tn(m_s[...], logit_rows)
+    router_rows = dot_tn(rcv2[0], logit_rows)
     vec[...] = jnp.zeros((8, D), F32)
     vec[3:4] = ffn
     router_rows = router_rows.reshape(REP, EP, 8, 128)
     for d in range(EP):
         wb[d * 128 : (d + 1) * 128, D:] = router_rows[:, d].reshape(128, 128).astype(BF)
     for cols in range(0, D, 256):
-        out_rows = dot_tn(att[...], branch[:, cols : cols + 256]).reshape(REP, EP, 8, 256)
+        out_rows = dot_tn(rcv2[1], branch[:, cols : cols + 256]).reshape(REP, EP, 8, 256)
         for d in range(EP):
             wb[d * 128 : (d + 1) * 128, cols : cols + 256] = out_rows[:, d].reshape(128, 256).astype(BF)
     red3.start()
@@ -1407,11 +1425,11 @@
         return carry
 
     lax.fori_loop(0, EP, close, 0, unroll=2)
-    red1.finish(gm)
     stats = [remote(sums, held.at[e], (s_st, r_st), k, {"ep": d}) for k, d in enumerate(others)]
     for copy in stats:
         copy.start()
     held[e] = sums[...]
+    red1.finish(gm)
     out_s[...] = (hid[...] + gm[...]).astype(BF)
     ends = [pltpu.make_async_copy(out_s, out_o, esem.at[0])]
     ends[0].start()
@@ -1553,12 +1571,6 @@
     pack_s[8:16] = jnp.where(iota((8, 128), 0) == 2, fours, eights)
     by_z.finish(eg_s, 0)
     by_y.finish(eg_s, FF)
-    red2.finish(gm)
-    values = x_s[1, pl.ds(pl.multiple_of(c * TOK, TOK), TOK)].astype(F32)
-    r1 = lax.rsqrt(jnp.mean(values * values, axis=1, keepdims=True) + EPSILON)
-    n1 = values * r1
-    z = gm[...] * gain_a[...]
-    gh[...] = gh[...] + r1 * (z - n1 * jnp.mean(z * n1, axis=1, keepdims=True))
     for copy in spread_e:
         copy.wait_recv()
     low_lanes = iota((8, 128), 1) < HEAD_DIM
@@ -1568,17 +1580,25 @@
         even, odd = dw_o[2 * d][:, 128:], dw_o[2 * d + 1][:, 128:]
         gk_s[:, d * 128 : (d + 1) * 128] = jnp.where(low_lanes, even, pltpu.roll(odd, HEAD_DIM, 1))
         gv_s[:, d * 128 : (d + 1) * 128] = jnp.where(low_lanes, pltpu.roll(even, HEAD_DIM, 1), odd)
-    pairs = [(gh, ig_o), (gq_s, gq_o), (gk_s, gk_o), (gv_s, gv_o), (go_s, go_o), (pack_s, pack_o), (eg_s, eg_o)]
+    pairs = [(gq_s, gq_o), (gk_s, gk_o), (gv_s, gv_o), (go_s, go_o), (pack_s, pack_o), (eg_s, eg_o)]
     for k, (src, dst) in enumerate(pairs):
         ends.append(pltpu.make_async_copy(src, dst, esem.at[1 + k]))
         ends[-1].start()
+    red2.finish(gm)
+    values = x_s[1, pl.ds(pl.multiple_of(c * TOK, TOK), TOK)].astype(F32)
+    r1 = lax.rsqrt(jnp.mean(values * values, axis=1, keepdims=True) + EPSILON)
+    n1 = values * r1
+    z = gm[...] * gain_a[...]
+    gh[...] = gh[...] + r1 * (z - n1 * jnp.mean(z * n1, axis=1, keepdims=True))
+    ends.append(pltpu.make_async_copy(gh, ig_o, esem.at[7]))
+    ends[-1].start()
     for copy in ends:
         copy.wait()
     for copy in heads + stats + spread_w + spread_d + spread_e + spread_v + spread_v2:
         copy.wait_send()
 
 
-W_OUT = 12
+ELSEWHERE = (7, 9, 12)
 X_ALL = 14
 
 
@@ -1586,7 +1606,7 @@
     def vm(dims, dtype=F32):
         return pltpu.VMEM(dims, dtype)
 
-    held = [vm((2, 2 * TOK, D), BF) if k == X_ALL else vm(a.shape, a.dtype) for k, a in enumerate(args) if k > 1 and k != W_OUT]
+    held = [vm((2, 2 * TOK, D), BF) if k == X_ALL else vm(a.shape, a.dtype) for k, a in enumerate(args) if k > 1 and k not in ELSEWHERE]
     results = [((TOK, D), BF), ((TOK, D), F32), ((8, D), F32), ((8, KV), F32), ((8, KV), F32), ((8, D), F32), ((16, 128), F32)]
     results.append(((PAIR, BLOCK, D), BF))
     landing = [vm((4, TOK, D), BF), vm((2, TOK, D), BF), vm((TOK, D), BF)]
@@ -1626,6 +1646,7 @@
             vm((4, TOK, D), BF),
         ]
         + landing
+        + [vm((2, TOK, D), BF)]
         + [vm((4, 128, WB), BF), vm((4, 128, WB), BF), vm((2, 128, WB), BF), vm((128, WB), BF)]
         + [DMA((10,))] * 6
         + [DMA((7,))] * 4
@@ -1642,9 +1663,9 @@
 
 
 def finish_kernel(
-    xa_in, xb_in, out_in, ig_in, gq_in, gk_in, gv_in, go_in, pack,
+    xa_in, xb_in, out_in, ig_in, gq_in, gk_in, gv_in, go_in, pack_in,
     out_o, ig_o, gq_o, gk_o, gv_o, go_o, gr_o, va_o, vq_o, vk_o, vf_o, gate_o, up_o, down_o,
-    x_s, gate_s, up_s, down_s, out_s, ig_s, gq_s, gk_s, gv_s, go_s, sem,
+    x_s, gate_s, up_s, down_s, out_s, ig_s, gq_s, gk_s, gv_s, go_s, pack, gr_s, va_s, vq_s, vk_s, vf_s, sem,
 ):
     loads = [
         pltpu.make_async_copy(xa_in, x_s.at[pl.ds(0, PAIR)], sem.at[9]),
@@ -1661,13 +1682,9 @@
         pltpu.make_async_copy(src, dst, sem.at[k])
         for k, (src, dst) in enumerate(zip(stages, [out_o, ig_o, gq_o, gk_o, gv_o, go_o]))
     ]
-    for copy in fetch:
+    load_pack = pltpu.make_async_copy(pack_in, pack, sem.at[11])
+    for copy in fetch + [load_pack]:
         copy.start()
-    gr_o[...] = pack[0:8, :EXPERTS]
-    va_o[...] = pack[8:9, :8]
-    vq_o[...] = pack[9:10, :8]
-    vk_o[...] = pack[10:11, :4]
-    vf_o[...] = pack[11:12, :8]
     for load, copy in zip(fetch, copies):
         load.wait()
         copy.start()
@@ -1676,8 +1693,16 @@
     gate_s[...] = x_s[:, :64, :FF].astype(F32)
     up_s[...] = x_s[:, :64, FF:].astype(F32)
     down_s[...] = x_s[:, 64:].astype(F32)
+    load_pack.wait()
+    gr_s[...] = pack[0:8, :EXPERTS]
+    va_s[...] = pack[8:9, :8]
+    vq_s[...] = pack[9:10, :8]
+    vk_s[...] = pack[10:11, :4]
+    vf_s[...] = pack[11:12, :8]
     pairs = [(gate_s, gate_o), (up_s, up_o), (down_s, down_o)]
+    pairs += [(gr_s, gr_o), (va_s, va_o), (vq_s, vq_o), (vk_s, vk_o), (vf_s, vf_o)]
     for k, (src, dst) in enumerate(pairs):
+        k = k if k < 5 else k + 1
         copies.append(pltpu.make_async_copy(src, dst, sem.at[6 + k]))
         copies[-1].start()
     for copy in copies:
@@ -1690,17 +1715,18 @@
         finish_kernel,
         out_shape=[shape(a.shape, a.dtype) for a in (out, ig, gq, gk, gv, go)]
         + [shape((8, EXPERTS)), shape((1, 8)), shape((1, 8)), shape((1, 4)), shape((1, 8)), gate, gate, down],
-        in_specs=[ANY] * 8 + [VM],
-        out_specs=[ANY] * 6 + [VM] * 5 + [ANY] * 3,
+        in_specs=[ANY] * 9,
+        out_specs=[ANY] * 14,
         scratch_shapes=[
             pltpu.VMEM((LOCAL, BLOCK, D), BF),
             pltpu.VMEM(gate.shape, F32),
             pltpu.VMEM(gate.shape, F32),
             pltpu.VMEM(down.shape, F32),
         ]
-        + [pltpu.VMEM(a.shape, a.dtype) for a in (out, ig, gq, gk, gv, go)]
+        + [pltpu.VMEM(a.shape, a.dtype) for a in (out, ig, gq, gk, gv, go, pack)]
+        + [pltpu.VMEM(dims, F32) for dims in ((8, EXPERTS), (1, 8), (1, 8), (1, 4), (1, 8))]
         + [
-            DMA((11,)),
+            DMA((16,)),
         ],
         compiler_params=pltpu.CompilerParams(vmem_limit_bytes=62 * MIB),
         name="finish",

time: 250 us -> 249 us (level)
  the two profiles are of different devices: /device:TPU:1 before, /device:TPU:33 now
where the time goes in v7:
time: 249 us; the launch traced here: 244 us
  Pallas kernels  229 us (92%)
  between operations  14.3 us (6%)
    pallas_call x1, Pallas kernels, back(): comm_call(back_kernel, 'back', 6, [shape(*result) for result in results],...  78.4 us
    pallas_call x1, Pallas kernels, front(): comm_call(front_kernel, 'front', 1, results, [ANY, ANY] + [VM] * 11 + [AN...  62.8 us
    pallas_call x1, Pallas kernels, experts_last(): comm_call(experts_last_kernel, 'experts_last', 4, [shape((TOK, D)), shape...  43.1 us
    pallas_call x1, Pallas kernels, experts_first(): comm_call(experts_first_kernel, 'experts_first', 2, [shape((LENGTH, D), B...  41.7 us
  transfers between devices with their start and end apart: 1, of which 0 were waited for; matrix products, arithmetic and copies ran while one was open for 0% of the time, Pallas kernels for 50%

profile of v7, /device:TPU:33, one launch (start us, length us, event | category | flops | bytes accessed | tf_op | source)
XLA Modules:
  0.0 243.6 jit_solution(10539078482717506558)
XLA Ops:
  7.2 0.0 reduce-scatter.2.cloned.1.call-start
  7.2 62.8 %front.1 = (bf16[2048,1024]{1,0:T(8,128)(2,1)}, bf16[2048,1024]{1,0:T(8,128)(2,1)}, f32[2048,256]{1,0:T(8,128)}, bf16[2048,128]{1,0:T(8,128)(2,1)}, bf16[2048,12...) custom-call(bf16[256,1024]{1,0:T(8,128)(2,1)} %tok.1, ...), custom_call_target="tpu_custom_call" | custom-call | tf_op jit(solution)/shard_map/front/pallas_call | solution.py:755
  70.0 41.7 %experts_first.1 = (bf16[2048,1024]{1,0:T(8,128)(2,1)}, f32[8,8,256]{2,1,0:T(8,128)}, bf16[2,704,1024]{2,1,0:T(8,128)(2,1)}, bf16[2,704,1024]{2,1,0:T(8,128)(2,1...) custom-call(bf16[256,1024]{1,0:T(8,128)(2,1)} %get-tuple-element.62.m_in, ...), custom_call_target="tpu_custom_call" | custom-call | tf_op jit(solution)/shard_map/experts_first/pallas_call | solution.py:1077
  111.8 0.0 reduce-scatter.2.cloned.1.call-update
  111.8 43.1 %experts_last.1 = (f32[256,1024]{1,0:T(8,128)}, bf16[2048,1024]{1,0:T(8,128)(2,1)}, f32[8,8,256]{2,1,0:T(8,128)}, bf16[2,16,96,1024]{3,2,1,0:T(8,128)(2,1)}) custom-call(bf16[2048,1024]{1,0:T(8,128)(2,1)} %get-tuple-element.66.m_in, f32[8,8,256]{2,1,0:T(8,128)} %get-tuple-element.67.t_in, bf16[2,704,1024]{2,1,0:T(8,128)(2,1)} %get-tuple-element.68.y_in, ...), custom_call_target="tpu_custom_call" | custom-call | tf_op jit(solution)/shard_map/experts_last/pallas_call | solution.py:1201
  154.9 78.4 %back.1 = (bf16[256,1024]{1,0:T(8,128)(2,1)}, f32[256,1024]{1,0:T(8,128)}, f32[8,1024]{1,0:T(8,128)}, f32[8,512]{1,0:T(8,128)}, f32[8,512]{1,0:T(8,128)}, /*inde...) custom-call(bf16[2,4,4,96,1024]{4,3,2,1,0:T(8,128)(2,1)} %bitcast.12, ...), custom_call_target="tpu_custom_call" | custom-call | tf_op jit(solution)/shard_map/back/pallas_call | solution.py:1613
  233.3 0.0 reduce-scatter.2.cloned.1.call-done.xa_in
  233.3 3.3 %finish.1 = (bf16[256,1024]{1,0:T(8,128)(2,1)}, f32[256,1024]{1,0:T(8,128)}, f32[8,1024]{1,0:T(8,128)}, f32[8,512]{1,0:T(8,128)}, f32[8,512]{1,0:T(8,128)}, /*in...) custom-call(bf16[2,96,1024]{2,1,0:T(8,128)(2,1)} %reduce-scatter.2.c, ...), custom_call_target="tpu_custom_call" | custom-call | tf_op jit(solution)/shard_map/finish/pallas_call | solution.py:1714
Async XLA Ops:
  7.2 226.1 %reduce-scatter.2.cloned.1.call-start = ((), (), s32[]{:S(2)}) async-start(), calls=%async_computation.1 | async-start | bytes 6684672 | tf_op jit(solution)/shard_map/reduce_scatter | solution.py:1763
Sparse Core Ops, SparseCore 0:
  111.9 82.9 reduce-scatter.1

commit v8 on v7

--- a/solution.py
+++ b/solution.py
@@ -852,13 +852,19 @@
         self.near_right()
         self.near_left()
 
-    def send_far(self):
+    def far_right(self):
         self.opp[0].wait_recv()
         self.merge_hop(2, 0)
         self.far[0].start()
+
+    def far_left(self):
         self.opp[1].wait_recv()
         self.merge_hop(1, self.h)
         self.far[1].start()
+
+    def send_far(self):
+        self.far_right()
+        self.far_left()
 
     def finish(self, out_ref):
         for copy in self.near + self.far:
@@ -899,7 +905,7 @@
     return jnp.where(hit, 1.0, 0.0).astype(BF)
 
 
-def expert_chip(q, e, start, tab, m_ref, g_ref, wgu, wd, a_s, act_s, gp_s, dgu_s, y_s, z_s, ggt):
+def expert_chip(q, e, start, tab, m_ref, g_ref, wgu, wd, a_s, act_s, gp_s, dgu_s, y_s, z_s, ggt, between=None):
     hits = [expert_hits(tab, e, start + n, q) for n in range(PAIR)]
     chosen = jnp.concatenate([one_hot(hit) for hit in hits], axis=0)
     rows = chip_rows(q)
@@ -933,6 +939,8 @@
         gg_row = jnp.sum(jnp.where(hits[n], gg, 0.0), axis=0, keepdims=True)
         ggt[2 * q, n : n + 1] = gg_row[:, :TOK]
         ggt[2 * q + 1, n : n + 1] = gg_row[:, TOK:]
+        if n == 0 and between is not None:
+            between()
 
 
 def expert_grads(n, a_s, act_s, gp_s, dgu_s, eg, eg_o, sems):
@@ -1137,15 +1145,23 @@
                     copy.wait()
 
         q = (x + 2 + k - (k // 2) * (2 * k - 1)) % 4
-        expert_chip(q, e, 2, tab, m_ref, g_ref, wgu, wd, a_s, act_s, gp_s, dgu_s, y_s, z_s, ggt)
-
-        @pl.when(k == 2)
-        def _():
-            red.near_left()
-
-        @pl.when(k == 3)
-        def _():
-            red.near_right()
+
+        def send():
+            @pl.when(k == 1)
+            def _():
+                red.send_opp()
+
+            @pl.when(k == 2)
+            def _():
+                red.near_left()
+
+            @pl.when(k == 3)
+            def _():
+                red.near_right()
+                red.far_right()
+                red.far_left()
+
+        expert_chip(q, e, 2, tab, m_ref, g_ref, wgu, wd, a_s, act_s, gp_s, dgu_s, y_s, z_s, ggt, send)
 
         @pl.when(k == 0)
         def _():
@@ -1155,15 +1171,9 @@
         swo[k] = mix_z[pl.ds(pl.multiple_of((1 - c) * TOK, TOK), TOK)]
         red.swap(k).start()
         snd[k] = mix_z[pl.ds(pl.multiple_of(c * TOK, TOK), TOK)]
-
-        @pl.when(k == 0)
-        def _():
-            red.send_opp()
-
         return carry
 
     lax.fori_loop(0, 4, chips, 0)
-    red.send_far()
     gates, own_gates = send_gates(ggt, gg_o, e, (s_g, r_g), lsem.at[3])
     for copy in gates + [own_gates]:
         copy.start()

time: 249 us -> 244 us (0.980)
  the two profiles are of different devices: /device:TPU:33 before, /device:TPU:1 now
where the time goes in v8:
time: 244 us; the launch traced here: 239 us
  Pallas kernels  225 us (92%)
  between operations  14.3 us (6%)
    pallas_call x1, Pallas kernels, back(): comm_call(back_kernel, 'back', 6, [shape(*result) for result in results],...  72.6 us
    pallas_call x1, Pallas kernels, front(): comm_call(front_kernel, 'front', 1, results, [ANY, ANY] + [VM] * 11 + [AN...  64.7 us
    pallas_call x1, Pallas kernels, experts_last(): comm_call(experts_last_kernel, 'experts_last', 4, [shape((TOK, D)), shape...  42.3 us
    pallas_call x1, Pallas kernels, experts_first(): comm_call(experts_first_kernel, 'experts_first', 2, [shape((LENGTH, D), B...  41.7 us
  transfers between devices with their start and end apart: 1, of which 0 were waited for; matrix products, arithmetic and copies ran while one was open for 0% of the time, Pallas kernels for 48%

profile of v8, /device:TPU:1, one launch (start us, length us, event | category | flops | bytes accessed | tf_op | source)
XLA Modules:
  0.0 238.9 jit_solution(3967312646499500719)
XLA Ops:
  7.2 0.0 reduce-scatter.2.cloned.1.call-start
  7.2 64.7 %front.1 = (bf16[2048,1024]{1,0:T(8,128)(2,1)}, bf16[2048,1024]{1,0:T(8,128)(2,1)}, f32[2048,256]{1,0:T(8,128)}, bf16[2048,128]{1,0:T(8,128)(2,1)}, bf16[2048,12...) custom-call(bf16[256,1024]{1,0:T(8,128)(2,1)} %tok.1, ...), custom_call_target="tpu_custom_call" | custom-call | tf_op jit(solution)/shard_map/front/pallas_call | solution.py:755
  71.9 41.7 %experts_first.1 = (bf16[2048,1024]{1,0:T(8,128)(2,1)}, f32[8,8,256]{2,1,0:T(8,128)}, bf16[2,704,1024]{2,1,0:T(8,128)(2,1)}, bf16[2,704,1024]{2,1,0:T(8,128)(2,1...) custom-call(bf16[256,1024]{1,0:T(8,128)(2,1)} %get-tuple-element.62.m_in, ...), custom_call_target="tpu_custom_call" | custom-call | tf_op jit(solution)/shard_map/experts_first/pallas_call | solution.py:1085
  113.7 0.0 reduce-scatter.2.cloned.1.call-update
  113.7 42.3 %experts_last.1 = (f32[256,1024]{1,0:T(8,128)}, bf16[2048,1024]{1,0:T(8,128)(2,1)}, f32[8,8,256]{2,1,0:T(8,128)}, bf16[2,16,96,1024]{3,2,1,0:T(8,128)(2,1)}) custom-call(bf16[2048,1024]{1,0:T(8,128)(2,1)} %get-tuple-element.66.m_in, f32[8,8,256]{2,1,0:T(8,128)} %get-tuple-element.67.t_in, bf16[2,704,1024]{2,1,0:T(8,128)(2,1)} %get-tuple-element.68.y_in, ...), custom_call_target="tpu_custom_call" | custom-call | tf_op jit(solution)/shard_map/experts_last/pallas_call | solution.py:1211
  156.0 72.6 %back.1 = (bf16[256,1024]{1,0:T(8,128)(2,1)}, f32[256,1024]{1,0:T(8,128)}, f32[8,1024]{1,0:T(8,128)}, f32[8,512]{1,0:T(8,128)}, f32[8,512]{1,0:T(8,128)}, /*inde...) custom-call(bf16[2,4,4,96,1024]{4,3,2,1,0:T(8,128)(2,1)} %bitcast.12, ...), custom_call_target="tpu_custom_call" | custom-call | tf_op jit(solution)/shard_map/back/pallas_call | solution.py:1623
  228.6 0.0 reduce-scatter.2.cloned.1.call-done.xa_in
  228.6 3.3 %finish.1 = (bf16[256,1024]{1,0:T(8,128)(2,1)}, f32[256,1024]{1,0:T(8,128)}, f32[8,1024]{1,0:T(8,128)}, f32[8,512]{1,0:T(8,128)}, f32[8,512]{1,0:T(8,128)}, /*in...) custom-call(bf16[2,96,1024]{2,1,0:T(8,128)(2,1)} %reduce-scatter.2.c, ...), custom_call_target="tpu_custom_call" | custom-call | tf_op jit(solution)/shard_map/finish/pallas_call | solution.py:1724
Async XLA Ops:
  7.2 221.4 %reduce-scatter.2.cloned.1.call-start = ((), (), s32[]{:S(2)}) async-start(), calls=%async_computation.1 | async-start | bytes 6684672 | tf_op jit(solution)/shard_map/reduce_scatter | solution.py:1773
Sparse Core Ops, SparseCore 0:
  113.8 83.8 reduce-scatter.1

commit v9 on v8

--- a/solution.py
+++ b/solution.py
@@ -694,7 +694,7 @@
     for copy in spread_o:
         copy.wait_recv()
     other_half.start()
-    lax.fori_loop(4, EP, later, 0)
+    lax.fori_loop(4, EP, later, 0, unroll=2)
 
     leave((a_o, a_h), (lse_o, lse_h))
     for d in others:

time: 244 us -> 244 us (level)
  no operation moved by 1% of the time
where the time goes in v9:
time: 244 us; the launch traced here: 239 us
  Pallas kernels  225 us (92%)
  between operations  14.3 us (6%)
    pallas_call x1, Pallas kernels, back(): comm_call(back_kernel, 'back', 6, [shape(*result) for result in results],...  73.5 us
    pallas_call x1, Pallas kernels, front(): comm_call(front_kernel, 'front', 1, results, [ANY, ANY] + [VM] * 11 + [AN...  64.7 us
    pallas_call x1, Pallas kernels, experts_first(): comm_call(experts_first_kernel, 'experts_first', 2, [shape((LENGTH, D), B...  42 us
    pallas_call x1, Pallas kernels, experts_last(): comm_call(experts_last_kernel, 'experts_last', 4, [shape((TOK, D)), shape...  41.4 us
  transfers between devices with their start and end apart: 1, of which 0 were waited for; matrix products, arithmetic and copies ran while one was open for 0% of the time, Pallas kernels for 48%

profile of v9, /device:TPU:1, one launch (start us, length us, event | category | flops | bytes accessed | tf_op | source)
XLA Modules:
  0.0 239.3 jit_solution(8631532367281557993)
XLA Ops:
  7.2 0.0 reduce-scatter.2.cloned.1.call-start
  7.2 64.7 %front.1 = (bf16[2048,1024]{1,0:T(8,128)(2,1)}, bf16[2048,1024]{1,0:T(8,128)(2,1)}, f32[2048,256]{1,0:T(8,128)}, bf16[2048,128]{1,0:T(8,128)(2,1)}, bf16[2048,12...) custom-call(bf16[256,1024]{1,0:T(8,128)(2,1)} %tok.1, ...), custom_call_target="tpu_custom_call" | custom-call | tf_op jit(solution)/shard_map/front/pallas_call | solution.py:755
  71.9 42.0 %experts_first.1 = (bf16[2048,1024]{1,0:T(8,128)(2,1)}, f32[8,8,256]{2,1,0:T(8,128)}, bf16[2,704,1024]{2,1,0:T(8,128)(2,1)}, bf16[2,704,1024]{2,1,0:T(8,128)(2,1...) custom-call(bf16[256,1024]{1,0:T(8,128)(2,1)} %get-tuple-element.62.m_in, ...), custom_call_target="tpu_custom_call" | custom-call | tf_op jit(solution)/shard_map/experts_first/pallas_call | solution.py:1085
  113.9 0.0 reduce-scatter.2.cloned.1.call-update
  114.0 41.4 %experts_last.1 = (f32[256,1024]{1,0:T(8,128)}, bf16[2048,1024]{1,0:T(8,128)(2,1)}, f32[8,8,256]{2,1,0:T(8,128)}, bf16[2,16,96,1024]{3,2,1,0:T(8,128)(2,1)}) custom-call(bf16[2048,1024]{1,0:T(8,128)(2,1)} %get-tuple-element.66.m_in, f32[8,8,256]{2,1,0:T(8,128)} %get-tuple-element.67.t_in, bf16[2,704,1024]{2,1,0:T(8,128)(2,1)} %get-tuple-element.68.y_in, ...), custom_call_target="tpu_custom_call" | custom-call | tf_op jit(solution)/shard_map/experts_last/pallas_call | solution.py:1211
  155.4 73.5 %back.1 = (bf16[256,1024]{1,0:T(8,128)(2,1)}, f32[256,1024]{1,0:T(8,128)}, f32[8,1024]{1,0:T(8,128)}, f32[8,512]{1,0:T(8,128)}, f32[8,512]{1,0:T(8,128)}, /*inde...) custom-call(bf16[2,4,4,96,1024]{4,3,2,1,0:T(8,128)(2,1)} %bitcast.12, ...), custom_call_target="tpu_custom_call" | custom-call | tf_op jit(solution)/shard_map/back/pallas_call | solution.py:1623
  228.9 0.0 reduce-scatter.2.cloned.1.call-done.xa_in
  229.0 3.3 %finish.1 = (bf16[256,1024]{1,0:T(8,128)(2,1)}, f32[256,1024]{1,0:T(8,128)}, f32[8,1024]{1,0:T(8,128)}, f32[8,512]{1,0:T(8,128)}, f32[8,512]{1,0:T(8,128)}, /*in...) custom-call(bf16[2,96,1024]{2,1,0:T(8,128)(2,1)} %reduce-scatter.2.c, ...), custom_call_target="tpu_custom_call" | custom-call | tf_op jit(solution)/shard_map/finish/pallas_call | solution.py:1724
Async XLA Ops:
  7.2 221.8 %reduce-scatter.2.cloned.1.call-start = ((), (), s32[]{:S(2)}) async-start(), calls=%async_computation.1 | async-start | bytes 6684672 | tf_op jit(solution)/shard_map/reduce_scatter | solution.py:1773
Sparse Core Ops, SparseCore 0:
  114.1 83.7 reduce-scatter.1
